TPU v7x, 32 devices: a whole 2x2x4 slice. The times are simulated.
32 devices in a mesh: tm: 8 (over z, y), obs: 4 (over x, core).
Axes of the slice: x: 2, y: 2, z: 4, core: 2. Of those that a mesh axis runs over, the one named last changes fastest.
Arguments:
- records: bfloat16 [32768, 512], P(('tm', 'obs')), may hold values from -0.25 to 0.25
- obs_values: bfloat16 [32768], P(('tm', 'obs')), may hold values from -18 to 18
- block_day: int32 [256], P(('tm', 'obs')), may hold values from 0 to 1
- block_count: int32 [256], P(('tm', 'obs')), may hold values from 1 to 128
- propagator_matrix: float32 [512, 512], replicated, may hold values from -1 to 1
- analysis_cov: float32 [512, 512], replicated, may hold values from -0.05 to 0.1, as said below
- unattenuated_multiplier: float32 [512, 512], P('obs'), may hold values from -0.3 to 1
- damping: float32 [16, 512], P('tm'), may hold values from 0 to 1
- prior_mean: float32 [512], P('obs'), may hold values from -6 to 6
Outputs:
- filtered: float32 [16, 512], P('tm', 'obs')
- smoothed: float32 [16, 512], P('tm', 'obs')
Inputs may be any that keep to these rules, and one draw needn't show every extreme that they name: `analysis_cov`: Symmetric.
All inputs are finite; a program needn't handle non-finite values.
Results may differ from a plain program's by a relative error of at most 0.0003.
Values may be sent and summed in bfloat16 or wider, within the bound.
No kernel may reach another device: no remote copies, remote signals or barrier semaphores. Data moves between devices by JAX's collectives and lax.ppermute only.
A program may use at most 192 MiB of HBM per device.

v0:
```python
import jax
import jax.numpy as jnp
from jax import lax
from jax.sharding import PartitionSpec as P


def carried_in(x, axis, combine, identity, reverse):
    peers, position = (lax.axis_size(axis), lax.axis_index(axis))
    everything = jax.tree.map(lambda part: lax.all_gather(part, axis), x)
    start = jax.tree.map(
        lambda part, zero: jnp.broadcast_to(jnp.asarray(zero, part.dtype), part.shape), x, identity
    )

    def lap(k, before):
        at = peers - 1 - k if reverse else k
        reached = at > position if reverse else at < position
        new = combine(before, jax.tree.map(lambda part: part[at], everything))
        return jax.tree.map(lambda a, b: jnp.where(reached, a, b), new, before)

    return lax.fori_loop(0, peers, lap, start)


def from_behind(x, axis, by):
    peers = lax.axis_size(axis)
    pairs = [(i, i + by) for i in range(peers) if 0 <= i + by < peers]
    return lax.ppermute(x, axis, pairs)


def day_grams(rows_all, values_all, days_of_block, counts_of_block, day_total):
    maximal_accuracy = lax.Precision.HIGHEST
    block_total = days_of_block.shape[0]
    slot_total = rows_all.shape[0] // block_total
    width = rows_all.shape[1]
    slot_index = lax.broadcasted_iota(jnp.int32, (block_total, slot_total), 1)
    valid_mask = slot_index < counts_of_block[:, None]
    nothing = jnp.zeros((), rows_all.dtype)
    held_rows = jnp.where(
        valid_mask[:, :, None], rows_all.reshape(block_total, slot_total, width), nothing
    )
    held_values = jnp.where(valid_mask, values_all.reshape(block_total, slot_total), nothing)
    day_mark = (
        days_of_block[:, None] == lax.broadcasted_iota(jnp.int32, (block_total, day_total), 1)
    ).astype(jnp.float32)
    block_info = jnp.einsum(
        "bk,bks->bs", held_values, held_rows, preferred_element_type=jnp.float32
    )
    info = jnp.einsum("bd,bs->ds", day_mark, block_info, precision=maximal_accuracy)

    def one_day(day_number):
        chosen = (days_of_block == day_number)[:, None, None]
        picked = jnp.where(chosen, held_rows, nothing).reshape(block_total * slot_total, width)
        return lax.dot_general(
            picked, picked, (((0,), (0,)), ((), ())), preferred_element_type=jnp.float32
        )

    omega = lax.map(one_day, jnp.arange(day_total, dtype=jnp.int32))
    return (omega, info)


def fold_rows(left_rows, running, pieces):
    maximal_accuracy = lax.Precision.HIGHEST
    return (
        jnp.dot(left_rows, pieces[0], precision=maximal_accuracy),
        running[1] + jnp.dot(left_rows, pieces[1], precision=maximal_accuracy),
    )


def compose(earlier, subsequent_dates):
    maximal_accuracy = lax.Precision.HIGHEST
    return (
        jnp.dot(subsequent_dates[0], earlier[0], precision=maximal_accuracy),
        jnp.dot(subsequent_dates[0], earlier[1], precision=maximal_accuracy) + subsequent_dates[1],
    )


def local(
    records,
    obs_values,
    block_day,
    block_count,
    propagator_matrix,
    analysis_cov,
    unattenuated_multiplier,
    damping,
    prior_mean,
):
    maximal_accuracy = lax.Precision.HIGHEST
    width = propagator_matrix.shape[0]
    row_count = prior_mean.shape[0]
    day_count = damping.shape[0]
    first_row = lax.axis_index("obs") * row_count
    got_rows, got_values, got_days, got_counts = (
        lax.all_to_all(records, "tm", split_axis=0, concat_axis=0, tiled=True),
        lax.all_to_all(obs_values, "tm", split_axis=0, concat_axis=0, tiled=True),
        lax.all_to_all(block_day, "tm", split_axis=0, concat_axis=0, tiled=True),
        lax.all_to_all(block_count, "tm", split_axis=0, concat_axis=0, tiled=True),
    )
    omega_part, info_part = day_grams(got_rows, got_values, got_days, got_counts, day_count)
    trans_rows = lax.dynamic_slice_in_dim(propagator_matrix, first_row, row_count, 0)
    damp_rows = lax.dynamic_slice_in_dim(damping, first_row, row_count, 1)
    moved_rows = damp_rows[:, :, None] * trans_rows[None, :, :]
    omega, info = lax.psum((omega_part, info_part), "obs")
    cov_rows = lax.dynamic_slice_in_dim(analysis_cov, first_row, row_count, 0)
    weighted = jnp.einsum("rs,dst->drt", cov_rows, omega, precision=maximal_accuracy)
    correction = jnp.einsum(
        "drs,st->drt", weighted * damping[:, None, :], propagator_matrix, precision=maximal_accuracy
    )
    shift_rows = jnp.einsum("bt,ft->fb", cov_rows, info, precision=maximal_accuracy)
    step_rows = moved_rows - correction

    def forward_day(day_index, stacks):
        products, offsets = stacks
        left_rows = lax.dynamic_index_in_dim(step_rows, day_index, 0, keepdims=False)
        previous = (
            lax.dynamic_index_in_dim(products, day_index - 1, 0, keepdims=False),
            lax.dynamic_index_in_dim(offsets, day_index - 1, 0, keepdims=False),
        )
        initial = (
            jnp.zeros((row_count, width), jnp.float32),
            lax.dynamic_index_in_dim(shift_rows, day_index, 0, keepdims=False),
        )
        new_map, new_offset = fold_rows(
            left_rows,
            initial,
            (
                lax.all_gather(previous[0], "obs", axis=0, tiled=True),
                lax.all_gather(previous[1], "obs", axis=0, tiled=True),
            ),
        )
        return (products.at[day_index].set(new_map), offsets.at[day_index].set(new_offset))

    products, offsets = lax.fori_loop(1, day_count, forward_day, (step_rows, shift_rows))
    full_map, full_offset, prior_full = (
        lax.all_gather(products[day_count - 1], "obs", axis=0, tiled=True),
        lax.all_gather(offsets[day_count - 1], "obs", axis=0, tiled=True),
        lax.all_gather(prior_mean, "obs", axis=0, tiled=True),
    )
    identity = jnp.eye(width, dtype=jnp.float32)
    before_map, before_offset = carried_in(
        (full_map, full_offset), "tm", compose, (identity, jnp.zeros((width,), jnp.float32)), False
    )
    start_state = jnp.dot(before_map, prior_full, precision=maximal_accuracy) + before_offset
    filt_rows = jnp.einsum("drs,s->dr", products, start_state, precision=maximal_accuracy) + offsets
    filtered_whole = lax.all_gather(filt_rows, "obs", axis=1, tiled=True)
    next_first = from_behind(damping[0:1], "tm", -1)
    attenuated_successor = jnp.concatenate([damping[1:], next_first], 0)
    predicted_vector = attenuated_successor * jnp.einsum(
        "ef,qf->eq", filtered_whole, propagator_matrix, precision=maximal_accuracy
    )
    gain_rows = unattenuated_multiplier[None, :, :] * attenuated_successor[:, None, :]
    const_rows = filt_rows - jnp.einsum(
        "bt,ft->fb",
        unattenuated_multiplier,
        attenuated_successor * predicted_vector,
        precision=maximal_accuracy,
    )

    def backward_day(step_index, stacks):
        chains, consts = stacks
        day_index = day_count - 2 - step_index
        left_rows = lax.dynamic_index_in_dim(gain_rows, day_index, 0, keepdims=False)
        previous = (
            lax.dynamic_index_in_dim(chains, day_index + 1, 0, keepdims=False),
            lax.dynamic_index_in_dim(consts, day_index + 1, 0, keepdims=False),
        )
        initial = (
            jnp.zeros((row_count, width), jnp.float32),
            lax.dynamic_index_in_dim(const_rows, day_index, 0, keepdims=False),
        )
        new_map, new_offset = fold_rows(
            left_rows,
            initial,
            (
                lax.all_gather(previous[0], "obs", axis=0, tiled=True),
                lax.all_gather(previous[1], "obs", axis=0, tiled=True),
            ),
        )
        return (chains.at[day_index].set(new_map), consts.at[day_index].set(new_offset))

    chains, consts = lax.fori_loop(0, day_count - 1, backward_day, (gain_rows, const_rows))
    back_map, back_offset = (
        lax.all_gather(chains[0], "obs", axis=0, tiled=True),
        lax.all_gather(consts[0], "obs", axis=0, tiled=True),
    )
    identity_back = jnp.eye(width, dtype=jnp.float32)
    _, after_offset = carried_in(
        (back_map, back_offset),
        "tm",
        compose,
        (identity_back, jnp.zeros((width,), jnp.float32)),
        True,
    )
    smooth_rows = jnp.einsum("drs,s->dr", chains, after_offset, precision=maximal_accuracy) + consts
    return (filt_rows, smooth_rows)


def solution(mesh):
    return jax.shard_map(
        local,
        mesh=mesh,
        in_specs=(
            P(("tm", "obs"), None),
            P(("tm", "obs")),
            P(("tm", "obs")),
            P(("tm", "obs")),
            P(),
            P(),
            P("obs", None),
            P("tm", None),
            P("obs"),
        ),
        out_specs=(P("tm", "obs"), P("tm", "obs")),
        check_vma=False,
    )
```

profile of v0, /device:TPU:0, one launch (start us, length us, event | category | flops | bytes accessed | tf_op | source)
XLA Modules:
  0.0 472.1 jit_solution(3095292670469854578)
XLA Ops:
  8.6 7.3 %all-to-all-start = ((s32[8,1,1]{2,1,0:T(1,128)}), s32[8,1,1]{2,1,0:T(1,128)S(1)}, u32[]{:S(2)}, u32[]{:S(2)}) async-start(s32[8,1,1]{2,1,0:T(1,128)} %copy.25), calls=%async_computation | async-start | bytes 8192 | tf_op jit(solution)/shard_map/all_to_all | solution.py:95
  16.6 5.7 %all-to-all-done = s32[8,1,1]{2,1,0:T(1,128)S(1)} async-done(((s32[8,1,1]{2,1,0:T(1,128)}), s32[8,1,1]{2,1,0:T(1,128)S(1)}, u32[]{:S(2)}, u32[]{:S(2)}) %all-to-all-start) | async-done | bytes 64 | tf_op jit(solution)/shard_map/all_to_all | solution.py:95
  22.3 8.8 %all_to_all.39 = s32[8,1,1]{2,1,0:T(1,128)S(1)} all-to-all(s32[8,1,1]{2,1,0:T(1,128)S(1)} %copy.26), channel_id=1, replica_groups=mesh['tm'=8,'obs'=4] {'tm'}, dimensions={0} | all-to-all | bytes 64 | tf_op jit(solution)/shard_map/all_to_all | solution.py:96
  35.3 23.0 %all-to-all-done.2 = bf16[8,128,512]{2,1,0:T(8,128)(2,1)S(1)} async-done(((bf16[8,128,512]{2,1,0:T(8,128)(2,1)}), bf16[8,128,512]{2,1,0:T(8,128)(2,1)S(1)}, u32[]{:S(2)}, u32[]{:S(2)}) %all-to-all-start.2) | async-done | bytes 1048608 | tf_op jit(solution)/shard_map/all_to_all | solution.py:93
  59.2 6.1 %while.58 = (s32[]{:T(128)}, f32[2,512,512]{1,2,0:T(8,128)}, s32[2]{0:T(128)S(1)}, s32[8]{0:T(128)S(1)}, bf16[8,128,512]{1,2,0:T(8,128)(2,1)S(1)}, /*index=5*/s32[]{:T(128)}) while((s32[]{:T(128)}, f32[2,512,512]{1,2,0:T(8,128)}, s32[2]{0:T(128)S(1)}, s32[8]{0:T(128)S(1)}, bf16[8,128,512]{1,2,0:T(8,128)(2,1)S(1)}, /*index=5*/s32[]{:T(128)}) %tuple.116), condition=%wide.region_1.2_spmd, body=%wide.region_0.1_spmd.sunk | while | flops 537395200 | bytes 2097297 | solution.py:56
  66.0 49.7 %all-reduce.2.cloned.1.call-done = f32[2,512,512]{1,2,0:T(8,128)} async-done(((f32[2,512,512]{1,2,0:T(8,128)}), f32[2,512,512]{1,2,0:T(8,128)}) %all-reduce.2.cloned.1.call-update) | async-done | bytes 2097168 | tf_op jit(solution)/shard_map/psum | solution.py:102
  127.4 10.5 %all-gather.24.cloned.1.call-done = f32[1,512,512]{2,1,0:T(8,128)} async-done(((f32[1,128,512]{2,1,0:T(8,128)}), f32[1,512,512]{2,1,0:T(8,128)}) %all-gather.24.cloned.1.call-update) | async-done | bytes 1048592 | tf_op jit(solution)/shard_map/while/body/eval_jaxpr/all_gather | solution.py:126
  140.7 15.7 %all-gather.28.cloned.1.call-done = f32[1,512,512]{2,1,0:T(8,128)} async-done(((f32[1,128,512]{2,1,0:T(8,128)}), f32[1,512,512]{2,1,0:T(8,128)}) %all-gather.28.cloned.1.call-update) | async-done | bytes 1048592 | tf_op jit(solution)/shard_map/while/body/eval_jaxpr/all_gather | solution.py:174
  159.0 15.5 %all-gather.20.cloned.1.call-done = f32[512,512]{1,0:T(8,128)} async-done(((f32[128,512]{1,0:T(8,128)}), f32[512,512]{1,0:T(8,128)}) %all-gather.20.cloned.1.call-update) | async-done | bytes 1048592 | tf_op jit(solution)/shard_map/all_gather | solution.py:134
  174.7 18.2 %all-gather.22.cloned.1.call-done = f32[512,512]{1,0:T(8,128)} async-done(((f32[128,512]{1,0:T(8,128)}), f32[512,512]{1,0:T(8,128)}) %all-gather.22.cloned.1.call-update) | async-done | bytes 1048592 | tf_op jit(solution)/shard_map/all_gather | solution.py:182
  193.5 5.5 %all-to-all-start.3 = ((bf16[8,128,1]{1,2,0:T(2,128)(2,1)}), bf16[8,128,1]{1,2,0:T(2,128)(2,1)S(1)}, u32[]{:S(2)}, u32[]{:S(2)}) async-start(bf16[8,128,1]{1,2,0:T(2,128)(2,1)} %copy.30), calls=%async_computation.3 | async-start | bytes 8192 | tf_op jit(solution)/shard_map/all_to_all | solution.py:94
  199.1 5.0 %all-gather.10 = f32[4,1,128]{2,1,0:T(1,128)S(1)} all-gather(f32[1,1,128]{2,1,0:T(1,128)S(1)} %bitcast.176), channel_id=1, replica_groups=mesh['tm'=8,'obs'=4] {'obs'}, dimensions={0}, use_global_device_ids=true | all-gather | bytes 2560 | tf_op jit(solution)/shard_map/all_gather | solution.py:136
  206.0 6.1 %psum.15 = f32[2,512]{1,0:T(2,128)S(1)} all-reduce(f32[2,512]{1,0:T(2,128)S(1)} %fusion.30), channel_id=1, replica_groups=mesh['tm'=8,'obs'=4] {'obs'}, use_global_device_ids=true, to_apply=%region_3.4 | all-reduce | flops 1024 | bytes 8192 | tf_op jit(solution)/shard_map/psum | solution.py:102
  213.3 5.1 %all-gather.2 = f32[1,512]{1,0:T(1,128)S(1)} all-gather(f32[1,128]{1,0:T(1,128)S(1)} %dynamic_slice.89), channel_id=4, replica_groups=mesh['tm'=8,'obs'=4] {'obs'}, dimensions={1}, use_global_device_ids=true | all-gather | bytes 2560 | tf_op jit(solution)/shard_map/while/body/eval_jaxpr/all_gather | solution.py:127
  219.6 5.1 %all-gather.8 = f32[4,1,128]{2,1,0:T(1,128)S(1)} all-gather(f32[1,1,128]{2,1,0:T(1,128)S(1)} %bitcast.169), channel_id=1, replica_groups=mesh['tm'=8,'obs'=4] {'obs'}, dimensions={0}, use_global_device_ids=true | all-gather | bytes 2560 | tf_op jit(solution)/shard_map/all_gather | solution.py:135
  224.7 26.4 %all-gather.9 = f32[8,1,512]{2,1,0:T(1,128)S(1)} all-gather(f32[1,1,512]{2,1,0:T(1,128)S(1)} %bitcast.165), channel_id=5, replica_groups=mesh['tm'=8,'obs'=4] {'tm'}, dimensions={0}, use_global_device_ids=true | all-gather | bytes 18432 | tf_op jit(solution)/shard_map/all_gather | solution.py:9
  251.9 68.2 %all-gather.26.cloned.1.call-done = f32[4096,512]{1,0:T(8,128)} async-done(((f32[512,512]{1,0:T(8,128)}), f32[4096,512]{1,0:T(8,128)}) %all-gather.26.cloned.1.call-update) | async-done | bytes 8388624 | tf_op jit(solution)/shard_map/all_gather | solution.py:9
  320.1 43.6 %while.59 = (s32[]{:T(128)}, f32[512,512]{1,0:T(8,128)S(1)}, f32[512]{0:T(512)S(1)}, s32[]{:T(128)}, f32[8,512,512]{2,1,0:T(8,128)}, /*index=5*/f32[8,512]{1,0:T(8,128)S(1)}, s32[]{:T(128)}, s32[]{:T(128)}) while((s32[]{:T(128)}, f32[512,512]{1,0:T(8,128)S(1)}, f32[512]{0:T(512)S(1)}, s32[]{:T(128)}, f32[8,512,512]{2,1,0:T(8,128)}, ...), condition=%wide.region_5.6_spmd.clone, body=%wide.region_4.5_spmd.clone.sunk | while | flops 1614022656 | bytes 7360639 | solution.py:20
  366.3 5.3 %all_gather.71 = f32[2,512]{1,0:T(2,128)S(1)} all-gather(f32[2,128]{1,0:T(2,128)S(1)} %add.145), channel_id=1, replica_groups=mesh['tm'=8,'obs'=4] {'obs'}, dimensions={1}, use_global_device_ids=true | all-gather | bytes 5120 | tf_op jit(solution)/shard_map/all_gather | solution.py:144
  372.8 5.1 %all-gather.6 = f32[1,512]{1,0:T(1,128)S(1)} all-gather(f32[1,128]{1,0:T(1,128)S(1)} %dynamic_slice.93), channel_id=8, replica_groups=mesh['tm'=8,'obs'=4] {'obs'}, dimensions={1}, use_global_device_ids=true | all-gather | bytes 2560 | tf_op jit(solution)/shard_map/while/body/eval_jaxpr/all_gather | solution.py:175
  378.1 5.1 %all-gather.11 = f32[4,1,128]{2,1,0:T(1,128)S(1)} all-gather(f32[1,1,128]{2,1,0:T(1,128)S(1)} %bitcast.167), channel_id=1, replica_groups=mesh['tm'=8,'obs'=4] {'obs'}, dimensions={0}, use_global_device_ids=true | all-gather | bytes 2560 | tf_op jit(solution)/shard_map/all_gather | solution.py:183
  383.2 26.7 %all-gather.12 = f32[8,1,512]{2,1,0:T(1,128)S(1)} all-gather(f32[1,1,512]{2,1,0:T(1,128)S(1)} %bitcast.166), channel_id=9, replica_groups=mesh['tm'=8,'obs'=4] {'tm'}, dimensions={0}, use_global_device_ids=true | all-gather | bytes 18432 | tf_op jit(solution)/shard_map/all_gather | solution.py:9
  409.9 36.0 %all-gather.30.cloned.1.call-done = f32[4096,512]{1,0:T(8,128)} async-done(((f32[512,512]{1,0:T(8,128)}), f32[4096,512]{1,0:T(8,128)}) %all-gather.30.cloned.1.call-update) | async-done | bytes 8388624 | tf_op jit(solution)/shard_map/all_gather | solution.py:9
  445.9 18.3 %while.60 = (s32[]{:T(128)}, f32[512]{0:T(512)S(1)}, s32[]{:T(128)}, f32[8,512,512]{2,1,0:T(8,128)}, f32[8,512]{1,0:T(8,128)S(1)}, /*index=5*/s32[]{:T(128)}, s32[]{:T(128)}, s32[]{:T(128)}, s32[]{:T(128)}) while((s32[]{:T(128)}, f32[512]{0:T(512)S(1)}, s32[]{:T(128)}, f32[8,512,512]{2,1,0:T(8,128)}, f32[8,512]{1,0:T(8,128)S(1)}, ...), condition=%wide.region_7.8_spmd.clone, body=%wide.region_6.7_spmd.clone.sunk | while | flops 3147784 | bytes 1069232 | solution.py:20
  (174 shorter events, 103.0 us)
Async XLA Ops:
  7.2 58.8 %copy-start = (f32[512,512]{1,0:T(8,128)S(1)}, f32[512,512]{1,0:T(8,128)}, u32[]{:S(2)}) copy-start(f32[512,512]{1,0:T(8,128)} %param.27) | copy-start | bytes 3145732
  8.6 13.7 %all-to-all-start = ((s32[8,1,1]{2,1,0:T(1,128)}), s32[8,1,1]{2,1,0:T(1,128)S(1)}, u32[]{:S(2)}, u32[]{:S(2)}) async-start(s32[8,1,1]{2,1,0:T(1,128)} %copy.25), calls=%async_computation | async-start | bytes 8192 | tf_op jit(solution)/shard_map/all_to_all | solution.py:95
  31.1 27.1 %all-to-all-start.2 = ((bf16[8,128,512]{2,1,0:T(8,128)(2,1)}), bf16[8,128,512]{2,1,0:T(8,128)(2,1)S(1)}, u32[]{:S(2)}, u32[]{:S(2)}) async-start(bf16[8,128,512]{2,1,0:T(8,128)(2,1)} %bitcast.153), calls=%async_computation.2 | async-start | bytes 2097152 | tf_op jit(solution)/shard_map/all_to_all | solution.py:93
  34.7 81.0 %all-reduce.2.cloned.1.call-start = ((), (), s32[]{:S(2)}) async-start(), calls=%async_computation.4 | async-start | bytes 4194304 | tf_op jit(solution)/shard_map/psum | solution.py:102
  65.3 0.7 copy-start.8
  65.3 72.6 %all-gather.24.cloned.1.call-start = ((), (), s32[]{:S(2)}) async-start(), calls=%async_computation.7 | async-start | bytes 1310720 | tf_op jit(solution)/shard_map/while/body/eval_jaxpr/all_gather | solution.py:126
  119.1 7.5 %copy-start.6 = (f32[128,512]{1,0:T(8,128)S(1)}, f32[128,512]{1,0:T(8,128)}, u32[]{:S(2)}) copy-start(f32[128,512]{1,0:T(8,128)} %param.29) | copy-start | bytes 786436
  120.2 20.4 %copy-start.3 = (f32[2,128,512]{2,1,0:T(8,128)}, f32[2,128,512]{2,1,0:T(8,128)S(1)}, u32[]{:S(2)}) copy-start(f32[2,128,512]{2,1,0:T(8,128)S(1)} %convolution_subtract_fusion) | copy-start | bytes 1572868
  121.0 35.4 %all-gather.28.cloned.1.call-start = ((), (), s32[]{:S(2)}) async-start(), calls=%async_computation.9 | async-start | bytes 1310720 | tf_op jit(solution)/shard_map/while/body/eval_jaxpr/all_gather | solution.py:174
  121.0 5.5 %collective-permute-start = (f32[1,512]{1,0:T(1,128)S(1)}, f32[1,512]{1,0:T(1,128)S(1)}, u32[]{:S(2)}, u32[]{:S(2)}) collective-permute-start(f32[1,512]{1,0:T(1,128)S(1)} %get-tuple-element.466), channel_id=1, source_target_pairs={{4,0},{8,4},{12,8},{16,12},{20,16},{24,20},{28,24},{5,1},{9,5},{13... | collective-permute-start | bytes 6152 | tf_op jit(solution)/shard_map/ppermute | solution.py:26
  126.6 32.4 %copy-start.1 = (f32[2,128,512]{2,1,0:T(8,128)}, f32[2,128,512]{2,1,0:T(8,128)S(1)}, u32[]{:S(2)}) copy-start(f32[2,128,512]{2,1,0:T(8,128)S(1)} %broadcast_multiply_fusion) | copy-start | bytes 1572868
  127.4 47.2 %all-gather.20.cloned.1.call-start = ((), (), s32[]{:S(2)}) async-start(), calls=%async_computation.5 | async-start | bytes 1310720 | tf_op jit(solution)/shard_map/all_gather | solution.py:134
  140.6 52.3 %copy-start.10 = (bf16[1024]{0:T(1024)(128)(2,1)S(1)}, bf16[1024]{0:T(1024)(128)(2,1)}, u32[]{:S(2)}) copy-start(bf16[1024]{0:T(1024)(128)(2,1)} %param.24) | copy-start | bytes 6148
  140.6 52.2 %all-gather.22.cloned.1.call-start = ((), (), s32[]{:S(2)}) async-start(), calls=%async_computation.6 | async-start | bytes 1310720 | tf_op jit(solution)/shard_map/all_gather | solution.py:182
  159.0 40.2 %copy-start.11 = (f32[128]{0:T(128)S(1)}, f32[128]{0:T(128)}, u32[]{:S(2)}) copy-start(f32[128]{0:T(128)} %param.31) | copy-start | bytes 1540
  159.0 161.1 %all-gather.26.cloned.1.call-start = ((), (), s32[]{:S(2)}) async-start(), calls=%async_computation.8 | async-start | bytes 9437184 | tf_op jit(solution)/shard_map/all_gather | solution.py:9
  174.6 76.5 %copy-start.5 = (f32[128,512]{1,0:T(8,128)S(1)}, f32[128,512]{1,0:T(8,128)}, u32[]{:S(2)}) copy-start(f32[128,512]{1,0:T(8,128)} %fusion.22) | copy-start | bytes 786436
  174.6 271.3 %all-gather.30.cloned.1.call-start = ((), (), s32[]{:S(2)}) async-start(), calls=%async_computation.10 | async-start | bytes 9437184 | tf_op jit(solution)/shard_map/all_gather | solution.py:9
  193.5 12.0 %all-to-all-start.3 = ((bf16[8,128,1]{1,2,0:T(2,128)(2,1)}), bf16[8,128,1]{1,2,0:T(2,128)(2,1)S(1)}, u32[]{:S(2)}, u32[]{:S(2)}) async-start(bf16[8,128,1]{1,2,0:T(2,128)(2,1)} %copy.30), calls=%async_computation.3 | async-start | bytes 8192 | tf_op jit(solution)/shard_map/all_to_all | solution.py:94
  363.7 8.8 %copy-start.7 = (f32[128,512]{1,0:T(8,128)S(1)}, f32[128,512]{1,0:T(8,128)}, u32[]{:S(2)}) copy-start(f32[128,512]{1,0:T(8,128)} %param.29) | copy-start | bytes 786436
  363.7 14.2 %copy-start.2 = (f32[2,128,512]{2,1,0:T(8,128)S(1)}, f32[2,128,512]{2,1,0:T(8,128)}, u32[]{:S(2)}) copy-start(f32[2,128,512]{2,1,0:T(8,128)} %copy-done.1) | copy-start | bytes 1572868
  363.7 46.2 %copy-start.4 = (f32[128,512]{1,0:T(8,128)S(1)}, f32[128,512]{1,0:T(8,128)}, u32[]{:S(2)}) copy-start(f32[128,512]{1,0:T(8,128)} %fusion.20) | copy-start | bytes 786436
  366.3 79.6 %copy-start.9 = (f32[2,128]{1,0:T(2,128)}, f32[2,128]{1,0:T(2,128)S(1)}, u32[]{:S(2)}) copy-start(f32[2,128]{1,0:T(2,128)S(1)} %add.145) | copy-start | bytes 3076
Sparse Core Ops, SparseCore 0:
  65.4 50.1 all-reduce.1
  121.1 16.7 all-gather.23
  139.6 16.7 all-gather.27
  157.8 16.7 all-gather.19
  176.1 16.7 all-gather.21
  195.0 125.0 all-gather.25
  322.4 123.3 all-gather.29
where the time goes:
time: 474 us; the launch traced here: 472 us
  waiting for transfers between devices  248 us (52%)
  blocking collectives  98.7 us (21%)
  matrix products  80.7 us (17%)
  starting transfers between devices  17.9 us (4%)
  between operations  14.4 us (3%)
  local copies, waits for them, and re-layouts  8.46 us (2%)
    all_gather x2, waiting for transfers between devices, carried_in(): everything = jax.tree.map(lambda part: lax.all_gather(part, axis), x)  104 us
    all_gather x2, blocking collectives, carried_in(): everything = jax.tree.map(lambda part: lax.all_gather(part, axis), x)  53.1 us
    psum x1, waiting for transfers between devices, local(): omega, info = lax.psum((omega_part, info_part), 'obs')  49.7 us
    dot_general x16, matrix products, compose(): jnp.dot(subsequent_dates[0], earlier[1], precision=maximal_accuracy)  35.3 us
    dot_general x8, matrix products, compose(): jnp.dot(subsequent_dates[0], earlier[0], precision=maximal_accuracy)  24.5 us
    all_to_all x1, waiting for transfers between devices, local(): lax.all_to_all(records, 'tm', split_axis=0, concat_axis=0, tiled=True)  23 us
    all_gather x1, waiting for transfers between devices, local(): lax.all_gather(chains[0], 'obs', axis=0, tiled=True)  18.2 us
    all_gather x1, waiting for transfers between devices, backward_day(): lax.all_gather(previous[0], 'obs', axis=0, tiled=True)  15.7 us
  transfers between devices with their start and end apart: 11, of which 11 were waited for; matrix products, arithmetic and copies ran while one was open for 13% of the time, Pallas kernels for 0%

commit v1 on v0

v1 whole, which is shorter than its diff:
```python
import functools

import jax
import jax.numpy as jnp
from jax import lax
from jax.experimental import pallas as pl
from jax.experimental.pallas import tpu as pltpu
from jax.sharding import PartitionSpec as P

LANES = 128
F32, BF16 = jnp.float32, jnp.bfloat16
VMEM = pl.BlockSpec(memory_space=pltpu.VMEM)
SMEM = pl.BlockSpec(memory_space=pltpu.SMEM)


def run(body, out, ins, scratch=(), limit=32, flops=0):
    specs = [x[1] if isinstance(x, tuple) else VMEM for x in ins]
    arrays = [x[0] if isinstance(x, tuple) else x for x in ins]
    moved = sum(a.size * a.dtype.itemsize for a in arrays)
    return pl.pallas_call(
        body,
        out_shape=[jax.ShapeDtypeStruct(s, d) for s, d in out],
        in_specs=specs,
        out_specs=[VMEM] * len(out),
        scratch_shapes=list(scratch),
        compiler_params=pltpu.CompilerParams(vmem_limit_bytes=limit * 1024 * 1024),
        cost_estimate=pl.CostEstimate(flops=flops, bytes_accessed=moved, transcendentals=0),
    )(*arrays)


def triangle(width):
    parts = width // LANES
    return [(i, j) for i in range(parts) for j in range(i + 1)]


def split(x):
    hi = x.astype(BF16)
    return hi, (x - hi.astype(F32)).astype(BF16)


def mm(x, hi, lo):
    xhi, xlo = split(x)
    dot = functools.partial(jnp.dot, preferred_element_type=F32)
    return dot(xhi, hi) + (dot(xlo, hi) + dot(xhi, lo))


def mv(x, hi, lo):
    wide = jnp.broadcast_to(x, (8, x.shape[1]))
    row = lax.broadcasted_iota(jnp.int32, wide.shape, 0)
    top = wide.astype(BF16).astype(F32)
    both = jnp.where(row == 0, top, jnp.where(row == 1, wide - top, 0.0)).astype(BF16)
    first = jnp.dot(both, hi, preferred_element_type=F32)
    second = jnp.dot(both, lo, preferred_element_type=F32)
    return first[0:1] + (first[1:2] + second[0:1])


def gram_kernel(ids, rows, meta, prior, keep, send, turned, marks):
    blocks, _, slots = meta.shape
    width = rows.shape[1]
    tiles = triangle(width)
    info_at = len(tiles)
    mine = (ids[1] % 2).astype(F32)
    group = min(blocks, 8)
    half = 2 * LANES

    def one(first, fresh):
        span = group * slots
        start = first * slots
        for k in range(group):
            at = slice(k * slots, (k + 1) * slots)
            valid = lax.broadcasted_iota(jnp.int32, (1, slots), 1).astype(F32) < meta[first + k, 2:3, :]
            here = meta[first + k, 1:2, :] == mine
            values = meta[first + k, 0:1, :]
            kept = jnp.where(valid & here, 1.0, 0.0)
            sent = jnp.where(valid & ~here, 1.0, 0.0)
            marks[:, at] = jnp.concatenate(
                [kept, sent, kept * values, sent * values, jnp.zeros((12, slots), F32)], 0
            ).astype(BF16)
        source = rows[pl.ds(start, span), :]
        turned[...] = source.T
        info = jnp.dot(marks[...], source, preferred_element_type=F32)
        for which, out in ((0, keep), (1, send)):
            for top in range(0, width, half):
                left = turned[top : top + half, :] * marks[which : which + 1, :]
                block = jnp.dot(left, source[:, : top + half], preferred_element_type=F32)
                for n, (i, j) in enumerate(tiles):
                    if top <= i * LANES < top + half:
                        r = i * LANES - top
                        piece = block[r : r + LANES, j * LANES : (j + 1) * LANES]
                        out[n] = piece if fresh else out[n] + piece
            for j in range(width // LANES):
                piece = info[2 + which : 3 + which, j * LANES : (j + 1) * LANES]
                out[info_at, j : j + 1, :] = piece if fresh else out[info_at, j : j + 1, :] + piece

    for out in (keep, send):
        out[info_at] = jnp.zeros((LANES, LANES), F32)
    if blocks == group:
        one(0, True)
    else:
        for out in (keep, send):
            out[...] = jnp.zeros(out.shape, F32)

        @pl.loop(0, blocks // group)
        def _(g):
            one(g * group, False)

    for out in (keep, send):
        for q in range(width // LANES):
            out[info_at, 4 + q : 5 + q, :] = jnp.where(ids[1] == q, prior[...], 0.0)


def chip_kernel(keep, got, chip, pay):
    last = keep.shape[0] - 1
    for n in range(last):
        total = keep[n] + got[n]
        chip[n] = total
        pay[n] = total.astype(BF16)
    small = keep[last, 0:16, :] + got[last, 0:16, :]
    chip[last] = jnp.zeros((LANES, LANES), F32)
    chip[last, 0:16, :] = small
    pay[last] = jnp.zeros((LANES, LANES), BF16)
    for part in range(3):
        piece = small.astype(BF16)
        pay[last, 16 * part : 16 * part + 16, :] = piece
        small = small - piece.astype(F32)


def day_kernel(chip, got, day):
    last = chip.shape[0] - 1
    for n in range(last):
        day[n] = chip[n] + got[n].astype(F32)
    day[last] = jnp.zeros((LANES, LANES), F32)
    small = [got[last, 16 * part : 16 * part + 16, :].astype(F32) for part in range(3)]
    day[last, 0:16, :] = chip[last, 0:16, :] + (small[0] + (small[1] + small[2]))


def prep_kernel(ids, m0, m1, m2, m3, trans, cov, pt, pthi, ptlo, mthi, mtlo, chi, clo):
    peers = 4
    rows = m0.shape[0]
    for step, part in enumerate((m0, m1, m2, m3)):
        owner = lax.rem(ids[1] - step + peers, peers)
        at = pl.ds(pl.multiple_of(owner * rows, rows), rows)
        hi, lo = split(part[...].T)
        mthi[:, at] = hi
        mtlo[:, at] = lo
    whole = trans[...].T
    pt[...] = whole
    pthi[...], ptlo[...] = split(whole)
    chi[...], clo[...] = split(cov[...])


def first_kernel(ids, own, other, damping, pthi, ptlo, chi, clo, omhi, omlo, info, start, y):
    width = pthi.shape[0]
    tiles = triangle(width)
    mine = ids[1] % 2
    for slot, src in ((mine, own), (1 - mine, other)):
        for n, (i, j) in enumerate(tiles):
            piece = src[n]
            hi, lo = split(piece)
            omhi[slot, i * LANES : (i + 1) * LANES, j * LANES : (j + 1) * LANES] = hi
            omlo[slot, i * LANES : (i + 1) * LANES, j * LANES : (j + 1) * LANES] = lo
            if i != j:
                hi, lo = split(piece.T)
                omhi[slot, j * LANES : (j + 1) * LANES, i * LANES : (i + 1) * LANES] = hi
                omlo[slot, j * LANES : (j + 1) * LANES, i * LANES : (i + 1) * LANES] = lo
        for j in range(width // LANES):
            info[slot, :, j * LANES : (j + 1) * LANES] = src[len(tiles), j : j + 1, :]
    state = jnp.concatenate(
        [own[len(tiles), 4 + q : 5 + q, :] for q in range(width // LANES)], 1
    )
    start[...] = jnp.where(ids[0] == 0, state, 0.0)
    for day in range(2):
        moved = mv(state, pthi[...], ptlo[...]) * damping[day : day + 1, :]
        gap = mv(moved, omhi[day], omlo[day]) - info[day]
        state = moved - mv(gap, chi[...], clo[...])
    y[...] = state


def maps_kernel(omhi, omlo, info, chi, clo, pt, damping, b1hi, b1lo, b2hi, b2lo, bchi, bclo, off):
    parts = ((b1hi, b1lo), (b2hi, b2lo))
    for day in range(2):
        moved = pt[...] * damping[day : day + 1, :]
        taken = mm(moved, omhi[day], omlo[day])
        step = moved - mm(taken, chi[...], clo[...])
        parts[day][0][...], parts[day][1][...] = split(step)
        off[day : day + 1, :] = mv(info[day], chi[...], clo[...])
    both = jnp.dot(b1hi[...], b2hi[...], preferred_element_type=F32) + (
        jnp.dot(b1lo[...], b2hi[...], preferred_element_type=F32)
        + jnp.dot(b1hi[...], b2lo[...], preferred_element_type=F32)
    )
    bchi[...], bclo[...] = split(both)
    off[2:3, :] = mv(off[0:1, :], b2hi[...], b2lo[...]) + off[1:2, :]


def hop_kernel(acc, got, bchi, bclo, off, total, y):
    state = acc[...] + got[...]
    total[...] = state
    y[...] = mv(state, bchi[...], bclo[...]) + off[2:3, :]


def last_kernel(acc, got, b1hi, b1lo, b2hi, b2lo, off, out):
    state = acc[...] + got[...]
    one = mv(state, b1hi[...], b1lo[...]) + off[0:1, :]
    two = mv(one, b2hi[...], b2lo[...]) + off[1:2, :]
    both = jnp.concatenate([one, two], 0)
    for c in range(out.shape[0]):
        out[c] = both


def back_kernel(ids, states, meta, pthi, ptlo, mthi, mtlo, filt, smooth, f, d, const):
    spans, days, width = states.shape
    total = spans * days
    parts = width // LANES
    for c in range(spans):
        f[c * days : (c + 1) * days, :] = states[c]
        for k in range(days):
            t = c * days + k - 1
            if t >= 0:
                for j in range(parts):
                    r = 8 + k * parts + j
                    d[t : t + 1, j * LANES : (j + 1) * LANES] = meta[c, r : r + 1, :]
    d[total - 1 : total, :] = jnp.zeros((1, width), F32)
    ahead = d[...] * mm(f[...], pthi[...], ptlo[...])
    const[...] = f[...] - mm(d[...] * ahead, mthi[...], mtlo[...])

    def step(k, state):
        t = total - 2 - k
        new = const[pl.ds(t, 1), :] + mv(d[pl.ds(t, 1), :] * state, mthi[...], mtlo[...])
        const[pl.ds(t, 1), :] = new
        return new

    lax.fori_loop(0, total - 1, step, const[total - 1 : total, :], unroll=total <= 16)
    for k in range(days):
        row = pl.ds(ids[0] * days + k, 1)
        for whole, out in ((f, filt), (const, smooth)):
            line = whole[row, :]
            mine = line[:, 0:LANES]
            for q in range(1, parts):
                mine = jnp.where(ids[1] == q, line[:, q * LANES : (q + 1) * LANES], mine)
            out[k : k + 1, :] = mine


def local(
    records,
    obs_values,
    block_day,
    block_count,
    propagator_matrix,
    analysis_cov,
    unattenuated_multiplier,
    damping,
    prior_mean,
):
    spans, peers = lax.axis_size("tm"), lax.axis_size("obs")
    blocks = block_day.shape[0]
    slots = records.shape[0] // blocks
    width = records.shape[1]
    days = damping.shape[0]
    assert peers == 4 and days == 2 and slots == LANES and blocks == spans
    ids = jnp.stack([lax.axis_index("tm"), lax.axis_index("obs")]).astype(jnp.int32)
    exchange = functools.partial(lax.all_to_all, axis_name="tm", split_axis=0, concat_axis=0, tiled=True)

    def swap(x, bit):
        return lax.ppermute(x, "obs", [(i, i ^ bit) for i in range(peers)])

    got_rows = exchange(records)
    lane = (blocks, 1, slots)
    meta = jnp.concatenate(
        [
            obs_values.reshape(lane).astype(F32),
            jnp.broadcast_to(block_day[:, None, None], lane).astype(F32),
            jnp.broadcast_to(block_count[:, None, None], lane).astype(F32),
            jnp.zeros((blocks, 5, slots), F32),
            jnp.broadcast_to(damping.reshape(1, days * width // LANES, LANES), (blocks, 8, LANES)),
        ],
        1,
    )
    got_meta = exchange(meta)
    gain = [unattenuated_multiplier] + [
        lax.ppermute(unattenuated_multiplier, "obs", [(i, (i + s) % peers) for i in range(peers)])
        for s in range(1, peers)
    ]
    full, parts = (width, width), len(triangle(width)) + 1
    pt, pthi, ptlo, mthi, mtlo, chi, clo = run(
        prep_kernel,
        [(full, F32)] + [(full, BF16)] * 6,
        [(ids, SMEM), *gain, propagator_matrix, analysis_cov],
    )
    packed = (parts, LANES, LANES)
    keep, send = run(
        gram_kernel,
        [(packed, F32)] * 2,
        [(ids, SMEM), got_rows, got_meta, prior_mean.reshape(1, -1)],
        [pltpu.VMEM((width, min(blocks, 8) * slots), BF16), pltpu.VMEM((16, min(blocks, 8) * slots), BF16)],
        flops=4 * width * width * blocks * slots,
    )
    chip, pay = run(chip_kernel, [(packed, F32), (packed, BF16)], [keep, swap(send, 1)])
    (own,) = run(day_kernel, [(packed, F32)], [chip, swap(pay, 2)])
    other = swap(own, 1)
    omhi, omlo, info, acc, y = run(
        first_kernel,
        [((days,) + full, BF16)] * 2 + [((days, 1, width), F32), ((1, width), F32), ((1, width), F32)],
        [(ids, SMEM), own, other, damping, pthi, ptlo, chi, clo],
    )
    b1hi, b1lo, b2hi, b2lo, bchi, bclo, off = run(
        maps_kernel,
        [(full, BF16)] * 6 + [((8, width), F32)],
        [omhi, omlo, info, chi, clo, pt, damping],
        flops=30 * width**3,
    )
    for k in range(spans - 1):
        got = lax.ppermute(y, "tm", [(k, k + 1)])
        if k < spans - 2:
            acc, y = run(hop_kernel, [((1, width), F32)] * 2, [acc, got, bchi, bclo, off])
    (sent,) = run(
        last_kernel, [((spans, days, width), F32)], [acc, got, b1hi, b1lo, b2hi, b2lo, off]
    )
    states = exchange(sent)
    total = spans * days
    out = ((days, LANES), F32)
    return run(
        back_kernel,
        [out, out],
        [(ids, SMEM), states, got_meta, pthi, ptlo, mthi, mtlo],
        [pltpu.VMEM((total, width), F32)] * 3,
    )


def solution(mesh):
    mapped = jax.shard_map(
        local,
        mesh=mesh,
        in_specs=(
            P(("tm", "obs"), None),
            P(("tm", "obs")),
            P(("tm", "obs")),
            P(("tm", "obs")),
            P(),
            P(),
            P("obs", None),
            P("tm", None),
            P("obs"),
        ),
        out_specs=(P("tm", "obs"), P("tm", "obs")),
        check_vma=False,
    )
    return lambda *args: tuple(mapped(*args))
```

time: 474 us -> 125 us (0.26)
  waiting for transfers between devices: 248 us -> 45.1 us
  matrix products: 80.7 us -> 0 us
  blocking collectives: 98.7 us -> 42.8 us
  Pallas kernels: 0 us -> 17.2 us
  between operations: 14.4 us -> 0.89 us
  local copies, waits for them, and re-layouts: 8.46 us -> 2.33 us
    all_gather x6 -> x0, waiting for transfers between devices: 164 us -> none  [the longest x2 104 us: carried_in(): everything = jax.tree.map(lambda part: lax.all_gather(part, axis), x)]
    all_gather x8 -> x0, blocking collectives: 83.8 us -> none  [the longest x2 53.1 us: carried_in(): everything = jax.tree.map(lambda part: lax.all_gather(part, axis), x)]
    dot_general x40 -> x0, matrix products: 80.7 us -> none  [the longest x16 35.3 us: compose(): jnp.dot(subsequent_dates[0], earlier[1], precision=maximal_accuracy)]
    psum x1 -> x0, waiting for transfers between devices: 49.7 us -> none  [local(): omega, info = lax.psum((omega_part, info_part), 'obs')]
    all_to_all x1 -> x2, blocking collectives: 8.82 us -> 42.8 us  [the longest x1 28.9 us: local(): states = exchange(sent)]
    pallas_call x0 -> x14, Pallas kernels: none -> 17.2 us  [run(): pl.pallas_call(body, out_shape=[jax.ShapeDtypeStruct(s, d) for s, d in ou...]
    ppermute x1 -> x13, waiting for transfers between devices: 4.18 us -> 20.5 us  [the longest x3 11.1 us: swap(): return lax.ppermute(x, 'obs', [(i, i ^ bit) for i in range(peers)])]
    all_to_all x3 -> x1, starting transfers between devices: 16.4 us -> 3.56 us  [local(): got_rows = exchange(records)]
  transfers between devices with their start and end apart: 11 -> 14, of which waited for: 11 -> 6; matrix products, arithmetic and copies ran while one was open for 13% -> 0% of each run, Pallas kernels for 0% -> 5%
where the time goes in v1:
time: 125 us
  waiting for transfers between devices  45.1 us (36%)
  blocking collectives  42.8 us (34%)
  Pallas kernels  17.2 us (14%)
  starting transfers between devices  15.9 us (13%)
  local copies, waits for them, and re-layouts  2.33 us (2%)
    all_to_all x1, blocking collectives, local(): states = exchange(sent)  28.9 us
    all_to_all x1, waiting for transfers between devices, local(): got_rows = exchange(records)  24.6 us
    pallas_call x14, Pallas kernels, run(): pl.pallas_call(body, out_shape=[jax.ShapeDtypeStruct(s, d) for s, d in ou...  17.2 us
    all_to_all x1, blocking collectives, local(): got_meta = exchange(meta)  14 us
    ppermute x3, waiting for transfers between devices, swap(): return lax.ppermute(x, 'obs', [(i, i ^ bit) for i in range(peers)])  11.1 us
    ppermute x3, waiting for transfers between devices, local(): lax.ppermute(unattenuated_multiplier, 'obs', [(i, (i + s) % peers) for i...  9.29 us
    ppermute x7, starting transfers between devices, local(): got = lax.ppermute(y, 'tm', [(k, k + 1)])  7.39 us
    all_to_all x1, starting transfers between devices, local(): got_rows = exchange(records)  3.56 us
  transfers between devices with their start and end apart: 14, of which 6 were waited for; matrix products, arithmetic and copies ran while one was open for 0% of the time, Pallas kernels for 5%

profile of v1, /device:TPU:0, one launch (start us, length us, event | category | flops | bytes accessed | tf_op | source)
XLA Modules:
  0.0 125.0 jit_solution(4390802672715117693)
XLA Ops:
  2.2 14.0 %all_to_all.21.meta = f32[8,16,128]{2,1,0:T(8,128)S(1)} all-to-all(f32[8,16,128]{2,1,0:T(8,128)S(1)} %concatenate.3), channel_id=1, replica_groups=mesh['tm'=8,'obs'=4] {'tm'}, dimensions={0} | all-to-all | bytes 131072 | tf_op jit(solution)/shard_map/all_to_all | solution.py:278
  16.2 3.6 %all-to-all-start = ((bf16[8,128,512]{2,1,0:T(8,128)(2,1)}), bf16[8,128,512]{2,1,0:T(8,128)(2,1)S(1)}, u32[]{:S(2)}, u32[]{:S(2)}) async-start(bf16[8,128,512]{2,1,0:T(8,128)(2,1)} %bitcast.8), calls=%async_computation | async-start | bytes 2097152 | tf_op jit(solution)/shard_map/all_to_all | solution.py:266
  19.8 24.6 %all-to-all-done = bf16[8,128,512]{2,1,0:T(8,128)(2,1)S(1)} async-done(((bf16[8,128,512]{2,1,0:T(8,128)(2,1)}), bf16[8,128,512]{2,1,0:T(8,128)(2,1)S(1)}, u32[]{:S(2)}, u32[]{:S(2)}) %all-to-all-start) | async-done | bytes 1048608 | tf_op jit(solution)/shard_map/all_to_all | solution.py:266
  45.2 1.7 %shard_map.104 = (f32[11,128,128]{2,1,0:T(8,128)S(1)}, f32[11,128,128]{2,1,0:T(8,128)S(1)}) custom-call(s32[2]{0:T(128)S(1)} %pad_add_fusion.ids, bf16[1024,512]{1,0:T(8,128)(2,1)S(1)} %bitcast.6, f32[8,16,128]{2,1,0:T(8,128)S(1)} %all_to_all.21.meta, f32[1,128]{1,0:T(1,128)S(1)} %bitcast.7), custom_call_target="tpu_custom_call" | custom-call | flops 1073741824 | bytes 1114632 | tf_op jit(solution)/shard_map/pallas_call | solution.py:20
  46.9 2.2 %collective-permute-done.got = f32[11,128,128]{2,1,0:T(8,128)S(1)} collective-permute-done((f32[11,128,128]{2,1,0:T(8,128)S(1)}, f32[11,128,128]{2,1,0:T(8,128)S(1)}, u32[]{:S(2)}, u32[]{:S(2)}) %collective-permute-start) | collective-permute-done | bytes 720928 | tf_op jit(solution)/shard_map/ppermute | solution.py:264
  49.2 1.6 %collective-permute-start.1 = (bf16[11,128,128]{2,1,0:T(8,128)(2,1)S(1)}, bf16[11,128,128]{2,1,0:T(8,128)(2,1)S(1)}, u32[]{:S(2)}, u32[]{:S(2)}) collective-permute-start(bf16[11,128,128]{2,1,0:T(8,128)(2,1)S(1)} %get-tuple-element.40), channel_id=1, source_target_pairs={{0,2},{1,3},{2,0},{3,1},{4,6},{5,7},{6,4},{7,5},{8,10},{9,11},{10,... | collective-permute-start | bytes 1081352 | tf_op jit(solution)/shard_map/ppermute | solution.py:264
  50.8 9.0 %collective-permute-done.1.got = bf16[11,128,128]{2,1,0:T(8,128)(2,1)S(1)} collective-permute-done((bf16[11,128,128]{2,1,0:T(8,128)(2,1)S(1)}, bf16[11,128,128]{2,1,0:T(8,128)(2,1)S(1)}, u32[]{:S(2)}, u32[]{:S(2)}) %collective-permute-start.1) | collective-permute-done | bytes 360480 | tf_op jit(solution)/shard_map/ppermute | solution.py:264
  59.9 0.8 copy-done.2
  60.7 1.5 %collective-permute-start.4 = (f32[128,512]{1,0:T(8,128)S(1)}, f32[128,512]{1,0:T(8,128)S(1)}, u32[]{:S(2)}, u32[]{:S(2)}) collective-permute-start(f32[128,512]{1,0:T(8,128)S(1)} %copy-done.2), channel_id=1, source_target_pairs={{0,2},{1,3},{2,0},{3,1},{4,6},{5,7},{6,4},{7,5},{8,10},{9,11},{10,... | collective-permute-start | bytes 786440 | tf_op jit(solution)/shard_map/ppermute | solution.py:280
  62.2 1.7 %collective-permute-start.5 = (f32[128,512]{1,0:T(8,128)S(1)}, f32[128,512]{1,0:T(8,128)S(1)}, u32[]{:S(2)}, u32[]{:S(2)}) collective-permute-start(f32[128,512]{1,0:T(8,128)S(1)} %copy-done.2), channel_id=1, source_target_pairs={{0,3},{1,0},{2,1},{3,2},{4,7},{5,4},{6,5},{7,6},{8,11},{9,8},{10,9... | collective-permute-start | bytes 786440 | tf_op jit(solution)/shard_map/ppermute | solution.py:280
  63.9 6.0 %collective-permute-done.4.m2 = f32[128,512]{1,0:T(8,128)S(1)} collective-permute-done((f32[128,512]{1,0:T(8,128)S(1)}, f32[128,512]{1,0:T(8,128)S(1)}, u32[]{:S(2)}, u32[]{:S(2)}) %collective-permute-start.4) | collective-permute-done | bytes 262176 | tf_op jit(solution)/shard_map/ppermute | solution.py:280
  69.9 3.0 %collective-permute-done.3.m1 = f32[128,512]{1,0:T(8,128)S(1)} collective-permute-done((f32[128,512]{1,0:T(8,128)S(1)}, f32[128,512]{1,0:T(8,128)S(1)}, u32[]{:S(2)}, u32[]{:S(2)}) %collective-permute-start.3) | collective-permute-done | bytes 262176 | tf_op jit(solution)/shard_map/ppermute | solution.py:280
  73.2 1.4 %shard_map.107 = (f32[512,512]{1,0:T(8,128)S(1)}, bf16[512,512]{1,0:T(8,128)(2,1)S(1)}, bf16[512,512]{1,0:T(8,128)(2,1)S(1)}, bf16[512,512]{1,0:T(8,128)(2,1)S(1...) custom-call(s32[2]{0:T(128)S(1)} %pad_add_fusion.ids, ...), custom_call_target="tpu_custom_call" | custom-call | bytes 3145736 | tf_op jit(solution)/shard_map/pallas_call | solution.py:20
  74.7 2.2 %shard_map.108 = (bf16[2,512,512]{2,1,0:T(8,128)(2,1)S(1)}, bf16[2,512,512]{2,1,0:T(8,128)(2,1)S(1)}, f32[2,1,512]{2,1,0:T(1,128)S(1)}, f32[1,512]{1,0:T(1,128)S(1)}, f32[1,512]{1,0:T(1,128)S(1)}) custom-call(s32[2]{0:T(128)S(1)} %pad_add_fusion.ids, f32[11,128,128]{2,1,0:T(8,128)S(1)} %shard_map.106.own, f32[11,128,128]{2,1,0:T(8,128)S(1)} %collective-permute-done.2.other, ...), custom_call_target="tpu_custom_call" | custom-call | bytes 3543048 | tf_op jit(solution)/shard_map/pallas_call | solution.py:20
  76.8 3.1 %collective-permute-start.6 = (f32[1,512]{1,0:T(1,128)S(1)}, f32[1,512]{1,0:T(1,128)S(1)}, u32[]{:S(2)}, u32[]{:S(2)}) collective-permute-start(f32[1,512]{1,0:T(1,128)S(1)} %get-tuple-element.46), channel_id=1, source_target_pairs={{0,4},{1,5},{2,6},{3,7}} | collective-permute-start | bytes 6152 | tf_op jit(solution)/shard_map/ppermute | solution.py:312
  80.0 4.8 %shard_map.109 = (bf16[512,512]{1,0:T(8,128)(2,1)S(1)}, bf16[512,512]{1,0:T(8,128)(2,1)S(1)}, bf16[512,512]{1,0:T(8,128)(2,1)S(1)}, bf16[512,512]{1,0:T(8,128)(2...) custom-call(bf16[2,512,512]{2,1,0:T(8,128)(2,1)S(1)} %get-tuple-element.47.omhi, ...), custom_call_target="tpu_custom_call" | custom-call | flops 4026531840 | bytes 4202496 | tf_op jit(solution)/shard_map/pallas_call | solution.py:20
  85.0 0.7 collective-permute-start.7
  85.9 0.7 collective-permute-start.8
  86.9 0.7 collective-permute-start.9
  87.8 0.7 collective-permute-start.10
  88.7 0.7 collective-permute-start.11
  89.7 0.7 collective-permute-start.12
  90.9 28.9 %all_to_all.22.states = f32[8,2,512]{2,1,0:T(2,128)S(1)} all-to-all(f32[8,2,512]{2,1,0:T(2,128)S(1)} %shard_map.116), channel_id=1, replica_groups=mesh['tm'=8,'obs'=4] {'tm'}, dimensions={0} | all-to-all | bytes 65536 | tf_op jit(solution)/shard_map/all_to_all | solution.py:318
  119.7 5.2 %shard_map.117 = (f32[2,128]{1,0:T(2,128)}, f32[2,128]{1,0:T(2,128)}) custom-call(s32[2]{0:T(128)S(1)} %pad_add_fusion.ids, f32[8,2,512]{2,1,0:T(2,128)S(1)} %all_to_all.22.states, f32[8,16,128]{2,1,0:T(8,128)S(1)} %all_to_all.21.meta, bf16[512,512]{1,0:T(8,128)(2,1)S(1)} %get-tuple-element.41.pthi, bf16[512,512]{1,0:T(8,128)(2,1)S(1)} %get-tuple-element.42.ptlo, ...), custom_call_target="tpu_custom_call" | custom-call | bytes 2195464 | tf_op jit(solution)/shard_map/pallas_call | solution.py:20
  (44 shorter events, 4.6 us)
Async XLA Ops:
  0.6 0.7 copy-start.6
  0.6 0.7 copy-start.5
  1.3 0.7 copy-start.3
  16.2 28.3 %all-to-all-start = ((bf16[8,128,512]{2,1,0:T(8,128)(2,1)}), bf16[8,128,512]{2,1,0:T(8,128)(2,1)S(1)}, u32[]{:S(2)}, u32[]{:S(2)}) async-start(bf16[8,128,512]{2,1,0:T(8,128)(2,1)} %bitcast.8), calls=%async_computation | async-start | bytes 2097152 | tf_op jit(solution)/shard_map/all_to_all | solution.py:266
  44.5 0.7 copy-start.4
  46.8 2.3 %collective-permute-start = (f32[11,128,128]{2,1,0:T(8,128)S(1)}, f32[11,128,128]{2,1,0:T(8,128)S(1)}, u32[]{:S(2)}, u32[]{:S(2)}) collective-permute-start(f32[11,128,128]{2,1,0:T(8,128)S(1)} %get-tuple-element.38), channel_id=1, source_target_pairs={{0,1},{1,0},{2,3},{3,2},{4,5},{5,4},{6,7},{7,6},{8,9},{9,8},{10,11... | collective-permute-start | bytes 2162696 | tf_op jit(solution)/shard_map/ppermute | solution.py:264
  49.1 24.1 %copy-start.1 = (f32[512,512]{1,0:T(8,128)S(1)}, f32[512,512]{1,0:T(8,128)}, u32[]{:S(2)}) copy-start(f32[512,512]{1,0:T(8,128)} %cov.1) | copy-start | bytes 3145732
  49.2 24.0 %copy-start = (f32[512,512]{1,0:T(8,128)S(1)}, f32[512,512]{1,0:T(8,128)}, u32[]{:S(2)}) copy-start(f32[512,512]{1,0:T(8,128)} %trans.1) | copy-start | bytes 3145732
  49.2 10.5 %collective-permute-start.1 = (bf16[11,128,128]{2,1,0:T(8,128)(2,1)S(1)}, bf16[11,128,128]{2,1,0:T(8,128)(2,1)S(1)}, u32[]{:S(2)}, u32[]{:S(2)}) collective-permute-start(bf16[11,128,128]{2,1,0:T(8,128)(2,1)S(1)} %get-tuple-element.40), channel_id=1, source_target_pairs={{0,2},{1,3},{2,0},{3,1},{4,6},{5,7},{6,4},{7,5},{8,10},{9,11},{10,... | collective-permute-start | bytes 1081352 | tf_op jit(solution)/shard_map/ppermute | solution.py:264
  59.7 1.0 copy-start.2
  59.8 14.9 %collective-permute-start.2 = (f32[11,128,128]{2,1,0:T(8,128)S(1)}, f32[11,128,128]{2,1,0:T(8,128)S(1)}, u32[]{:S(2)}, u32[]{:S(2)}) collective-permute-start(f32[11,128,128]{2,1,0:T(8,128)S(1)} %shard_map.106.own), channel_id=1, source_target_pairs={{0,1},{1,0},{2,3},{3,2},{4,5},{5,4},{6,7},{7,6},{8,9},{9,8},{10,11... | collective-permute-start | bytes 2162696 | tf_op jit(solution)/shard_map/ppermute | solution.py:264
  60.7 9.2 %collective-permute-start.4 = (f32[128,512]{1,0:T(8,128)S(1)}, f32[128,512]{1,0:T(8,128)S(1)}, u32[]{:S(2)}, u32[]{:S(2)}) collective-permute-start(f32[128,512]{1,0:T(8,128)S(1)} %copy-done.2), channel_id=1, source_target_pairs={{0,2},{1,3},{2,0},{3,1},{4,6},{5,7},{6,4},{7,5},{8,10},{9,11},{10,... | collective-permute-start | bytes 786440 | tf_op jit(solution)/shard_map/ppermute | solution.py:280
  62.2 10.7 %collective-permute-start.3 = (f32[128,512]{1,0:T(8,128)S(1)}, f32[128,512]{1,0:T(8,128)S(1)}, u32[]{:S(2)}, u32[]{:S(2)}) collective-permute-start(f32[128,512]{1,0:T(8,128)S(1)} %copy-done.2), channel_id=1, source_target_pairs={{0,1},{1,2},{2,3},{3,0},{4,5},{5,6},{6,7},{7,4},{8,9},{9,10},{10,1... | collective-permute-start | bytes 786440 | tf_op jit(solution)/shard_map/ppermute | solution.py:280
  62.2 11.0 %collective-permute-start.5 = (f32[128,512]{1,0:T(8,128)S(1)}, f32[128,512]{1,0:T(8,128)S(1)}, u32[]{:S(2)}, u32[]{:S(2)}) collective-permute-start(f32[128,512]{1,0:T(8,128)S(1)} %copy-done.2), channel_id=1, source_target_pairs={{0,3},{1,0},{2,1},{3,2},{4,7},{5,4},{6,5},{7,6},{8,11},{9,8},{10,9... | collective-permute-start | bytes 786440 | tf_op jit(solution)/shard_map/ppermute | solution.py:280
  76.8 8.0 %collective-permute-start.6 = (f32[1,512]{1,0:T(1,128)S(1)}, f32[1,512]{1,0:T(1,128)S(1)}, u32[]{:S(2)}, u32[]{:S(2)}) collective-permute-start(f32[1,512]{1,0:T(1,128)S(1)} %get-tuple-element.46), channel_id=1, source_target_pairs={{0,4},{1,5},{2,6},{3,7}} | collective-permute-start | bytes 6152 | tf_op jit(solution)/shard_map/ppermute | solution.py:312
  85.0 0.7 collective-permute-start.7
  85.9 0.7 collective-permute-start.8
  86.9 0.7 collective-permute-start.9
  87.8 0.7 collective-permute-start.10
  88.7 0.7 collective-permute-start.11
  89.7 0.7 collective-permute-start.12

commit v2 on v1

v2 whole, which is shorter than its diff:
```python
import functools

import jax
import jax.numpy as jnp
from jax import lax
from jax.experimental import pallas as pl
from jax.experimental.pallas import tpu as pltpu
from jax.sharding import PartitionSpec as P

LANES = 128
F32, BF16 = jnp.float32, jnp.bfloat16
VMEM = pl.BlockSpec(memory_space=pltpu.VMEM)
SMEM = pl.BlockSpec(memory_space=pltpu.SMEM)


def run(body, out, ins, scratch=(), limit=32, flops=0):
    specs = [x[1] if isinstance(x, tuple) else VMEM for x in ins]
    arrays = [x[0] if isinstance(x, tuple) else x for x in ins]
    moved = sum(a.size * a.dtype.itemsize for a in arrays)
    return pl.pallas_call(
        body,
        out_shape=[jax.ShapeDtypeStruct(s, d) for s, d in out],
        in_specs=specs,
        out_specs=[VMEM] * len(out),
        scratch_shapes=list(scratch),
        compiler_params=pltpu.CompilerParams(vmem_limit_bytes=limit * 1024 * 1024),
        cost_estimate=pl.CostEstimate(flops=flops, bytes_accessed=moved, transcendentals=0),
    )(*arrays)


def triangle(width):
    parts = width // LANES
    return [(i, j) for i in range(parts) for j in range(i + 1)]


def split(x):
    hi = x.astype(BF16)
    return hi, (x - hi.astype(F32)).astype(BF16)


def mm(x, hi, lo):
    xhi, xlo = split(x)
    dot = functools.partial(jnp.dot, preferred_element_type=F32)
    return dot(xhi, hi) + (dot(xlo, hi) + dot(xhi, lo))


def mv(x, hi, lo):
    wide = jnp.broadcast_to(x, (8, x.shape[1]))
    row = lax.broadcasted_iota(jnp.int32, wide.shape, 0)
    top = wide.astype(BF16).astype(F32)
    both = jnp.where(row == 0, top, jnp.where(row == 1, wide - top, 0.0)).astype(BF16)
    first = jnp.dot(both, hi, preferred_element_type=F32)
    second = jnp.dot(both, lo, preferred_element_type=F32)
    return first[0:1] + (first[1:2] + second[0:1])


def parts3(x):
    out = []
    for _ in range(3):
        piece = x.astype(BF16).astype(F32)
        out.append(piece)
        x = x - piece
    return out


def owner_plane(span):
    return 1 + span % 2


EXTRA = 16


def pack_kernel(day, count, rows, values, prior, damping, out):
    blocks = out.shape[0]
    slots = out.shape[1] - EXTRA
    width = out.shape[2]
    first, second, third = parts3(prior[...])
    below = jnp.concatenate(
        [jnp.concatenate([second, third, jnp.zeros((1, width - 2 * LANES), F32)], 1)]
        + parts3(damping[...])
        + [jnp.zeros((EXTRA - 8, width), F32)],
        0,
    )
    for k in range(blocks):
        out[k, 0:slots, :] = rows[k * slots : (k + 1) * slots, :]
        line = jnp.concatenate(
            [
                values[k : k + 1, :],
                jnp.full((1, LANES), day[k], jnp.int32).astype(F32),
                jnp.full((1, LANES), count[k], jnp.int32).astype(F32),
                first,
            ],
            1,
        )
        out[k, slots : slots + EXTRA, :] = jnp.concatenate([line, below], 0).astype(BF16)


def gram_kernel(got, gain, own, extra, pay, prior, gain_out, turned, marks):
    blocks = got.shape[0]
    slots = got.shape[1] - EXTRA
    width = got.shape[2]
    chunks = width // LANES
    tiles = triangle(width)
    group = min(blocks, 8)
    half = 2 * LANES
    gain_out[...] = gain[...]
    extra[...] = jnp.zeros(extra.shape, F32)

    def one(first, fresh):
        for k in range(group):
            at = slice(k * slots, (k + 1) * slots)
            line = got[first + k, slots : slots + EXTRA, :].astype(F32)
            valid = lax.broadcasted_iota(jnp.int32, (1, slots), 1).astype(F32) < line[0:1, 2 * LANES : 3 * LANES]
            day = line[0:1, LANES : 2 * LANES]
            values = line[0:1, 0:LANES]
            kept = [jnp.where(valid & (day == d), 1.0, 0.0) for d in (0.0, 1.0)]
            marks[:, at] = jnp.concatenate(
                kept + [kept[0] * values, kept[1] * values, jnp.zeros((12, slots), F32)], 0
            ).astype(BF16)
            turned[:, at] = got[first + k, 0:slots, :].T
        source = jnp.concatenate([got[first + k, 0:slots, :] for k in range(group)], 0)
        info = jnp.dot(marks[...], source, preferred_element_type=F32)
        for d in range(2):
            for top in range(0, width, half):
                left = turned[top : top + half, :] * marks[d : d + 1, :]
                block = jnp.dot(left, source[:, : top + half], preferred_element_type=F32)
                for n, (i, j) in enumerate(tiles):
                    if top <= i * LANES < top + half:
                        r = i * LANES - top
                        piece = block[r : r + LANES, j * LANES : (j + 1) * LANES]
                        at = d * len(tiles) + n
                        own[at] = piece if fresh else own[at] + piece
            for j in range(chunks):
                piece = info[2 + d : 3 + d, j * LANES : (j + 1) * LANES]
                r = 12 * d + j
                extra[r : r + 1, :] = piece if fresh else extra[r : r + 1, :] + piece

    if blocks == group:
        one(0, True)
    else:
        own[...] = jnp.zeros(own.shape, F32)

        @pl.loop(0, blocks // group)
        def _(g):
            one(g * group, False)

    for d in range(2):
        for part, piece in enumerate(parts3(extra[12 * d : 12 * d + chunks, :])):
            extra[12 * d + 4 * part : 12 * d + 4 * part + chunks, :] = piece
    for q in range(chunks):
        line = got[q, slots : slots + EXTRA, :].astype(F32)
        prior[:, q * LANES : (q + 1) * LANES] = line[0:1, 3 * LANES : 4 * LANES] + (
            line[1:2, 0:LANES] + line[1:2, LANES : 2 * LANES]
        )
    for y in range(blocks // 4):
        line = got[4 * y, slots : slots + EXTRA, :].astype(F32)
        for k in range(6):
            for j in range(chunks):
                r = 24 + 24 * y + 4 * k + j
                extra[r : r + 1, :] = line[2 + k : 3 + k, j * LANES : (j + 1) * LANES]
    for n in range(own.shape[0]):
        pay[n] = own[n].astype(BF16)
    for n in range(extra.shape[0] // LANES):
        pay[own.shape[0] + n] = extra[n * LANES : (n + 1) * LANES, :].astype(BF16)


def prep_kernel(ids, m0, m1, m2, m3, trans, cov, pt, pthi, ptlo, mthi, mtlo, chi, clo):
    peers = 4
    rows = m0.shape[0]
    for step, part in enumerate((m0, m1, m2, m3)):
        owner = lax.rem(ids[2] - step + peers, peers)
        at = pl.ds(pl.multiple_of(owner * rows, rows), rows)
        hi, lo = split(part[...].T)
        mthi[:, at] = hi
        mtlo[:, at] = lo
    whole = trans[...].T
    pt[...] = whole
    pthi[...], ptlo[...] = split(whole)
    chi[...], clo[...] = split(cov[...])


def two_days(state, damping, pthi, ptlo, omhi, omlo, info, chi, clo):
    for day in range(2):
        moved = mv(state, pthi[...], ptlo[...]) * damping[day : day + 1, :]
        gap = mv(moved, omhi[day], omlo[day]) - info[day]
        state = moved - mv(gap, chi[...], clo[...])
    return state


def owner_kernel(
    ids, own, extra, g1, g2, g3, prior, pthi, ptlo, chi, clo, omhi, omlo, info, mine, start, y, table, small
):
    planes = 4
    width = pthi.shape[0]
    chunks = width // LANES
    tiles = triangle(width)
    got = (g1, g2, g3)
    for day in range(2):
        for n, (i, j) in enumerate(tiles):
            at = day * len(tiles) + n
            piece = own[at] + (g1[at].astype(F32) + (g2[at].astype(F32) + g3[at].astype(F32)))
            hi, lo = split(piece)
            omhi[day, i * LANES : (i + 1) * LANES, j * LANES : (j + 1) * LANES] = hi
            omlo[day, i * LANES : (i + 1) * LANES, j * LANES : (j + 1) * LANES] = lo
            if i != j:
                hi, lo = split(piece.T)
                omhi[day, j * LANES : (j + 1) * LANES, i * LANES : (i + 1) * LANES] = hi
                omlo[day, j * LANES : (j + 1) * LANES, i * LANES : (i + 1) * LANES] = lo
    for s in range(planes):
        if s == 0:
            small[0] = extra[...]
        else:
            for n in range(extra.shape[0] // LANES):
                small[s, n * LANES : (n + 1) * LANES, :] = got[s - 1][own.shape[0] + n].astype(F32)

    def row(s, first, gap):
        return jnp.concatenate(
            [
                small[s, first + j : first + j + 1, :]
                + (
                    small[s, first + gap + j : first + gap + j + 1, :]
                    + small[s, first + 2 * gap + j : first + 2 * gap + j + 1, :]
                )
                for j in range(chunks)
            ],
            1,
        )

    for day in range(2):
        info[day] = row(0, 12 * day, 4) + (row(1, 12 * day, 4) + (row(2, 12 * day, 4) + row(3, 12 * day, 4)))
    held = table.shape[0] // 2 // planes
    for s in range(planes):
        plane = lax.rem(ids[0] + s, planes)
        for k in range(held):
            for day in range(2):
                table[pl.ds(2 * (plane * held + k) + day, 1), :] = row(s, 24 + 24 * k + 4 * day, 8)
    for day in range(2):
        mine[day : day + 1, :] = table[pl.ds(2 * ids[1] + day, 1), :]
    state = prior[...]
    start[...] = jnp.where((ids[1] == 0) & (ids[0] == owner_plane(0)), state, 0.0)
    y[...] = two_days(state, mine, pthi, ptlo, omhi, omlo, info, chi, clo)


def direct_kernel(acc, got, mine, pthi, ptlo, omhi, omlo, info, chi, clo, total, y):
    state = acc[...] + got[...]
    total[...] = state
    y[...] = two_days(state, mine, pthi, ptlo, omhi, omlo, info, chi, clo)


def maps_kernel(after, omhi, omlo, info, chi, clo, pt, damping, b1hi, b1lo, b2hi, b2lo, bchi, bclo, off):
    parts = ((b1hi, b1lo), (b2hi, b2lo))
    for day in range(2):
        moved = pt[...] * damping[day : day + 1, :]
        taken = mm(moved, omhi[day], omlo[day])
        step = moved - mm(taken, chi[...], clo[...])
        parts[day][0][...], parts[day][1][...] = split(step)
        off[day : day + 1, :] = mv(info[day], chi[...], clo[...])
    both = jnp.dot(b1hi[...], b2hi[...], preferred_element_type=F32) + (
        jnp.dot(b1lo[...], b2hi[...], preferred_element_type=F32)
        + jnp.dot(b1hi[...], b2lo[...], preferred_element_type=F32)
    )
    bchi[...], bclo[...] = split(both)
    off[2:3, :] = mv(off[0:1, :], b2hi[...], b2lo[...]) + off[1:2, :]


def hop_kernel(acc, got, bchi, bclo, off, total, y):
    state = acc[...] + got[...]
    total[...] = state
    y[...] = mv(state, bchi[...], bclo[...]) + off[2:3, :]


def last_kernel(acc, got, b1hi, b1lo, b2hi, b2lo, off, damping, out):
    state = acc[...] + got[...]
    one = mv(state, b1hi[...], b1lo[...]) + off[0:1, :]
    two = mv(one, b2hi[...], b2lo[...]) + off[1:2, :]
    both = jnp.concatenate([one, two, damping[...]], 0)
    for c in range(out.shape[0]):
        out[c] = both


def back_kernel(ids, states, pthi, ptlo, mthi, mtlo, filt, smooth, f, d, const):
    total, width = f.shape
    spans = total // 2
    chunks = width // LANES
    for c in range(spans):
        one = states[owner_plane(c) * spans + c]
        f[2 * c : 2 * c + 2, :] = one[0:2]
        if c:
            d[2 * c - 1 : 2 * c + 1, :] = one[2:4]
        else:
            d[0:1, :] = one[3:4]
    d[total - 1 : total, :] = jnp.zeros((1, width), F32)
    ahead = d[...] * mm(f[...], pthi[...], ptlo[...])
    const[...] = f[...] - mm(d[...] * ahead, mthi[...], mtlo[...])

    def step(k, state):
        t = total - 2 - k
        new = const[pl.ds(t, 1), :] + mv(d[pl.ds(t, 1), :] * state, mthi[...], mtlo[...])
        const[pl.ds(t, 1), :] = new
        return new

    lax.fori_loop(0, total - 1, step, const[total - 1 : total, :], unroll=total <= 16)
    for k in range(2):
        row = pl.ds(ids[3] * 2 + k, 1)
        for whole, out in ((f, filt), (const, smooth)):
            line = whole[row, :]
            mine = line[:, 0:LANES]
            for q in range(1, chunks):
                mine = jnp.where(ids[2] == q, line[:, q * LANES : (q + 1) * LANES], mine)
            out[k : k + 1, :] = mine


def local(
    records,
    obs_values,
    block_day,
    block_count,
    propagator_matrix,
    analysis_cov,
    unattenuated_multiplier,
    damping,
    prior_mean,
):
    planes, held, peers = (lax.axis_size(a) for a in ("z", "y", "obs"))
    spans = planes * held
    blocks = block_day.shape[0]
    slots = records.shape[0] // blocks
    width = records.shape[1]
    days = damping.shape[0]
    assert planes == peers == 4 and days == 2 and slots == LANES and blocks == spans
    z, y, o = (lax.axis_index(a) for a in ("z", "y", "obs"))
    ids = jnp.stack([z, y * peers + o, o, z * held + y]).astype(jnp.int32)
    everyone = ("z", "y", "obs")

    def owner(span):
        return owner_plane(span) * spans + span

    tiles = len(triangle(width))
    extras = -(-(24 + 24 * held) // LANES)
    full, row = (width, width), ((1, width), F32)
    (sent,) = run(
        pack_kernel,
        [((blocks, slots + EXTRA, width), BF16)],
        [
            (block_day, SMEM),
            (block_count, SMEM),
            records,
            obs_values.astype(F32).reshape(blocks, slots),
            prior_mean.reshape(1, -1),
            damping,
        ],
    )
    got = lax.all_to_all(sent, ("y", "obs"), split_axis=0, concat_axis=0, tiled=True)
    span_slots = min(blocks, 8) * slots
    own, extra, pay, prior, gain = run(
        gram_kernel,
        [
            ((2 * tiles, LANES, LANES), F32),
            ((extras * LANES, LANES), F32),
            ((2 * tiles + extras, LANES, LANES), BF16),
            row,
            (unattenuated_multiplier.shape, F32),
        ],
        [got, unattenuated_multiplier],
        [pltpu.VMEM((width, span_slots), BF16), pltpu.VMEM((16, span_slots), BF16)],
        flops=4 * width * width * blocks * slots,
    )
    plane_sums = [
        lax.ppermute(
            pay, everyone, [((owner_plane(p) + s) % planes * spans + p, owner(p)) for p in range(spans)]
        )
        for s in range(1, planes)
    ]
    gains = [gain] + [
        lax.ppermute(gain, "obs", [(i, (i + s) % peers) for i in range(peers)]) for s in range(1, peers)
    ]
    pt, pthi, ptlo, mthi, mtlo, chi, clo = run(
        prep_kernel,
        [(full, F32)] + [(full, BF16)] * 6,
        [(ids, SMEM), *gains, propagator_matrix, analysis_cov],
    )
    omhi, omlo, info, mine, acc, y = run(
        owner_kernel,
        [((days,) + full, BF16)] * 2 + [((days, 1, width), F32), ((days, width), F32), row, row],
        [(ids, SMEM), own, extra, *plane_sums, prior, pthi, ptlo, chi, clo],
        [pltpu.VMEM((spans * days, width), F32), pltpu.VMEM((planes, extras * LANES, LANES), F32)],
    )
    for k in range(spans - 1):
        received = lax.ppermute(y, everyone, [(owner(k), owner(k + 1))])
        if k == 0:
            acc, y = run(
                direct_kernel, [row, row], [acc, received, mine, pthi, ptlo, omhi, omlo, info, chi, clo]
            )
            b1hi, b1lo, b2hi, b2lo, bchi, bclo, off = run(
                maps_kernel,
                [(full, BF16)] * 6 + [((8, width), F32)],
                [y, omhi, omlo, info, chi, clo, pt, mine],
                flops=30 * width**3,
            )
        elif k < spans - 2:
            acc, y = run(hop_kernel, [row, row], [acc, received, bchi, bclo, off])
    (answer,) = run(
        last_kernel,
        [((spans * peers, 2 * days, width), F32)],
        [acc, received, b1hi, b1lo, b2hi, b2lo, off, mine],
    )
    states = lax.all_to_all(answer, everyone, split_axis=0, concat_axis=0, tiled=True)
    out = ((days, LANES), F32)
    return run(
        back_kernel,
        [out, out],
        [(ids, SMEM), states, pthi, ptlo, mthi, mtlo],
        [pltpu.VMEM((spans * days, width), F32)] * 3,
    )


def solution(mesh):
    spans, peers = mesh.devices.shape
    finer = jax.sharding.Mesh(mesh.devices.reshape(peers, spans // peers, peers), ("z", "y", "obs"))
    tm = ("z", "y")
    mapped = jax.shard_map(
        local,
        mesh=finer,
        in_specs=(
            P(("z", "y", "obs"), None),
            P(("z", "y", "obs")),
            P(("z", "y", "obs")),
            P(("z", "y", "obs")),
            P(),
            P(),
            P("obs", None),
            P(tm, None),
            P("obs"),
        ),
        out_specs=(P(tm, "obs"), P(tm, "obs")),
        check_vma=False,
    )
    return lambda *args: tuple(mapped(*args))
```

time: 125 us -> 105 us (0.84)
  waiting for transfers between devices: 45.1 us -> 10.5 us
  blocking collectives: 42.8 us -> 50.5 us
  Pallas kernels: 17.2 us -> 20.7 us
  local copies, waits for them, and re-layouts: 2.33 us -> 5.53 us
    all_to_all x1 -> x0, waiting for transfers between devices: 24.6 us -> none  [local(): got_rows = exchange(records)]
    ppermute x13, waiting for transfers between devices: 20.5 us -> 10.5 us  [the longest x3 10.5 us: local(): lax.ppermute(gain, 'obs', [(i, (i + s) % peers) for i in range(peers)])]
    all_to_all x2, blocking collectives: 42.8 us -> 50.5 us  [the longest x1 28.7 us: local(): lax.all_to_all(answer, everyone, split_axis=0, concat_axis=0, tiled=True)]
    all_to_all x1 -> x0, starting transfers between devices: 3.56 us -> none  [local(): got_rows = exchange(records)]
    pallas_call x14 -> x13, Pallas kernels: 17.2 us -> 20.7 us  [run(): pl.pallas_call(body, out_shape=[jax.ShapeDtypeStruct(s, d) for s, d in ou...]
    unnamed x14 -> x20, local copies, waits for them, and re-layouts: 2.14 us -> 5.53 us
    ppermute x13, starting transfers between devices: 12.3 us -> 15.7 us  [the longest x3 7.38 us: local(): lax.ppermute(pay, everyone, [((owner_plane(p) + s) % planes * spans + p,...]
  transfers between devices with their start and end apart: 14 -> 13, of which waited for: 6 -> 3; matrix products, arithmetic and copies ran while one was open for 0% -> 0% of each run, Pallas kernels for 5% -> 6%
where the time goes in v2:
time: 105 us; the launch traced here: 104 us
  blocking collectives  50.5 us (48%)
  Pallas kernels  20.7 us (20%)
  starting transfers between devices  15.7 us (15%)
  waiting for transfers between devices  10.5 us (10%)
  local copies, waits for them, and re-layouts  5.53 us (5%)
    all_to_all x1, blocking collectives, local(): lax.all_to_all(answer, everyone, split_axis=0, concat_axis=0, tiled=True)  28.7 us
    all_to_all x1, blocking collectives, local(): lax.all_to_all(sent, ('y', 'obs'), split_axis=0, concat_axis=0, tiled=True)  21.9 us
    pallas_call x13, Pallas kernels, run(): pl.pallas_call(body, out_shape=[jax.ShapeDtypeStruct(s, d) for s, d in ou...  20.7 us
    ppermute x3, waiting for transfers between devices, local(): lax.ppermute(gain, 'obs', [(i, (i + s) % peers) for i in range(peers)])  10.5 us
    ppermute x3, starting transfers between devices, local(): lax.ppermute(pay, everyone, [((owner_plane(p) + s) % planes * spans + p,...  7.38 us
    unnamed x20, local copies, waits for them, and re-layouts  5.53 us
    ppermute x7, starting transfers between devices, local(): received = lax.ppermute(y, everyone, [(owner(k), owner(k + 1))])  4.86 us
    ppermute x3, starting transfers between devices, local(): lax.ppermute(gain, 'obs', [(i, (i + s) % peers) for i in range(peers)])  3.43 us
  transfers between devices with their start and end apart: 13, of which 3 were waited for; matrix products, arithmetic and copies ran while one was open for 0% of the time, Pallas kernels for 6%

profile of v2, /device:TPU:0, one launch (start us, length us, event | category | flops | bytes accessed | tf_op | source)
XLA Modules:
  0.0 104.5 jit_solution(17372928710239307737)
XLA Ops:
  1.3 1.2 %copy-done = bf16[1024,512]{1,0:T(8,128)(2,1)S(1)} copy-done((bf16[1024,512]{1,0:T(8,128)(2,1)S(1)}, bf16[1024,512]{1,0:T(8,128)(2,1)}, u32[]{:S(2)}) %copy-start) | copy-done | bytes 1048600
  5.8 21.9 %all_to_all.10.got = bf16[8,144,512]{2,1,0:T(8,128)(2,1)S(1)} all-to-all(bf16[8,144,512]{2,1,0:T(8,128)(2,1)S(1)} %shard_map.104), channel_id=1, replica_groups=mesh['z'=4,'y'=2,'obs'=4] {'y','obs'}, dimensions={0} | all-to-all | bytes 2359296 | tf_op jit(solution)/shard_map/all_to_all | solution.py:353
  27.7 2.1 %shard_map.105 = (f32[20,128,128]{2,1,0:T(8,128)S(1)}, f32[128,128]{1,0:T(8,128)S(1)}, bf16[21,128,128]{2,1,0:T(8,128)(2,1)}, f32[1,512]{1,0:T(1,128)S(1)}, f32[128,512]{1,0:T(8,128)}) custom-call(bf16[8,144,512]{2,1,0:T(8,128)(2,1)S(1)} %all_to_all.10.got, f32[128,512]{1,0:T(8,128)S(1)} %copy-done.9), custom_call_target="tpu_custom_call" | custom-call | flops 1073741824 | bytes 1441792 | tf_op jit(solution)/shard_map/pallas_call | solution.py:20
  29.8 4.3 %collective-permute-start.2 = (bf16[21,128,128]{2,1,0:T(8,128)(2,1)}, bf16[21,128,128]{2,1,0:T(8,128)(2,1)}, u32[]{:S(2)}, u32[]{:S(2)}) collective-permute-start(bf16[21,128,128]{2,1,0:T(8,128)(2,1)} %get-tuple-element.41), channel_id=1, source_target_pairs={{0,8},{9,17},{2,10},{11,19},{4,12},{13,21},{6,14},{15,23}} | collective-permute-start | bytes 2064392 | tf_op jit(solution)/shard_map/ppermute | solution.py:369
  34.2 1.5 %collective-permute-start.1 = (bf16[21,128,128]{2,1,0:T(8,128)(2,1)}, bf16[21,128,128]{2,1,0:T(8,128)(2,1)}, u32[]{:S(2)}, u32[]{:S(2)}) collective-permute-start(bf16[21,128,128]{2,1,0:T(8,128)(2,1)} %get-tuple-element.41), channel_id=1, source_target_pairs={{24,8},{1,17},{26,10},{3,19},{28,12},{5,21},{30,14},{7,23}} | collective-permute-start | bytes 2064392 | tf_op jit(solution)/shard_map/ppermute | solution.py:369
  35.7 1.5 %collective-permute-start = (bf16[21,128,128]{2,1,0:T(8,128)(2,1)}, bf16[21,128,128]{2,1,0:T(8,128)(2,1)}, u32[]{:S(2)}, u32[]{:S(2)}) collective-permute-start(bf16[21,128,128]{2,1,0:T(8,128)(2,1)} %get-tuple-element.41), channel_id=1, source_target_pairs={{16,8},{25,17},{18,10},{27,19},{20,12},{29,21},{22,14},{31,23}} | collective-permute-start | bytes 2064392 | tf_op jit(solution)/shard_map/ppermute | solution.py:369
  37.7 1.3 %collective-permute-start.4 = (f32[128,512]{1,0:T(8,128)}, f32[128,512]{1,0:T(8,128)}, u32[]{:S(2)}, u32[]{:S(2)}) collective-permute-start(f32[128,512]{1,0:T(8,128)} %get-tuple-element.43.m0), channel_id=1, source_target_pairs={{0,2},{1,3},{2,0},{3,1},{4,6},{5,7},{6,4},{7,5},{8,10},{9,11},{10,... | collective-permute-start | bytes 786440 | tf_op jit(solution)/shard_map/ppermute | solution.py:375
  39.0 5.3 %collective-permute-done.5.m3 = f32[128,512]{1,0:T(8,128)S(1)} collective-permute-done((f32[128,512]{1,0:T(8,128)}, f32[128,512]{1,0:T(8,128)S(1)}, u32[]{:S(2)}, u32[]{:S(2)}) %collective-permute-start.5) | collective-permute-done | bytes 262176 | tf_op jit(solution)/shard_map/ppermute | solution.py:375
  44.3 0.7 copy-done.3
  45.0 1.6 %collective-permute-start.3 = (f32[128,512]{1,0:T(8,128)}, f32[128,512]{1,0:T(8,128)}, u32[]{:S(2)}, u32[]{:S(2)}) collective-permute-start(f32[128,512]{1,0:T(8,128)} %get-tuple-element.43.m0), channel_id=1, source_target_pairs={{0,1},{1,2},{2,3},{3,0},{4,5},{5,6},{6,7},{7,4},{8,9},{9,10},{10,1... | collective-permute-start | bytes 786440 | tf_op jit(solution)/shard_map/ppermute | solution.py:375
  46.7 2.9 %collective-permute-done.4.m2 = f32[128,512]{1,0:T(8,128)} collective-permute-done((f32[128,512]{1,0:T(8,128)}, f32[128,512]{1,0:T(8,128)}, u32[]{:S(2)}, u32[]{:S(2)}) %collective-permute-start.4) | collective-permute-done | bytes 262176 | tf_op jit(solution)/shard_map/ppermute | solution.py:375
  49.6 2.2 %collective-permute-done.3.m1 = f32[128,512]{1,0:T(8,128)} collective-permute-done((f32[128,512]{1,0:T(8,128)}, f32[128,512]{1,0:T(8,128)}, u32[]{:S(2)}, u32[]{:S(2)}) %collective-permute-start.3) | collective-permute-done | bytes 262176 | tf_op jit(solution)/shard_map/ppermute | solution.py:375
  51.9 0.9 copy-done.4
  52.8 2.0 %shard_map.106 = (f32[512,512]{1,0:T(8,128)S(1)}, bf16[512,512]{1,0:T(8,128)(2,1)S(1)}, bf16[512,512]{1,0:T(8,128)(2,1)S(1)}, bf16[512,512]{1,0:T(8,128)(2,1)S(1...) custom-call(s32[4]{0:T(128)S(1)} %pad_add_fusion.ids, ...), custom_call_target="tpu_custom_call" | custom-call | bytes 3145744 | tf_op jit(solution)/shard_map/pallas_call | solution.py:20
  54.9 3.1 %shard_map.107 = (bf16[2,512,512]{2,1,0:T(8,128)(2,1)S(1)}, bf16[2,512,512]{2,1,0:T(8,128)(2,1)S(1)}, f32[2,1,512]{2,1,0:T(1,128)S(1)}, f32[2,512]{1,0:T(2,128)S...) custom-call(s32[4]{0:T(128)S(1)} %pad_add_fusion.ids, f32[20,128,128]{2,1,0:T(8,128)S(1)} %get-tuple-element.39.own, ...), custom_call_target="tpu_custom_call" | custom-call | bytes 5539856 | tf_op jit(solution)/shard_map/pallas_call | solution.py:20
  58.6 1.4 %shard_map.108 = (f32[1,512]{1,0:T(1,128)S(1)}, f32[1,512]{1,0:T(1,128)S(1)}) custom-call(f32[1,512]{1,0:T(1,128)S(1)} %get-tuple-element.48.acc, f32[1,512]{1,0:T(1,128)S(1)} %collective-permute-done.6.got, f32[2,512]{1,0:T(2,128)S(1)} %get-tuple-element.50.mine.damping, bf16[512,512]{1,0:T(8,128)(2,1)S(1)} %get-tuple-element.44.pthi, ...), custom_call_target="tpu_custom_call" | custom-call | bytes 4206592 | tf_op jit(solution)/shard_map/pallas_call | solution.py:20
  60.7 4.7 %shard_map.109 = (bf16[512,512]{1,0:T(8,128)(2,1)S(1)}, bf16[512,512]{1,0:T(8,128)(2,1)S(1)}, bf16[512,512]{1,0:T(8,128)(2,1)S(1)}, bf16[512,512]{1,0:T(8,128)(2...) custom-call(f32[1,512]{1,0:T(1,128)S(1)} %get-tuple-element.55.after, ...), custom_call_target="tpu_custom_call" | custom-call | flops 4026531840 | bytes 4204544 | tf_op jit(solution)/shard_map/pallas_call | solution.py:20
  65.6 0.7 collective-permute-start.8
  66.6 0.7 collective-permute-start.9
  67.5 0.7 collective-permute-start.10
  68.4 0.7 collective-permute-start.11
  69.4 0.7 collective-permute-start.12
  70.6 28.7 %all_to_all.11.states = f32[32,4,512]{2,1,0:T(4,128)S(1)} all-to-all(f32[32,4,512]{2,1,0:T(4,128)S(1)} %shard_map.115), channel_id=1, replica_groups=mesh['z'=4,'y'=2,'obs'=4] {'z','y','obs'}, dimensions={0} | all-to-all | bytes 524288 | tf_op jit(solution)/shard_map/all_to_all | solution.py:407
  99.3 5.2 %shard_map.116 = (f32[2,128]{1,0:T(2,128)}, f32[2,128]{1,0:T(2,128)}) custom-call(s32[4]{0:T(128)S(1)} %pad_add_fusion.ids, f32[32,4,512]{2,1,0:T(4,128)S(1)} %all_to_all.11.states, bf16[512,512]{1,0:T(8,128)(2,1)S(1)} %get-tuple-element.44.pthi, bf16[512,512]{1,0:T(8,128)(2,1)S(1)} %get-tuple-element.45.ptlo, bf16[512,512]{1,0:T(8,128)(2,1)S(1)} %get-tuple-element.74.mthi, ...), custom_call_target="tpu_custom_call" | custom-call | bytes 2359312 | tf_op jit(solution)/shard_map/pallas_call | solution.py:20
  (39 shorter events, 7.4 us)
Async XLA Ops:
  1.3 1.2 %copy-start = (bf16[1024,512]{1,0:T(8,128)(2,1)S(1)}, bf16[1024,512]{1,0:T(8,128)(2,1)}, u32[]{:S(2)}) copy-start(bf16[1024,512]{1,0:T(8,128)(2,1)} %rows.1) | copy-start | bytes 3145732
  2.5 0.7 copy-start.5
  3.2 0.7 copy-start.6
  3.9 0.7 copy-start.7
  4.5 0.7 copy-start.8
  5.8 21.9 %copy-start.9 = (f32[128,512]{1,0:T(8,128)S(1)}, f32[128,512]{1,0:T(8,128)}, u32[]{:S(2)}) copy-start(f32[128,512]{1,0:T(8,128)} %gain.1) | copy-start | bytes 786436
  27.7 24.2 %copy-start.1 = (f32[512,512]{1,0:T(8,128)S(1)}, f32[512,512]{1,0:T(8,128)}, u32[]{:S(2)}) copy-start(f32[512,512]{1,0:T(8,128)} %trans.1) | copy-start | bytes 3145732
  27.7 24.2 %copy-start.2 = (f32[512,512]{1,0:T(8,128)S(1)}, f32[512,512]{1,0:T(8,128)}, u32[]{:S(2)}) copy-start(f32[512,512]{1,0:T(8,128)} %cov.1) | copy-start | bytes 3145732
  29.8 25.0 %collective-permute-start.2 = (bf16[21,128,128]{2,1,0:T(8,128)(2,1)}, bf16[21,128,128]{2,1,0:T(8,128)(2,1)}, u32[]{:S(2)}, u32[]{:S(2)}) collective-permute-start(bf16[21,128,128]{2,1,0:T(8,128)(2,1)} %get-tuple-element.41), channel_id=1, source_target_pairs={{0,8},{9,17},{2,10},{11,19},{4,12},{13,21},{6,14},{15,23}} | collective-permute-start | bytes 2064392 | tf_op jit(solution)/shard_map/ppermute | solution.py:369
  34.2 20.7 %collective-permute-start.1 = (bf16[21,128,128]{2,1,0:T(8,128)(2,1)}, bf16[21,128,128]{2,1,0:T(8,128)(2,1)}, u32[]{:S(2)}, u32[]{:S(2)}) collective-permute-start(bf16[21,128,128]{2,1,0:T(8,128)(2,1)} %get-tuple-element.41), channel_id=1, source_target_pairs={{24,8},{1,17},{26,10},{3,19},{28,12},{5,21},{30,14},{7,23}} | collective-permute-start | bytes 2064392 | tf_op jit(solution)/shard_map/ppermute | solution.py:369
  35.7 19.2 %collective-permute-start = (bf16[21,128,128]{2,1,0:T(8,128)(2,1)}, bf16[21,128,128]{2,1,0:T(8,128)(2,1)}, u32[]{:S(2)}, u32[]{:S(2)}) collective-permute-start(bf16[21,128,128]{2,1,0:T(8,128)(2,1)} %get-tuple-element.41), channel_id=1, source_target_pairs={{16,8},{25,17},{18,10},{27,19},{20,12},{29,21},{22,14},{31,23}} | collective-permute-start | bytes 2064392 | tf_op jit(solution)/shard_map/ppermute | solution.py:369
  37.2 7.1 %collective-permute-start.5 = (f32[128,512]{1,0:T(8,128)}, f32[128,512]{1,0:T(8,128)S(1)}, u32[]{:S(2)}, u32[]{:S(2)}) collective-permute-start(f32[128,512]{1,0:T(8,128)} %get-tuple-element.43.m0), channel_id=1, source_target_pairs={{0,3},{1,0},{2,1},{3,2},{4,7},{5,4},{6,5},{7,6},{8,11},{9,8},{10,9... | collective-permute-start | bytes 786440 | tf_op jit(solution)/shard_map/ppermute | solution.py:375
  37.7 12.0 %collective-permute-start.4 = (f32[128,512]{1,0:T(8,128)}, f32[128,512]{1,0:T(8,128)}, u32[]{:S(2)}, u32[]{:S(2)}) collective-permute-start(f32[128,512]{1,0:T(8,128)} %get-tuple-element.43.m0), channel_id=1, source_target_pairs={{0,2},{1,3},{2,0},{3,1},{4,6},{5,7},{6,4},{7,5},{8,10},{9,11},{10,... | collective-permute-start | bytes 786440 | tf_op jit(solution)/shard_map/ppermute | solution.py:375
  44.3 0.7 copy-start.3
  45.0 6.8 %collective-permute-start.3 = (f32[128,512]{1,0:T(8,128)}, f32[128,512]{1,0:T(8,128)}, u32[]{:S(2)}, u32[]{:S(2)}) collective-permute-start(f32[128,512]{1,0:T(8,128)} %get-tuple-element.43.m0), channel_id=1, source_target_pairs={{0,1},{1,2},{2,3},{3,0},{4,5},{5,6},{6,7},{7,4},{8,9},{9,10},{10,1... | collective-permute-start | bytes 786440 | tf_op jit(solution)/shard_map/ppermute | solution.py:375
  51.9 1.0 copy-start.4
  58.0 0.7 collective-permute-start.6
  60.0 5.4 %collective-permute-start.7 = (f32[1,512]{1,0:T(1,128)S(1)}, f32[1,512]{1,0:T(1,128)S(1)}, u32[]{:S(2)}, u32[]{:S(2)}) collective-permute-start(f32[1,512]{1,0:T(1,128)S(1)} %get-tuple-element.55.after), channel_id=1, source_target_pairs={{17,10}} | collective-permute-start | bytes 6152 | tf_op jit(solution)/shard_map/ppermute | solution.py:389
  65.6 0.7 collective-permute-start.8
  66.6 0.7 collective-permute-start.9
  67.5 0.7 collective-permute-start.10
  68.4 0.7 collective-permute-start.11
  69.4 0.7 collective-permute-start.12

commit v3 on v2

--- a/solution.py
+++ b/solution.py
@@ -11,6 +11,7 @@
 F32, BF16 = jnp.float32, jnp.bfloat16
 VMEM = pl.BlockSpec(memory_space=pltpu.VMEM)
 SMEM = pl.BlockSpec(memory_space=pltpu.SMEM)
+HBM = pl.BlockSpec(memory_space=pl.ANY)
 
 
 def run(body, out, ins, scratch=(), limit=32, flops=0):
@@ -63,36 +64,54 @@
     return out
 
 
+def place(span):
+    return span ^ (span >> 1)
+
+
 def owner_plane(span):
-    return 1 + span % 2
+    return 1 + place(span) % 2
 
 
 EXTRA = 16
 
 
-def pack_kernel(day, count, rows, values, prior, damping, out):
+def pack_kernel(day, count, rows, values, prior, damping, out, day_s, count_s, values_v, prior_v, damping_v, sems):
     blocks = out.shape[0]
     slots = out.shape[1] - EXTRA
     width = out.shape[2]
-    first, second, third = parts3(prior[...])
+    small = [(day, day_s), (count, count_s), (values, values_v), (prior, prior_v), (damping, damping_v)]
+    copies = [pltpu.make_async_copy(src, dst, sems.at[n]) for n, (src, dst) in enumerate(small)]
+    large = [
+        pltpu.make_async_copy(
+            rows.at[pl.ds(k * slots, slots)], out.at[place(k), pl.ds(0, slots)], sems.at[len(small) + k]
+        )
+        for k in range(blocks)
+    ]
+    for copy in copies + large:
+        copy.start()
+    for copy in copies:
+        copy.wait()
+    first, second, third = parts3(prior_v[...])
     below = jnp.concatenate(
         [jnp.concatenate([second, third, jnp.zeros((1, width - 2 * LANES), F32)], 1)]
-        + parts3(damping[...])
+        + parts3(damping_v[...])
         + [jnp.zeros((EXTRA - 8, width), F32)],
         0,
     )
+    held = values_v[...].astype(F32)
     for k in range(blocks):
-        out[k, 0:slots, :] = rows[k * slots : (k + 1) * slots, :]
         line = jnp.concatenate(
             [
-                values[k : k + 1, :],
-                jnp.full((1, LANES), day[k], jnp.int32).astype(F32),
-                jnp.full((1, LANES), count[k], jnp.int32).astype(F32),
+                held[k : k + 1, :],
+                jnp.full((1, LANES), day_s[k], jnp.int32).astype(F32),
+                jnp.full((1, LANES), count_s[k], jnp.int32).astype(F32),
                 first,
             ],
             1,
         )
-        out[k, slots : slots + EXTRA, :] = jnp.concatenate([line, below], 0).astype(BF16)
+        out[place(k), slots : slots + EXTRA, :] = jnp.concatenate([line, below], 0).astype(BF16)
+    for copy in large:
+        copy.wait()
 
 
 def gram_kernel(got, gain, own, extra, pay, prior, gain_out, turned, marks):
@@ -104,7 +123,6 @@
     group = min(blocks, 8)
     half = 2 * LANES
     gain_out[...] = gain[...]
-    extra[...] = jnp.zeros(extra.shape, F32)
 
     def one(first, fresh):
         for k in range(group):
@@ -132,21 +150,21 @@
                         own[at] = piece if fresh else own[at] + piece
             for j in range(chunks):
                 piece = info[2 + d : 3 + d, j * LANES : (j + 1) * LANES]
-                r = 12 * d + j
+                r = 4 * d + j
                 extra[r : r + 1, :] = piece if fresh else extra[r : r + 1, :] + piece
 
     if blocks == group:
         one(0, True)
     else:
         own[...] = jnp.zeros(own.shape, F32)
+        extra[...] = jnp.zeros(extra.shape, F32)
 
         @pl.loop(0, blocks // group)
         def _(g):
             one(g * group, False)
 
-    for d in range(2):
-        for part, piece in enumerate(parts3(extra[12 * d : 12 * d + chunks, :])):
-            extra[12 * d + 4 * part : 12 * d + 4 * part + chunks, :] = piece
+    for n in range(own.shape[0]):
+        pay[n] = own[n].astype(BF16)
     for q in range(chunks):
         line = got[q, slots : slots + EXTRA, :].astype(F32)
         prior[:, q * LANES : (q + 1) * LANES] = line[0:1, 3 * LANES : 4 * LANES] + (
@@ -154,29 +172,28 @@
         )
     for y in range(blocks // 4):
         line = got[4 * y, slots : slots + EXTRA, :].astype(F32)
-        for k in range(6):
+        both = line[2:4] + (line[4:6] + line[6:8])
+        for day in range(2):
             for j in range(chunks):
-                r = 24 + 24 * y + 4 * k + j
-                extra[r : r + 1, :] = line[2 + k : 3 + k, j * LANES : (j + 1) * LANES]
-    for n in range(own.shape[0]):
-        pay[n] = own[n].astype(BF16)
-    for n in range(extra.shape[0] // LANES):
-        pay[own.shape[0] + n] = extra[n * LANES : (n + 1) * LANES, :].astype(BF16)
-
-
-def prep_kernel(ids, m0, m1, m2, m3, trans, cov, pt, pthi, ptlo, mthi, mtlo, chi, clo):
-    peers = 4
-    rows = m0.shape[0]
-    for step, part in enumerate((m0, m1, m2, m3)):
-        owner = lax.rem(ids[2] - step + peers, peers)
-        at = pl.ds(pl.multiple_of(owner * rows, rows), rows)
-        hi, lo = split(part[...].T)
-        mthi[:, at] = hi
-        mtlo[:, at] = lo
+                r = 8 + 8 * y + 4 * day + j
+                extra[r : r + 1, :] = both[day : day + 1, j * LANES : (j + 1) * LANES]
+
+
+def prep_kernel(trans, cov, pt, pthi, ptlo, chi, clo):
     whole = trans[...].T
     pt[...] = whole
     pthi[...], ptlo[...] = split(whole)
     chi[...], clo[...] = split(cov[...])
+
+
+def gain_kernel(after, ids, m0, m1, m2, m3, mthi, mtlo):
+    rows = m0.shape[0]
+    for step, part in enumerate((m0, m1, m2, m3)):
+        holder = ids[2] ^ step
+        at = pl.ds(pl.multiple_of(holder * rows, rows), rows)
+        hi, lo = split(part[...].T)
+        mthi[:, at] = hi
+        mtlo[:, at] = lo
 
 
 def two_days(state, damping, pthi, ptlo, omhi, omlo, info, chi, clo):
@@ -188,13 +205,13 @@
 
 
 def owner_kernel(
-    ids, own, extra, g1, g2, g3, prior, pthi, ptlo, chi, clo, omhi, omlo, info, mine, start, y, table, small
+    ids, own, g1, g2, g3, e0, e1, e2, e3, prior, pthi, ptlo, chi, clo, m1, m2, m3,
+    omhi, omlo, info, mine, table, start, y,
 ):
     planes = 4
     width = pthi.shape[0]
     chunks = width // LANES
     tiles = triangle(width)
-    got = (g1, g2, g3)
     for day in range(2):
         for n, (i, j) in enumerate(tiles):
             at = day * len(tiles) + n
@@ -206,34 +223,18 @@
                 hi, lo = split(piece.T)
                 omhi[day, j * LANES : (j + 1) * LANES, i * LANES : (i + 1) * LANES] = hi
                 omlo[day, j * LANES : (j + 1) * LANES, i * LANES : (i + 1) * LANES] = lo
-    for s in range(planes):
-        if s == 0:
-            small[0] = extra[...]
-        else:
-            for n in range(extra.shape[0] // LANES):
-                small[s, n * LANES : (n + 1) * LANES, :] = got[s - 1][own.shape[0] + n].astype(F32)
-
-    def row(s, first, gap):
-        return jnp.concatenate(
-            [
-                small[s, first + j : first + j + 1, :]
-                + (
-                    small[s, first + gap + j : first + gap + j + 1, :]
-                    + small[s, first + 2 * gap + j : first + 2 * gap + j + 1, :]
-                )
-                for j in range(chunks)
-            ],
-            1,
-        )
+
+    def row(part, first):
+        return jnp.concatenate([part[first + j : first + j + 1, :] for j in range(chunks)], 1)
 
     for day in range(2):
-        info[day] = row(0, 12 * day, 4) + (row(1, 12 * day, 4) + (row(2, 12 * day, 4) + row(3, 12 * day, 4)))
+        info[day] = row(e0, 4 * day) + (row(e1, 4 * day) + (row(e2, 4 * day) + row(e3, 4 * day)))
     held = table.shape[0] // 2 // planes
-    for s in range(planes):
+    for s, part in enumerate((e0, e1, e2, e3)):
         plane = lax.rem(ids[0] + s, planes)
         for k in range(held):
             for day in range(2):
-                table[pl.ds(2 * (plane * held + k) + day, 1), :] = row(s, 24 + 24 * k + 4 * day, 8)
+                table[pl.ds(2 * (plane * held + k) + day, 1), :] = row(part, 8 + 8 * k + 4 * day)
     for day in range(2):
         mine[day : day + 1, :] = table[pl.ds(2 * ids[1] + day, 1), :]
     state = prior[...]
@@ -263,32 +264,28 @@
     off[2:3, :] = mv(off[0:1, :], b2hi[...], b2lo[...]) + off[1:2, :]
 
 
-def hop_kernel(acc, got, bchi, bclo, off, total, y):
+def hop_kernel(after, acc, got, bchi, bclo, off, total, y):
     state = acc[...] + got[...]
     total[...] = state
     y[...] = mv(state, bchi[...], bclo[...]) + off[2:3, :]
 
 
-def last_kernel(acc, got, b1hi, b1lo, b2hi, b2lo, off, damping, out):
+def last_kernel(acc, got, b1hi, b1lo, b2hi, b2lo, off, out):
     state = acc[...] + got[...]
     one = mv(state, b1hi[...], b1lo[...]) + off[0:1, :]
     two = mv(one, b2hi[...], b2lo[...]) + off[1:2, :]
-    both = jnp.concatenate([one, two, damping[...]], 0)
+    both = jnp.concatenate([one, two], 0)
     for c in range(out.shape[0]):
         out[c] = both
 
 
-def back_kernel(ids, states, pthi, ptlo, mthi, mtlo, filt, smooth, f, d, const):
+def back_kernel(ids, states, table, pthi, ptlo, mthi, mtlo, filt, smooth, f, d, const):
     total, width = f.shape
     spans = total // 2
     chunks = width // LANES
     for c in range(spans):
-        one = states[owner_plane(c) * spans + c]
-        f[2 * c : 2 * c + 2, :] = one[0:2]
-        if c:
-            d[2 * c - 1 : 2 * c + 1, :] = one[2:4]
-        else:
-            d[0:1, :] = one[3:4]
+        f[2 * c : 2 * c + 2, :] = states[owner_plane(c) * spans + place(c)]
+    d[0 : total - 1, :] = table[1:total, :]
     d[total - 1 : total, :] = jnp.zeros((1, width), F32)
     ahead = d[...] * mm(f[...], pthi[...], ptlo[...])
     const[...] = f[...] - mm(d[...] * ahead, mthi[...], mtlo[...])
@@ -329,25 +326,39 @@
     days = damping.shape[0]
     assert planes == peers == 4 and days == 2 and slots == LANES and blocks == spans
     z, y, o = (lax.axis_index(a) for a in ("z", "y", "obs"))
-    ids = jnp.stack([z, y * peers + o, o, z * held + y]).astype(jnp.int32)
+    at = y * peers + o
+    span = at
+    for bit in range(1, spans.bit_length()):
+        span = span ^ (at >> bit)
+    ids = jnp.stack([z, span, o, z * held + y]).astype(jnp.int32)
     everyone = ("z", "y", "obs")
 
     def owner(span):
-        return owner_plane(span) * spans + span
+        return owner_plane(span) * spans + place(span)
 
     tiles = len(triangle(width))
-    extras = -(-(24 + 24 * held) // LANES)
     full, row = (width, width), ((1, width), F32)
     (sent,) = run(
         pack_kernel,
         [((blocks, slots + EXTRA, width), BF16)],
         [
-            (block_day, SMEM),
-            (block_count, SMEM),
-            records,
-            obs_values.astype(F32).reshape(blocks, slots),
-            prior_mean.reshape(1, -1),
-            damping,
+            (x, HBM)
+            for x in (
+                block_day,
+                block_count,
+                records,
+                obs_values.reshape(blocks, slots),
+                prior_mean.reshape(1, -1),
+                damping,
+            )
+        ],
+        [
+            pltpu.SMEM((blocks,), jnp.int32),
+            pltpu.SMEM((blocks,), jnp.int32),
+            pltpu.VMEM((blocks, slots), BF16),
+            pltpu.VMEM((1, width // peers), F32),
+            pltpu.VMEM((days, width), F32),
+            pltpu.SemaphoreType.DMA((5 + blocks,)),
         ],
     )
     got = lax.all_to_all(sent, ("y", "obs"), split_axis=0, concat_axis=0, tiled=True)
@@ -356,8 +367,8 @@
         gram_kernel,
         [
             ((2 * tiles, LANES, LANES), F32),
-            ((extras * LANES, LANES), F32),
-            ((2 * tiles + extras, LANES, LANES), BF16),
+            ((8 + 8 * held, LANES), F32),
+            ((2 * tiles, LANES, LANES), BF16),
             row,
             (unattenuated_multiplier.shape, F32),
         ],
@@ -367,23 +378,27 @@
     )
     plane_sums = [
         lax.ppermute(
-            pay, everyone, [((owner_plane(p) + s) % planes * spans + p, owner(p)) for p in range(spans)]
+            pay, everyone, [((owner_plane(p) + s) % planes * spans + place(p), owner(p)) for p in range(spans)]
         )
         for s in range(1, planes)
     ]
-    gains = [gain] + [
-        lax.ppermute(gain, "obs", [(i, (i + s) % peers) for i in range(peers)]) for s in range(1, peers)
+    extras = [extra] + [
+        lax.ppermute(extra, "z", [((i + s) % planes, i) for i in range(planes)]) for s in range(1, planes)
     ]
-    pt, pthi, ptlo, mthi, mtlo, chi, clo = run(
-        prep_kernel,
-        [(full, F32)] + [(full, BF16)] * 6,
-        [(ids, SMEM), *gains, propagator_matrix, analysis_cov],
-    )
-    omhi, omlo, info, mine, acc, y = run(
+
+    def swap(x, bit):
+        return lax.ppermute(x, "obs", [(i, i ^ bit) for i in range(peers)])
+
+    across = swap(gain, 2)
+    gains = [gain, swap(gain, 1), across, swap(across, 1)]
+    pt, pthi, ptlo, chi, clo = run(
+        prep_kernel, [(full, F32)] + [(full, BF16)] * 4, [propagator_matrix, analysis_cov]
+    )
+    omhi, omlo, info, mine, table, acc, y = run(
         owner_kernel,
-        [((days,) + full, BF16)] * 2 + [((days, 1, width), F32), ((days, width), F32), row, row],
-        [(ids, SMEM), own, extra, *plane_sums, prior, pthi, ptlo, chi, clo],
-        [pltpu.VMEM((spans * days, width), F32), pltpu.VMEM((planes, extras * LANES, LANES), F32)],
+        [((days,) + full, BF16)] * 2
+        + [((days, 1, width), F32), ((days, width), F32), ((spans * days, width), F32), row, row],
+        [(ids, SMEM), own, *plane_sums, *extras, prior, pthi, ptlo, chi, clo, *[(g, HBM) for g in gains[1:]]],
     )
     for k in range(spans - 1):
         received = lax.ppermute(y, everyone, [(owner(k), owner(k + 1))])
@@ -397,19 +412,23 @@
                 [y, omhi, omlo, info, chi, clo, pt, mine],
                 flops=30 * width**3,
             )
+            side = y
         elif k < spans - 2:
-            acc, y = run(hop_kernel, [row, row], [acc, received, bchi, bclo, off])
+            acc, y = run(hop_kernel, [row, row], [(side, HBM), acc, received, bchi, bclo, off])
+            if k == 2:
+                mthi, mtlo = run(gain_kernel, [(full, BF16)] * 2, [(y, HBM), (ids, SMEM), *gains])
+                side = mthi
     (answer,) = run(
         last_kernel,
-        [((spans * peers, 2 * days, width), F32)],
-        [acc, received, b1hi, b1lo, b2hi, b2lo, off, mine],
+        [((spans * peers, days, width), F32)],
+        [acc, received, b1hi, b1lo, b2hi, b2lo, off],
     )
     states = lax.all_to_all(answer, everyone, split_axis=0, concat_axis=0, tiled=True)
     out = ((days, LANES), F32)
     return run(
         back_kernel,
         [out, out],
-        [(ids, SMEM), states, pthi, ptlo, mthi, mtlo],
+        [(ids, SMEM), states, table, pthi, ptlo, mthi, mtlo],
         [pltpu.VMEM((spans * days, width), F32)] * 3,
     )
 

time: 105 us -> 110 us (1.048)
  waiting for transfers between devices: 10.5 us -> 24.6 us
  blocking collectives: 50.5 us -> 44.1 us
  starting transfers between devices: 15.7 us -> 13.3 us
    ppermute x6 -> x9, waiting for transfers between devices: 10.5 us -> 24.6 us  [the longest x3 23.6 us: local(): lax.ppermute(extra, 'z', [((i + s) % planes, i) for i in range(planes)])]
    all_to_all x1, blocking collectives: 28.7 us -> 22.2 us  [local(): lax.all_to_all(answer, everyone, split_axis=0, concat_axis=0, tiled=True)]
    ppermute x6 -> x9, starting transfers between devices: 10.8 us -> 8.42 us  [the longest x3 7.34 us: local(): lax.ppermute(pay, everyone, [((owner_plane(p) + s) % planes * spans + pla...]
    unnamed x20 -> x18, local copies, waits for them, and re-layouts: 5.53 us -> 4.56 us
    pallas_call x13 -> x14, Pallas kernels: 20.7 us -> 21.6 us  [run(): pl.pallas_call(body, out_shape=[jax.ShapeDtypeStruct(s, d) for s, d in ou...]
  transfers between devices with their start and end apart: 13 -> 16, of which waited for: 3 -> 5; matrix products, arithmetic and copies ran while one was open for 0% -> 0% of each run, Pallas kernels for 6% -> 6%
where the time goes in v3:
time: 110 us; the launch traced here: 109 us
  blocking collectives  44.1 us (40%)
  waiting for transfers between devices  24.6 us (22%)
  Pallas kernels  21.6 us (20%)
  starting transfers between devices  13.3 us (12%)
  local copies, waits for them, and re-layouts  4.56 us (4%)
    ppermute x3, waiting for transfers between devices, local(): lax.ppermute(extra, 'z', [((i + s) % planes, i) for i in range(planes)])  23.6 us
    all_to_all x1, blocking collectives, local(): lax.all_to_all(answer, everyone, split_axis=0, concat_axis=0, tiled=True)  22.2 us
    all_to_all x1, blocking collectives, local(): lax.all_to_all(sent, ('y', 'obs'), split_axis=0, concat_axis=0, tiled=True)  21.9 us
    pallas_call x14, Pallas kernels, run(): pl.pallas_call(body, out_shape=[jax.ShapeDtypeStruct(s, d) for s, d in ou...  21.6 us
    ppermute x3, starting transfers between devices, local(): lax.ppermute(pay, everyone, [((owner_plane(p) + s) % planes * spans + pla...  7.34 us
    ppermute x7, starting transfers between devices, local(): received = lax.ppermute(y, everyone, [(owner(k), owner(k + 1))])  4.86 us
    unnamed x18, local copies, waits for them, and re-layouts  4.56 us
  transfers between devices with their start and end apart: 16, of which 5 were waited for; matrix products, arithmetic and copies ran while one was open for 0% of the time, Pallas kernels for 6%

profile of v3, /device:TPU:0, one launch (start us, length us, event | category | flops | bytes accessed | tf_op | source)
XLA Modules:
  0.0 109.1 jit_solution(14224721970215385391)
XLA Ops:
  0.6 1.2 %copy-done.2 = bf16[1024,512]{1,0:T(8,128)(2,1)S(1)} copy-done((bf16[1024,512]{1,0:T(8,128)(2,1)S(1)}, bf16[1024,512]{1,0:T(8,128)(2,1)}, u32[]{:S(2)}) %copy-start.2) | copy-done | bytes 1048600
  1.9 0.7 copy-done.3
  2.5 0.7 copy-done.4
  5.2 1.5 %shard_map.104 = bf16[8,144,512]{2,1,0:T(8,128)(2,1)S(1)} custom-call(s32[8]{0:T(128)S(1)} %copy-done.5, s32[8]{0:T(128)S(1)} %copy-done.6, bf16[1024,512]{1,0:T(8,128)(2,1)S(1)} %copy-done.2, bf16[8,128]{1,0:T(8,128)(2,1)S(1)} %bitcast.6, f32[1,128]{1,0:T(1,128)S(1)} %bitcast.7, f32[2,512]{1,0:T(2,128)S(1)} %copy-done.3), custom_call_target="tpu_custom_call" | custom-call | bytes 1055296 | tf_op jit(solution)/shard_map/pallas_call | solution.py:21
  6.7 21.9 %all_to_all.10.got = bf16[8,144,512]{2,1,0:T(8,128)(2,1)S(1)} all-to-all(bf16[8,144,512]{2,1,0:T(8,128)(2,1)S(1)} %shard_map.104), channel_id=1, replica_groups=mesh['z'=4,'y'=2,'obs'=4] {'y','obs'}, dimensions={0} | all-to-all | bytes 2359296 | tf_op jit(solution)/shard_map/all_to_all | solution.py:364
  28.6 2.1 %shard_map.105 = (f32[20,128,128]{2,1,0:T(8,128)S(1)}, f32[24,128]{1,0:T(8,128)S(1)}, bf16[20,128,128]{2,1,0:T(8,128)(2,1)}, f32[1,512]{1,0:T(1,128)S(1)}, f32[128,512]{1,0:T(8,128)}) custom-call(bf16[8,144,512]{2,1,0:T(8,128)(2,1)S(1)} %all_to_all.10.got, f32[128,512]{1,0:T(8,128)S(1)} %copy-done.8), custom_call_target="tpu_custom_call" | custom-call | flops 1073741824 | bytes 1441792 | tf_op jit(solution)/shard_map/pallas_call | solution.py:21
  30.7 4.3 %collective-permute-start.2 = (bf16[20,128,128]{2,1,0:T(8,128)(2,1)}, bf16[20,128,128]{2,1,0:T(8,128)(2,1)}, u32[]{:S(2)}, u32[]{:S(2)}) collective-permute-start(bf16[20,128,128]{2,1,0:T(8,128)(2,1)} %get-tuple-element.41), channel_id=1, source_target_pairs={{0,8},{9,17},{11,19},{2,10},{6,14},{15,23},{13,21},{4,12}} | collective-permute-start | bytes 1966088 | tf_op jit(solution)/shard_map/ppermute | solution.py:380
  35.0 1.5 %collective-permute-start.1 = (bf16[20,128,128]{2,1,0:T(8,128)(2,1)}, bf16[20,128,128]{2,1,0:T(8,128)(2,1)}, u32[]{:S(2)}, u32[]{:S(2)}) collective-permute-start(bf16[20,128,128]{2,1,0:T(8,128)(2,1)} %get-tuple-element.41), channel_id=1, source_target_pairs={{24,8},{1,17},{3,19},{26,10},{30,14},{7,23},{5,21},{28,12}} | collective-permute-start | bytes 1966088 | tf_op jit(solution)/shard_map/ppermute | solution.py:380
  36.5 1.5 %collective-permute-start = (bf16[20,128,128]{2,1,0:T(8,128)(2,1)}, bf16[20,128,128]{2,1,0:T(8,128)(2,1)}, u32[]{:S(2)}, u32[]{:S(2)}) collective-permute-start(bf16[20,128,128]{2,1,0:T(8,128)(2,1)} %get-tuple-element.41), channel_id=1, source_target_pairs={{16,8},{25,17},{27,19},{18,10},{22,14},{31,23},{29,21},{20,12}} | collective-permute-start | bytes 1966088 | tf_op jit(solution)/shard_map/ppermute | solution.py:380
  38.6 15.3 %collective-permute-done.5.e3 = f32[24,128]{1,0:T(8,128)S(1)} collective-permute-done((f32[24,128]{1,0:T(8,128)S(1)}, f32[24,128]{1,0:T(8,128)S(1)}, u32[]{:S(2)}, u32[]{:S(2)}) %collective-permute-start.5) | collective-permute-done | bytes 12320 | tf_op jit(solution)/shard_map/ppermute | solution.py:386
  53.9 4.6 %collective-permute-done.4.e2 = f32[24,128]{1,0:T(8,128)S(1)} collective-permute-done((f32[24,128]{1,0:T(8,128)S(1)}, f32[24,128]{1,0:T(8,128)S(1)}, u32[]{:S(2)}, u32[]{:S(2)}) %collective-permute-start.4) | collective-permute-done | bytes 12320 | tf_op jit(solution)/shard_map/ppermute | solution.py:386
  58.5 3.7 %collective-permute-done.3.e1 = f32[24,128]{1,0:T(8,128)S(1)} collective-permute-done((f32[24,128]{1,0:T(8,128)S(1)}, f32[24,128]{1,0:T(8,128)S(1)}, u32[]{:S(2)}, u32[]{:S(2)}) %collective-permute-start.3) | collective-permute-done | bytes 12320 | tf_op jit(solution)/shard_map/ppermute | solution.py:386
  64.4 3.0 %shard_map.107 = (bf16[2,512,512]{2,1,0:T(8,128)(2,1)S(1)}, bf16[2,512,512]{2,1,0:T(8,128)(2,1)S(1)}, f32[2,1,512]{2,1,0:T(1,128)S(1)}, f32[2,512]{1,0:T(2,128)S...) custom-call(s32[4]{0:T(128)S(1)} %pad_add_fusion.ids, ...), custom_call_target="tpu_custom_call" | custom-call | bytes 6211600 | tf_op jit(solution)/shard_map/pallas_call | solution.py:21
  67.5 0.7 collective-permute-start.9
  68.1 1.4 %shard_map.108 = (f32[1,512]{1,0:T(1,128)S(1)}, f32[1,512]{1,0:T(1,128)S(1)}) custom-call(f32[1,512]{1,0:T(1,128)S(1)} %get-tuple-element.49.acc, f32[1,512]{1,0:T(1,128)S(1)} %collective-permute-done.9.got, f32[2,512]{1,0:T(2,128)S(1)} %get-tuple-element.51.mine.damping, bf16[512,512]{1,0:T(8,128)(2,1)S(1)} %get-tuple-element.44.pthi, ...), custom_call_target="tpu_custom_call" | custom-call | bytes 4206592 | tf_op jit(solution)/shard_map/pallas_call | solution.py:21
  70.2 4.7 %shard_map.109 = (bf16[512,512]{1,0:T(8,128)(2,1)S(1)}, bf16[512,512]{1,0:T(8,128)(2,1)S(1)}, bf16[512,512]{1,0:T(8,128)(2,1)S(1)}, bf16[512,512]{1,0:T(8,128)(2...) custom-call(f32[1,512]{1,0:T(1,128)S(1)} %get-tuple-element.55.after, ...), custom_call_target="tpu_custom_call" | custom-call | flops 4026531840 | bytes 4204544 | tf_op jit(solution)/shard_map/pallas_call | solution.py:21
  75.1 0.7 collective-permute-start.11
  76.1 0.7 collective-permute-start.12
  76.8 1.5 %shard_map.112 = (bf16[512,512]{1,0:T(8,128)(2,1)S(1)}, bf16[512,512]{1,0:T(8,128)(2,1)S(1)}) custom-call(f32[1,512]{1,0:T(1,128)S(1)} %get-tuple-element.63.after, s32[4]{0:T(128)S(1)} %pad_add_fusion.ids, f32[128,512]{1,0:T(8,128)} %get-tuple-element.48.m0, f32[128,512]{1,0:T(8,128)} %collective-permute-done.6.m1, f32[128,512]{1,0:T(8,128)} %collective-permute-done.7.m2, ...), custom_call_target="tpu_custom_call" | custom-call | bytes 1050640 | tf_op jit(solution)/shard_map/pallas_call | solution.py:21
  78.5 0.7 collective-permute-start.13
  79.5 0.7 collective-permute-start.14
  80.4 0.7 collective-permute-start.15
  81.6 22.2 %all_to_all.11.states = f32[32,2,512]{2,1,0:T(2,128)S(1)} all-to-all(f32[32,2,512]{2,1,0:T(2,128)S(1)} %shard_map.116), channel_id=1, replica_groups=mesh['z'=4,'y'=2,'obs'=4] {'z','y','obs'}, dimensions={0} | all-to-all | bytes 262144 | tf_op jit(solution)/shard_map/all_to_all | solution.py:426
  103.9 5.2 %shard_map.117 = (f32[2,128]{1,0:T(2,128)}, f32[2,128]{1,0:T(2,128)}) custom-call(s32[4]{0:T(128)S(1)} %pad_add_fusion.ids, f32[32,2,512]{2,1,0:T(2,128)S(1)} %all_to_all.11.states, f32[16,512]{1,0:T(8,128)S(1)} %get-tuple-element.76.table, bf16[512,512]{1,0:T(8,128)(2,1)S(1)} %get-tuple-element.44.pthi, bf16[512,512]{1,0:T(8,128)(2,1)S(1)} %get-tuple-element.45.ptlo, ...), custom_call_target="tpu_custom_call" | custom-call | bytes 2261008 | tf_op jit(solution)/shard_map/pallas_call | solution.py:21
  (43 shorter events, 7.0 us)
Async XLA Ops:
  0.6 1.2 %copy-start.2 = (bf16[1024,512]{1,0:T(8,128)(2,1)S(1)}, bf16[1024,512]{1,0:T(8,128)(2,1)}, u32[]{:S(2)}) copy-start(bf16[1024,512]{1,0:T(8,128)(2,1)} %rows.1) | copy-start | bytes 3145732
  1.9 0.7 copy-start.3
  2.5 0.7 copy-start.4
  3.2 0.7 copy-start.5
  3.9 0.7 copy-start.6
  6.7 21.9 %copy-start.8 = (f32[128,512]{1,0:T(8,128)S(1)}, f32[128,512]{1,0:T(8,128)}, u32[]{:S(2)}) copy-start(f32[128,512]{1,0:T(8,128)} %gain.1) | copy-start | bytes 786436
  28.6 34.1 %copy-start = (f32[512,512]{1,0:T(8,128)S(1)}, f32[512,512]{1,0:T(8,128)}, u32[]{:S(2)}) copy-start(f32[512,512]{1,0:T(8,128)} %trans.1) | copy-start | bytes 3145732
  28.6 34.1 %copy-start.1 = (f32[512,512]{1,0:T(8,128)S(1)}, f32[512,512]{1,0:T(8,128)}, u32[]{:S(2)}) copy-start(f32[512,512]{1,0:T(8,128)} %cov.1) | copy-start | bytes 3145732
  30.7 33.7 %collective-permute-start.2 = (bf16[20,128,128]{2,1,0:T(8,128)(2,1)}, bf16[20,128,128]{2,1,0:T(8,128)(2,1)}, u32[]{:S(2)}, u32[]{:S(2)}) collective-permute-start(bf16[20,128,128]{2,1,0:T(8,128)(2,1)} %get-tuple-element.41), channel_id=1, source_target_pairs={{0,8},{9,17},{11,19},{2,10},{6,14},{15,23},{13,21},{4,12}} | collective-permute-start | bytes 1966088 | tf_op jit(solution)/shard_map/ppermute | solution.py:380
  35.0 29.4 %collective-permute-start.1 = (bf16[20,128,128]{2,1,0:T(8,128)(2,1)}, bf16[20,128,128]{2,1,0:T(8,128)(2,1)}, u32[]{:S(2)}, u32[]{:S(2)}) collective-permute-start(bf16[20,128,128]{2,1,0:T(8,128)(2,1)} %get-tuple-element.41), channel_id=1, source_target_pairs={{24,8},{1,17},{3,19},{26,10},{30,14},{7,23},{5,21},{28,12}} | collective-permute-start | bytes 1966088 | tf_op jit(solution)/shard_map/ppermute | solution.py:380
  36.5 27.9 %collective-permute-start = (bf16[20,128,128]{2,1,0:T(8,128)(2,1)}, bf16[20,128,128]{2,1,0:T(8,128)(2,1)}, u32[]{:S(2)}, u32[]{:S(2)}) collective-permute-start(bf16[20,128,128]{2,1,0:T(8,128)(2,1)} %get-tuple-element.41), channel_id=1, source_target_pairs={{16,8},{25,17},{27,19},{18,10},{22,14},{31,23},{29,21},{20,12}} | collective-permute-start | bytes 1966088 | tf_op jit(solution)/shard_map/ppermute | solution.py:380
  38.0 24.1 %collective-permute-start.7 = (f32[128,512]{1,0:T(8,128)}, f32[128,512]{1,0:T(8,128)}, u32[]{:S(2)}, u32[]{:S(2)}) collective-permute-start(f32[128,512]{1,0:T(8,128)} %get-tuple-element.48.m0), channel_id=1, source_target_pairs={{0,2},{1,3},{2,0},{3,1},{4,6},{5,7},{6,4},{7,5},{8,10},{9,11},{10,... | collective-permute-start | bytes 786440 | tf_op jit(solution)/shard_map/ppermute | solution.py:390
  38.6 15.3 %collective-permute-start.5 = (f32[24,128]{1,0:T(8,128)S(1)}, f32[24,128]{1,0:T(8,128)S(1)}, u32[]{:S(2)}, u32[]{:S(2)}) collective-permute-start(f32[24,128]{1,0:T(8,128)S(1)} %get-tuple-element.42.e0), channel_id=1, source_target_pairs={{24,0},{0,8},{8,16},{16,24},{25,1},{1,9},{9,17},{17,25},{26,2},{2,... | collective-permute-start | bytes 36872 | tf_op jit(solution)/shard_map/ppermute | solution.py:386
  53.9 4.6 %collective-permute-start.4 = (f32[24,128]{1,0:T(8,128)S(1)}, f32[24,128]{1,0:T(8,128)S(1)}, u32[]{:S(2)}, u32[]{:S(2)}) collective-permute-start(f32[24,128]{1,0:T(8,128)S(1)} %get-tuple-element.42.e0), channel_id=1, source_target_pairs={{16,0},{24,8},{0,16},{8,24},{17,1},{25,9},{1,17},{9,25},{18,2},{26... | collective-permute-start | bytes 36872 | tf_op jit(solution)/shard_map/ppermute | solution.py:386
  58.5 3.7 %collective-permute-start.3 = (f32[24,128]{1,0:T(8,128)S(1)}, f32[24,128]{1,0:T(8,128)S(1)}, u32[]{:S(2)}, u32[]{:S(2)}) collective-permute-start(f32[24,128]{1,0:T(8,128)S(1)} %get-tuple-element.42.e0), channel_id=1, source_target_pairs={{8,0},{16,8},{24,16},{0,24},{9,1},{17,9},{25,17},{1,25},{10,2},{18... | collective-permute-start | bytes 36872 | tf_op jit(solution)/shard_map/ppermute | solution.py:386
  62.2 1.9 %collective-permute-start.6 = (f32[128,512]{1,0:T(8,128)}, f32[128,512]{1,0:T(8,128)}, u32[]{:S(2)}, u32[]{:S(2)}) collective-permute-start(f32[128,512]{1,0:T(8,128)} %get-tuple-element.48.m0), channel_id=1, source_target_pairs={{0,1},{1,0},{2,3},{3,2},{4,5},{5,4},{6,7},{7,6},{8,9},{9,8},{10,11... | collective-permute-start | bytes 786440 | tf_op jit(solution)/shard_map/ppermute | solution.py:390
  62.2 2.2 %collective-permute-start.8 = (f32[128,512]{1,0:T(8,128)}, f32[128,512]{1,0:T(8,128)}, u32[]{:S(2)}, u32[]{:S(2)}) collective-permute-start(f32[128,512]{1,0:T(8,128)} %collective-permute-done.7.m2), channel_id=1, source_target_pairs={{0,1},{1,0},{2,3},{3,2},{4,5},{5,4},{6,7},{7,6},{8,9},{9,8},{10,11... | collective-permute-start | bytes 786440 | tf_op jit(solution)/shard_map/ppermute | solution.py:390
  67.5 0.7 collective-permute-start.9
  69.5 5.4 %collective-permute-start.10 = (f32[1,512]{1,0:T(1,128)S(1)}, f32[1,512]{1,0:T(1,128)S(1)}, u32[]{:S(2)}, u32[]{:S(2)}) collective-permute-start(f32[1,512]{1,0:T(1,128)S(1)} %get-tuple-element.55.after), channel_id=1, source_target_pairs={{17,19}} | collective-permute-start | bytes 6152 | tf_op jit(solution)/shard_map/ppermute | solution.py:404
  75.1 0.7 collective-permute-start.11
  76.1 2.3 %collective-permute-start.12 = (f32[1,512]{1,0:T(1,128)S(1)}, f32[1,512]{1,0:T(1,128)S(1)}, u32[]{:S(2)}, u32[]{:S(2)}) collective-permute-start(f32[1,512]{1,0:T(1,128)S(1)} %get-tuple-element.63.after), channel_id=1, source_target_pairs={{10,14}} | collective-permute-start | bytes 6152 | tf_op jit(solution)/shard_map/ppermute | solution.py:404
  78.5 0.7 collective-permute-start.13
  79.5 0.7 collective-permute-start.14
  80.4 0.7 collective-permute-start.15
  (1 other events, 0.7 us)

commit v4 on v3

--- a/solution.py
+++ b/solution.py
@@ -11,7 +11,8 @@
 F32, BF16 = jnp.float32, jnp.bfloat16
 VMEM = pl.BlockSpec(memory_space=pltpu.VMEM)
 SMEM = pl.BlockSpec(memory_space=pltpu.SMEM)
-HBM = pl.BlockSpec(memory_space=pl.ANY)
+ANY = pl.BlockSpec(memory_space=pl.ANY)
+HBM = pl.BlockSpec(memory_space=pltpu.HBM)
 
 
 def run(body, out, ins, scratch=(), limit=32, flops=0):
@@ -123,6 +124,7 @@
     group = min(blocks, 8)
     half = 2 * LANES
     gain_out[...] = gain[...]
+    extra[...] = jnp.zeros(extra.shape, F32)
 
     def one(first, fresh):
         for k in range(group):
@@ -150,21 +152,21 @@
                         own[at] = piece if fresh else own[at] + piece
             for j in range(chunks):
                 piece = info[2 + d : 3 + d, j * LANES : (j + 1) * LANES]
-                r = 4 * d + j
+                r = 12 * d + j
                 extra[r : r + 1, :] = piece if fresh else extra[r : r + 1, :] + piece
 
     if blocks == group:
         one(0, True)
     else:
         own[...] = jnp.zeros(own.shape, F32)
-        extra[...] = jnp.zeros(extra.shape, F32)
 
         @pl.loop(0, blocks // group)
         def _(g):
             one(g * group, False)
 
-    for n in range(own.shape[0]):
-        pay[n] = own[n].astype(BF16)
+    for d in range(2):
+        for part, piece in enumerate(parts3(extra[12 * d : 12 * d + chunks, :])):
+            extra[12 * d + 4 * part : 12 * d + 4 * part + chunks, :] = piece
     for q in range(chunks):
         line = got[q, slots : slots + EXTRA, :].astype(F32)
         prior[:, q * LANES : (q + 1) * LANES] = line[0:1, 3 * LANES : 4 * LANES] + (
@@ -172,11 +174,14 @@
         )
     for y in range(blocks // 4):
         line = got[4 * y, slots : slots + EXTRA, :].astype(F32)
-        both = line[2:4] + (line[4:6] + line[6:8])
-        for day in range(2):
+        for k in range(6):
             for j in range(chunks):
-                r = 8 + 8 * y + 4 * day + j
-                extra[r : r + 1, :] = both[day : day + 1, j * LANES : (j + 1) * LANES]
+                r = 24 + 24 * y + 4 * k + j
+                extra[r : r + 1, :] = line[2 + k : 3 + k, j * LANES : (j + 1) * LANES]
+    for n in range(own.shape[0]):
+        pay[n] = own[n].astype(BF16)
+    for n in range(extra.shape[0] // LANES):
+        pay[own.shape[0] + n] = extra[n * LANES : (n + 1) * LANES, :].astype(BF16)
 
 
 def prep_kernel(trans, cov, pt, pthi, ptlo, chi, clo):
@@ -205,13 +210,14 @@
 
 
 def owner_kernel(
-    ids, own, g1, g2, g3, e0, e1, e2, e3, prior, pthi, ptlo, chi, clo, m1, m2, m3,
-    omhi, omlo, info, mine, table, start, y,
+    ids, own, extra, g1, g2, g3, prior, pthi, ptlo, chi, clo, m1, m2, m3,
+    omhi, omlo, info, mine, start, y, table, small,
 ):
     planes = 4
     width = pthi.shape[0]
     chunks = width // LANES
     tiles = triangle(width)
+    got = (g1, g2, g3)
     for day in range(2):
         for n, (i, j) in enumerate(tiles):
             at = day * len(tiles) + n
@@ -223,18 +229,34 @@
                 hi, lo = split(piece.T)
                 omhi[day, j * LANES : (j + 1) * LANES, i * LANES : (i + 1) * LANES] = hi
                 omlo[day, j * LANES : (j + 1) * LANES, i * LANES : (i + 1) * LANES] = lo
-
-    def row(part, first):
-        return jnp.concatenate([part[first + j : first + j + 1, :] for j in range(chunks)], 1)
+    for s in range(planes):
+        if s == 0:
+            small[0] = extra[...]
+        else:
+            for n in range(extra.shape[0] // LANES):
+                small[s, n * LANES : (n + 1) * LANES, :] = got[s - 1][own.shape[0] + n].astype(F32)
+
+    def row(s, first, gap):
+        return jnp.concatenate(
+            [
+                small[s, first + j : first + j + 1, :]
+                + (
+                    small[s, first + gap + j : first + gap + j + 1, :]
+                    + small[s, first + 2 * gap + j : first + 2 * gap + j + 1, :]
+                )
+                for j in range(chunks)
+            ],
+            1,
+        )
 
     for day in range(2):
-        info[day] = row(e0, 4 * day) + (row(e1, 4 * day) + (row(e2, 4 * day) + row(e3, 4 * day)))
+        info[day] = row(0, 12 * day, 4) + (row(1, 12 * day, 4) + (row(2, 12 * day, 4) + row(3, 12 * day, 4)))
     held = table.shape[0] // 2 // planes
-    for s, part in enumerate((e0, e1, e2, e3)):
+    for s in range(planes):
         plane = lax.rem(ids[0] + s, planes)
         for k in range(held):
             for day in range(2):
-                table[pl.ds(2 * (plane * held + k) + day, 1), :] = row(part, 8 + 8 * k + 4 * day)
+                table[pl.ds(2 * (plane * held + k) + day, 1), :] = row(s, 24 + 24 * k + 4 * day, 8)
     for day in range(2):
         mine[day : day + 1, :] = table[pl.ds(2 * ids[1] + day, 1), :]
     state = prior[...]
@@ -270,22 +292,26 @@
     y[...] = mv(state, bchi[...], bclo[...]) + off[2:3, :]
 
 
-def last_kernel(acc, got, b1hi, b1lo, b2hi, b2lo, off, out):
+def last_kernel(acc, got, b1hi, b1lo, b2hi, b2lo, off, damping, out):
     state = acc[...] + got[...]
     one = mv(state, b1hi[...], b1lo[...]) + off[0:1, :]
     two = mv(one, b2hi[...], b2lo[...]) + off[1:2, :]
-    both = jnp.concatenate([one, two], 0)
+    both = jnp.concatenate([one, two, damping[...]], 0)
     for c in range(out.shape[0]):
         out[c] = both
 
 
-def back_kernel(ids, states, table, pthi, ptlo, mthi, mtlo, filt, smooth, f, d, const):
+def back_kernel(ids, states, pthi, ptlo, mthi, mtlo, filt, smooth, f, d, const):
     total, width = f.shape
     spans = total // 2
     chunks = width // LANES
     for c in range(spans):
-        f[2 * c : 2 * c + 2, :] = states[owner_plane(c) * spans + place(c)]
-    d[0 : total - 1, :] = table[1:total, :]
+        one = states[owner_plane(c) * spans + place(c)]
+        f[2 * c : 2 * c + 2, :] = one[0:2]
+        if c:
+            d[2 * c - 1 : 2 * c + 1, :] = one[2:4]
+        else:
+            d[0:1, :] = one[3:4]
     d[total - 1 : total, :] = jnp.zeros((1, width), F32)
     ahead = d[...] * mm(f[...], pthi[...], ptlo[...])
     const[...] = f[...] - mm(d[...] * ahead, mthi[...], mtlo[...])
@@ -337,6 +363,7 @@
         return owner_plane(span) * spans + place(span)
 
     tiles = len(triangle(width))
+    extra_tiles = -(-(24 + 24 * held) // LANES)
     full, row = (width, width), ((1, width), F32)
     (sent,) = run(
         pack_kernel,
@@ -360,6 +387,7 @@
             pltpu.VMEM((days, width), F32),
             pltpu.SemaphoreType.DMA((5 + blocks,)),
         ],
+        limit=60,
     )
     got = lax.all_to_all(sent, ("y", "obs"), split_axis=0, concat_axis=0, tiled=True)
     span_slots = min(blocks, 8) * slots
@@ -367,8 +395,8 @@
         gram_kernel,
         [
             ((2 * tiles, LANES, LANES), F32),
-            ((8 + 8 * held, LANES), F32),
-            ((2 * tiles, LANES, LANES), BF16),
+            ((extra_tiles * LANES, LANES), F32),
+            ((2 * tiles + extra_tiles, LANES, LANES), BF16),
             row,
             (unattenuated_multiplier.shape, F32),
         ],
@@ -382,10 +410,6 @@
         )
         for s in range(1, planes)
     ]
-    extras = [extra] + [
-        lax.ppermute(extra, "z", [((i + s) % planes, i) for i in range(planes)]) for s in range(1, planes)
-    ]
-
     def swap(x, bit):
         return lax.ppermute(x, "obs", [(i, i ^ bit) for i in range(peers)])
 
@@ -394,11 +418,12 @@
     pt, pthi, ptlo, chi, clo = run(
         prep_kernel, [(full, F32)] + [(full, BF16)] * 4, [propagator_matrix, analysis_cov]
     )
-    omhi, omlo, info, mine, table, acc, y = run(
+    omhi, omlo, info, mine, acc, y = run(
         owner_kernel,
         [((days,) + full, BF16)] * 2
-        + [((days, 1, width), F32), ((days, width), F32), ((spans * days, width), F32), row, row],
-        [(ids, SMEM), own, *plane_sums, *extras, prior, pthi, ptlo, chi, clo, *[(g, HBM) for g in gains[1:]]],
+        + [((days, 1, width), F32), ((days, width), F32), row, row],
+        [(ids, SMEM), own, extra, *plane_sums, prior, pthi, ptlo, chi, clo, *[(g, ANY) for g in gains[1:]]],
+        [pltpu.VMEM((spans * days, width), F32), pltpu.VMEM((planes, extra_tiles * LANES, LANES), F32)],
     )
     for k in range(spans - 1):
         received = lax.ppermute(y, everyone, [(owner(k), owner(k + 1))])
@@ -414,21 +439,21 @@
             )
             side = y
         elif k < spans - 2:
-            acc, y = run(hop_kernel, [row, row], [(side, HBM), acc, received, bchi, bclo, off])
+            acc, y = run(hop_kernel, [row, row], [(side, ANY), acc, received, bchi, bclo, off])
             if k == 2:
-                mthi, mtlo = run(gain_kernel, [(full, BF16)] * 2, [(y, HBM), (ids, SMEM), *gains])
+                mthi, mtlo = run(gain_kernel, [(full, BF16)] * 2, [(y, ANY), (ids, SMEM), *gains])
                 side = mthi
     (answer,) = run(
         last_kernel,
-        [((spans * peers, days, width), F32)],
-        [acc, received, b1hi, b1lo, b2hi, b2lo, off],
+        [((spans * peers, 2 * days, width), F32)],
+        [acc, received, b1hi, b1lo, b2hi, b2lo, off, mine],
     )
     states = lax.all_to_all(answer, everyone, split_axis=0, concat_axis=0, tiled=True)
     out = ((days, LANES), F32)
     return run(
         back_kernel,
         [out, out],
-        [(ids, SMEM), states, table, pthi, ptlo, mthi, mtlo],
+        [(ids, SMEM), states, pthi, ptlo, mthi, mtlo],
         [pltpu.VMEM((spans * days, width), F32)] * 3,
     )
 

time: 110 us -> 99 us (0.900)
  waiting for transfers between devices: 24.6 us -> 9.97 us
  blocking collectives: 44.1 us -> 52.2 us
  local copies, waits for them, and re-layouts: 4.56 us -> 0.01 us
    ppermute x3 -> x0, waiting for transfers between devices: 23.6 us -> none  [local(): lax.ppermute(extra, 'z', [((i + s) % planes, i) for i in range(planes)])]
    ppermute x3, waiting for transfers between devices: 1.03 us -> 9.28 us  [swap(): return lax.ppermute(x, 'obs', [(i, i ^ bit) for i in range(peers)])]
    all_to_all x1, blocking collectives: 22.2 us -> 30.1 us  [local(): lax.all_to_all(answer, everyone, split_axis=0, concat_axis=0, tiled=True)]
    unnamed x18 -> x6, local copies, waits for them, and re-layouts: 4.56 us -> 0.01 us
  transfers between devices with their start and end apart: 16 -> 13, of which waited for: 5 -> 3; matrix products, arithmetic and copies ran while one was open for 0% -> 0% of each run, Pallas kernels for 6% -> 7%
where the time goes in v4:
time: 99 us; the launch traced here: 98.6 us
  blocking collectives  52.2 us (53%)
  Pallas kernels  22.7 us (23%)
  starting transfers between devices  12.8 us (13%)
  waiting for transfers between devices  9.97 us (10%)
    all_to_all x1, blocking collectives, local(): lax.all_to_all(answer, everyone, split_axis=0, concat_axis=0, tiled=True)  30.1 us
    pallas_call x14, Pallas kernels, run(): pl.pallas_call(body, out_shape=[jax.ShapeDtypeStruct(s, d) for s, d in ou...  22.7 us
    all_to_all x1, blocking collectives, local(): lax.all_to_all(sent, ('y', 'obs'), split_axis=0, concat_axis=0, tiled=True)  22.1 us
    ppermute x3, waiting for transfers between devices, swap(): return lax.ppermute(x, 'obs', [(i, i ^ bit) for i in range(peers)])  9.28 us
    ppermute x3, starting transfers between devices, local(): lax.ppermute(pay, everyone, [((owner_plane(p) + s) % planes * spans + pla...  7.4 us
    ppermute x7, starting transfers between devices, local(): received = lax.ppermute(y, everyone, [(owner(k), owner(k + 1))])  4.86 us
  transfers between devices with their start and end apart: 13, of which 3 were waited for; matrix products, arithmetic and copies ran while one was open for 0% of the time, Pallas kernels for 7%

profile of v4, /device:TPU:0, one launch (start us, length us, event | category | flops | bytes accessed | tf_op | source)
XLA Modules:
  0.0 98.6 jit_solution(18335979803032730713)
XLA Ops:
  0.6 2.5 %shard_map.104 = bf16[8,144,512]{2,1,0:T(8,128)(2,1)} custom-call(s32[8]{0:T(128)} %day.1, s32[8]{0:T(128)} %count.1, bf16[1024,512]{1,0:T(8,128)(2,1)} %rows.1, bf16[8,128]{1,0:T(8,128)(2,1)} %bitcast.6, f32[1,128]{1,0:T(1,128)} %bitcast.7, f32[2,512]{1,0:T(2,128)} %damping.1), custom_call_target="tpu_custom_call" | custom-call | bytes 1055296 | tf_op jit(solution)/shard_map/pallas_call | solution.py:22
  3.1 22.1 %all_to_all.10.got = bf16[8,144,512]{2,1,0:T(8,128)(2,1)S(1)} all-to-all(bf16[8,144,512]{2,1,0:T(8,128)(2,1)} %shard_map.104), channel_id=1, replica_groups=mesh['z'=4,'y'=2,'obs'=4] {'y','obs'}, dimensions={0} | all-to-all | bytes 2359296 | tf_op jit(solution)/shard_map/all_to_all | solution.py:392
  25.2 2.1 %shard_map.105 = (f32[20,128,128]{2,1,0:T(8,128)S(1)}, f32[128,128]{1,0:T(8,128)S(1)}, bf16[21,128,128]{2,1,0:T(8,128)(2,1)}, f32[1,512]{1,0:T(1,128)S(1)}, f32[128,512]{1,0:T(8,128)}) custom-call(bf16[8,144,512]{2,1,0:T(8,128)(2,1)S(1)} %all_to_all.10.got, f32[128,512]{1,0:T(8,128)S(1)} %copy-done.2), custom_call_target="tpu_custom_call" | custom-call | flops 1073741824 | bytes 1441792 | tf_op jit(solution)/shard_map/pallas_call | solution.py:22
  27.3 4.3 %collective-permute-start.2 = (bf16[21,128,128]{2,1,0:T(8,128)(2,1)}, bf16[21,128,128]{2,1,0:T(8,128)(2,1)}, u32[]{:S(2)}, u32[]{:S(2)}) collective-permute-start(bf16[21,128,128]{2,1,0:T(8,128)(2,1)} %get-tuple-element.41), channel_id=1, source_target_pairs={{0,8},{9,17},{11,19},{2,10},{6,14},{15,23},{13,21},{4,12}} | collective-permute-start | bytes 2064392 | tf_op jit(solution)/shard_map/ppermute | solution.py:408
  31.6 1.5 %collective-permute-start.1 = (bf16[21,128,128]{2,1,0:T(8,128)(2,1)}, bf16[21,128,128]{2,1,0:T(8,128)(2,1)}, u32[]{:S(2)}, u32[]{:S(2)}) collective-permute-start(bf16[21,128,128]{2,1,0:T(8,128)(2,1)} %get-tuple-element.41), channel_id=1, source_target_pairs={{24,8},{1,17},{3,19},{26,10},{30,14},{7,23},{5,21},{28,12}} | collective-permute-start | bytes 2064392 | tf_op jit(solution)/shard_map/ppermute | solution.py:408
  33.1 1.6 %collective-permute-start = (bf16[21,128,128]{2,1,0:T(8,128)(2,1)}, bf16[21,128,128]{2,1,0:T(8,128)(2,1)}, u32[]{:S(2)}, u32[]{:S(2)}) collective-permute-start(bf16[21,128,128]{2,1,0:T(8,128)(2,1)} %get-tuple-element.41), channel_id=1, source_target_pairs={{16,8},{25,17},{27,19},{18,10},{22,14},{31,23},{29,21},{20,12}} | collective-permute-start | bytes 2064392 | tf_op jit(solution)/shard_map/ppermute | solution.py:408
  34.7 0.6 collective-permute-start.4
  35.3 8.1 %collective-permute-done.4.m2 = f32[128,512]{1,0:T(8,128)} collective-permute-done((f32[128,512]{1,0:T(8,128)}, f32[128,512]{1,0:T(8,128)}, u32[]{:S(2)}, u32[]{:S(2)}) %collective-permute-start.4) | collective-permute-done | bytes 262176 | tf_op jit(solution)/shard_map/ppermute | solution.py:414
  43.4 0.6 shard_map.106
  44.1 1.2 %collective-permute-done.5.m3 = f32[128,512]{1,0:T(8,128)} collective-permute-done((f32[128,512]{1,0:T(8,128)}, f32[128,512]{1,0:T(8,128)}, u32[]{:S(2)}, u32[]{:S(2)}) %collective-permute-start.5) | collective-permute-done | bytes 262176 | tf_op jit(solution)/shard_map/ppermute | solution.py:414
  45.3 0.7 collective-permute-done.2.g3
  45.9 3.1 %shard_map.107 = (bf16[2,512,512]{2,1,0:T(8,128)(2,1)S(1)}, bf16[2,512,512]{2,1,0:T(8,128)(2,1)S(1)}, f32[2,1,512]{2,1,0:T(1,128)S(1)}, f32[2,512]{1,0:T(2,128)S...) custom-call(s32[4]{0:T(128)S(1)} %pad_add_fusion.ids, f32[20,128,128]{2,1,0:T(8,128)S(1)} %get-tuple-element.39.own, ...), custom_call_target="tpu_custom_call" | custom-call | bytes 6326288 | tf_op jit(solution)/shard_map/pallas_call | solution.py:22
  49.0 0.7 collective-permute-start.6
  49.7 1.4 %shard_map.108 = (f32[1,512]{1,0:T(1,128)S(1)}, f32[1,512]{1,0:T(1,128)S(1)}) custom-call(f32[1,512]{1,0:T(1,128)S(1)} %get-tuple-element.48.acc, f32[1,512]{1,0:T(1,128)S(1)} %collective-permute-done.6.got, f32[2,512]{1,0:T(2,128)S(1)} %get-tuple-element.50.mine.damping, bf16[512,512]{1,0:T(8,128)(2,1)S(1)} %get-tuple-element.43.pthi, ...), custom_call_target="tpu_custom_call" | custom-call | bytes 4206592 | tf_op jit(solution)/shard_map/pallas_call | solution.py:22
  51.1 0.7 collective-permute-start.7
  51.8 4.7 %shard_map.109 = (bf16[512,512]{1,0:T(8,128)(2,1)S(1)}, bf16[512,512]{1,0:T(8,128)(2,1)S(1)}, bf16[512,512]{1,0:T(8,128)(2,1)S(1)}, bf16[512,512]{1,0:T(8,128)(2...) custom-call(f32[1,512]{1,0:T(1,128)S(1)} %get-tuple-element.54.after, ...), custom_call_target="tpu_custom_call" | custom-call | flops 4026531840 | bytes 4204544 | tf_op jit(solution)/shard_map/pallas_call | solution.py:22
  56.7 0.7 collective-permute-start.8
  57.7 0.7 collective-permute-start.9
  58.4 1.5 %shard_map.112 = (bf16[512,512]{1,0:T(8,128)(2,1)S(1)}, bf16[512,512]{1,0:T(8,128)(2,1)S(1)}) custom-call(f32[1,512]{1,0:T(1,128)S(1)} %get-tuple-element.62.after, s32[4]{0:T(128)S(1)} %pad_add_fusion.ids, f32[128,512]{1,0:T(8,128)} %get-tuple-element.47.m0, f32[128,512]{1,0:T(8,128)} %collective-permute-done.3.m1, f32[128,512]{1,0:T(8,128)} %collective-permute-done.4.m2, ...), custom_call_target="tpu_custom_call" | custom-call | bytes 1050640 | tf_op jit(solution)/shard_map/pallas_call | solution.py:22
  60.1 0.7 collective-permute-start.10
  61.1 0.7 collective-permute-start.11
  62.0 0.7 collective-permute-start.12
  63.2 30.1 %all_to_all.11.states = f32[32,4,512]{2,1,0:T(4,128)S(1)} all-to-all(f32[32,4,512]{2,1,0:T(4,128)S(1)} %shard_map.116), channel_id=1, replica_groups=mesh['z'=4,'y'=2,'obs'=4] {'z','y','obs'}, dimensions={0} | all-to-all | bytes 524288 | tf_op jit(solution)/shard_map/all_to_all | solution.py:451
  93.4 5.2 %shard_map.117 = (f32[2,128]{1,0:T(2,128)}, f32[2,128]{1,0:T(2,128)}) custom-call(s32[4]{0:T(128)S(1)} %pad_add_fusion.ids, f32[32,4,512]{2,1,0:T(4,128)S(1)} %all_to_all.11.states, bf16[512,512]{1,0:T(8,128)(2,1)S(1)} %get-tuple-element.43.pthi, bf16[512,512]{1,0:T(8,128)(2,1)S(1)} %get-tuple-element.44.ptlo, ...), custom_call_target="tpu_custom_call" | custom-call | bytes 2359312 | tf_op jit(solution)/shard_map/pallas_call | solution.py:22
  (25 shorter events, 1.6 us)
Async XLA Ops:
  3.1 22.1 %copy-start.2 = (f32[128,512]{1,0:T(8,128)S(1)}, f32[128,512]{1,0:T(8,128)}, u32[]{:S(2)}) copy-start(f32[128,512]{1,0:T(8,128)} %gain.1) | copy-start | bytes 786436
  25.2 18.2 %copy-start = (f32[512,512]{1,0:T(8,128)S(1)}, f32[512,512]{1,0:T(8,128)}, u32[]{:S(2)}) copy-start(f32[512,512]{1,0:T(8,128)} %trans.1) | copy-start | bytes 3145732
  25.2 18.2 %copy-start.1 = (f32[512,512]{1,0:T(8,128)S(1)}, f32[512,512]{1,0:T(8,128)}, u32[]{:S(2)}) copy-start(f32[512,512]{1,0:T(8,128)} %cov.1) | copy-start | bytes 3145732
  27.3 18.6 %collective-permute-start.2 = (bf16[21,128,128]{2,1,0:T(8,128)(2,1)}, bf16[21,128,128]{2,1,0:T(8,128)(2,1)}, u32[]{:S(2)}, u32[]{:S(2)}) collective-permute-start(bf16[21,128,128]{2,1,0:T(8,128)(2,1)} %get-tuple-element.41), channel_id=1, source_target_pairs={{0,8},{9,17},{11,19},{2,10},{6,14},{15,23},{13,21},{4,12}} | collective-permute-start | bytes 2064392 | tf_op jit(solution)/shard_map/ppermute | solution.py:408
  31.6 14.3 %collective-permute-start.1 = (bf16[21,128,128]{2,1,0:T(8,128)(2,1)}, bf16[21,128,128]{2,1,0:T(8,128)(2,1)}, u32[]{:S(2)}, u32[]{:S(2)}) collective-permute-start(bf16[21,128,128]{2,1,0:T(8,128)(2,1)} %get-tuple-element.41), channel_id=1, source_target_pairs={{24,8},{1,17},{3,19},{26,10},{30,14},{7,23},{5,21},{28,12}} | collective-permute-start | bytes 2064392 | tf_op jit(solution)/shard_map/ppermute | solution.py:408
  33.1 12.8 %collective-permute-start = (bf16[21,128,128]{2,1,0:T(8,128)(2,1)}, bf16[21,128,128]{2,1,0:T(8,128)(2,1)}, u32[]{:S(2)}, u32[]{:S(2)}) collective-permute-start(bf16[21,128,128]{2,1,0:T(8,128)(2,1)} %get-tuple-element.41), channel_id=1, source_target_pairs={{16,8},{25,17},{27,19},{18,10},{22,14},{31,23},{29,21},{20,12}} | collective-permute-start | bytes 2064392 | tf_op jit(solution)/shard_map/ppermute | solution.py:408
  34.7 8.7 %collective-permute-start.4 = (f32[128,512]{1,0:T(8,128)}, f32[128,512]{1,0:T(8,128)}, u32[]{:S(2)}, u32[]{:S(2)}) collective-permute-start(f32[128,512]{1,0:T(8,128)} %get-tuple-element.47.m0), channel_id=1, source_target_pairs={{0,2},{1,3},{2,0},{3,1},{4,6},{5,7},{6,4},{7,5},{8,10},{9,11},{10,... | collective-permute-start | bytes 786440 | tf_op jit(solution)/shard_map/ppermute | solution.py:414
  35.3 8.8 %collective-permute-start.3 = (f32[128,512]{1,0:T(8,128)}, f32[128,512]{1,0:T(8,128)}, u32[]{:S(2)}, u32[]{:S(2)}) collective-permute-start(f32[128,512]{1,0:T(8,128)} %get-tuple-element.47.m0), channel_id=1, source_target_pairs={{0,1},{1,0},{2,3},{3,2},{4,5},{5,4},{6,7},{7,6},{8,9},{9,8},{10,11... | collective-permute-start | bytes 786440 | tf_op jit(solution)/shard_map/ppermute | solution.py:414
  43.4 1.9 %collective-permute-start.5 = (f32[128,512]{1,0:T(8,128)}, f32[128,512]{1,0:T(8,128)}, u32[]{:S(2)}, u32[]{:S(2)}) collective-permute-start(f32[128,512]{1,0:T(8,128)} %collective-permute-done.4.m2), channel_id=1, source_target_pairs={{0,1},{1,0},{2,3},{3,2},{4,5},{5,4},{6,7},{7,6},{8,9},{9,8},{10,11... | collective-permute-start | bytes 786440 | tf_op jit(solution)/shard_map/ppermute | solution.py:414
  49.0 0.7 collective-permute-start.6
  51.1 5.4 %collective-permute-start.7 = (f32[1,512]{1,0:T(1,128)S(1)}, f32[1,512]{1,0:T(1,128)S(1)}, u32[]{:S(2)}, u32[]{:S(2)}) collective-permute-start(f32[1,512]{1,0:T(1,128)S(1)} %get-tuple-element.54.after), channel_id=1, source_target_pairs={{17,19}} | collective-permute-start | bytes 6152 | tf_op jit(solution)/shard_map/ppermute | solution.py:429
  56.7 0.7 collective-permute-start.8
  57.7 2.3 %collective-permute-start.9 = (f32[1,512]{1,0:T(1,128)S(1)}, f32[1,512]{1,0:T(1,128)S(1)}, u32[]{:S(2)}, u32[]{:S(2)}) collective-permute-start(f32[1,512]{1,0:T(1,128)S(1)} %get-tuple-element.62.after), channel_id=1, source_target_pairs={{10,14}} | collective-permute-start | bytes 6152 | tf_op jit(solution)/shard_map/ppermute | solution.py:429
  60.1 0.7 collective-permute-start.10
  61.1 0.7 collective-permute-start.11
  62.0 0.7 collective-permute-start.12

commit v5 on v4

--- a/solution.py
+++ b/solution.py
@@ -15,7 +15,7 @@
 HBM = pl.BlockSpec(memory_space=pltpu.HBM)
 
 
-def run(body, out, ins, scratch=(), limit=32, flops=0):
+def run(body, out, ins, scratch=(), limit=32, flops=0, outs=VMEM):
     specs = [x[1] if isinstance(x, tuple) else VMEM for x in ins]
     arrays = [x[0] if isinstance(x, tuple) else x for x in ins]
     moved = sum(a.size * a.dtype.itemsize for a in arrays)
@@ -23,7 +23,7 @@
         body,
         out_shape=[jax.ShapeDtypeStruct(s, d) for s, d in out],
         in_specs=specs,
-        out_specs=[VMEM] * len(out),
+        out_specs=[outs] * len(out),
         scratch_shapes=list(scratch),
         compiler_params=pltpu.CompilerParams(vmem_limit_bytes=limit * 1024 * 1024),
         cost_estimate=pl.CostEstimate(flops=flops, bytes_accessed=moved, transcendentals=0),
@@ -73,10 +73,13 @@
     return 1 + place(span) % 2
 
 
-EXTRA = 16
-
-
-def pack_kernel(day, count, rows, values, prior, damping, out, day_s, count_s, values_v, prior_v, damping_v, sems):
+EXTRA = 8
+DIAG, DAMP = 24, 48
+
+
+def pack_kernel(
+    day, count, rows, values, prior, damping, out, day_s, count_s, values_v, prior_v, damping_v, meta, sems
+):
     blocks = out.shape[0]
     slots = out.shape[1] - EXTRA
     width = out.shape[2]
@@ -94,10 +97,7 @@
         copy.wait()
     first, second, third = parts3(prior_v[...])
     below = jnp.concatenate(
-        [jnp.concatenate([second, third, jnp.zeros((1, width - 2 * LANES), F32)], 1)]
-        + parts3(damping_v[...])
-        + [jnp.zeros((EXTRA - 8, width), F32)],
-        0,
+        [jnp.concatenate([second, third, jnp.zeros((1, width - 2 * LANES), F32)], 1)] + parts3(damping_v[...]), 0
     )
     held = values_v[...].astype(F32)
     for k in range(blocks):
@@ -110,8 +110,10 @@
             ],
             1,
         )
-        out[place(k), slots : slots + EXTRA, :] = jnp.concatenate([line, below], 0).astype(BF16)
-    for copy in large:
+        meta[place(k)] = jnp.concatenate([line, below], 0).astype(BF16)
+    tail = pltpu.make_async_copy(meta, out.at[:, pl.ds(slots, EXTRA)], sems.at[len(small) + blocks])
+    tail.start()
+    for copy in large + [tail]:
         copy.wait()
 
 
@@ -164,9 +166,23 @@
         def _(g):
             one(g * group, False)
 
+    row = lax.broadcasted_iota(jnp.int32, (LANES, LANES), 0)
+    column = lax.broadcasted_iota(jnp.int32, (LANES, LANES), 1)
+    sides = [n for n, (i, j) in enumerate(tiles) if i != j]
+    middles = [n for n, (i, j) in enumerate(tiles) if i == j]
     for d in range(2):
         for part, piece in enumerate(parts3(extra[12 * d : 12 * d + chunks, :])):
             extra[12 * d + 4 * part : 12 * d + 4 * part + chunks, :] = piece
+        for m, n in enumerate(sides):
+            pay[d * len(sides) + m] = own[d * len(tiles) + n].astype(BF16)
+    for i, n in enumerate(middles):
+        squares = [own[d * len(tiles) + n] for d in range(2)]
+        pay[2 * len(sides) + i] = jnp.where(row >= column, squares[0], squares[1]).astype(BF16)
+        for d in range(2):
+            line = jnp.sum(jnp.where(row == column, squares[d], 0.0), axis=0, keepdims=True)
+            for part, piece in enumerate(parts3(line)):
+                r = DIAG + 12 * d + 4 * part + i
+                extra[r : r + 1, :] = piece
     for q in range(chunks):
         line = got[q, slots : slots + EXTRA, :].astype(F32)
         prior[:, q * LANES : (q + 1) * LANES] = line[0:1, 3 * LANES : 4 * LANES] + (
@@ -176,12 +192,11 @@
         line = got[4 * y, slots : slots + EXTRA, :].astype(F32)
         for k in range(6):
             for j in range(chunks):
-                r = 24 + 24 * y + 4 * k + j
+                r = DAMP + 24 * y + 4 * k + j
                 extra[r : r + 1, :] = line[2 + k : 3 + k, j * LANES : (j + 1) * LANES]
-    for n in range(own.shape[0]):
-        pay[n] = own[n].astype(BF16)
+    small_at = pay.shape[0] - extra.shape[0] // LANES
     for n in range(extra.shape[0] // LANES):
-        pay[own.shape[0] + n] = extra[n * LANES : (n + 1) * LANES, :].astype(BF16)
+        pay[small_at + n] = extra[n * LANES : (n + 1) * LANES, :].astype(BF16)
 
 
 def prep_kernel(trans, cov, pt, pthi, ptlo, chi, clo):
@@ -210,53 +225,63 @@
 
 
 def owner_kernel(
-    ids, own, extra, g1, g2, g3, prior, pthi, ptlo, chi, clo, m1, m2, m3,
+    ids, own, extra, g1, g2, g3, g4, prior, pthi, ptlo, chi, clo, m1, m2, m3,
     omhi, omlo, info, mine, start, y, table, small,
 ):
     planes = 4
     width = pthi.shape[0]
     chunks = width // LANES
     tiles = triangle(width)
-    got = (g1, g2, g3)
+    got = (g1, g2, g3, g4)
+    share = jnp.where(ids[0] == 2, 1.0, 0.0)
+    row = lax.broadcasted_iota(jnp.int32, (LANES, LANES), 0)
+    column = lax.broadcasted_iota(jnp.int32, (LANES, LANES), 1)
+    small_at = g1.shape[0] - extra.shape[0] // LANES
+    small[0] = extra[...]
+    for s, part in enumerate(got):
+        for n in range(extra.shape[0] // LANES):
+            small[s + 1, n * LANES : (n + 1) * LANES, :] = part[small_at + n].astype(F32)
+
+    def line(s, first, gap):
+        return small[s, first : first + 1, :] + (
+            small[s, first + gap : first + gap + 1, :] + small[s, first + 2 * gap : first + 2 * gap + 1, :]
+        )
+
+    def summed(first, gap):
+        others = line(1, first, gap) + (line(2, first, gap) + (line(3, first, gap) + line(4, first, gap)))
+        return line(0, first, gap) * share + others
+
+    def added(at):
+        return (g1[at].astype(F32) + g2[at].astype(F32)) + (g3[at].astype(F32) + g4[at].astype(F32))
+
+    def put(day, i, j, piece):
+        hi, lo = split(piece)
+        omhi[day, i * LANES : (i + 1) * LANES, j * LANES : (j + 1) * LANES] = hi
+        omlo[day, i * LANES : (i + 1) * LANES, j * LANES : (j + 1) * LANES] = lo
+
+    sides = [n for n, (i, j) in enumerate(tiles) if i != j]
+    middles = [n for n, (i, j) in enumerate(tiles) if i == j]
+    for i, n in enumerate(middles):
+        both = added(2 * len(sides) + i)
+        for day, part in enumerate((jnp.where(row > column, both, 0.0), jnp.where(row < column, both, 0.0))):
+            others = sum(line(s, DIAG + 12 * day + i, 4) for s in range(1, 5))
+            piece = own[day * len(tiles) + n] * share + (part + part.T)
+            put(day, i, i, piece + jnp.where(row == column, others, 0.0))
     for day in range(2):
-        for n, (i, j) in enumerate(tiles):
-            at = day * len(tiles) + n
-            piece = own[at] + (g1[at].astype(F32) + (g2[at].astype(F32) + g3[at].astype(F32)))
-            hi, lo = split(piece)
-            omhi[day, i * LANES : (i + 1) * LANES, j * LANES : (j + 1) * LANES] = hi
-            omlo[day, i * LANES : (i + 1) * LANES, j * LANES : (j + 1) * LANES] = lo
-            if i != j:
-                hi, lo = split(piece.T)
-                omhi[day, j * LANES : (j + 1) * LANES, i * LANES : (i + 1) * LANES] = hi
-                omlo[day, j * LANES : (j + 1) * LANES, i * LANES : (i + 1) * LANES] = lo
-    for s in range(planes):
-        if s == 0:
-            small[0] = extra[...]
-        else:
-            for n in range(extra.shape[0] // LANES):
-                small[s, n * LANES : (n + 1) * LANES, :] = got[s - 1][own.shape[0] + n].astype(F32)
-
-    def row(s, first, gap):
-        return jnp.concatenate(
-            [
-                small[s, first + j : first + j + 1, :]
-                + (
-                    small[s, first + gap + j : first + gap + j + 1, :]
-                    + small[s, first + 2 * gap + j : first + 2 * gap + j + 1, :]
-                )
-                for j in range(chunks)
-            ],
-            1,
-        )
-
-    for day in range(2):
-        info[day] = row(0, 12 * day, 4) + (row(1, 12 * day, 4) + (row(2, 12 * day, 4) + row(3, 12 * day, 4)))
+        for m, n in enumerate(sides):
+            i, j = tiles[n]
+            piece = own[day * len(tiles) + n] * share + added(day * len(sides) + m)
+            put(day, i, j, piece)
+            put(day, j, i, piece.T)
+        info[day] = jnp.concatenate([summed(12 * day + j, 4) for j in range(chunks)], 1)
     held = table.shape[0] // 2 // planes
     for s in range(planes):
         plane = lax.rem(ids[0] + s, planes)
         for k in range(held):
             for day in range(2):
-                table[pl.ds(2 * (plane * held + k) + day, 1), :] = row(s, 24 + 24 * k + 4 * day, 8)
+                table[pl.ds(2 * (plane * held + k) + day, 1), :] = jnp.concatenate(
+                    [line(s, DAMP + 24 * k + 4 * day + j, 8) for j in range(chunks)], 1
+                )
     for day in range(2):
         mine[day : day + 1, :] = table[pl.ds(2 * ids[1] + day, 1), :]
     state = prior[...]
@@ -306,7 +331,7 @@
     spans = total // 2
     chunks = width // LANES
     for c in range(spans):
-        one = states[owner_plane(c) * spans + place(c)]
+        one = states[owner_plane(c) * spans + (place(c) | 1)]
         f[2 * c : 2 * c + 2, :] = one[0:2]
         if c:
             d[2 * c - 1 : 2 * c + 1, :] = one[2:4]
@@ -353,19 +378,19 @@
     assert planes == peers == 4 and days == 2 and slots == LANES and blocks == spans
     z, y, o = (lax.axis_index(a) for a in ("z", "y", "obs"))
     at = y * peers + o
-    span = at
+    span = seat = jnp.where(z == 1, at - at % 2, at)
     for bit in range(1, spans.bit_length()):
-        span = span ^ (at >> bit)
+        span = span ^ (seat >> bit)
     ids = jnp.stack([z, span, o, z * held + y]).astype(jnp.int32)
     everyone = ("z", "y", "obs")
 
     def owner(span):
-        return owner_plane(span) * spans + place(span)
+        return owner_plane(span) * spans + (place(span) | 1)
 
     tiles = len(triangle(width))
-    extra_tiles = -(-(24 + 24 * held) // LANES)
+    extra_tiles = -(-(DAMP + 24 * held) // LANES)
     full, row = (width, width), ((1, width), F32)
-    (sent,) = run(
+    sent = run(
         pack_kernel,
         [((blocks, slots + EXTRA, width), BF16)],
         [
@@ -385,10 +410,12 @@
             pltpu.VMEM((blocks, slots), BF16),
             pltpu.VMEM((1, width // peers), F32),
             pltpu.VMEM((days, width), F32),
-            pltpu.SemaphoreType.DMA((5 + blocks,)),
+            pltpu.VMEM((blocks, EXTRA, width), BF16),
+            pltpu.SemaphoreType.DMA((6 + blocks,)),
         ],
         limit=60,
-    )
+        outs=HBM,
+    )[0]
     got = lax.all_to_all(sent, ("y", "obs"), split_axis=0, concat_axis=0, tiled=True)
     span_slots = min(blocks, 8) * slots
     own, extra, pay, prior, gain = run(
@@ -396,7 +423,7 @@
         [
             ((2 * tiles, LANES, LANES), F32),
             ((extra_tiles * LANES, LANES), F32),
-            ((2 * tiles + extra_tiles, LANES, LANES), BF16),
+            ((2 * tiles - width // LANES + extra_tiles, LANES, LANES), BF16),
             row,
             (unattenuated_multiplier.shape, F32),
         ],
@@ -410,6 +437,12 @@
         )
         for s in range(1, planes)
     ]
+    plane_sums.append(
+        lax.ppermute(
+            pay, everyone, [(spans + place(p), owner(p)) for p in range(spans) if place(p) % 2 == 0]
+        )
+    )
+
     def swap(x, bit):
         return lax.ppermute(x, "obs", [(i, i ^ bit) for i in range(peers)])
 
@@ -423,7 +456,7 @@
         [((days,) + full, BF16)] * 2
         + [((days, 1, width), F32), ((days, width), F32), row, row],
         [(ids, SMEM), own, extra, *plane_sums, prior, pthi, ptlo, chi, clo, *[(g, ANY) for g in gains[1:]]],
-        [pltpu.VMEM((spans * days, width), F32), pltpu.VMEM((planes, extra_tiles * LANES, LANES), F32)],
+        [pltpu.VMEM((spans * days, width), F32), pltpu.VMEM((planes + 1, extra_tiles * LANES, LANES), F32)],
     )
     for k in range(spans - 1):
         received = lax.ppermute(y, everyone, [(owner(k), owner(k + 1))])

time: 99 us -> 127 us (1.28)
  Pallas kernels: 22.7 us -> 53.2 us
  waiting for transfers between devices: 9.97 us -> 4.01 us
  starting transfers between devices: 12.8 us -> 14.7 us
  local copies, waits for them, and re-layouts: 0.01 us -> 1.41 us
    pallas_call x14, Pallas kernels: 22.7 us -> 53.2 us  [run(): pl.pallas_call(body, out_shape=[jax.ShapeDtypeStruct(s, d) for s, d in ou...]
    ppermute x3, waiting for transfers between devices: 9.28 us -> 1.25 us  [swap(): return lax.ppermute(x, 'obs', [(i, i ^ bit) for i in range(peers)])]
    ppermute x3, waiting for transfers between devices: 0.67 us -> 2.73 us  [local(): lax.ppermute(pay, everyone, [((owner_plane(p) + s) % planes * spans + pla...]
    ppermute x3, starting transfers between devices: 0.57 us -> 2.07 us  [swap(): return lax.ppermute(x, 'obs', [(i, i ^ bit) for i in range(peers)])]
    ppermute x0 -> x1, starting transfers between devices: none -> 1.47 us  [local(): lax.ppermute(pay, everyone, [(spans + place(p), owner(p)) for p in range(...]
    unnamed x6 -> x14, local copies, waits for them, and re-layouts: 0.01 us -> 1.41 us
  transfers between devices with their start and end apart: 13 -> 14, of which waited for: 3 -> 3; matrix products, arithmetic and copies ran while one was open for 0% -> 0% of each run, Pallas kernels for 7% -> 5%
where the time goes in v5:
time: 127 us
  Pallas kernels  53.2 us (42%)
  blocking collectives  52.7 us (41%)
  starting transfers between devices  14.7 us (12%)
  waiting for transfers between devices  4.01 us (3%)
  local copies, waits for them, and re-layouts  1.41 us (1%)
    pallas_call x14, Pallas kernels, run(): pl.pallas_call(body, out_shape=[jax.ShapeDtypeStruct(s, d) for s, d in ou...  53.2 us
    all_to_all x1, blocking collectives, local(): lax.all_to_all(answer, everyone, split_axis=0, concat_axis=0, tiled=True)  31.3 us
    all_to_all x1, blocking collectives, local(): lax.all_to_all(sent, ('y', 'obs'), split_axis=0, concat_axis=0, tiled=True)  21.4 us
    ppermute x3, starting transfers between devices, local(): lax.ppermute(pay, everyone, [((owner_plane(p) + s) % planes * spans + pla...  6.32 us
    ppermute x7, starting transfers between devices, local(): received = lax.ppermute(y, everyone, [(owner(k), owner(k + 1))])  4.86 us
    ppermute x3, waiting for transfers between devices, local(): lax.ppermute(pay, everyone, [((owner_plane(p) + s) % planes * spans + pla...  2.73 us
  transfers between devices with their start and end apart: 14, of which 3 were waited for; matrix products, arithmetic and copies ran while one was open for 0% of the time, Pallas kernels for 5%

profile of v5, /device:TPU:0, one launch (start us, length us, event | category | flops | bytes accessed | tf_op | source)
XLA Modules:
  0.0 126.9 jit_solution(17086769177392807673)
XLA Ops:
  0.6 33.0 %shard_map.104 = bf16[8,136,512]{2,1,0:T(8,128)(2,1)} custom-call(s32[8]{0:T(128)} %day.1, s32[8]{0:T(128)} %count.1, bf16[1024,512]{1,0:T(8,128)(2,1)} %rows.1, bf16[8,128]{1,0:T(8,128)(2,1)} %bitcast.6, f32[1,128]{1,0:T(1,128)} %bitcast.7, f32[2,512]{1,0:T(2,128)} %damping.1), custom_call_target="tpu_custom_call" | custom-call | bytes 1055296 | tf_op jit(solution)/shard_map/pallas_call | solution.py:22
  33.6 21.4 %all_to_all.10.got = bf16[8,136,512]{2,1,0:T(8,128)(2,1)S(1)} all-to-all(bf16[8,136,512]{2,1,0:T(8,128)(2,1)} %shard_map.104), channel_id=1, replica_groups=mesh['z'=4,'y'=2,'obs'=4] {'y','obs'}, dimensions={0} | all-to-all | bytes 2228224 | tf_op jit(solution)/shard_map/all_to_all | solution.py:419
  55.0 2.0 %shard_map.105 = (f32[20,128,128]{2,1,0:T(8,128)S(1)}, f32[128,128]{1,0:T(8,128)S(1)}, bf16[17,128,128]{2,1,0:T(8,128)(2,1)}, f32[1,512]{1,0:T(1,128)S(1)}, f32[128,512]{1,0:T(8,128)S(1)}) custom-call(bf16[8,136,512]{2,1,0:T(8,128)(2,1)S(1)} %all_to_all.10.got, f32[128,512]{1,0:T(8,128)S(1)} %copy-done.6), custom_call_target="tpu_custom_call" | custom-call | flops 1073741824 | bytes 1376256 | tf_op jit(solution)/shard_map/pallas_call | solution.py:22
  57.6 1.5 %collective-permute-start.3 = (bf16[17,128,128]{2,1,0:T(8,128)(2,1)}, bf16[17,128,128]{2,1,0:T(8,128)(2,1)}, u32[]{:S(2)}, u32[]{:S(2)}) collective-permute-start(bf16[17,128,128]{2,1,0:T(8,128)(2,1)} %get-tuple-element.41), channel_id=1, source_target_pairs={{8,9},{10,11},{14,15},{12,13}} | collective-permute-start | bytes 1671176 | tf_op jit(solution)/shard_map/ppermute | solution.py:441
  59.1 3.4 %collective-permute-start.2 = (bf16[17,128,128]{2,1,0:T(8,128)(2,1)}, bf16[17,128,128]{2,1,0:T(8,128)(2,1)}, u32[]{:S(2)}, u32[]{:S(2)}) collective-permute-start(bf16[17,128,128]{2,1,0:T(8,128)(2,1)} %get-tuple-element.41), channel_id=1, source_target_pairs={{0,9},{9,17},{11,19},{2,11},{6,15},{15,23},{13,21},{4,13}} | collective-permute-start | bytes 1671176 | tf_op jit(solution)/shard_map/ppermute | solution.py:435
  62.4 1.5 %collective-permute-start.1 = (bf16[17,128,128]{2,1,0:T(8,128)(2,1)}, bf16[17,128,128]{2,1,0:T(8,128)(2,1)}, u32[]{:S(2)}, u32[]{:S(2)}) collective-permute-start(bf16[17,128,128]{2,1,0:T(8,128)(2,1)} %get-tuple-element.41), channel_id=1, source_target_pairs={{24,9},{1,17},{3,19},{26,11},{30,15},{7,23},{5,21},{28,13}} | collective-permute-start | bytes 1671176 | tf_op jit(solution)/shard_map/ppermute | solution.py:435
  63.9 1.5 %collective-permute-start = (bf16[17,128,128]{2,1,0:T(8,128)(2,1)}, bf16[17,128,128]{2,1,0:T(8,128)(2,1)}, u32[]{:S(2)}, u32[]{:S(2)}) collective-permute-start(bf16[17,128,128]{2,1,0:T(8,128)(2,1)} %get-tuple-element.41), channel_id=1, source_target_pairs={{16,9},{25,17},{27,19},{18,11},{22,15},{31,23},{29,21},{20,13}} | collective-permute-start | bytes 1671176 | tf_op jit(solution)/shard_map/ppermute | solution.py:435
  65.4 1.1 collective-permute-start.4
  66.5 0.7 copy-done.4
  67.7 0.7 copy-done.2
  69.5 0.8 collective-permute-done.6.m3
  70.3 2.7 %collective-permute-done.2.g3 = bf16[17,128,128]{2,1,0:T(8,128)(2,1)} collective-permute-done((bf16[17,128,128]{2,1,0:T(8,128)(2,1)}, bf16[17,128,128]{2,1,0:T(8,128)(2,1)}, u32[]{:S(2)}, u32[]{:S(2)}) %collective-permute-start.2) | collective-permute-done | bytes 557088 | tf_op jit(solution)/shard_map/ppermute | solution.py:435
  73.0 3.3 %shard_map.107 = (bf16[2,512,512]{2,1,0:T(8,128)(2,1)S(1)}, bf16[2,512,512]{2,1,0:T(8,128)(2,1)S(1)}, f32[2,1,512]{2,1,0:T(1,128)S(1)}, f32[2,512]{1,0:T(2,128)S...) custom-call(s32[4]{0:T(128)S(1)} %pad_add_fusion.ids, f32[20,128,128]{2,1,0:T(8,128)S(1)} %get-tuple-element.39.own, ...), custom_call_target="tpu_custom_call" | custom-call | bytes 6490128 | tf_op jit(solution)/shard_map/pallas_call | solution.py:22
  76.3 0.7 collective-permute-start.7
  77.0 1.4 %shard_map.108 = (f32[1,512]{1,0:T(1,128)S(1)}, f32[1,512]{1,0:T(1,128)S(1)}) custom-call(f32[1,512]{1,0:T(1,128)S(1)} %get-tuple-element.48.acc, f32[1,512]{1,0:T(1,128)S(1)} %collective-permute-done.7.got, f32[2,512]{1,0:T(2,128)S(1)} %get-tuple-element.50.mine.damping, bf16[512,512]{1,0:T(8,128)(2,1)S(1)} %get-tuple-element.43.pthi, ...), custom_call_target="tpu_custom_call" | custom-call | bytes 4206592 | tf_op jit(solution)/shard_map/pallas_call | solution.py:22
  79.1 4.8 %shard_map.109 = (bf16[512,512]{1,0:T(8,128)(2,1)S(1)}, bf16[512,512]{1,0:T(8,128)(2,1)S(1)}, bf16[512,512]{1,0:T(8,128)(2,1)S(1)}, bf16[512,512]{1,0:T(8,128)(2...) custom-call(f32[1,512]{1,0:T(1,128)S(1)} %get-tuple-element.54.after, ...), custom_call_target="tpu_custom_call" | custom-call | flops 4026531840 | bytes 4204544 | tf_op jit(solution)/shard_map/pallas_call | solution.py:22
  84.1 0.7 collective-permute-start.9
  85.0 0.7 collective-permute-start.10
  85.7 1.4 %shard_map.112 = (bf16[512,512]{1,0:T(8,128)(2,1)S(1)}, bf16[512,512]{1,0:T(8,128)(2,1)S(1)}) custom-call(f32[1,512]{1,0:T(1,128)S(1)} %get-tuple-element.62.after, s32[4]{0:T(128)S(1)} %pad_add_fusion.ids, f32[128,512]{1,0:T(8,128)S(1)} %copy-done.5, f32[128,512]{1,0:T(8,128)S(1)} %copy-done.3, f32[128,512]{1,0:T(8,128)} %collective-permute-done.5.m2, ...), custom_call_target="tpu_custom_call" | custom-call | bytes 1050640 | tf_op jit(solution)/shard_map/pallas_call | solution.py:22
  87.3 0.7 collective-permute-start.11
  88.2 0.7 collective-permute-start.12
  89.2 0.7 collective-permute-start.13
  90.4 31.3 %all_to_all.11.states = f32[32,4,512]{2,1,0:T(4,128)S(1)} all-to-all(f32[32,4,512]{2,1,0:T(4,128)S(1)} %shard_map.116), channel_id=1, replica_groups=mesh['z'=4,'y'=2,'obs'=4] {'z','y','obs'}, dimensions={0} | all-to-all | bytes 524288 | tf_op jit(solution)/shard_map/all_to_all | solution.py:484
  121.7 5.2 %shard_map.117 = (f32[2,128]{1,0:T(2,128)}, f32[2,128]{1,0:T(2,128)}) custom-call(s32[4]{0:T(128)S(1)} %pad_add_fusion.ids, f32[32,4,512]{2,1,0:T(4,128)S(1)} %all_to_all.11.states, bf16[512,512]{1,0:T(8,128)(2,1)S(1)} %get-tuple-element.43.pthi, bf16[512,512]{1,0:T(8,128)(2,1)S(1)} %get-tuple-element.44.ptlo, ...), custom_call_target="tpu_custom_call" | custom-call | bytes 2359312 | tf_op jit(solution)/shard_map/pallas_call | solution.py:22
  (35 shorter events, 4.3 us)
Async XLA Ops:
  33.6 21.4 %copy-start.6 = (f32[128,512]{1,0:T(8,128)S(1)}, f32[128,512]{1,0:T(8,128)}, u32[]{:S(2)}) copy-start(f32[128,512]{1,0:T(8,128)} %gain.1) | copy-start | bytes 786436
  55.0 13.7 %copy-start = (f32[512,512]{1,0:T(8,128)S(1)}, f32[512,512]{1,0:T(8,128)}, u32[]{:S(2)}) copy-start(f32[512,512]{1,0:T(8,128)} %trans.1) | copy-start | bytes 3145732
  55.0 13.7 %copy-start.1 = (f32[512,512]{1,0:T(8,128)S(1)}, f32[512,512]{1,0:T(8,128)}, u32[]{:S(2)}) copy-start(f32[512,512]{1,0:T(8,128)} %cov.1) | copy-start | bytes 3145732
  57.0 8.4 %collective-permute-start.5 = (f32[128,512]{1,0:T(8,128)S(1)}, f32[128,512]{1,0:T(8,128)}, u32[]{:S(2)}, u32[]{:S(2)}) collective-permute-start(f32[128,512]{1,0:T(8,128)S(1)} %get-tuple-element.47.m0), channel_id=1, source_target_pairs={{0,2},{1,3},{2,0},{3,1},{4,6},{5,7},{6,4},{7,5},{8,10},{9,11},{10,... | collective-permute-start | bytes 786440 | tf_op jit(solution)/shard_map/ppermute | solution.py:447
  57.6 12.7 %collective-permute-start.3 = (bf16[17,128,128]{2,1,0:T(8,128)(2,1)}, bf16[17,128,128]{2,1,0:T(8,128)(2,1)}, u32[]{:S(2)}, u32[]{:S(2)}) collective-permute-start(bf16[17,128,128]{2,1,0:T(8,128)(2,1)} %get-tuple-element.41), channel_id=1, source_target_pairs={{8,9},{10,11},{14,15},{12,13}} | collective-permute-start | bytes 1671176 | tf_op jit(solution)/shard_map/ppermute | solution.py:441
  59.1 13.9 %collective-permute-start.2 = (bf16[17,128,128]{2,1,0:T(8,128)(2,1)}, bf16[17,128,128]{2,1,0:T(8,128)(2,1)}, u32[]{:S(2)}, u32[]{:S(2)}) collective-permute-start(bf16[17,128,128]{2,1,0:T(8,128)(2,1)} %get-tuple-element.41), channel_id=1, source_target_pairs={{0,9},{9,17},{11,19},{2,11},{6,15},{15,23},{13,21},{4,13}} | collective-permute-start | bytes 1671176 | tf_op jit(solution)/shard_map/ppermute | solution.py:435
  62.4 10.5 %collective-permute-start.1 = (bf16[17,128,128]{2,1,0:T(8,128)(2,1)}, bf16[17,128,128]{2,1,0:T(8,128)(2,1)}, u32[]{:S(2)}, u32[]{:S(2)}) collective-permute-start(bf16[17,128,128]{2,1,0:T(8,128)(2,1)} %get-tuple-element.41), channel_id=1, source_target_pairs={{24,9},{1,17},{3,19},{26,11},{30,15},{7,23},{5,21},{28,13}} | collective-permute-start | bytes 1671176 | tf_op jit(solution)/shard_map/ppermute | solution.py:435
  63.9 9.1 %collective-permute-start = (bf16[17,128,128]{2,1,0:T(8,128)(2,1)}, bf16[17,128,128]{2,1,0:T(8,128)(2,1)}, u32[]{:S(2)}, u32[]{:S(2)}) collective-permute-start(bf16[17,128,128]{2,1,0:T(8,128)(2,1)} %get-tuple-element.41), channel_id=1, source_target_pairs={{16,9},{25,17},{27,19},{18,11},{22,15},{31,23},{29,21},{20,13}} | collective-permute-start | bytes 1671176 | tf_op jit(solution)/shard_map/ppermute | solution.py:435
  65.4 2.3 %collective-permute-start.4 = (f32[128,512]{1,0:T(8,128)S(1)}, f32[128,512]{1,0:T(8,128)S(1)}, u32[]{:S(2)}, u32[]{:S(2)}) collective-permute-start(f32[128,512]{1,0:T(8,128)S(1)} %get-tuple-element.47.m0), channel_id=1, source_target_pairs={{0,1},{1,0},{2,3},{3,2},{4,5},{5,4},{6,7},{7,6},{8,9},{9,8},{10,11... | collective-permute-start | bytes 786440 | tf_op jit(solution)/shard_map/ppermute | solution.py:447
  66.5 0.7 copy-start.4
  67.7 0.7 copy-start.2
  68.4 1.9 %collective-permute-start.6 = (f32[128,512]{1,0:T(8,128)}, f32[128,512]{1,0:T(8,128)}, u32[]{:S(2)}, u32[]{:S(2)}) collective-permute-start(f32[128,512]{1,0:T(8,128)} %collective-permute-done.5.m2), channel_id=1, source_target_pairs={{0,1},{1,0},{2,3},{3,2},{4,5},{5,4},{6,7},{7,6},{8,9},{9,8},{10,11... | collective-permute-start | bytes 786440 | tf_op jit(solution)/shard_map/ppermute | solution.py:447
  68.8 4.2 %copy-start.3 = (f32[128,512]{1,0:T(8,128)S(1)}, f32[128,512]{1,0:T(8,128)}, u32[]{:S(2)}) copy-start(f32[128,512]{1,0:T(8,128)} %copy-done.2) | copy-start | bytes 786436
  76.3 0.7 collective-permute-start.7
  78.4 5.4 %collective-permute-start.8 = (f32[1,512]{1,0:T(1,128)S(1)}, f32[1,512]{1,0:T(1,128)S(1)}, u32[]{:S(2)}, u32[]{:S(2)}) collective-permute-start(f32[1,512]{1,0:T(1,128)S(1)} %get-tuple-element.54.after), channel_id=1, source_target_pairs={{17,19}} | collective-permute-start | bytes 6152 | tf_op jit(solution)/shard_map/ppermute | solution.py:462
  83.8 1.9 %copy-start.5 = (f32[128,512]{1,0:T(8,128)S(1)}, f32[128,512]{1,0:T(8,128)}, u32[]{:S(2)}) copy-start(f32[128,512]{1,0:T(8,128)} %copy-done.4) | copy-start | bytes 786436
  84.1 0.7 collective-permute-start.9
  85.0 2.1 %collective-permute-start.10 = (f32[1,512]{1,0:T(1,128)S(1)}, f32[1,512]{1,0:T(1,128)S(1)}, u32[]{:S(2)}, u32[]{:S(2)}) collective-permute-start(f32[1,512]{1,0:T(1,128)S(1)} %get-tuple-element.62.after), channel_id=1, source_target_pairs={{11,15}} | collective-permute-start | bytes 6152 | tf_op jit(solution)/shard_map/ppermute | solution.py:462
  87.3 0.7 collective-permute-start.11
  88.2 0.7 collective-permute-start.12
  89.2 0.7 collective-permute-start.13

commit v6 on v5

--- a/solution.py
+++ b/solution.py
@@ -78,7 +78,7 @@
 
 
 def pack_kernel(
-    day, count, rows, values, prior, damping, out, day_s, count_s, values_v, prior_v, damping_v, meta, sems
+    day, count, rows, values, prior, damping, out, day_s, count_s, values_v, prior_v, damping_v, stage, sems
 ):
     blocks = out.shape[0]
     slots = out.shape[1] - EXTRA
@@ -87,7 +87,7 @@
     copies = [pltpu.make_async_copy(src, dst, sems.at[n]) for n, (src, dst) in enumerate(small)]
     large = [
         pltpu.make_async_copy(
-            rows.at[pl.ds(k * slots, slots)], out.at[place(k), pl.ds(0, slots)], sems.at[len(small) + k]
+            rows.at[pl.ds(k * slots, slots)], stage.at[place(k), pl.ds(0, slots)], sems.at[len(small) + k]
         )
         for k in range(blocks)
     ]
@@ -110,10 +110,15 @@
             ],
             1,
         )
-        meta[place(k)] = jnp.concatenate([line, below], 0).astype(BF16)
-    tail = pltpu.make_async_copy(meta, out.at[:, pl.ds(slots, EXTRA)], sems.at[len(small) + blocks])
-    tail.start()
-    for copy in large + [tail]:
+        stage[place(k), slots : slots + EXTRA, :] = jnp.concatenate([line, below], 0).astype(BF16)
+    sends = [
+        pltpu.make_async_copy(stage.at[place(k)], out.at[place(k)], sems.at[len(small) + blocks + k])
+        for k in range(blocks)
+    ]
+    for k in range(blocks):
+        large[k].wait()
+        sends[k].start()
+    for copy in sends:
         copy.wait()
 
 
@@ -225,7 +230,7 @@
 
 
 def owner_kernel(
-    ids, own, extra, g1, g2, g3, g4, prior, pthi, ptlo, chi, clo, m1, m2, m3,
+    ids, own, extra, g4, g3, g2, g1, prior, pthi, ptlo, chi, clo, m1, m2, m3,
     omhi, omlo, info, mine, start, y, table, small,
 ):
     planes = 4
@@ -410,8 +415,8 @@
             pltpu.VMEM((blocks, slots), BF16),
             pltpu.VMEM((1, width // peers), F32),
             pltpu.VMEM((days, width), F32),
-            pltpu.VMEM((blocks, EXTRA, width), BF16),
-            pltpu.SemaphoreType.DMA((6 + blocks,)),
+            pltpu.VMEM((blocks, slots + EXTRA, width), BF16),
+            pltpu.SemaphoreType.DMA((5 + 2 * blocks,)),
         ],
         limit=60,
         outs=HBM,
@@ -433,15 +438,14 @@
     )
     plane_sums = [
         lax.ppermute(
+            pay, everyone, [(spans + place(p), owner(p)) for p in range(spans) if place(p) % 2 == 0]
+        )
+    ] + [
+        lax.ppermute(
             pay, everyone, [((owner_plane(p) + s) % planes * spans + place(p), owner(p)) for p in range(spans)]
         )
-        for s in range(1, planes)
+        for s in range(planes - 1, 0, -1)
     ]
-    plane_sums.append(
-        lax.ppermute(
-            pay, everyone, [(spans + place(p), owner(p)) for p in range(spans) if place(p) % 2 == 0]
-        )
-    )
 
     def swap(x, bit):
         return lax.ppermute(x, "obs", [(i, i ^ bit) for i in range(peers)])

time: 127 us -> 92.5 us (0.73)
  Pallas kernels: 53.2 us -> 22.4 us
  blocking collectives: 52.7 us -> 46.2 us
  waiting for transfers between devices: 4.01 us -> 6.42 us
    pallas_call x14, Pallas kernels: 53.2 us -> 22.4 us  [run(): pl.pallas_call(body, out_shape=[jax.ShapeDtypeStruct(s, d) for s, d in ou...]
    all_to_all x1, blocking collectives: 31.3 us -> 24.9 us  [local(): lax.all_to_all(answer, everyone, split_axis=0, concat_axis=0, tiled=True)]
    ppermute x3, waiting for transfers between devices: 2.73 us -> 5.15 us  [local(): lax.ppermute(pay, everyone, [((owner_plane(p) + s) % planes * spans + pla...]
  transfers between devices with their start and end apart: 14 -> 14, of which waited for: 3 -> 3; matrix products, arithmetic and copies ran while one was open for 0% -> 0% of each run, Pallas kernels for 5% -> 7%
where the time goes in v6:
time: 92.5 us; the launch traced here: 92.1 us
  blocking collectives  46.2 us (50%)
  Pallas kernels  22.4 us (24%)
  starting transfers between devices  14.7 us (16%)
  waiting for transfers between devices  6.42 us (7%)
  local copies, waits for them, and re-layouts  1.41 us (2%)
    all_to_all x1, blocking collectives, local(): lax.all_to_all(answer, everyone, split_axis=0, concat_axis=0, tiled=True)  24.9 us
    pallas_call x14, Pallas kernels, run(): pl.pallas_call(body, out_shape=[jax.ShapeDtypeStruct(s, d) for s, d in ou...  22.4 us
    all_to_all x1, blocking collectives, local(): lax.all_to_all(sent, ('y', 'obs'), split_axis=0, concat_axis=0, tiled=True)  21.4 us
    ppermute x3, starting transfers between devices, local(): lax.ppermute(pay, everyone, [((owner_plane(p) + s) % planes * spans + pla...  6.14 us
    ppermute x3, waiting for transfers between devices, local(): lax.ppermute(pay, everyone, [((owner_plane(p) + s) % planes * spans + pla...  5.15 us
    ppermute x7, starting transfers between devices, local(): received = lax.ppermute(y, everyone, [(owner(k), owner(k + 1))])  4.86 us
    ppermute x3, starting transfers between devices, swap(): return lax.ppermute(x, 'obs', [(i, i ^ bit) for i in range(peers)])  2.23 us
  transfers between devices with their start and end apart: 14, of which 3 were waited for; matrix products, arithmetic and copies ran while one was open for 0% of the time, Pallas kernels for 7%

profile of v6, /device:TPU:0, one launch (start us, length us, event | category | flops | bytes accessed | tf_op | source)
XLA Modules:
  0.0 92.1 jit_solution(10790094180052378066)
XLA Ops:
  0.6 2.2 %shard_map.104 = bf16[8,136,512]{2,1,0:T(8,128)(2,1)} custom-call(s32[8]{0:T(128)} %day.1, s32[8]{0:T(128)} %count.1, bf16[1024,512]{1,0:T(8,128)(2,1)} %rows.1, bf16[8,128]{1,0:T(8,128)(2,1)} %bitcast.6, f32[1,128]{1,0:T(1,128)} %bitcast.7, f32[2,512]{1,0:T(2,128)} %damping.1), custom_call_target="tpu_custom_call" | custom-call | bytes 1055296 | tf_op jit(solution)/shard_map/pallas_call | solution.py:22
  2.9 21.4 %all_to_all.10.got = bf16[8,136,512]{2,1,0:T(8,128)(2,1)S(1)} all-to-all(bf16[8,136,512]{2,1,0:T(8,128)(2,1)} %shard_map.104), channel_id=1, replica_groups=mesh['z'=4,'y'=2,'obs'=4] {'y','obs'}, dimensions={0} | all-to-all | bytes 2228224 | tf_op jit(solution)/shard_map/all_to_all | solution.py:424
  24.2 2.0 %shard_map.105 = (f32[20,128,128]{2,1,0:T(8,128)S(1)}, f32[128,128]{1,0:T(8,128)S(1)}, bf16[17,128,128]{2,1,0:T(8,128)(2,1)}, f32[1,512]{1,0:T(1,128)S(1)}, f32[128,512]{1,0:T(8,128)S(1)}) custom-call(bf16[8,136,512]{2,1,0:T(8,128)(2,1)S(1)} %all_to_all.10.got, f32[128,512]{1,0:T(8,128)S(1)} %copy-done.6), custom_call_target="tpu_custom_call" | custom-call | flops 1073741824 | bytes 1376256 | tf_op jit(solution)/shard_map/pallas_call | solution.py:22
  26.8 1.5 %collective-permute-start.3 = (bf16[17,128,128]{2,1,0:T(8,128)(2,1)}, bf16[17,128,128]{2,1,0:T(8,128)(2,1)}, u32[]{:S(2)}, u32[]{:S(2)}) collective-permute-start(bf16[17,128,128]{2,1,0:T(8,128)(2,1)} %get-tuple-element.41), channel_id=1, source_target_pairs={{16,9},{25,17},{27,19},{18,11},{22,15},{31,23},{29,21},{20,13}} | collective-permute-start | bytes 1671176 | tf_op jit(solution)/shard_map/ppermute | solution.py:444
  28.3 1.5 %collective-permute-start.2 = (bf16[17,128,128]{2,1,0:T(8,128)(2,1)}, bf16[17,128,128]{2,1,0:T(8,128)(2,1)}, u32[]{:S(2)}, u32[]{:S(2)}) collective-permute-start(bf16[17,128,128]{2,1,0:T(8,128)(2,1)} %get-tuple-element.41), channel_id=1, source_target_pairs={{24,9},{1,17},{3,19},{26,11},{30,15},{7,23},{5,21},{28,13}} | collective-permute-start | bytes 1671176 | tf_op jit(solution)/shard_map/ppermute | solution.py:444
  29.7 3.2 %collective-permute-start.1 = (bf16[17,128,128]{2,1,0:T(8,128)(2,1)}, bf16[17,128,128]{2,1,0:T(8,128)(2,1)}, u32[]{:S(2)}, u32[]{:S(2)}) collective-permute-start(bf16[17,128,128]{2,1,0:T(8,128)(2,1)} %get-tuple-element.41), channel_id=1, source_target_pairs={{0,9},{9,17},{11,19},{2,11},{6,15},{15,23},{13,21},{4,13}} | collective-permute-start | bytes 1671176 | tf_op jit(solution)/shard_map/ppermute | solution.py:444
  33.0 1.5 %collective-permute-start = (bf16[17,128,128]{2,1,0:T(8,128)(2,1)}, bf16[17,128,128]{2,1,0:T(8,128)(2,1)}, u32[]{:S(2)}, u32[]{:S(2)}) collective-permute-start(bf16[17,128,128]{2,1,0:T(8,128)(2,1)} %get-tuple-element.41), channel_id=1, source_target_pairs={{8,9},{10,11},{14,15},{12,13}} | collective-permute-start | bytes 1671176 | tf_op jit(solution)/shard_map/ppermute | solution.py:440
  34.4 1.3 %collective-permute-start.4 = (f32[128,512]{1,0:T(8,128)S(1)}, f32[128,512]{1,0:T(8,128)S(1)}, u32[]{:S(2)}, u32[]{:S(2)}) collective-permute-start(f32[128,512]{1,0:T(8,128)S(1)} %get-tuple-element.47.m0), channel_id=1, source_target_pairs={{0,1},{1,0},{2,3},{3,2},{4,5},{5,4},{6,7},{7,6},{8,9},{9,8},{10,11... | collective-permute-start | bytes 786440 | tf_op jit(solution)/shard_map/ppermute | solution.py:451
  35.7 0.7 copy-done.4
  36.9 0.7 copy-done.2
  38.7 0.8 collective-permute-done.6.m3
  39.5 5.1 %collective-permute-done.1.g3 = bf16[17,128,128]{2,1,0:T(8,128)(2,1)} collective-permute-done((bf16[17,128,128]{2,1,0:T(8,128)(2,1)}, bf16[17,128,128]{2,1,0:T(8,128)(2,1)}, u32[]{:S(2)}, u32[]{:S(2)}) %collective-permute-start.1) | collective-permute-done | bytes 557088 | tf_op jit(solution)/shard_map/ppermute | solution.py:444
  44.6 3.3 %shard_map.107 = (bf16[2,512,512]{2,1,0:T(8,128)(2,1)S(1)}, bf16[2,512,512]{2,1,0:T(8,128)(2,1)S(1)}, f32[2,1,512]{2,1,0:T(1,128)S(1)}, f32[2,512]{1,0:T(2,128)S...) custom-call(s32[4]{0:T(128)S(1)} %pad_add_fusion.ids, f32[20,128,128]{2,1,0:T(8,128)S(1)} %get-tuple-element.39.own, ...), custom_call_target="tpu_custom_call" | custom-call | bytes 6490128 | tf_op jit(solution)/shard_map/pallas_call | solution.py:22
  47.9 0.7 collective-permute-start.7
  48.6 1.4 %shard_map.108 = (f32[1,512]{1,0:T(1,128)S(1)}, f32[1,512]{1,0:T(1,128)S(1)}) custom-call(f32[1,512]{1,0:T(1,128)S(1)} %get-tuple-element.48.acc, f32[1,512]{1,0:T(1,128)S(1)} %collective-permute-done.7.got, f32[2,512]{1,0:T(2,128)S(1)} %get-tuple-element.50.mine.damping, bf16[512,512]{1,0:T(8,128)(2,1)S(1)} %get-tuple-element.43.pthi, ...), custom_call_target="tpu_custom_call" | custom-call | bytes 4206592 | tf_op jit(solution)/shard_map/pallas_call | solution.py:22
  50.7 4.8 %shard_map.109 = (bf16[512,512]{1,0:T(8,128)(2,1)S(1)}, bf16[512,512]{1,0:T(8,128)(2,1)S(1)}, bf16[512,512]{1,0:T(8,128)(2,1)S(1)}, bf16[512,512]{1,0:T(8,128)(2...) custom-call(f32[1,512]{1,0:T(1,128)S(1)} %get-tuple-element.54.after, ...), custom_call_target="tpu_custom_call" | custom-call | flops 4026531840 | bytes 4204544 | tf_op jit(solution)/shard_map/pallas_call | solution.py:22
  55.7 0.7 collective-permute-start.9
  56.6 0.7 collective-permute-start.10
  57.3 1.4 %shard_map.112 = (bf16[512,512]{1,0:T(8,128)(2,1)S(1)}, bf16[512,512]{1,0:T(8,128)(2,1)S(1)}) custom-call(f32[1,512]{1,0:T(1,128)S(1)} %get-tuple-element.62.after, s32[4]{0:T(128)S(1)} %pad_add_fusion.ids, f32[128,512]{1,0:T(8,128)S(1)} %copy-done.5, f32[128,512]{1,0:T(8,128)S(1)} %copy-done.3, f32[128,512]{1,0:T(8,128)} %collective-permute-done.5.m2, ...), custom_call_target="tpu_custom_call" | custom-call | bytes 1050640 | tf_op jit(solution)/shard_map/pallas_call | solution.py:22
  58.9 0.7 collective-permute-start.11
  59.9 0.7 collective-permute-start.12
  60.8 0.7 collective-permute-start.13
  62.0 24.9 %all_to_all.11.states = f32[32,4,512]{2,1,0:T(4,128)S(1)} all-to-all(f32[32,4,512]{2,1,0:T(4,128)S(1)} %shard_map.116), channel_id=1, replica_groups=mesh['z'=4,'y'=2,'obs'=4] {'z','y','obs'}, dimensions={0} | all-to-all | bytes 524288 | tf_op jit(solution)/shard_map/all_to_all | solution.py:488
  86.9 5.2 %shard_map.117 = (f32[2,128]{1,0:T(2,128)}, f32[2,128]{1,0:T(2,128)}) custom-call(s32[4]{0:T(128)S(1)} %pad_add_fusion.ids, f32[32,4,512]{2,1,0:T(4,128)S(1)} %all_to_all.11.states, bf16[512,512]{1,0:T(8,128)(2,1)S(1)} %get-tuple-element.43.pthi, bf16[512,512]{1,0:T(8,128)(2,1)S(1)} %get-tuple-element.44.ptlo, ...), custom_call_target="tpu_custom_call" | custom-call | bytes 2359312 | tf_op jit(solution)/shard_map/pallas_call | solution.py:22
  (35 shorter events, 4.3 us)
Async XLA Ops:
  2.8 21.4 %copy-start.6 = (f32[128,512]{1,0:T(8,128)S(1)}, f32[128,512]{1,0:T(8,128)}, u32[]{:S(2)}) copy-start(f32[128,512]{1,0:T(8,128)} %gain.1) | copy-start | bytes 786436
  24.2 13.7 %copy-start = (f32[512,512]{1,0:T(8,128)S(1)}, f32[512,512]{1,0:T(8,128)}, u32[]{:S(2)}) copy-start(f32[512,512]{1,0:T(8,128)} %trans.1) | copy-start | bytes 3145732
  24.2 13.7 %copy-start.1 = (f32[512,512]{1,0:T(8,128)S(1)}, f32[512,512]{1,0:T(8,128)}, u32[]{:S(2)}) copy-start(f32[512,512]{1,0:T(8,128)} %cov.1) | copy-start | bytes 3145732
  26.3 8.2 %collective-permute-start.5 = (f32[128,512]{1,0:T(8,128)S(1)}, f32[128,512]{1,0:T(8,128)}, u32[]{:S(2)}, u32[]{:S(2)}) collective-permute-start(f32[128,512]{1,0:T(8,128)S(1)} %get-tuple-element.47.m0), channel_id=1, source_target_pairs={{0,2},{1,3},{2,0},{3,1},{4,6},{5,7},{6,4},{7,5},{8,10},{9,11},{10,... | collective-permute-start | bytes 786440 | tf_op jit(solution)/shard_map/ppermute | solution.py:451
  26.8 12.7 %collective-permute-start.3 = (bf16[17,128,128]{2,1,0:T(8,128)(2,1)}, bf16[17,128,128]{2,1,0:T(8,128)(2,1)}, u32[]{:S(2)}, u32[]{:S(2)}) collective-permute-start(bf16[17,128,128]{2,1,0:T(8,128)(2,1)} %get-tuple-element.41), channel_id=1, source_target_pairs={{16,9},{25,17},{27,19},{18,11},{22,15},{31,23},{29,21},{20,13}} | collective-permute-start | bytes 1671176 | tf_op jit(solution)/shard_map/ppermute | solution.py:444
  28.3 11.2 %collective-permute-start.2 = (bf16[17,128,128]{2,1,0:T(8,128)(2,1)}, bf16[17,128,128]{2,1,0:T(8,128)(2,1)}, u32[]{:S(2)}, u32[]{:S(2)}) collective-permute-start(bf16[17,128,128]{2,1,0:T(8,128)(2,1)} %get-tuple-element.41), channel_id=1, source_target_pairs={{24,9},{1,17},{3,19},{26,11},{30,15},{7,23},{5,21},{28,13}} | collective-permute-start | bytes 1671176 | tf_op jit(solution)/shard_map/ppermute | solution.py:444
  29.7 14.9 %collective-permute-start.1 = (bf16[17,128,128]{2,1,0:T(8,128)(2,1)}, bf16[17,128,128]{2,1,0:T(8,128)(2,1)}, u32[]{:S(2)}, u32[]{:S(2)}) collective-permute-start(bf16[17,128,128]{2,1,0:T(8,128)(2,1)} %get-tuple-element.41), channel_id=1, source_target_pairs={{0,9},{9,17},{11,19},{2,11},{6,15},{15,23},{13,21},{4,13}} | collective-permute-start | bytes 1671176 | tf_op jit(solution)/shard_map/ppermute | solution.py:444
  33.0 11.7 %collective-permute-start = (bf16[17,128,128]{2,1,0:T(8,128)(2,1)}, bf16[17,128,128]{2,1,0:T(8,128)(2,1)}, u32[]{:S(2)}, u32[]{:S(2)}) collective-permute-start(bf16[17,128,128]{2,1,0:T(8,128)(2,1)} %get-tuple-element.41), channel_id=1, source_target_pairs={{8,9},{10,11},{14,15},{12,13}} | collective-permute-start | bytes 1671176 | tf_op jit(solution)/shard_map/ppermute | solution.py:440
  34.4 2.5 %collective-permute-start.4 = (f32[128,512]{1,0:T(8,128)S(1)}, f32[128,512]{1,0:T(8,128)S(1)}, u32[]{:S(2)}, u32[]{:S(2)}) collective-permute-start(f32[128,512]{1,0:T(8,128)S(1)} %get-tuple-element.47.m0), channel_id=1, source_target_pairs={{0,1},{1,0},{2,3},{3,2},{4,5},{5,4},{6,7},{7,6},{8,9},{9,8},{10,11... | collective-permute-start | bytes 786440 | tf_op jit(solution)/shard_map/ppermute | solution.py:451
  35.7 0.7 copy-start.4
  36.9 0.7 copy-start.2
  37.6 1.9 %collective-permute-start.6 = (f32[128,512]{1,0:T(8,128)}, f32[128,512]{1,0:T(8,128)}, u32[]{:S(2)}, u32[]{:S(2)}) collective-permute-start(f32[128,512]{1,0:T(8,128)} %collective-permute-done.5.m2), channel_id=1, source_target_pairs={{0,1},{1,0},{2,3},{3,2},{4,5},{5,4},{6,7},{7,6},{8,9},{9,8},{10,11... | collective-permute-start | bytes 786440 | tf_op jit(solution)/shard_map/ppermute | solution.py:451
  38.0 6.7 %copy-start.3 = (f32[128,512]{1,0:T(8,128)S(1)}, f32[128,512]{1,0:T(8,128)}, u32[]{:S(2)}) copy-start(f32[128,512]{1,0:T(8,128)} %copy-done.2) | copy-start | bytes 786436
  47.9 0.7 collective-permute-start.7
  50.0 5.4 %collective-permute-start.8 = (f32[1,512]{1,0:T(1,128)S(1)}, f32[1,512]{1,0:T(1,128)S(1)}, u32[]{:S(2)}, u32[]{:S(2)}) collective-permute-start(f32[1,512]{1,0:T(1,128)S(1)} %get-tuple-element.54.after), channel_id=1, source_target_pairs={{17,19}} | collective-permute-start | bytes 6152 | tf_op jit(solution)/shard_map/ppermute | solution.py:466
  55.4 1.9 %copy-start.5 = (f32[128,512]{1,0:T(8,128)S(1)}, f32[128,512]{1,0:T(8,128)}, u32[]{:S(2)}) copy-start(f32[128,512]{1,0:T(8,128)} %copy-done.4) | copy-start | bytes 786436
  55.7 0.7 collective-permute-start.9
  56.6 2.1 %collective-permute-start.10 = (f32[1,512]{1,0:T(1,128)S(1)}, f32[1,512]{1,0:T(1,128)S(1)}, u32[]{:S(2)}, u32[]{:S(2)}) collective-permute-start(f32[1,512]{1,0:T(1,128)S(1)} %get-tuple-element.62.after), channel_id=1, source_target_pairs={{11,15}} | collective-permute-start | bytes 6152 | tf_op jit(solution)/shard_map/ppermute | solution.py:466
  58.9 0.7 collective-permute-start.11
  59.9 0.7 collective-permute-start.12
  60.8 0.7 collective-permute-start.13

commit v7 on v6

--- a/solution.py
+++ b/solution.py
@@ -221,17 +221,23 @@
         mtlo[:, at] = lo
 
 
-def two_days(state, damping, pthi, ptlo, omhi, omlo, info, chi, clo):
-    for day in range(2):
-        moved = mv(state, pthi[...], ptlo[...]) * damping[day : day + 1, :]
-        gap = mv(moved, omhi[day], omlo[day]) - info[day]
-        state = moved - mv(gap, chi[...], clo[...])
-    return state
+def few(x, hi, lo):
+    top = x.astype(BF16).astype(F32)
+    both = jnp.concatenate([top, x - top, jnp.zeros((4, x.shape[1]), F32)], 0).astype(BF16)
+    first = jnp.dot(both, hi, preferred_element_type=F32)
+    second = jnp.dot(both, lo, preferred_element_type=F32)
+    return first[0:2] + (first[2:4] + second[0:2])
+
+
+def one_day(day, state, damping, pthi, ptlo, omhi, omlo, info, chi, clo):
+    moved = mv(state, pthi[...], ptlo[...]) * damping[day : day + 1, :]
+    gap = mv(moved, omhi[day], omlo[day]) - info[day]
+    return moved - mv(gap, chi[...], clo[...])
 
 
 def owner_kernel(
     ids, own, extra, g4, g3, g2, g1, prior, pthi, ptlo, chi, clo, m1, m2, m3,
-    omhi, omlo, info, mine, start, y, table, small,
+    omhi, omlo, info, mine, table, start, y, small,
 ):
     planes = 4
     width = pthi.shape[0]
@@ -266,18 +272,21 @@
 
     sides = [n for n, (i, j) in enumerate(tiles) if i != j]
     middles = [n for n, (i, j) in enumerate(tiles) if i == j]
-    for i, n in enumerate(middles):
-        both = added(2 * len(sides) + i)
-        for day, part in enumerate((jnp.where(row > column, both, 0.0), jnp.where(row < column, both, 0.0))):
+
+    def unpack(day):
+        for i, n in enumerate(middles):
+            both = added(2 * len(sides) + i)
+            part = jnp.where(row < column if day else row > column, both, 0.0)
             others = sum(line(s, DIAG + 12 * day + i, 4) for s in range(1, 5))
             piece = own[day * len(tiles) + n] * share + (part + part.T)
             put(day, i, i, piece + jnp.where(row == column, others, 0.0))
-    for day in range(2):
         for m, n in enumerate(sides):
             i, j = tiles[n]
             piece = own[day * len(tiles) + n] * share + added(day * len(sides) + m)
             put(day, i, j, piece)
             put(day, j, i, piece.T)
+
+    for day in range(2):
         info[day] = jnp.concatenate([summed(12 * day + j, 4) for j in range(chunks)], 1)
     held = table.shape[0] // 2 // planes
     for s in range(planes):
@@ -289,15 +298,34 @@
                 )
     for day in range(2):
         mine[day : day + 1, :] = table[pl.ds(2 * ids[1] + day, 1), :]
-    state = prior[...]
-    start[...] = jnp.where((ids[1] == 0) & (ids[0] == owner_plane(0)), state, 0.0)
-    y[...] = two_days(state, mine, pthi, ptlo, omhi, omlo, info, chi, clo)
-
-
-def direct_kernel(acc, got, mine, pthi, ptlo, omhi, omlo, info, chi, clo, total, y):
-    state = acc[...] + got[...]
-    total[...] = state
-    y[...] = two_days(state, mine, pthi, ptlo, omhi, omlo, info, chi, clo)
+    first = (ids[1] == 0) & (ids[0] == owner_plane(0))
+    start[...] = jnp.where(first, prior[...], 0.0)
+
+    @pl.when(first)
+    def _():
+        state = prior[...]
+        for day in range(2):
+            unpack(day)
+            state = one_day(day, state, mine, pthi, ptlo, omhi, omlo, info, chi, clo)
+        y[...] = state
+
+    @pl.when(jnp.logical_not(first))
+    def _():
+        for day in range(2):
+            unpack(day)
+        y[...] = jnp.zeros(y.shape, F32)
+
+
+def direct_kernel(ids, acc, got, mine, pthi, ptlo, omhi, omlo, info, chi, clo, total, y):
+    total[...] = acc[...] + got[...]
+    y[...] = jnp.zeros(y.shape, F32)
+
+    @pl.when(ids[1] == 1)
+    def _():
+        state = total[...]
+        for day in range(2):
+            state = one_day(day, state, mine, pthi, ptlo, omhi, omlo, info, chi, clo)
+        y[...] = state
 
 
 def maps_kernel(after, omhi, omlo, info, chi, clo, pt, damping, b1hi, b1lo, b2hi, b2lo, bchi, bclo, off):
@@ -322,45 +350,76 @@
     y[...] = mv(state, bchi[...], bclo[...]) + off[2:3, :]
 
 
-def last_kernel(acc, got, b1hi, b1lo, b2hi, b2lo, off, damping, out):
+def pairs_kernel(ids, table, mthi, mtlo, khi, klo):
+    spans = table.shape[0] // 2
+
+    @pl.when(ids[1] == spans - 1)
+    def _():
+        whole = mthi[...].astype(F32) + mtlo[...].astype(F32)
+
+        @pl.loop(0, khi.shape[0])
+        def _(k):
+            scaled = whole * table[pl.ds(2 * (spans - 2 - k) + 1, 1), :]
+            khi[k], klo[k] = split(mm(scaled, mthi[...], mtlo[...]))
+
+
+def last_kernel(
+    ids, acc, got, b1hi, b1lo, b2hi, b2lo, off, table, pthi, ptlo, mthi, mtlo, khi, klo, out, shares
+):
+    total, width = shares.shape
+    spans = total // 2
+    chunks = width // LANES
+    span = ids[1]
     state = acc[...] + got[...]
     one = mv(state, b1hi[...], b1lo[...]) + off[0:1, :]
     two = mv(one, b2hi[...], b2lo[...]) + off[1:2, :]
-    both = jnp.concatenate([one, two, damping[...]], 0)
-    for c in range(out.shape[0]):
-        out[c] = both
-
-
-def back_kernel(ids, states, pthi, ptlo, mthi, mtlo, filt, smooth, f, d, const):
-    total, width = f.shape
-    spans = total // 2
-    chunks = width // LANES
+    within = table[pl.ds(2 * span + 1, 1), :]
+    after = table[pl.ds(jnp.minimum(2 * span + 2, total - 1), 1), :] * jnp.where(span == spans - 1, 0.0, 1.0)
+    damped = jnp.concatenate([within, after], 0)
+    both = jnp.concatenate([one, two], 0)
+    const = both - few(few(both, pthi[...], ptlo[...]) * damped * damped, mthi[...], mtlo[...])
+    even = const[0:1] + mv(const[1:2] * within, mthi[...], mtlo[...])
+    shares[...] = jnp.zeros(shares.shape, F32)
+    shares[pl.ds(2 * span + 1, 1), :] = const[1:2]
+    shares[pl.ds(2 * span, 1), :] = even
+
+    def step(k, v):
+        t = 2 * span - 1 - k
+        v = mv(v * table[pl.ds(t + 1, 1), :], mthi[...], mtlo[...])
+        shares[pl.ds(t, 1), :] = v
+        return v
+
+    @pl.when(span < spans - 1)
+    def _():
+        lax.fori_loop(0, 2 * span, step, even)
+
+    @pl.when(span == spans - 1)
+    def _():
+        v, damped_rows = even, []
+        for k in range(khi.shape[0]):
+            t = 2 * (spans - 1 - k)
+            v = v * table[t : t + 1, :]
+            damped_rows.append(v)
+            v = mv(v, khi[k], klo[k])
+            shares[t - 2 : t - 1, :] = v
+        batch = jnp.concatenate(damped_rows + [jnp.zeros((1, width), F32)] * (-len(damped_rows) % 8), 0)
+        odd = mm(batch, mthi[...], mtlo[...])
+        for k in range(khi.shape[0]):
+            t = 2 * (spans - 1 - k)
+            shares[t - 1 : t, :] = odd[k : k + 1]
+        lax.fori_loop(2 * khi.shape[0], 2 * span, step, v)
+
     for c in range(spans):
-        one = states[owner_plane(c) * spans + (place(c) | 1)]
-        f[2 * c : 2 * c + 2, :] = one[0:2]
-        if c:
-            d[2 * c - 1 : 2 * c + 1, :] = one[2:4]
-        else:
-            d[0:1, :] = one[3:4]
-    d[total - 1 : total, :] = jnp.zeros((1, width), F32)
-    ahead = d[...] * mm(f[...], pthi[...], ptlo[...])
-    const[...] = f[...] - mm(d[...] * ahead, mthi[...], mtlo[...])
-
-    def step(k, state):
-        t = total - 2 - k
-        new = const[pl.ds(t, 1), :] + mv(d[pl.ds(t, 1), :] * state, mthi[...], mtlo[...])
-        const[pl.ds(t, 1), :] = new
-        return new
-
-    lax.fori_loop(0, total - 1, step, const[total - 1 : total, :], unroll=total <= 16)
-    for k in range(2):
-        row = pl.ds(ids[3] * 2 + k, 1)
-        for whole, out in ((f, filt), (const, smooth)):
-            line = whole[row, :]
-            mine = line[:, 0:LANES]
-            for q in range(1, chunks):
-                mine = jnp.where(ids[2] == q, line[:, q * LANES : (q + 1) * LANES], mine)
-            out[k : k + 1, :] = mine
+        for q in range(chunks):
+            out[c * chunks + q, 0:2, :] = shares[2 * c : 2 * c + 2, q * LANES : (q + 1) * LANES]
+    for q in range(chunks):
+        out[span * chunks + q, 2:4, :] = both[:, q * LANES : (q + 1) * LANES]
+
+
+def add_kernel(ids, parts, filt, smooth):
+    spans = parts.shape[0] // 4
+    filt[...] = parts[ids[4], 2:4, :]
+    smooth[...] = sum(parts[owner_plane(c) * spans + (place(c) | 1), 0:2, :] for c in range(spans))
 
 
 def local(
@@ -386,7 +445,9 @@
     span = seat = jnp.where(z == 1, at - at % 2, at)
     for bit in range(1, spans.bit_length()):
         span = span ^ (seat >> bit)
-    ids = jnp.stack([z, span, o, z * held + y]).astype(jnp.int32)
+    c = z * held + y
+    seat = c ^ (c >> 1)
+    ids = jnp.stack([z, span, o, c, (1 + seat % 2) * spans + (seat | 1)]).astype(jnp.int32)
     everyone = ("z", "y", "obs")
 
     def owner(span):
@@ -455,18 +516,20 @@
     pt, pthi, ptlo, chi, clo = run(
         prep_kernel, [(full, F32)] + [(full, BF16)] * 4, [propagator_matrix, analysis_cov]
     )
-    omhi, omlo, info, mine, acc, y = run(
+    omhi, omlo, info, mine, table, acc, y = run(
         owner_kernel,
         [((days,) + full, BF16)] * 2
-        + [((days, 1, width), F32), ((days, width), F32), row, row],
+        + [((days, 1, width), F32), ((days, width), F32), ((spans * days, width), F32), row, row],
         [(ids, SMEM), own, extra, *plane_sums, prior, pthi, ptlo, chi, clo, *[(g, ANY) for g in gains[1:]]],
-        [pltpu.VMEM((spans * days, width), F32), pltpu.VMEM((planes + 1, extra_tiles * LANES, LANES), F32)],
+        [pltpu.VMEM((planes + 1, extra_tiles * LANES, LANES), F32)],
     )
     for k in range(spans - 1):
         received = lax.ppermute(y, everyone, [(owner(k), owner(k + 1))])
         if k == 0:
             acc, y = run(
-                direct_kernel, [row, row], [acc, received, mine, pthi, ptlo, omhi, omlo, info, chi, clo]
+                direct_kernel,
+                [row, row],
+                [(ids, SMEM), acc, received, mine, pthi, ptlo, omhi, omlo, info, chi, clo],
             )
             b1hi, b1lo, b2hi, b2lo, bchi, bclo, off = run(
                 maps_kernel,
@@ -479,20 +542,23 @@
             acc, y = run(hop_kernel, [row, row], [(side, ANY), acc, received, bchi, bclo, off])
             if k == 2:
                 mthi, mtlo = run(gain_kernel, [(full, BF16)] * 2, [(y, ANY), (ids, SMEM), *gains])
-                side = mthi
+                khi, klo = run(
+                    pairs_kernel,
+                    [((min(spans - 1, 7),) + full, BF16)] * 2,
+                    [(ids, SMEM), table, mthi, mtlo],
+                )
+                side = khi
     (answer,) = run(
         last_kernel,
-        [((spans * peers, 2 * days, width), F32)],
-        [acc, received, b1hi, b1lo, b2hi, b2lo, off, mine],
-    )
-    states = lax.all_to_all(answer, everyone, split_axis=0, concat_axis=0, tiled=True)
+        [((spans * peers, 8, LANES), F32)],
+        [
+            (ids, SMEM), acc, received, b1hi, b1lo, b2hi, b2lo, off, table, pthi, ptlo, mthi, mtlo, khi, klo
+        ],
+        [pltpu.VMEM((spans * days, width), F32)],
+    )
+    parts = lax.all_to_all(answer, everyone, split_axis=0, concat_axis=0, tiled=True)
     out = ((days, LANES), F32)
-    return run(
-        back_kernel,
-        [out, out],
-        [(ids, SMEM), states, pthi, ptlo, mthi, mtlo],
-        [pltpu.VMEM((spans * days, width), F32)] * 3,
-    )
+    return run(add_kernel, [out, out], [(ids, SMEM), parts])
 
 
 def solution(mesh):

time: 92.5 us -> 90.7 us (0.981)
  local copies, waits for them, and re-layouts: 1.41 us -> 5.89 us
  Pallas kernels: 22.4 us -> 18.4 us
  waiting for transfers between devices: 6.42 us -> 2.93 us
  blocking collectives: 46.2 us -> 47.3 us
    unnamed x14 -> x20, local copies, waits for them, and re-layouts: 1.41 us -> 5.81 us
    pallas_call x14 -> x15, Pallas kernels: 22.4 us -> 18.4 us  [run(): pl.pallas_call(body, out_shape=[jax.ShapeDtypeStruct(s, d) for s, d in ou...]
    ppermute x3, waiting for transfers between devices: 5.15 us -> 2.45 us  [local(): lax.ppermute(pay, everyone, [((owner_plane(p) + s) % planes * spans + pla...]
    all_to_all x1, blocking collectives: 24.9 us -> 25.9 us  [local(): lax.all_to_all(answer, everyone, split_axis=0, concat_axis=0, tiled=True)]
  transfers between devices with their start and end apart: 14 -> 14, of which waited for: 3 -> 2; matrix products, arithmetic and copies ran while one was open for 0% -> 0% of each run, Pallas kernels for 7% -> 8%
where the time goes in v7:
time: 90.7 us; the launch traced here: 90.1 us
  blocking collectives  47.3 us (52%)
  Pallas kernels  18.4 us (20%)
  starting transfers between devices  14.7 us (16%)
  local copies, waits for them, and re-layouts  5.89 us (6%)
  waiting for transfers between devices  2.93 us (3%)
    all_to_all x1, blocking collectives, local(): lax.all_to_all(answer, everyone, split_axis=0, concat_axis=0, tiled=True)  25.9 us
    all_to_all x1, blocking collectives, local(): lax.all_to_all(sent, ('y', 'obs'), split_axis=0, concat_axis=0, tiled=True)  21.4 us
    pallas_call x15, Pallas kernels, run(): pl.pallas_call(body, out_shape=[jax.ShapeDtypeStruct(s, d) for s, d in ou...  18.4 us
    ppermute x3, starting transfers between devices, local(): lax.ppermute(pay, everyone, [((owner_plane(p) + s) % planes * spans + pla...  6.15 us
    unnamed x20, local copies, waits for them, and re-layouts  5.81 us
    ppermute x7, starting transfers between devices, local(): received = lax.ppermute(y, everyone, [(owner(k), owner(k + 1))])  4.86 us
    ppermute x3, waiting for transfers between devices, local(): lax.ppermute(pay, everyone, [((owner_plane(p) + s) % planes * spans + pla...  2.45 us
    ppermute x3, starting transfers between devices, swap(): return lax.ppermute(x, 'obs', [(i, i ^ bit) for i in range(peers)])  2.25 us
  transfers between devices with their start and end apart: 14, of which 2 were waited for; matrix products, arithmetic and copies ran while one was open for 0% of the time, Pallas kernels for 8%

profile of v7, /device:TPU:0, one launch (start us, length us, event | category | flops | bytes accessed | tf_op | source)
XLA Modules:
  0.0 90.1 jit_solution(16937984530906874066)
XLA Ops:
  0.6 2.2 %shard_map.104 = bf16[8,136,512]{2,1,0:T(8,128)(2,1)} custom-call(s32[8]{0:T(128)} %day.1, s32[8]{0:T(128)} %count.1, bf16[1024,512]{1,0:T(8,128)(2,1)} %rows.1, bf16[8,128]{1,0:T(8,128)(2,1)} %bitcast.7, f32[1,128]{1,0:T(1,128)} %bitcast.8, f32[2,512]{1,0:T(2,128)} %damping.1), custom_call_target="tpu_custom_call" | custom-call | bytes 1055296 | tf_op jit(solution)/shard_map/pallas_call | solution.py:22
  2.9 21.4 %all_to_all.10.got = bf16[8,136,512]{2,1,0:T(8,128)(2,1)S(1)} all-to-all(bf16[8,136,512]{2,1,0:T(8,128)(2,1)} %shard_map.104), channel_id=1, replica_groups=mesh['z'=4,'y'=2,'obs'=4] {'y','obs'}, dimensions={0} | all-to-all | bytes 2228224 | tf_op jit(solution)/shard_map/all_to_all | solution.py:485
  24.2 2.1 %shard_map.105 = (f32[20,128,128]{2,1,0:T(8,128)S(1)}, f32[128,128]{1,0:T(8,128)S(1)}, bf16[17,128,128]{2,1,0:T(8,128)(2,1)}, f32[1,512]{1,0:T(1,128)S(1)}, f32[128,512]{1,0:T(8,128)S(1)}) custom-call(bf16[8,136,512]{2,1,0:T(8,128)(2,1)S(1)} %all_to_all.10.got, f32[128,512]{1,0:T(8,128)S(1)} %copy-done.9), custom_call_target="tpu_custom_call" | custom-call | flops 1073741824 | bytes 1376256 | tf_op jit(solution)/shard_map/pallas_call | solution.py:22
  26.9 1.5 %collective-permute-start.3 = (bf16[17,128,128]{2,1,0:T(8,128)(2,1)}, bf16[17,128,128]{2,1,0:T(8,128)(2,1)}, u32[]{:S(2)}, u32[]{:S(2)}) collective-permute-start(bf16[17,128,128]{2,1,0:T(8,128)(2,1)} %get-tuple-element.44), channel_id=1, source_target_pairs={{16,9},{25,17},{27,19},{18,11},{22,15},{31,23},{29,21},{20,13}} | collective-permute-start | bytes 1671176 | tf_op jit(solution)/shard_map/ppermute | solution.py:505
  28.3 1.5 %collective-permute-start.2 = (bf16[17,128,128]{2,1,0:T(8,128)(2,1)}, bf16[17,128,128]{2,1,0:T(8,128)(2,1)}, u32[]{:S(2)}, u32[]{:S(2)}) collective-permute-start(bf16[17,128,128]{2,1,0:T(8,128)(2,1)} %get-tuple-element.44), channel_id=1, source_target_pairs={{24,9},{1,17},{3,19},{26,11},{30,15},{7,23},{5,21},{28,13}} | collective-permute-start | bytes 1671176 | tf_op jit(solution)/shard_map/ppermute | solution.py:505
  29.8 3.2 %collective-permute-start.1 = (bf16[17,128,128]{2,1,0:T(8,128)(2,1)}, bf16[17,128,128]{2,1,0:T(8,128)(2,1)}, u32[]{:S(2)}, u32[]{:S(2)}) collective-permute-start(bf16[17,128,128]{2,1,0:T(8,128)(2,1)} %get-tuple-element.44), channel_id=1, source_target_pairs={{0,9},{9,17},{11,19},{2,11},{6,15},{15,23},{13,21},{4,13}} | collective-permute-start | bytes 1671176 | tf_op jit(solution)/shard_map/ppermute | solution.py:505
  33.0 1.5 %collective-permute-start = (bf16[17,128,128]{2,1,0:T(8,128)(2,1)}, bf16[17,128,128]{2,1,0:T(8,128)(2,1)}, u32[]{:S(2)}, u32[]{:S(2)}) collective-permute-start(bf16[17,128,128]{2,1,0:T(8,128)(2,1)} %get-tuple-element.44), channel_id=1, source_target_pairs={{8,9},{10,11},{14,15},{12,13}} | collective-permute-start | bytes 1671176 | tf_op jit(solution)/shard_map/ppermute | solution.py:501
  34.5 1.3 %collective-permute-start.4 = (f32[128,512]{1,0:T(8,128)S(1)}, f32[128,512]{1,0:T(8,128)S(1)}, u32[]{:S(2)}, u32[]{:S(2)}) collective-permute-start(f32[128,512]{1,0:T(8,128)S(1)} %get-tuple-element.50.m0), channel_id=1, source_target_pairs={{0,1},{1,0},{2,3},{3,2},{4,5},{5,4},{6,7},{7,6},{8,9},{9,8},{10,11... | collective-permute-start | bytes 786440 | tf_op jit(solution)/shard_map/ppermute | solution.py:512
  35.8 0.7 copy-done.5
  38.0 1.2 %copy-done = f32[512,512]{1,0:T(8,128)S(1)} copy-done((f32[512,512]{1,0:T(8,128)S(1)}, f32[512,512]{1,0:T(8,128)}, u32[]{:S(2)}) %copy-start) | copy-done | bytes 1048600
  39.3 1.2 %copy-done.1 = f32[512,512]{1,0:T(8,128)S(1)} copy-done((f32[512,512]{1,0:T(8,128)S(1)}, f32[512,512]{1,0:T(8,128)}, u32[]{:S(2)}) %copy-start.1) | copy-done | bytes 1048600
  41.1 1.0 %copy-done.7 = f32[512,512]{1,0:T(8,128)} copy-done((f32[512,512]{1,0:T(8,128)}, f32[512,512]{1,0:T(8,128)S(1)}, u32[]{:S(2)}) %copy-start.7) | copy-done | bytes 1048600
  42.2 2.4 %collective-permute-done.1.g3 = bf16[17,128,128]{2,1,0:T(8,128)(2,1)} collective-permute-done((bf16[17,128,128]{2,1,0:T(8,128)(2,1)}, bf16[17,128,128]{2,1,0:T(8,128)(2,1)}, u32[]{:S(2)}, u32[]{:S(2)}) %collective-permute-start.1) | collective-permute-done | bytes 557088 | tf_op jit(solution)/shard_map/ppermute | solution.py:505
  44.7 0.9 %copy-done.3 = f32[128,512]{1,0:T(8,128)S(1)} copy-done((f32[128,512]{1,0:T(8,128)S(1)}, f32[128,512]{1,0:T(8,128)}, u32[]{:S(2)}) %copy-start.3) | copy-done | bytes 262168
  45.6 2.5 %shard_map.107 = (bf16[2,512,512]{2,1,0:T(8,128)(2,1)S(1)}, bf16[2,512,512]{2,1,0:T(8,128)(2,1)S(1)}, f32[2,1,512]{2,1,0:T(1,128)S(1)}, f32[2,512]{1,0:T(2,128)S...) custom-call(s32[5]{0:T(128)S(1)} %stack.23.ids, ...), custom_call_target="tpu_custom_call" | custom-call | bytes 6490132 | tf_op jit(solution)/shard_map/pallas_call | solution.py:22
  50.0 4.7 %shard_map.109 = (bf16[512,512]{1,0:T(8,128)(2,1)S(1)}, bf16[512,512]{1,0:T(8,128)(2,1)S(1)}, bf16[512,512]{1,0:T(8,128)(2,1)S(1)}, bf16[512,512]{1,0:T(8,128)(2...) custom-call(f32[1,512]{1,0:T(1,128)S(1)} %get-tuple-element.58.after, ...), custom_call_target="tpu_custom_call" | custom-call | flops 4026531840 | bytes 4204544 | tf_op jit(solution)/shard_map/pallas_call | solution.py:22
  55.0 0.7 collective-permute-start.9
  56.7 1.4 %shard_map.112 = (bf16[512,512]{1,0:T(8,128)(2,1)S(1)}, bf16[512,512]{1,0:T(8,128)(2,1)S(1)}) custom-call(f32[1,512]{1,0:T(1,128)S(1)} %get-tuple-element.66.after, s32[5]{0:T(128)S(1)} %stack.23.ids, f32[128,512]{1,0:T(8,128)S(1)} %copy-done.6, f32[128,512]{1,0:T(8,128)S(1)} %copy-done.4, f32[128,512]{1,0:T(8,128)} %collective-permute-done.5.m2, ...), custom_call_target="tpu_custom_call" | custom-call | bytes 1050644 | tf_op jit(solution)/shard_map/pallas_call | solution.py:22
  58.8 0.7 collective-permute-start.11
  59.8 0.7 collective-permute-start.12
  60.7 0.7 collective-permute-start.13
  61.4 1.7 %shard_map.117 = f32[32,8,128]{2,1,0:T(8,128)S(1)} custom-call(s32[5]{0:T(128)S(1)} %stack.23.ids, f32[1,512]{1,0:T(1,128)S(1)} %get-tuple-element.75.acc, f32[1,512]{1,0:T(1,128)S(1)} %collective-permute-done.13.got, bf16[512,512]{1,0:T(8,128)(2,1)S(1)} %get-tuple-element.77.b1hi, bf16[512,512]{1,0:T(8,128)(2,1)S(1)} %get-tuple-element.78.b1lo, ...), custom_call_target="tpu_custom_call" | custom-call | bytes 11587604 | tf_op jit(solution)/shard_map/pallas_call | solution.py:22
  63.1 25.9 %all_to_all.11.parts = f32[32,8,128]{2,1,0:T(8,128)S(1)} all-to-all(f32[32,8,128]{2,1,0:T(8,128)S(1)} %shard_map.117), channel_id=1, replica_groups=mesh['z'=4,'y'=2,'obs'=4] {'z','y','obs'}, dimensions={0} | all-to-all | bytes 262144 | tf_op jit(solution)/shard_map/all_to_all | solution.py:559
  89.0 1.1 %shard_map.118 = (f32[2,128]{1,0:T(2,128)}, f32[2,128]{1,0:T(2,128)}) custom-call(s32[5]{0:T(128)S(1)} %stack.23.ids, f32[32,8,128]{2,1,0:T(8,128)S(1)} %all_to_all.11.parts), custom_call_target="tpu_custom_call" | custom-call | bytes 131092 | tf_op jit(solution)/shard_map/pallas_call | solution.py:22
  (42 shorter events, 7.0 us)
Async XLA Ops:
  2.9 21.4 %copy-start.9 = (f32[128,512]{1,0:T(8,128)S(1)}, f32[128,512]{1,0:T(8,128)}, u32[]{:S(2)}) copy-start(f32[128,512]{1,0:T(8,128)} %gain.1) | copy-start | bytes 786436
  26.3 8.2 %collective-permute-start.5 = (f32[128,512]{1,0:T(8,128)S(1)}, f32[128,512]{1,0:T(8,128)}, u32[]{:S(2)}, u32[]{:S(2)}) collective-permute-start(f32[128,512]{1,0:T(8,128)S(1)} %get-tuple-element.50.m0), channel_id=1, source_target_pairs={{0,2},{1,3},{2,0},{3,1},{4,6},{5,7},{6,4},{7,5},{8,10},{9,11},{10,... | collective-permute-start | bytes 786440 | tf_op jit(solution)/shard_map/ppermute | solution.py:512
  26.9 15.3 %collective-permute-start.3 = (bf16[17,128,128]{2,1,0:T(8,128)(2,1)}, bf16[17,128,128]{2,1,0:T(8,128)(2,1)}, u32[]{:S(2)}, u32[]{:S(2)}) collective-permute-start(bf16[17,128,128]{2,1,0:T(8,128)(2,1)} %get-tuple-element.44), channel_id=1, source_target_pairs={{16,9},{25,17},{27,19},{18,11},{22,15},{31,23},{29,21},{20,13}} | collective-permute-start | bytes 1671176 | tf_op jit(solution)/shard_map/ppermute | solution.py:505
  28.3 13.9 %collective-permute-start.2 = (bf16[17,128,128]{2,1,0:T(8,128)(2,1)}, bf16[17,128,128]{2,1,0:T(8,128)(2,1)}, u32[]{:S(2)}, u32[]{:S(2)}) collective-permute-start(bf16[17,128,128]{2,1,0:T(8,128)(2,1)} %get-tuple-element.44), channel_id=1, source_target_pairs={{24,9},{1,17},{3,19},{26,11},{30,15},{7,23},{5,21},{28,13}} | collective-permute-start | bytes 1671176 | tf_op jit(solution)/shard_map/ppermute | solution.py:505
  29.8 14.9 %collective-permute-start.1 = (bf16[17,128,128]{2,1,0:T(8,128)(2,1)}, bf16[17,128,128]{2,1,0:T(8,128)(2,1)}, u32[]{:S(2)}, u32[]{:S(2)}) collective-permute-start(bf16[17,128,128]{2,1,0:T(8,128)(2,1)} %get-tuple-element.44), channel_id=1, source_target_pairs={{0,9},{9,17},{11,19},{2,11},{6,15},{15,23},{13,21},{4,13}} | collective-permute-start | bytes 1671176 | tf_op jit(solution)/shard_map/ppermute | solution.py:505
  33.0 11.6 %collective-permute-start = (bf16[17,128,128]{2,1,0:T(8,128)(2,1)}, bf16[17,128,128]{2,1,0:T(8,128)(2,1)}, u32[]{:S(2)}, u32[]{:S(2)}) collective-permute-start(bf16[17,128,128]{2,1,0:T(8,128)(2,1)} %get-tuple-element.44), channel_id=1, source_target_pairs={{8,9},{10,11},{14,15},{12,13}} | collective-permute-start | bytes 1671176 | tf_op jit(solution)/shard_map/ppermute | solution.py:501
  34.5 2.5 %collective-permute-start.4 = (f32[128,512]{1,0:T(8,128)S(1)}, f32[128,512]{1,0:T(8,128)S(1)}, u32[]{:S(2)}, u32[]{:S(2)}) collective-permute-start(f32[128,512]{1,0:T(8,128)S(1)} %get-tuple-element.50.m0), channel_id=1, source_target_pairs={{0,1},{1,0},{2,3},{3,2},{4,5},{5,4},{6,7},{7,6},{8,9},{9,8},{10,11... | collective-permute-start | bytes 786440 | tf_op jit(solution)/shard_map/ppermute | solution.py:512
  35.8 0.7 copy-start.5
  37.0 0.7 copy-start.2
  37.7 4.5 %collective-permute-start.6 = (f32[128,512]{1,0:T(8,128)}, f32[128,512]{1,0:T(8,128)}, u32[]{:S(2)}, u32[]{:S(2)}) collective-permute-start(f32[128,512]{1,0:T(8,128)} %collective-permute-done.5.m2), channel_id=1, source_target_pairs={{0,1},{1,0},{2,3},{3,2},{4,5},{5,4},{6,7},{7,6},{8,9},{9,8},{10,11... | collective-permute-start | bytes 786440 | tf_op jit(solution)/shard_map/ppermute | solution.py:512
  38.0 1.2 %copy-start = (f32[512,512]{1,0:T(8,128)S(1)}, f32[512,512]{1,0:T(8,128)}, u32[]{:S(2)}) copy-start(f32[512,512]{1,0:T(8,128)} %trans.1) | copy-start | bytes 3145732
  39.3 1.2 %copy-start.1 = (f32[512,512]{1,0:T(8,128)S(1)}, f32[512,512]{1,0:T(8,128)}, u32[]{:S(2)}) copy-start(f32[512,512]{1,0:T(8,128)} %cov.1) | copy-start | bytes 3145732
  41.1 1.0 %copy-start.7 = (f32[512,512]{1,0:T(8,128)}, f32[512,512]{1,0:T(8,128)S(1)}, u32[]{:S(2)}) copy-start(f32[512,512]{1,0:T(8,128)S(1)} %get-tuple-element.60.pt) | copy-start | bytes 3145732
  44.7 1.0 %copy-start.3 = (f32[128,512]{1,0:T(8,128)S(1)}, f32[128,512]{1,0:T(8,128)}, u32[]{:S(2)}) copy-start(f32[128,512]{1,0:T(8,128)} %copy-done.2) | copy-start | bytes 786436
  48.1 0.7 collective-permute-start.7
  48.8 1.2 %copy-start.8 = (f32[512,512]{1,0:T(8,128)S(1)}, f32[512,512]{1,0:T(8,128)}, u32[]{:S(2)}) copy-start(f32[512,512]{1,0:T(8,128)} %copy-done.7) | copy-start | bytes 3145732
  49.3 5.4 %collective-permute-start.8 = (f32[1,512]{1,0:T(1,128)S(1)}, f32[1,512]{1,0:T(1,128)S(1)}, u32[]{:S(2)}, u32[]{:S(2)}) collective-permute-start(f32[1,512]{1,0:T(1,128)S(1)} %get-tuple-element.58.after), channel_id=1, source_target_pairs={{17,19}} | collective-permute-start | bytes 6152 | tf_op jit(solution)/shard_map/ppermute | solution.py:527
  54.8 1.9 %copy-start.4 = (f32[128,512]{1,0:T(8,128)S(1)}, f32[128,512]{1,0:T(8,128)}, u32[]{:S(2)}) copy-start(f32[128,512]{1,0:T(8,128)} %copy-done.2) | copy-start | bytes 786436
  54.8 1.9 %copy-start.6 = (f32[128,512]{1,0:T(8,128)S(1)}, f32[128,512]{1,0:T(8,128)}, u32[]{:S(2)}) copy-start(f32[128,512]{1,0:T(8,128)} %copy-done.5) | copy-start | bytes 786436
  55.0 0.7 collective-permute-start.9
  55.9 2.7 %collective-permute-start.10 = (f32[1,512]{1,0:T(1,128)S(1)}, f32[1,512]{1,0:T(1,128)S(1)}, u32[]{:S(2)}, u32[]{:S(2)}) collective-permute-start(f32[1,512]{1,0:T(1,128)S(1)} %get-tuple-element.66.after), channel_id=1, source_target_pairs={{11,15}} | collective-permute-start | bytes 6152 | tf_op jit(solution)/shard_map/ppermute | solution.py:527
  58.8 0.7 collective-permute-start.11
  59.8 0.7 collective-permute-start.12
  60.7 0.7 collective-permute-start.13

commit v8 on v7

--- a/solution.py
+++ b/solution.py
@@ -15,7 +15,7 @@
 HBM = pl.BlockSpec(memory_space=pltpu.HBM)
 
 
-def run(body, out, ins, scratch=(), limit=32, flops=0, outs=VMEM):
+def run(body, out, ins, scratch=(), limit=16, flops=0, outs=VMEM):
     specs = [x[1] if isinstance(x, tuple) else VMEM for x in ins]
     arrays = [x[0] if isinstance(x, tuple) else x for x in ins]
     moved = sum(a.size * a.dtype.itemsize for a in arrays)
@@ -211,7 +211,7 @@
     chi[...], clo[...] = split(cov[...])
 
 
-def gain_kernel(after, ids, m0, m1, m2, m3, mthi, mtlo):
+def gain_kernel(ids, m0, m1, m2, m3, mthi, mtlo):
     rows = m0.shape[0]
     for step, part in enumerate((m0, m1, m2, m3)):
         holder = ids[2] ^ step
@@ -235,9 +235,36 @@
     return moved - mv(gap, chi[...], clo[...])
 
 
+def spread(extra, got, small):
+    small_at = got[0].shape[0] - extra.shape[0] // LANES
+    small[0] = extra[...]
+    for s, part in enumerate(got):
+        for n in range(extra.shape[0] // LANES):
+            small[s + 1, n * LANES : (n + 1) * LANES, :] = part[small_at + n].astype(F32)
+
+
+def line_of(small, s, first, gap):
+    return small[s, first : first + 1, :] + (
+        small[s, first + gap : first + gap + 1, :] + small[s, first + 2 * gap : first + 2 * gap + 1, :]
+    )
+
+
+def table_kernel(after, ids, extra, g1, g2, g3, table, small):
+    planes = 4
+    chunks = table.shape[1] // LANES
+    held = table.shape[0] // 2 // planes
+    spread(extra, (g1, g2, g3), small)
+    for s in range(planes):
+        plane = lax.rem(ids[0] + s, planes)
+        for k in range(held):
+            for day in range(2):
+                table[pl.ds(2 * (plane * held + k) + day, 1), :] = jnp.concatenate(
+                    [line_of(small, s, DAMP + 24 * k + 4 * day + j, 8) for j in range(chunks)], 1
+                )
+
+
 def owner_kernel(
-    ids, own, extra, g4, g3, g2, g1, prior, pthi, ptlo, chi, clo, m1, m2, m3,
-    omhi, omlo, info, mine, table, start, y, small,
+    ids, own, extra, g4, g3, g1, g2, prior, pthi, ptlo, chi, clo, after, omhi, omlo, info, mine, start, y, small
 ):
     planes = 4
     width = pthi.shape[0]
@@ -247,16 +274,10 @@
     share = jnp.where(ids[0] == 2, 1.0, 0.0)
     row = lax.broadcasted_iota(jnp.int32, (LANES, LANES), 0)
     column = lax.broadcasted_iota(jnp.int32, (LANES, LANES), 1)
-    small_at = g1.shape[0] - extra.shape[0] // LANES
-    small[0] = extra[...]
-    for s, part in enumerate(got):
-        for n in range(extra.shape[0] // LANES):
-            small[s + 1, n * LANES : (n + 1) * LANES, :] = part[small_at + n].astype(F32)
+    spread(extra, got, small)
 
     def line(s, first, gap):
-        return small[s, first : first + 1, :] + (
-            small[s, first + gap : first + gap + 1, :] + small[s, first + 2 * gap : first + 2 * gap + 1, :]
-        )
+        return line_of(small, s, first, gap)
 
     def summed(first, gap):
         others = line(1, first, gap) + (line(2, first, gap) + (line(3, first, gap) + line(4, first, gap)))
@@ -288,16 +309,14 @@
 
     for day in range(2):
         info[day] = jnp.concatenate([summed(12 * day + j, 4) for j in range(chunks)], 1)
-    held = table.shape[0] // 2 // planes
-    for s in range(planes):
-        plane = lax.rem(ids[0] + s, planes)
-        for k in range(held):
-            for day in range(2):
-                table[pl.ds(2 * (plane * held + k) + day, 1), :] = jnp.concatenate(
-                    [line(s, DAMP + 24 * k + 4 * day + j, 8) for j in range(chunks)], 1
-                )
+    held = ids[5]
+    source = lax.rem(ids[1] // held - ids[0] + planes, planes)
     for day in range(2):
-        mine[day : day + 1, :] = table[pl.ds(2 * ids[1] + day, 1), :]
+        for j in range(chunks):
+            r = DAMP + 24 * lax.rem(ids[1], held) + 4 * day + j
+            mine[day : day + 1, j * LANES : (j + 1) * LANES] = small[source, pl.ds(r, 1), :] + (
+                small[source, pl.ds(r + 8, 1), :] + small[source, pl.ds(r + 16, 1), :]
+            )
     first = (ids[1] == 0) & (ids[0] == owner_plane(0))
     start[...] = jnp.where(first, prior[...], 0.0)
 
@@ -316,19 +335,14 @@
         y[...] = jnp.zeros(y.shape, F32)
 
 
-def direct_kernel(ids, acc, got, mine, pthi, ptlo, omhi, omlo, info, chi, clo, total, y):
-    total[...] = acc[...] + got[...]
-    y[...] = jnp.zeros(y.shape, F32)
-
-    @pl.when(ids[1] == 1)
-    def _():
-        state = total[...]
-        for day in range(2):
-            state = one_day(day, state, mine, pthi, ptlo, omhi, omlo, info, chi, clo)
-        y[...] = state
-
-
-def maps_kernel(after, omhi, omlo, info, chi, clo, pt, damping, b1hi, b1lo, b2hi, b2lo, bchi, bclo, off):
+def second_kernel(acc, got, b1hi, b1lo, b2hi, b2lo, off, total, y):
+    state = acc[...] + got[...]
+    total[...] = state
+    state = mv(state, b1hi[...], b1lo[...]) + off[0:1, :]
+    y[...] = mv(state, b2hi[...], b2lo[...]) + off[1:2, :]
+
+
+def maps_kernel(after, omhi, omlo, info, chi, clo, pt, damping, b1hi, b1lo, b2hi, b2lo, off):
     parts = ((b1hi, b1lo), (b2hi, b2lo))
     for day in range(2):
         moved = pt[...] * damping[day : day + 1, :]
@@ -336,21 +350,24 @@
         step = moved - mm(taken, chi[...], clo[...])
         parts[day][0][...], parts[day][1][...] = split(step)
         off[day : day + 1, :] = mv(info[day], chi[...], clo[...])
+
+
+def both_kernel(after, b1hi, b1lo, b2hi, b2lo, off, bchi, bclo, offset):
     both = jnp.dot(b1hi[...], b2hi[...], preferred_element_type=F32) + (
         jnp.dot(b1lo[...], b2hi[...], preferred_element_type=F32)
         + jnp.dot(b1hi[...], b2lo[...], preferred_element_type=F32)
     )
     bchi[...], bclo[...] = split(both)
-    off[2:3, :] = mv(off[0:1, :], b2hi[...], b2lo[...]) + off[1:2, :]
-
-
-def hop_kernel(after, acc, got, bchi, bclo, off, total, y):
+    offset[...] = mv(off[0:1, :], b2hi[...], b2lo[...]) + off[1:2, :]
+
+
+def hop_kernel(after, acc, got, bchi, bclo, offset, total, y):
     state = acc[...] + got[...]
     total[...] = state
-    y[...] = mv(state, bchi[...], bclo[...]) + off[2:3, :]
-
-
-def pairs_kernel(ids, table, mthi, mtlo, khi, klo):
+    y[...] = mv(state, bchi[...], bclo[...]) + offset[...]
+
+
+def pairs_kernel(after, ids, table, mthi, mtlo, khi, klo):
     spans = table.shape[0] // 2
 
     @pl.when(ids[1] == spans - 1)
@@ -447,7 +464,7 @@
         span = span ^ (seat >> bit)
     c = z * held + y
     seat = c ^ (c >> 1)
-    ids = jnp.stack([z, span, o, c, (1 + seat % 2) * spans + (seat | 1)]).astype(jnp.int32)
+    ids = jnp.stack([z, span, o, c, (1 + seat % 2) * spans + (seat | 1), held]).astype(jnp.int32)
     everyone = ("z", "y", "obs")
 
     def owner(span):
@@ -497,55 +514,62 @@
         [pltpu.VMEM((width, span_slots), BF16), pltpu.VMEM((16, span_slots), BF16)],
         flops=4 * width * width * blocks * slots,
     )
-    plane_sums = [
-        lax.ppermute(
-            pay, everyone, [(spans + place(p), owner(p)) for p in range(spans) if place(p) % 2 == 0]
-        )
-    ] + [
-        lax.ppermute(
+    def swap(x, bit):
+        return lax.ppermute(x, "obs", [(i, i ^ bit) for i in range(peers)])
+
+    def plane_sum(s):
+        return lax.ppermute(
             pay, everyone, [((owner_plane(p) + s) % planes * spans + place(p), owner(p)) for p in range(spans)]
         )
-        for s in range(planes - 1, 0, -1)
-    ]
-
-    def swap(x, bit):
-        return lax.ppermute(x, "obs", [(i, i ^ bit) for i in range(peers)])
 
     across = swap(gain, 2)
-    gains = [gain, swap(gain, 1), across, swap(across, 1)]
+    beside = swap(gain, 1)
+    fourth = lax.ppermute(
+        pay, everyone, [(spans + place(p), owner(p)) for p in range(spans) if place(p) % 2 == 0]
+    )
+    third, first, second = plane_sum(3), plane_sum(1), plane_sum(2)
+    mthi, mtlo = run(
+        gain_kernel, [(full, BF16)] * 2, [(ids, SMEM), gain, beside, across, swap(across, 1)]
+    )
     pt, pthi, ptlo, chi, clo = run(
         prep_kernel, [(full, F32)] + [(full, BF16)] * 4, [propagator_matrix, analysis_cov]
     )
-    omhi, omlo, info, mine, table, acc, y = run(
+    smalls = pltpu.VMEM((planes + 1, extra_tiles * LANES, LANES), F32)
+    omhi, omlo, info, mine, acc, y = run(
         owner_kernel,
-        [((days,) + full, BF16)] * 2
-        + [((days, 1, width), F32), ((days, width), F32), ((spans * days, width), F32), row, row],
-        [(ids, SMEM), own, extra, *plane_sums, prior, pthi, ptlo, chi, clo, *[(g, ANY) for g in gains[1:]]],
-        [pltpu.VMEM((planes + 1, extra_tiles * LANES, LANES), F32)],
+        [((days,) + full, BF16)] * 2 + [((days, 1, width), F32), ((days, width), F32), row, row],
+        [
+            (ids, SMEM), own, extra, fourth, third, first, second, prior, pthi, ptlo, chi, clo, (mthi, ANY)
+        ],
+        [smalls],
     )
     for k in range(spans - 1):
         received = lax.ppermute(y, everyone, [(owner(k), owner(k + 1))])
         if k == 0:
-            acc, y = run(
-                direct_kernel,
-                [row, row],
-                [(ids, SMEM), acc, received, mine, pthi, ptlo, omhi, omlo, info, chi, clo],
+            b1hi, b1lo, b2hi, b2lo, off = run(
+                maps_kernel,
+                [(full, BF16)] * 4 + [((8, width), F32)],
+                [(y, ANY), omhi, omlo, info, chi, clo, pt, mine],
+                flops=24 * width**3,
             )
-            b1hi, b1lo, b2hi, b2lo, bchi, bclo, off = run(
-                maps_kernel,
-                [(full, BF16)] * 6 + [((8, width), F32)],
-                [y, omhi, omlo, info, chi, clo, pt, mine],
-                flops=30 * width**3,
+            acc, y = run(second_kernel, [row, row], [acc, received, b1hi, b1lo, b2hi, b2lo, off])
+            bchi, bclo, offset = run(
+                both_kernel, [(full, BF16)] * 2 + [row], [(y, ANY), b1hi, b1lo, b2hi, b2lo, off]
             )
-            side = y
+            (table,) = run(
+                table_kernel,
+                [((spans * days, width), F32)],
+                [(offset, ANY), (ids, SMEM), extra, first, second, third],
+                [smalls],
+            )
+            side = table
         elif k < spans - 2:
-            acc, y = run(hop_kernel, [row, row], [(side, ANY), acc, received, bchi, bclo, off])
+            acc, y = run(hop_kernel, [row, row], [(side, ANY), acc, received, bchi, bclo, offset])
             if k == 2:
-                mthi, mtlo = run(gain_kernel, [(full, BF16)] * 2, [(y, ANY), (ids, SMEM), *gains])
                 khi, klo = run(
                     pairs_kernel,
                     [((min(spans - 1, 7),) + full, BF16)] * 2,
-                    [(ids, SMEM), table, mthi, mtlo],
+                    [(y, ANY), (ids, SMEM), table, mthi, mtlo],
                 )
                 side = khi
     (answer,) = run(

time: 90.7 us -> 91.9 us (1.013)
  local copies, waits for them, and re-layouts: 5.89 us -> 10.9 us
  starting transfers between devices: 14.7 us -> 11.6 us
    unnamed x20 -> x30, local copies, waits for them, and re-layouts: 5.81 us -> 10.8 us
    ppermute x3, waiting for transfers between devices: 2.45 us -> 0.01 us  [plane_sum(): lax.ppermute(pay, everyone, [((owner_plane(p) + s) % planes * spans + pla...]
    ppermute x3, waiting for transfers between devices: 0.45 us -> 2.28 us  [swap(): return lax.ppermute(x, 'obs', [(i, i ^ bit) for i in range(peers)])]
    ppermute x3, starting transfers between devices: 2.25 us -> 0.7 us  [swap(): return lax.ppermute(x, 'obs', [(i, i ^ bit) for i in range(peers)])]
    pallas_call x15 -> x17, Pallas kernels: 18.4 us -> 18.1 us  [run(): pl.pallas_call(body, out_shape=[jax.ShapeDtypeStruct(s, d) for s, d in ou...]
  transfers between devices with their start and end apart: 14 -> 14, of which waited for: 2 -> 2; matrix products, arithmetic and copies ran while one was open for 0% -> 0% of each run, Pallas kernels for 8% -> 9%
where the time goes in v8:
time: 91.9 us; the launch traced here: 91.4 us
  blocking collectives  47.5 us (52%)
  Pallas kernels  18.1 us (20%)
  starting transfers between devices  11.6 us (13%)
  local copies, waits for them, and re-layouts  10.9 us (12%)
  waiting for transfers between devices  2.3 us (3%)
  between operations  0.96 us (1%)
    all_to_all x1, blocking collectives, local(): lax.all_to_all(answer, everyone, split_axis=0, concat_axis=0, tiled=True)  26.2 us
    all_to_all x1, blocking collectives, local(): lax.all_to_all(sent, ('y', 'obs'), split_axis=0, concat_axis=0, tiled=True)  21.4 us
    pallas_call x17, Pallas kernels, run(): pl.pallas_call(body, out_shape=[jax.ShapeDtypeStruct(s, d) for s, d in ou...  18.1 us
    unnamed x30, local copies, waits for them, and re-layouts  10.8 us
    ppermute x3, starting transfers between devices, plane_sum(): lax.ppermute(pay, everyone, [((owner_plane(p) + s) % planes * spans + pla...  5.35 us
    ppermute x7, starting transfers between devices, local(): received = lax.ppermute(y, everyone, [(owner(k), owner(k + 1))])  4.86 us
    ppermute x3, waiting for transfers between devices, swap(): return lax.ppermute(x, 'obs', [(i, i ^ bit) for i in range(peers)])  2.28 us
  transfers between devices with their start and end apart: 14, of which 2 were waited for; matrix products, arithmetic and copies ran while one was open for 0% of the time, Pallas kernels for 9%

profile of v8, /device:TPU:0, one launch (start us, length us, event | category | flops | bytes accessed | tf_op | source)
XLA Modules:
  0.0 91.4 jit_solution(4163908361028006455)
XLA Ops:
  0.6 2.2 %shard_map.104 = bf16[8,136,512]{2,1,0:T(8,128)(2,1)} custom-call(s32[8]{0:T(128)} %day.1, s32[8]{0:T(128)} %count.1, bf16[1024,512]{1,0:T(8,128)(2,1)} %rows.1, bf16[8,128]{1,0:T(8,128)(2,1)} %bitcast.7, f32[1,128]{1,0:T(1,128)} %bitcast.8, f32[2,512]{1,0:T(2,128)} %damping.1), custom_call_target="tpu_custom_call" | custom-call | bytes 1055296 | tf_op jit(solution)/shard_map/pallas_call | solution.py:22
  2.9 21.4 %all_to_all.10.got = bf16[8,136,512]{2,1,0:T(8,128)(2,1)S(1)} all-to-all(bf16[8,136,512]{2,1,0:T(8,128)(2,1)} %shard_map.104), channel_id=1, replica_groups=mesh['z'=4,'y'=2,'obs'=4] {'y','obs'}, dimensions={0} | all-to-all | bytes 2228224 | tf_op jit(solution)/shard_map/all_to_all | solution.py:502
  24.2 2.0 %shard_map.105 = (f32[20,128,128]{2,1,0:T(8,128)S(1)}, f32[128,128]{1,0:T(8,128)S(1)}, bf16[17,128,128]{2,1,0:T(8,128)(2,1)}, f32[1,512]{1,0:T(1,128)S(1)}, f32[128,512]{1,0:T(8,128)S(1)}) custom-call(bf16[8,136,512]{2,1,0:T(8,128)(2,1)S(1)} %all_to_all.10.got, f32[128,512]{1,0:T(8,128)S(1)} %copy-done.14), custom_call_target="tpu_custom_call" | custom-call | flops 1073741824 | bytes 1376256 | tf_op jit(solution)/shard_map/pallas_call | solution.py:22
  26.3 1.1 %copy-done = f32[20,128,128]{2,1,0:T(8,128)} copy-done((f32[20,128,128]{2,1,0:T(8,128)}, f32[20,128,128]{2,1,0:T(8,128)S(1)}, u32[]{:S(2)}) %copy-start) | copy-done | bytes 1310744
  29.3 4.0 %collective-permute-start.1 = (bf16[17,128,128]{2,1,0:T(8,128)(2,1)}, bf16[17,128,128]{2,1,0:T(8,128)(2,1)S(1)}, u32[]{:S(2)}, u32[]{:S(2)}) collective-permute-start(bf16[17,128,128]{2,1,0:T(8,128)(2,1)} %get-tuple-element.44), channel_id=1, source_target_pairs={{0,9},{9,17},{11,19},{2,11},{6,15},{15,23},{13,21},{4,13}} | collective-permute-start | bytes 1671176 | tf_op jit(solution)/shard_map/ppermute | solution.py:521
  34.0 1.4 %collective-permute-done.5.m2 = f32[128,512]{1,0:T(8,128)} collective-permute-done((f32[128,512]{1,0:T(8,128)S(1)}, f32[128,512]{1,0:T(8,128)}, u32[]{:S(2)}, u32[]{:S(2)}) %collective-permute-start.5) | collective-permute-done | bytes 262176 | tf_op jit(solution)/shard_map/ppermute | solution.py:518
  36.1 0.8 collective-permute-done.4.m1
  37.8 1.2 %copy-done.2 = f32[512,512]{1,0:T(8,128)S(1)} copy-done((f32[512,512]{1,0:T(8,128)S(1)}, f32[512,512]{1,0:T(8,128)}, u32[]{:S(2)}) %copy-start.2) | copy-done | bytes 1048600
  39.0 1.2 %copy-done.3 = f32[512,512]{1,0:T(8,128)S(1)} copy-done((f32[512,512]{1,0:T(8,128)S(1)}, f32[512,512]{1,0:T(8,128)}, u32[]{:S(2)}) %copy-start.3) | copy-done | bytes 1048600
  40.9 0.8 copy-done.4
  41.7 0.8 copy-done.6
  42.5 1.0 %copy-done.12 = f32[512,512]{1,0:T(8,128)} copy-done((f32[512,512]{1,0:T(8,128)}, f32[512,512]{1,0:T(8,128)S(1)}, u32[]{:S(2)}) %copy-start.12) | copy-done | bytes 1048600
  43.6 1.0 %copy-done.9 = f32[128,512]{1,0:T(8,128)S(1)} copy-done((f32[128,512]{1,0:T(8,128)S(1)}, f32[128,512]{1,0:T(8,128)}, u32[]{:S(2)}) %copy-start.9) | copy-done | bytes 262168
  44.6 0.9 %copy-done.11 = f32[128,512]{1,0:T(8,128)S(1)} copy-done((f32[128,512]{1,0:T(8,128)S(1)}, f32[128,512]{1,0:T(8,128)}, u32[]{:S(2)}) %copy-start.11) | copy-done | bytes 262168
  45.5 1.4 %shard_map.107 = (bf16[512,512]{1,0:T(8,128)(2,1)S(1)}, bf16[512,512]{1,0:T(8,128)(2,1)S(1)}) custom-call(s32[6]{0:T(128)S(1)} %stack.23.ids, f32[128,512]{1,0:T(8,128)S(1)} %copy-done.9, f32[128,512]{1,0:T(8,128)S(1)} %copy-done.11, f32[128,512]{1,0:T(8,128)} %collective-permute-done.5.m2, f32[128,512]{1,0:T(8,128)} %collective-permute-done.6.m3), custom_call_target="tpu_custom_call" | custom-call | bytes 1048600 | tf_op jit(solution)/shard_map/pallas_call | solution.py:22
  47.0 1.3 %copy-done.1 = f32[20,128,128]{2,1,0:T(8,128)S(1)} copy-done((f32[20,128,128]{2,1,0:T(8,128)S(1)}, f32[20,128,128]{2,1,0:T(8,128)}, u32[]{:S(2)}) %copy-start.1) | copy-done | bytes 1310744
  48.3 1.4 %shard_map.108 = (bf16[2,512,512]{2,1,0:T(8,128)(2,1)S(1)}, bf16[2,512,512]{2,1,0:T(8,128)(2,1)S(1)}, f32[2,1,512]{2,1,0:T(1,128)S(1)}, f32[2,512]{1,0:T(2,128)S...) custom-call(s32[6]{0:T(128)S(1)} %stack.23.ids, f32[20,128,128]{2,1,0:T(8,128)S(1)} %copy-done.1, ...), custom_call_target="tpu_custom_call" | custom-call | bytes 6227992 | tf_op jit(solution)/shard_map/pallas_call | solution.py:22
  50.4 3.8 %shard_map.109 = (bf16[512,512]{1,0:T(8,128)(2,1)S(1)}, bf16[512,512]{1,0:T(8,128)(2,1)S(1)}, bf16[512,512]{1,0:T(8,128)(2,1)S(1)}, bf16[512,512]{1,0:T(8,128)(2,1)S(1)}, f32[8,512]{1,0:T(8,128)S(1)}) custom-call(f32[1,512]{1,0:T(1,128)S(1)} %get-tuple-element.53.after, bf16[2,512,512]{2,1,0:T(8,128)(2,1)S(1)} %get-tuple-element.54.omhi, ...), custom_call_target="tpu_custom_call" | custom-call | flops 3221225472 | bytes 4204544 | tf_op jit(solution)/shard_map/pallas_call | solution.py:22
  55.4 1.1 %shard_map.111 = (bf16[512,512]{1,0:T(8,128)(2,1)S(1)}, bf16[512,512]{1,0:T(8,128)(2,1)S(1)}, f32[1,512]{1,0:T(1,128)S(1)}) custom-call(f32[1,512]{1,0:T(1,128)S(1)} %get-tuple-element.64.after, bf16[512,512]{1,0:T(8,128)(2,1)S(1)} %get-tuple-element.59.b1hi, bf16[512,512]{1,0:T(8,128)(2,1)S(1)} %get-tuple-element.60.b1lo, ...), custom_call_target="tpu_custom_call" | custom-call | bytes 2115584 | tf_op jit(solution)/shard_map/pallas_call | solution.py:22
  57.3 0.7 collective-permute-start.9
  58.3 0.7 collective-permute-start.10
  62.3 1.7 %shard_map.119 = f32[32,8,128]{2,1,0:T(8,128)S(1)} custom-call(s32[6]{0:T(128)S(1)} %stack.23.ids, f32[1,512]{1,0:T(1,128)S(1)} %get-tuple-element.79.acc, f32[1,512]{1,0:T(1,128)S(1)} %collective-permute-done.13.got, bf16[512,512]{1,0:T(8,128)(2,1)S(1)} %get-tuple-element.59.b1hi, bf16[512,512]{1,0:T(8,128)(2,1)S(1)} %get-tuple-element.60.b1lo, ...), custom_call_target="tpu_custom_call" | custom-call | bytes 11587608 | tf_op jit(solution)/shard_map/pallas_call | solution.py:22
  64.1 26.2 %all_to_all.11.parts = f32[32,8,128]{2,1,0:T(8,128)S(1)} all-to-all(f32[32,8,128]{2,1,0:T(8,128)S(1)} %shard_map.119), channel_id=1, replica_groups=mesh['z'=4,'y'=2,'obs'=4] {'z','y','obs'}, dimensions={0} | all-to-all | bytes 262144 | tf_op jit(solution)/shard_map/all_to_all | solution.py:583
  90.3 1.1 %shard_map.120 = (f32[2,128]{1,0:T(2,128)}, f32[2,128]{1,0:T(2,128)}) custom-call(s32[6]{0:T(128)S(1)} %stack.23.ids, f32[32,8,128]{2,1,0:T(8,128)S(1)} %all_to_all.11.parts), custom_call_target="tpu_custom_call" | custom-call | bytes 131096 | tf_op jit(solution)/shard_map/pallas_call | solution.py:22
  (54 shorter events, 11.1 us)
Async XLA Ops:
  2.9 21.4 %copy-start.14 = (f32[128,512]{1,0:T(8,128)S(1)}, f32[128,512]{1,0:T(8,128)}, u32[]{:S(2)}) copy-start(f32[128,512]{1,0:T(8,128)} %gain.1) | copy-start | bytes 786436
  26.2 1.1 %copy-start = (f32[20,128,128]{2,1,0:T(8,128)}, f32[20,128,128]{2,1,0:T(8,128)S(1)}, u32[]{:S(2)}) copy-start(f32[20,128,128]{2,1,0:T(8,128)S(1)} %get-tuple-element.42.own) | copy-start | bytes 3932164
  27.3 8.1 %collective-permute-start.5 = (f32[128,512]{1,0:T(8,128)S(1)}, f32[128,512]{1,0:T(8,128)}, u32[]{:S(2)}, u32[]{:S(2)}) collective-permute-start(f32[128,512]{1,0:T(8,128)S(1)} %get-tuple-element.50.m0), channel_id=1, source_target_pairs={{0,2},{1,3},{2,0},{3,1},{4,6},{5,7},{6,4},{7,5},{8,10},{9,11},{10,... | collective-permute-start | bytes 786440 | tf_op jit(solution)/shard_map/ppermute | solution.py:518
  27.9 19.0 %collective-permute-start.3 = (bf16[17,128,128]{2,1,0:T(8,128)(2,1)}, bf16[17,128,128]{2,1,0:T(8,128)(2,1)S(1)}, u32[]{:S(2)}, u32[]{:S(2)}) collective-permute-start(bf16[17,128,128]{2,1,0:T(8,128)(2,1)} %get-tuple-element.44), channel_id=1, source_target_pairs={{24,9},{1,17},{3,19},{26,11},{30,15},{7,23},{5,21},{28,13}} | collective-permute-start | bytes 1671176 | tf_op jit(solution)/shard_map/ppermute | solution.py:521
  28.6 18.3 %collective-permute-start.2 = (bf16[17,128,128]{2,1,0:T(8,128)(2,1)}, bf16[17,128,128]{2,1,0:T(8,128)(2,1)S(1)}, u32[]{:S(2)}, u32[]{:S(2)}) collective-permute-start(bf16[17,128,128]{2,1,0:T(8,128)(2,1)} %get-tuple-element.44), channel_id=1, source_target_pairs={{16,9},{25,17},{27,19},{18,11},{22,15},{31,23},{29,21},{20,13}} | collective-permute-start | bytes 1671176 | tf_op jit(solution)/shard_map/ppermute | solution.py:521
  29.3 17.6 %collective-permute-start.1 = (bf16[17,128,128]{2,1,0:T(8,128)(2,1)}, bf16[17,128,128]{2,1,0:T(8,128)(2,1)S(1)}, u32[]{:S(2)}, u32[]{:S(2)}) collective-permute-start(bf16[17,128,128]{2,1,0:T(8,128)(2,1)} %get-tuple-element.44), channel_id=1, source_target_pairs={{0,9},{9,17},{11,19},{2,11},{6,15},{15,23},{13,21},{4,13}} | collective-permute-start | bytes 1671176 | tf_op jit(solution)/shard_map/ppermute | solution.py:521
  33.3 13.7 %collective-permute-start = (bf16[17,128,128]{2,1,0:T(8,128)(2,1)}, bf16[17,128,128]{2,1,0:T(8,128)(2,1)S(1)}, u32[]{:S(2)}, u32[]{:S(2)}) collective-permute-start(bf16[17,128,128]{2,1,0:T(8,128)(2,1)} %get-tuple-element.44), channel_id=1, source_target_pairs={{8,9},{10,11},{14,15},{12,13}} | collective-permute-start | bytes 1671176 | tf_op jit(solution)/shard_map/ppermute | solution.py:527
  35.4 1.5 %collective-permute-start.4 = (f32[128,512]{1,0:T(8,128)S(1)}, f32[128,512]{1,0:T(8,128)S(1)}, u32[]{:S(2)}, u32[]{:S(2)}) collective-permute-start(f32[128,512]{1,0:T(8,128)S(1)} %get-tuple-element.50.m0), channel_id=1, source_target_pairs={{0,1},{1,0},{2,3},{3,2},{4,5},{5,4},{6,7},{7,6},{8,9},{9,8},{10,11... | collective-permute-start | bytes 786440 | tf_op jit(solution)/shard_map/ppermute | solution.py:518
  37.7 5.9 %collective-permute-start.6 = (f32[128,512]{1,0:T(8,128)}, f32[128,512]{1,0:T(8,128)}, u32[]{:S(2)}, u32[]{:S(2)}) collective-permute-start(f32[128,512]{1,0:T(8,128)} %collective-permute-done.5.m2), channel_id=1, source_target_pairs={{0,1},{1,0},{2,3},{3,2},{4,5},{5,4},{6,7},{7,6},{8,9},{9,8},{10,11... | collective-permute-start | bytes 786440 | tf_op jit(solution)/shard_map/ppermute | solution.py:518
  37.8 1.2 %copy-start.2 = (f32[512,512]{1,0:T(8,128)S(1)}, f32[512,512]{1,0:T(8,128)}, u32[]{:S(2)}) copy-start(f32[512,512]{1,0:T(8,128)} %trans.1) | copy-start | bytes 3145732
  39.0 1.2 %copy-start.3 = (f32[512,512]{1,0:T(8,128)S(1)}, f32[512,512]{1,0:T(8,128)}, u32[]{:S(2)}) copy-start(f32[512,512]{1,0:T(8,128)} %cov.1) | copy-start | bytes 3145732
  42.5 1.0 %copy-start.12 = (f32[512,512]{1,0:T(8,128)}, f32[512,512]{1,0:T(8,128)S(1)}, u32[]{:S(2)}) copy-start(f32[512,512]{1,0:T(8,128)S(1)} %get-tuple-element.57.pt) | copy-start | bytes 3145732
  43.5 3.4 %copy-start.5 = (bf16[512,512]{1,0:T(8,128)(2,1)S(1)}, bf16[512,512]{1,0:T(8,128)(2,1)}, u32[]{:S(2)}) copy-start(bf16[512,512]{1,0:T(8,128)(2,1)} %copy-done.4) | copy-start | bytes 1572868
  43.5 3.4 %copy-start.7 = (bf16[512,512]{1,0:T(8,128)(2,1)S(1)}, bf16[512,512]{1,0:T(8,128)(2,1)}, u32[]{:S(2)}) copy-start(bf16[512,512]{1,0:T(8,128)(2,1)} %copy-done.6) | copy-start | bytes 1572868
  43.5 1.0 %copy-start.9 = (f32[128,512]{1,0:T(8,128)S(1)}, f32[128,512]{1,0:T(8,128)}, u32[]{:S(2)}) copy-start(f32[128,512]{1,0:T(8,128)} %copy-done.8) | copy-start | bytes 786436
  47.0 1.3 %copy-start.1 = (f32[20,128,128]{2,1,0:T(8,128)S(1)}, f32[20,128,128]{2,1,0:T(8,128)}, u32[]{:S(2)}) copy-start(f32[20,128,128]{2,1,0:T(8,128)} %copy-done) | copy-start | bytes 3932164
  48.3 2.1 %copy-start.13 = (f32[512,512]{1,0:T(8,128)S(1)}, f32[512,512]{1,0:T(8,128)}, u32[]{:S(2)}) copy-start(f32[512,512]{1,0:T(8,128)} %copy-done.12) | copy-start | bytes 3145732
  49.7 4.5 %collective-permute-start.7 = (f32[1,512]{1,0:T(1,128)S(1)}, f32[1,512]{1,0:T(1,128)S(1)}, u32[]{:S(2)}, u32[]{:S(2)}) collective-permute-start(f32[1,512]{1,0:T(1,128)S(1)} %get-tuple-element.53.after), channel_id=1, source_target_pairs={{9,17}} | collective-permute-start | bytes 6152 | tf_op jit(solution)/shard_map/ppermute | solution.py:547
  54.7 2.4 %collective-permute-start.8 = (f32[1,512]{1,0:T(1,128)S(1)}, f32[1,512]{1,0:T(1,128)S(1)}, u32[]{:S(2)}, u32[]{:S(2)}) collective-permute-start(f32[1,512]{1,0:T(1,128)S(1)} %get-tuple-element.64.after), channel_id=1, source_target_pairs={{17,19}} | collective-permute-start | bytes 6152 | tf_op jit(solution)/shard_map/ppermute | solution.py:547
  57.3 0.7 collective-permute-start.9
  58.3 1.3 %collective-permute-start.10 = (f32[1,512]{1,0:T(1,128)S(1)}, f32[1,512]{1,0:T(1,128)S(1)}, u32[]{:S(2)}, u32[]{:S(2)}) collective-permute-start(f32[1,512]{1,0:T(1,128)S(1)} %get-tuple-element.71.after), channel_id=1, source_target_pairs={{11,15}} | collective-permute-start | bytes 6152 | tf_op jit(solution)/shard_map/ppermute | solution.py:547
  59.8 0.7 collective-permute-start.11
  60.7 0.7 collective-permute-start.12
  61.6 0.7 collective-permute-start.13
  (5 other events, 3.9 us)

commit v9 on v8

--- a/solution.py
+++ b/solution.py
@@ -28,6 +28,20 @@
         compiler_params=pltpu.CompilerParams(vmem_limit_bytes=limit * 1024 * 1024),
         cost_estimate=pl.CostEstimate(flops=flops, bytes_accessed=moved, transcendentals=0),
     )(*arrays)
+
+
+def here():
+    z, y, o = (lax.axis_index(a) for a in ("z", "y", "obs"))
+    held, peers = lax.axis_size("y"), lax.axis_size("obs")
+    spans = held * peers
+    at = y * peers + o
+    seat = jnp.where(z == 1, at - lax.rem(at, 2), at)
+    span = seat
+    for bit in range(1, spans.bit_length()):
+        span = span ^ (seat >> bit)
+    c = z * held + y
+    seat = c ^ (c >> 1)
+    return z, span, o, c, (1 + (seat & 1)) * spans + (seat | 1), held
 
 
 def triangle(width):
@@ -211,7 +225,8 @@
     chi[...], clo[...] = split(cov[...])
 
 
-def gain_kernel(ids, m0, m1, m2, m3, mthi, mtlo):
+def gain_kernel(m0, m1, m2, m3, mthi, mtlo):
+    ids = here()
     rows = m0.shape[0]
     for step, part in enumerate((m0, m1, m2, m3)):
         holder = ids[2] ^ step
@@ -249,7 +264,8 @@
     )
 
 
-def table_kernel(after, ids, extra, g1, g2, g3, table, small):
+def table_kernel(after, extra, g1, g2, g3, table, small):
+    ids = here()
     planes = 4
     chunks = table.shape[1] // LANES
     held = table.shape[0] // 2 // planes
@@ -264,8 +280,9 @@
 
 
 def owner_kernel(
-    ids, own, extra, g4, g3, g1, g2, prior, pthi, ptlo, chi, clo, after, omhi, omlo, info, mine, start, y, small
+    own, extra, g4, g3, g1, g2, prior, pthi, ptlo, chi, clo, after, omhi, omlo, info, mine, start, y, small
 ):
+    ids = here()
     planes = 4
     width = pthi.shape[0]
     chunks = width // LANES
@@ -367,7 +384,8 @@
     y[...] = mv(state, bchi[...], bclo[...]) + offset[...]
 
 
-def pairs_kernel(after, ids, table, mthi, mtlo, khi, klo):
+def pairs_kernel(after, table, mthi, mtlo, khi, klo):
+    ids = here()
     spans = table.shape[0] // 2
 
     @pl.when(ids[1] == spans - 1)
@@ -381,8 +399,9 @@
 
 
 def last_kernel(
-    ids, acc, got, b1hi, b1lo, b2hi, b2lo, off, table, pthi, ptlo, mthi, mtlo, khi, klo, out, shares
+    acc, got, b1hi, b1lo, b2hi, b2lo, off, table, pthi, ptlo, mthi, mtlo, khi, klo, out, shares
 ):
+    ids = here()
     total, width = shares.shape
     spans = total // 2
     chunks = width // LANES
@@ -433,7 +452,8 @@
         out[span * chunks + q, 2:4, :] = both[:, q * LANES : (q + 1) * LANES]
 
 
-def add_kernel(ids, parts, filt, smooth):
+def add_kernel(parts, filt, smooth):
+    ids = here()
     spans = parts.shape[0] // 4
     filt[...] = parts[ids[4], 2:4, :]
     smooth[...] = sum(parts[owner_plane(c) * spans + (place(c) | 1), 0:2, :] for c in range(spans))
@@ -457,14 +477,6 @@
     width = records.shape[1]
     days = damping.shape[0]
     assert planes == peers == 4 and days == 2 and slots == LANES and blocks == spans
-    z, y, o = (lax.axis_index(a) for a in ("z", "y", "obs"))
-    at = y * peers + o
-    span = seat = jnp.where(z == 1, at - at % 2, at)
-    for bit in range(1, spans.bit_length()):
-        span = span ^ (seat >> bit)
-    c = z * held + y
-    seat = c ^ (c >> 1)
-    ids = jnp.stack([z, span, o, c, (1 + seat % 2) * spans + (seat | 1), held]).astype(jnp.int32)
     everyone = ("z", "y", "obs")
 
     def owner(span):
@@ -529,7 +541,7 @@
     )
     third, first, second = plane_sum(3), plane_sum(1), plane_sum(2)
     mthi, mtlo = run(
-        gain_kernel, [(full, BF16)] * 2, [(ids, SMEM), gain, beside, across, swap(across, 1)]
+        gain_kernel, [(full, BF16)] * 2, [gain, beside, across, swap(across, 1)]
     )
     pt, pthi, ptlo, chi, clo = run(
         prep_kernel, [(full, F32)] + [(full, BF16)] * 4, [propagator_matrix, analysis_cov]
@@ -539,7 +551,7 @@
         owner_kernel,
         [((days,) + full, BF16)] * 2 + [((days, 1, width), F32), ((days, width), F32), row, row],
         [
-            (ids, SMEM), own, extra, fourth, third, first, second, prior, pthi, ptlo, chi, clo, (mthi, ANY)
+            own, extra, fourth, third, first, second, prior, pthi, ptlo, chi, clo, (mthi, ANY)
         ],
         [smalls],
     )
@@ -559,7 +571,7 @@
             (table,) = run(
                 table_kernel,
                 [((spans * days, width), F32)],
-                [(offset, ANY), (ids, SMEM), extra, first, second, third],
+                [(offset, ANY), extra, first, second, third],
                 [smalls],
             )
             side = table
@@ -569,20 +581,20 @@
                 khi, klo = run(
                     pairs_kernel,
                     [((min(spans - 1, 7),) + full, BF16)] * 2,
-                    [(y, ANY), (ids, SMEM), table, mthi, mtlo],
+                    [(y, ANY), table, mthi, mtlo],
                 )
                 side = khi
     (answer,) = run(
         last_kernel,
         [((spans * peers, 8, LANES), F32)],
         [
-            (ids, SMEM), acc, received, b1hi, b1lo, b2hi, b2lo, off, table, pthi, ptlo, mthi, mtlo, khi, klo
+            acc, received, b1hi, b1lo, b2hi, b2lo, off, table, pthi, ptlo, mthi, mtlo, khi, klo
         ],
         [pltpu.VMEM((spans * days, width), F32)],
     )
     parts = lax.all_to_all(answer, everyone, split_axis=0, concat_axis=0, tiled=True)
     out = ((days, LANES), F32)
-    return run(add_kernel, [out, out], [(ids, SMEM), parts])
+    return run(add_kernel, [out, out], [parts])
 
 
 def solution(mesh):

time: 91.9 us -> 84.8 us (0.923)
  local copies, waits for them, and re-layouts: 10.9 us -> 0.01 us
  waiting for transfers between devices: 2.3 us -> 9.01 us
  Pallas kernels: 18.1 us -> 13.5 us
  blocking collectives: 47.5 us -> 49.4 us
    unnamed x30 -> x6, local copies, waits for them, and re-layouts: 10.8 us -> 0.01 us
    ppermute x3, waiting for transfers between devices: 0.01 us -> 5.33 us  [plane_sum(): lax.ppermute(pay, everyone, [((owner_plane(p) + s) % planes * spans + pla...]
    pallas_call x17, Pallas kernels: 18.1 us -> 13.5 us  [run(): pl.pallas_call(body, out_shape=[jax.ShapeDtypeStruct(s, d) for s, d in ou...]
    all_to_all x1, blocking collectives: 26.2 us -> 28 us  [local(): lax.all_to_all(answer, everyone, split_axis=0, concat_axis=0, tiled=True)]
    ppermute x3, waiting for transfers between devices: 2.28 us -> 3.64 us  [swap(): return lax.ppermute(x, 'obs', [(i, i ^ bit) for i in range(peers)])]
  transfers between devices with their start and end apart: 14 -> 14, of which waited for: 2 -> 4; matrix products, arithmetic and copies ran while one was open for 0% -> 0% of each run, Pallas kernels for 9% -> 7%
where the time goes in v9:
time: 84.8 us; the launch traced here: 84.4 us
  blocking collectives  49.4 us (58%)
  Pallas kernels  13.5 us (16%)
  starting transfers between devices  11.7 us (14%)
  waiting for transfers between devices  9.01 us (11%)
  between operations  0.89 us (1%)
    all_to_all x1, blocking collectives, local(): lax.all_to_all(answer, everyone, split_axis=0, concat_axis=0, tiled=True)  28 us
    all_to_all x1, blocking collectives, local(): lax.all_to_all(sent, ('y', 'obs'), split_axis=0, concat_axis=0, tiled=True)  21.4 us
    pallas_call x17, Pallas kernels, run(): pl.pallas_call(body, out_shape=[jax.ShapeDtypeStruct(s, d) for s, d in ou...  13.5 us
    ppermute x3, starting transfers between devices, plane_sum(): lax.ppermute(pay, everyone, [((owner_plane(p) + s) % planes * spans + pla...  5.35 us
    ppermute x3, waiting for transfers between devices, plane_sum(): lax.ppermute(pay, everyone, [((owner_plane(p) + s) % planes * spans + pla...  5.33 us
    ppermute x7, starting transfers between devices, local(): received = lax.ppermute(y, everyone, [(owner(k), owner(k + 1))])  4.86 us
    ppermute x3, waiting for transfers between devices, swap(): return lax.ppermute(x, 'obs', [(i, i ^ bit) for i in range(peers)])  3.64 us
  transfers between devices with their start and end apart: 14, of which 4 were waited for; matrix products, arithmetic and copies ran while one was open for 0% of the time, Pallas kernels for 7%

profile of v9, /device:TPU:0, one launch (start us, length us, event | category | flops | bytes accessed | tf_op | source)
XLA Modules:
  0.0 84.4 jit_solution(15025917781873283983)
XLA Ops:
  0.6 2.2 %shard_map.104 = bf16[8,136,512]{2,1,0:T(8,128)(2,1)} custom-call(s32[8]{0:T(128)} %day.1, s32[8]{0:T(128)} %count.1, bf16[1024,512]{1,0:T(8,128)(2,1)} %rows.1, bf16[8,128]{1,0:T(8,128)(2,1)} %bitcast.2, f32[1,128]{1,0:T(1,128)} %bitcast.3, f32[2,512]{1,0:T(2,128)} %damping.1), custom_call_target="tpu_custom_call" | custom-call | bytes 1055296 | tf_op jit(solution)/shard_map/pallas_call | solution.py:22
  2.9 21.4 %all_to_all.10.got = bf16[8,136,512]{2,1,0:T(8,128)(2,1)S(1)} all-to-all(bf16[8,136,512]{2,1,0:T(8,128)(2,1)} %shard_map.104), channel_id=1, replica_groups=mesh['z'=4,'y'=2,'obs'=4] {'y','obs'}, dimensions={0} | all-to-all | bytes 2228224 | tf_op jit(solution)/shard_map/all_to_all | solution.py:514
  24.2 1.2 %shard_map.105 = (f32[20,128,128]{2,1,0:T(8,128)S(1)}, f32[128,128]{1,0:T(8,128)S(1)}, bf16[17,128,128]{2,1,0:T(8,128)(2,1)S(1)}, f32[1,512]{1,0:T(1,128)S(1)}, f32[128,512]{1,0:T(8,128)S(1)}) custom-call(bf16[8,136,512]{2,1,0:T(8,128)(2,1)S(1)} %all_to_all.10.got, f32[128,512]{1,0:T(8,128)S(1)} %copy-done.2), custom_call_target="tpu_custom_call" | custom-call | flops 1073741824 | bytes 1376256 | tf_op jit(solution)/shard_map/pallas_call | solution.py:22
  25.5 0.6 collective-permute-start.5
  26.1 0.7 collective-permute-start.3
  26.8 0.7 collective-permute-start.2
  27.5 4.0 %collective-permute-start.1 = (bf16[17,128,128]{2,1,0:T(8,128)(2,1)S(1)}, bf16[17,128,128]{2,1,0:T(8,128)(2,1)S(1)}, u32[]{:S(2)}, u32[]{:S(2)}) collective-permute-start(bf16[17,128,128]{2,1,0:T(8,128)(2,1)S(1)} %get-tuple-element.44), channel_id=1, source_target_pairs={{0,9},{9,17},{11,19},{2,11},{6,15},{15,23},{13,21},{4,13}} | collective-permute-start | bytes 1671176 | tf_op jit(solution)/shard_map/ppermute | solution.py:533
  31.5 0.7 collective-permute-start
  32.2 1.3 %collective-permute-done.5.m2 = f32[128,512]{1,0:T(8,128)S(1)} collective-permute-done((f32[128,512]{1,0:T(8,128)S(1)}, f32[128,512]{1,0:T(8,128)S(1)}, u32[]{:S(2)}, u32[]{:S(2)}) %collective-permute-start.5) | collective-permute-done | bytes 262176 | tf_op jit(solution)/shard_map/ppermute | solution.py:530
  33.5 1.5 %collective-permute-done.4.m1 = f32[128,512]{1,0:T(8,128)S(1)} collective-permute-done((f32[128,512]{1,0:T(8,128)S(1)}, f32[128,512]{1,0:T(8,128)S(1)}, u32[]{:S(2)}, u32[]{:S(2)}) %collective-permute-start.4) | collective-permute-done | bytes 262176 | tf_op jit(solution)/shard_map/ppermute | solution.py:530
  35.8 0.8 collective-permute-done.6.m3
  37.0 5.3 %collective-permute-done.1.g3 = bf16[17,128,128]{2,1,0:T(8,128)(2,1)S(1)} collective-permute-done((bf16[17,128,128]{2,1,0:T(8,128)(2,1)S(1)}, bf16[17,128,128]{2,1,0:T(8,128)(2,1)S(1)}, u32[]{:S(2)}, u32[]{:S(2)}) %collective-permute-start.1) | collective-permute-done | bytes 557088 | tf_op jit(solution)/shard_map/ppermute | solution.py:533
  42.3 0.9 %shard_map.108 = (bf16[2,512,512]{2,1,0:T(8,128)(2,1)S(1)}, bf16[2,512,512]{2,1,0:T(8,128)(2,1)S(1)}, f32[2,1,512]{2,1,0:T(1,128)S(1)}, f32[2,512]{1,0:T(2,128)S...) custom-call(f32[20,128,128]{2,1,0:T(8,128)S(1)} %get-tuple-element.42.own, f32[128,128]{1,0:T(8,128)S(1)} %get-tuple-element.43.extra, ...), custom_call_target="tpu_custom_call" | custom-call | bytes 6227968 | tf_op jit(solution)/shard_map/pallas_call | solution.py:22
  43.2 0.7 collective-permute-start.7
  43.8 3.8 %shard_map.109 = (bf16[512,512]{1,0:T(8,128)(2,1)S(1)}, bf16[512,512]{1,0:T(8,128)(2,1)S(1)}, bf16[512,512]{1,0:T(8,128)(2,1)S(1)}, bf16[512,512]{1,0:T(8,128)(2,1)S(1)}, f32[8,512]{1,0:T(8,128)S(1)}) custom-call(f32[1,512]{1,0:T(1,128)S(1)} %get-tuple-element.53.after, bf16[2,512,512]{2,1,0:T(8,128)(2,1)S(1)} %get-tuple-element.54.omhi, ...), custom_call_target="tpu_custom_call" | custom-call | flops 3221225472 | bytes 4204544 | tf_op jit(solution)/shard_map/pallas_call | solution.py:22
  48.1 0.7 collective-permute-start.8
  48.8 1.1 %shard_map.111 = (bf16[512,512]{1,0:T(8,128)(2,1)S(1)}, bf16[512,512]{1,0:T(8,128)(2,1)S(1)}, f32[1,512]{1,0:T(1,128)S(1)}) custom-call(f32[1,512]{1,0:T(1,128)S(1)} %get-tuple-element.64.after, bf16[512,512]{1,0:T(8,128)(2,1)S(1)} %get-tuple-element.59.b1hi, bf16[512,512]{1,0:T(8,128)(2,1)S(1)} %get-tuple-element.60.b1lo, ...), custom_call_target="tpu_custom_call" | custom-call | bytes 2115584 | tf_op jit(solution)/shard_map/pallas_call | solution.py:22
  50.2 0.7 collective-permute-start.9
  51.1 0.7 collective-permute-start.10
  52.1 0.7 collective-permute-start.11
  53.0 0.7 collective-permute-start.12
  53.9 0.7 collective-permute-start.13
  54.7 1.2 %shard_map.119 = f32[32,8,128]{2,1,0:T(8,128)S(1)} custom-call(f32[1,512]{1,0:T(1,128)S(1)} %get-tuple-element.79.acc, f32[1,512]{1,0:T(1,128)S(1)} %collective-permute-done.13.got, bf16[512,512]{1,0:T(8,128)(2,1)S(1)} %get-tuple-element.59.b1hi, bf16[512,512]{1,0:T(8,128)(2,1)S(1)} %get-tuple-element.60.b1lo, bf16[512,512]{1,0:T(8,128)(2,1)S(1)} %get-tuple-element.61.b2hi, ...), custom_call_target="tpu_custom_call" | custom-call | bytes 11587584 | tf_op jit(solution)/shard_map/pallas_call | solution.py:22
  55.9 28.0 %all_to_all.11.parts = f32[32,8,128]{2,1,0:T(8,128)S(1)} all-to-all(f32[32,8,128]{2,1,0:T(8,128)S(1)} %shard_map.119), channel_id=1, replica_groups=mesh['z'=4,'y'=2,'obs'=4] {'z','y','obs'}, dimensions={0} | all-to-all | bytes 262144 | tf_op jit(solution)/shard_map/all_to_all | solution.py:595
  (29 shorter events, 3.3 us)
Async XLA Ops:
  2.8 21.4 %copy-start.2 = (f32[128,512]{1,0:T(8,128)S(1)}, f32[128,512]{1,0:T(8,128)}, u32[]{:S(2)}) copy-start(f32[128,512]{1,0:T(8,128)} %gain.1) | copy-start | bytes 786436
  24.2 11.0 %copy-start = (f32[512,512]{1,0:T(8,128)S(1)}, f32[512,512]{1,0:T(8,128)}, u32[]{:S(2)}) copy-start(f32[512,512]{1,0:T(8,128)} %trans.1) | copy-start | bytes 3145732
  24.2 11.0 %copy-start.1 = (f32[512,512]{1,0:T(8,128)S(1)}, f32[512,512]{1,0:T(8,128)}, u32[]{:S(2)}) copy-start(f32[512,512]{1,0:T(8,128)} %cov.1) | copy-start | bytes 3145732
  25.5 8.0 %collective-permute-start.5 = (f32[128,512]{1,0:T(8,128)S(1)}, f32[128,512]{1,0:T(8,128)S(1)}, u32[]{:S(2)}, u32[]{:S(2)}) collective-permute-start(f32[128,512]{1,0:T(8,128)S(1)} %get-tuple-element.50.m0), channel_id=1, source_target_pairs={{0,2},{1,3},{2,0},{3,1},{4,6},{5,7},{6,4},{7,5},{8,10},{9,11},{10,... | collective-permute-start | bytes 786440 | tf_op jit(solution)/shard_map/ppermute | solution.py:530
  26.1 10.8 %collective-permute-start.3 = (bf16[17,128,128]{2,1,0:T(8,128)(2,1)S(1)}, bf16[17,128,128]{2,1,0:T(8,128)(2,1)S(1)}, u32[]{:S(2)}, u32[]{:S(2)}) collective-permute-start(bf16[17,128,128]{2,1,0:T(8,128)(2,1)S(1)} %get-tuple-element.44), channel_id=1, source_target_pairs={{24,9},{1,17},{3,19},{26,11},{30,15},{7,23},{5,21},{28,13}} | collective-permute-start | bytes 1671176 | tf_op jit(solution)/shard_map/ppermute | solution.py:533
  26.8 10.2 %collective-permute-start.2 = (bf16[17,128,128]{2,1,0:T(8,128)(2,1)S(1)}, bf16[17,128,128]{2,1,0:T(8,128)(2,1)S(1)}, u32[]{:S(2)}, u32[]{:S(2)}) collective-permute-start(bf16[17,128,128]{2,1,0:T(8,128)(2,1)S(1)} %get-tuple-element.44), channel_id=1, source_target_pairs={{16,9},{25,17},{27,19},{18,11},{22,15},{31,23},{29,21},{20,13}} | collective-permute-start | bytes 1671176 | tf_op jit(solution)/shard_map/ppermute | solution.py:533
  27.5 14.8 %collective-permute-start.1 = (bf16[17,128,128]{2,1,0:T(8,128)(2,1)S(1)}, bf16[17,128,128]{2,1,0:T(8,128)(2,1)S(1)}, u32[]{:S(2)}, u32[]{:S(2)}) collective-permute-start(bf16[17,128,128]{2,1,0:T(8,128)(2,1)S(1)} %get-tuple-element.44), channel_id=1, source_target_pairs={{0,9},{9,17},{11,19},{2,11},{6,15},{15,23},{13,21},{4,13}} | collective-permute-start | bytes 1671176 | tf_op jit(solution)/shard_map/ppermute | solution.py:533
  31.5 10.8 %collective-permute-start = (bf16[17,128,128]{2,1,0:T(8,128)(2,1)S(1)}, bf16[17,128,128]{2,1,0:T(8,128)(2,1)S(1)}, u32[]{:S(2)}, u32[]{:S(2)}) collective-permute-start(bf16[17,128,128]{2,1,0:T(8,128)(2,1)S(1)} %get-tuple-element.44), channel_id=1, source_target_pairs={{8,9},{10,11},{14,15},{12,13}} | collective-permute-start | bytes 1671176 | tf_op jit(solution)/shard_map/ppermute | solution.py:539
  33.5 1.5 %collective-permute-start.4 = (f32[128,512]{1,0:T(8,128)S(1)}, f32[128,512]{1,0:T(8,128)S(1)}, u32[]{:S(2)}, u32[]{:S(2)}) collective-permute-start(f32[128,512]{1,0:T(8,128)S(1)} %get-tuple-element.50.m0), channel_id=1, source_target_pairs={{0,1},{1,0},{2,3},{3,2},{4,5},{5,4},{6,7},{7,6},{8,9},{9,8},{10,11... | collective-permute-start | bytes 786440 | tf_op jit(solution)/shard_map/ppermute | solution.py:530
  35.0 1.5 %collective-permute-start.6 = (f32[128,512]{1,0:T(8,128)S(1)}, f32[128,512]{1,0:T(8,128)S(1)}, u32[]{:S(2)}, u32[]{:S(2)}) collective-permute-start(f32[128,512]{1,0:T(8,128)S(1)} %collective-permute-done.5.m2), channel_id=1, source_target_pairs={{0,1},{1,0},{2,3},{3,2},{4,5},{5,4},{6,7},{7,6},{8,9},{9,8},{10,11... | collective-permute-start | bytes 786440 | tf_op jit(solution)/shard_map/ppermute | solution.py:530
  43.2 4.5 %collective-permute-start.7 = (f32[1,512]{1,0:T(1,128)S(1)}, f32[1,512]{1,0:T(1,128)S(1)}, u32[]{:S(2)}, u32[]{:S(2)}) collective-permute-start(f32[1,512]{1,0:T(1,128)S(1)} %get-tuple-element.53.after), channel_id=1, source_target_pairs={{9,17}} | collective-permute-start | bytes 6152 | tf_op jit(solution)/shard_map/ppermute | solution.py:559
  48.1 1.8 %collective-permute-start.8 = (f32[1,512]{1,0:T(1,128)S(1)}, f32[1,512]{1,0:T(1,128)S(1)}, u32[]{:S(2)}, u32[]{:S(2)}) collective-permute-start(f32[1,512]{1,0:T(1,128)S(1)} %get-tuple-element.64.after), channel_id=1, source_target_pairs={{17,19}} | collective-permute-start | bytes 6152 | tf_op jit(solution)/shard_map/ppermute | solution.py:559
  50.2 0.7 collective-permute-start.9
  51.1 0.8 collective-permute-start.10
  52.1 0.7 collective-permute-start.11
  53.0 0.7 collective-permute-start.12
  53.9 0.7 collective-permute-start.13

commit v10 on v9

--- a/solution.py
+++ b/solution.py
@@ -15,7 +15,7 @@
 HBM = pl.BlockSpec(memory_space=pltpu.HBM)
 
 
-def run(body, out, ins, scratch=(), limit=16, flops=0, outs=VMEM):
+def run(body, out, ins, scratch=(), limit=16, flops=0, outs=VMEM, same=None):
     specs = [x[1] if isinstance(x, tuple) else VMEM for x in ins]
     arrays = [x[0] if isinstance(x, tuple) else x for x in ins]
     moved = sum(a.size * a.dtype.itemsize for a in arrays)
@@ -25,6 +25,7 @@
         in_specs=specs,
         out_specs=[outs] * len(out),
         scratch_shapes=list(scratch),
+        input_output_aliases=same or {},
         compiler_params=pltpu.CompilerParams(vmem_limit_bytes=limit * 1024 * 1024),
         cost_estimate=pl.CostEstimate(flops=flops, bytes_accessed=moved, transcendentals=0),
     )(*arrays)
@@ -225,10 +226,15 @@
     chi[...], clo[...] = split(cov[...])
 
 
-def gain_kernel(m0, m1, m2, m3, mthi, mtlo):
+def stack_kernel(one, two, out):
+    out[0] = one[...]
+    out[1] = two[...]
+
+
+def gain_kernel(held, got, mthi, mtlo):
     ids = here()
-    rows = m0.shape[0]
-    for step, part in enumerate((m0, m1, m2, m3)):
+    rows = held.shape[1]
+    for step, part in enumerate((held.at[0], got.at[0], held.at[1], got.at[1])):
         holder = ids[2] ^ step
         at = pl.ds(pl.multiple_of(holder * rows, rows), rows)
         hi, lo = split(part[...].T)
@@ -352,21 +358,31 @@
         y[...] = jnp.zeros(y.shape, F32)
 
 
-def second_kernel(acc, got, b1hi, b1lo, b2hi, b2lo, off, total, y):
-    state = acc[...] + got[...]
-    total[...] = state
-    state = mv(state, b1hi[...], b1lo[...]) + off[0:1, :]
-    y[...] = mv(state, b2hi[...], b2lo[...]) + off[1:2, :]
-
-
-def maps_kernel(after, omhi, omlo, info, chi, clo, pt, damping, b1hi, b1lo, b2hi, b2lo, off):
+def second_kernel(acc, got, mine, pthi, ptlo, omhi, omlo, info, chi, clo, total, y):
+    total[...] = acc[...] + got[...]
+    y[...] = jnp.zeros(y.shape, F32)
+
+    @pl.when(here()[1] == 1)
+    def _():
+        state = acc[...] + got[...]
+        for day in range(2):
+            state = one_day(day, state, mine, pthi, ptlo, omhi, omlo, info, chi, clo)
+        y[...] = state
+
+
+def maps_kernel(after, omhi, omlo, info, chi, clo, pt, damping, *rest):
+    late = len(rest) == 10
+    b1hi, b1lo, b2hi, b2lo, off = rest[-5:]
     parts = ((b1hi, b1lo), (b2hi, b2lo))
-    for day in range(2):
-        moved = pt[...] * damping[day : day + 1, :]
-        taken = mm(moved, omhi[day], omlo[day])
-        step = moved - mm(taken, chi[...], clo[...])
-        parts[day][0][...], parts[day][1][...] = split(step)
-        off[day : day + 1, :] = mv(info[day], chi[...], clo[...])
+
+    @pl.when((here()[1] == 1) == late)
+    def _():
+        for day in range(2):
+            moved = pt[...] * damping[day : day + 1, :]
+            taken = mm(moved, omhi[day], omlo[day])
+            step = moved - mm(taken, chi[...], clo[...])
+            parts[day][0][...], parts[day][1][...] = split(step)
+            off[day : day + 1, :] = mv(info[day], chi[...], clo[...])
 
 
 def both_kernel(after, b1hi, b1lo, b2hi, b2lo, off, bchi, bclo, offset):
@@ -384,40 +400,51 @@
     y[...] = mv(state, bchi[...], bclo[...]) + offset[...]
 
 
-def pairs_kernel(after, table, mthi, mtlo, khi, klo):
-    ids = here()
-    spans = table.shape[0] // 2
-
-    @pl.when(ids[1] == spans - 1)
+def whole_of(hi, lo):
+    return hi[...].astype(F32) + lo[...].astype(F32)
+
+
+def pairs_kernel(
+    after, b1hi, b1lo, bchi, bclo, off, offset, table, pthi, ptlo, mthi, mtlo,
+    khi, klo, ohi, olo, ehi, elo, shift, held,
+):
+    span = here()[1]
+    total = table.shape[0]
+    spans = total // 2
+
+    @pl.when(span >= spans - 2)
     def _():
-        whole = mthi[...].astype(F32) + mtlo[...].astype(F32)
-
         @pl.loop(0, khi.shape[0])
         def _(k):
-            scaled = whole * table[pl.ds(2 * (spans - 2 - k) + 1, 1), :]
+            scaled = whole_of(mthi, mtlo) * table[pl.ds(2 * (spans - 2 - k) + 1, 1), :]
             khi[k], klo[k] = split(mm(scaled, mthi[...], mtlo[...]))
 
+        within = table[pl.ds(2 * span + 1, 1), :]
+        after_d = table[pl.ds(jnp.minimum(2 * span + 2, total - 1), 1), :] * jnp.where(span == spans - 1, 0.0, 1.0)
+        one, two = off[0:1, :], offset[...]
+        odd = two - mv(mv(two, pthi[...], ptlo[...]) * (after_d * after_d), mthi[...], mtlo[...])
+        even = one + mv(
+            odd * within - mv(one, pthi[...], ptlo[...]) * (within * within), mthi[...], mtlo[...]
+        )
+        shift[0:1, :] = odd
+        shift[1:2, :] = even
+        moved = mm(whole_of(bchi, bclo), pthi[...], ptlo[...]) * (after_d * after_d)
+        held[...] = whole_of(bchi, bclo) - mm(moved, mthi[...], mtlo[...])
+        ohi[...], olo[...] = split(held[...])
+        moved = mm(whole_of(b1hi, b1lo), pthi[...], ptlo[...]) * (within * within)
+        moved = held[...] * within - moved
+        ehi[...], elo[...] = split(whole_of(b1hi, b1lo) + mm(moved, mthi[...], mtlo[...]))
+
 
 def last_kernel(
-    acc, got, b1hi, b1lo, b2hi, b2lo, off, table, pthi, ptlo, mthi, mtlo, khi, klo, out, shares
+    acc, got, b1hi, b1lo, b2hi, b2lo, bchi, bclo, off, offset, table, pthi, ptlo, mthi, mtlo,
+    khi, klo, ohi, olo, ehi, elo, shift, out, shares, means,
 ):
-    ids = here()
+    span = here()[1]
     total, width = shares.shape
     spans = total // 2
     chunks = width // LANES
-    span = ids[1]
-    state = acc[...] + got[...]
-    one = mv(state, b1hi[...], b1lo[...]) + off[0:1, :]
-    two = mv(one, b2hi[...], b2lo[...]) + off[1:2, :]
-    within = table[pl.ds(2 * span + 1, 1), :]
-    after = table[pl.ds(jnp.minimum(2 * span + 2, total - 1), 1), :] * jnp.where(span == spans - 1, 0.0, 1.0)
-    damped = jnp.concatenate([within, after], 0)
-    both = jnp.concatenate([one, two], 0)
-    const = both - few(few(both, pthi[...], ptlo[...]) * damped * damped, mthi[...], mtlo[...])
-    even = const[0:1] + mv(const[1:2] * within, mthi[...], mtlo[...])
     shares[...] = jnp.zeros(shares.shape, F32)
-    shares[pl.ds(2 * span + 1, 1), :] = const[1:2]
-    shares[pl.ds(2 * span, 1), :] = even
 
     def step(k, v):
         t = 2 * span - 1 - k
@@ -425,31 +452,50 @@
         shares[pl.ds(t, 1), :] = v
         return v
 
-    @pl.when(span < spans - 1)
+    @pl.when(span < spans - 2)
     def _():
+        state = acc[...] + got[...]
+        one = mv(state, b1hi[...], b1lo[...]) + off[0:1, :]
+        two = mv(one, b2hi[...], b2lo[...]) + off[1:2, :]
+        both = jnp.concatenate([one, two], 0)
+        within = table[pl.ds(2 * span + 1, 1), :]
+        damped = jnp.concatenate([within, table[pl.ds(2 * span + 2, 1), :]], 0)
+        const = both - few(few(both, pthi[...], ptlo[...]) * damped * damped, mthi[...], mtlo[...])
+        even = const[0:1] + mv(const[1:2] * within, mthi[...], mtlo[...])
+        shares[pl.ds(2 * span + 1, 1), :] = const[1:2]
+        shares[pl.ds(2 * span, 1), :] = even
+        means[0:2, :] = both
         lax.fori_loop(0, 2 * span, step, even)
 
-    @pl.when(span == spans - 1)
+    @pl.when(span >= spans - 2)
     def _():
+        state = acc[...] + got[...]
+        even = mv(state, ehi[...], elo[...]) + shift[1:2, :]
         v, damped_rows = even, []
         for k in range(khi.shape[0]):
             t = 2 * (spans - 1 - k)
-            v = v * table[t : t + 1, :]
-            damped_rows.append(v)
-            v = mv(v, khi[k], klo[k])
+            damped = v * table[t : t + 1, :]
+            damped_rows.append(damped)
+            reached = mv(damped, khi[k], klo[k])
+            v = reached if k else jnp.where(span == spans - 1, reached, v)
             shares[t - 2 : t - 1, :] = v
+        odd = mv(state, ohi[...], olo[...]) + shift[0:1, :]
+        means[0:1, :] = mv(state, b1hi[...], b1lo[...]) + off[0:1, :]
+        means[1:2, :] = mv(state, bchi[...], bclo[...]) + offset[...]
         batch = jnp.concatenate(damped_rows + [jnp.zeros((1, width), F32)] * (-len(damped_rows) % 8), 0)
-        odd = mm(batch, mthi[...], mtlo[...])
+        batch = mm(batch, mthi[...], mtlo[...])
         for k in range(khi.shape[0]):
             t = 2 * (spans - 1 - k)
-            shares[t - 1 : t, :] = odd[k : k + 1]
-        lax.fori_loop(2 * khi.shape[0], 2 * span, step, v)
+            shares[t - 1 : t, :] = batch[k : k + 1]
+        shares[pl.ds(2 * span + 1, 1), :] = odd
+        shares[pl.ds(2 * span, 1), :] = even
+        lax.fori_loop(2 * khi.shape[0] - 2 * (spans - 1 - span), 2 * span, step, v)
 
     for c in range(spans):
         for q in range(chunks):
             out[c * chunks + q, 0:2, :] = shares[2 * c : 2 * c + 2, q * LANES : (q + 1) * LANES]
     for q in range(chunks):
-        out[span * chunks + q, 2:4, :] = both[:, q * LANES : (q + 1) * LANES]
+        out[span * chunks + q, 2:4, :] = means[0:2, q * LANES : (q + 1) * LANES]
 
 
 def add_kernel(parts, filt, smooth):
@@ -534,15 +580,12 @@
             pay, everyone, [((owner_plane(p) + s) % planes * spans + place(p), owner(p)) for p in range(spans)]
         )
 
-    across = swap(gain, 2)
-    beside = swap(gain, 1)
     fourth = lax.ppermute(
         pay, everyone, [(spans + place(p), owner(p)) for p in range(spans) if place(p) % 2 == 0]
     )
     third, first, second = plane_sum(3), plane_sum(1), plane_sum(2)
-    mthi, mtlo = run(
-        gain_kernel, [(full, BF16)] * 2, [gain, beside, across, swap(across, 1)]
-    )
+    (gains,) = run(stack_kernel, [((2,) + gain.shape, F32)], [gain, swap(gain, 2)])
+    mthi, mtlo = run(gain_kernel, [(full, BF16)] * 2, [gains, swap(gains, 1)])
     pt, pthi, ptlo, chi, clo = run(
         prep_kernel, [(full, F32)] + [(full, BF16)] * 4, [propagator_matrix, analysis_cov]
     )
@@ -558,13 +601,20 @@
     for k in range(spans - 1):
         received = lax.ppermute(y, everyone, [(owner(k), owner(k + 1))])
         if k == 0:
+            maps = [(full, BF16)] * 4 + [((8, width), F32)]
+            given = [omhi, omlo, info, chi, clo, pt, mine]
+            flops = 24 * width**3
+            days_maps = run(maps_kernel, maps, [(y, ANY), *given], flops=flops)
+            acc, y = run(
+                second_kernel, [row, row], [acc, received, mine, pthi, ptlo, omhi, omlo, info, chi, clo]
+            )
             b1hi, b1lo, b2hi, b2lo, off = run(
                 maps_kernel,
-                [(full, BF16)] * 4 + [((8, width), F32)],
-                [(y, ANY), omhi, omlo, info, chi, clo, pt, mine],
-                flops=24 * width**3,
+                maps,
+                [(y, ANY), *given, *days_maps],
+                flops=flops,
+                same={8 + n: n for n in range(5)},
             )
-            acc, y = run(second_kernel, [row, row], [acc, received, b1hi, b1lo, b2hi, b2lo, off])
             bchi, bclo, offset = run(
                 both_kernel, [(full, BF16)] * 2 + [row], [(y, ANY), b1hi, b1lo, b2hi, b2lo, off]
             )
@@ -578,19 +628,24 @@
         elif k < spans - 2:
             acc, y = run(hop_kernel, [row, row], [(side, ANY), acc, received, bchi, bclo, offset])
             if k == 2:
-                khi, klo = run(
+                ahead = run(
                     pairs_kernel,
-                    [((min(spans - 1, 7),) + full, BF16)] * 2,
-                    [(y, ANY), table, mthi, mtlo],
+                    [((min(spans - 1, 7),) + full, BF16)] * 2 + [(full, BF16)] * 4 + [((8, width), F32)],
+                    [
+                        (y, ANY), b1hi, b1lo, bchi, bclo, off, offset, table, pthi, ptlo, mthi, mtlo
+                    ],
+                    [pltpu.VMEM(full, F32)],
                 )
-                side = khi
+                side = ahead[0]
+
     (answer,) = run(
         last_kernel,
         [((spans * peers, 8, LANES), F32)],
         [
-            acc, received, b1hi, b1lo, b2hi, b2lo, off, table, pthi, ptlo, mthi, mtlo, khi, klo
+            acc, received, b1hi, b1lo, b2hi, b2lo, bchi, bclo, off, offset, table, pthi, ptlo, mthi, mtlo,
+            *ahead,
         ],
-        [pltpu.VMEM((spans * days, width), F32)],
+        [pltpu.VMEM((spans * days, width), F32), pltpu.VMEM((8, width), F32)],
     )
     parts = lax.all_to_all(answer, everyone, split_axis=0, concat_axis=0, tiled=True)
     out = ((days, LANES), F32)

time: 84.8 us -> 85.6 us (level)
  blocking collectives: 49.4 us -> 50.4 us
    ppermute x3, waiting for transfers between devices: 5.33 us -> 6.39 us  [plane_sum(): lax.ppermute(pay, everyone, [((owner_plane(p) + s) % planes * spans + pla...]
    ppermute x3 -> x2, waiting for transfers between devices: 3.64 us -> 2.59 us  [swap(): return lax.ppermute(x, 'obs', [(i, i ^ bit) for i in range(peers)])]
    all_to_all x1, blocking collectives: 28 us -> 29.1 us  [local(): lax.all_to_all(answer, everyone, split_axis=0, concat_axis=0, tiled=True)]
    pallas_call x17 -> x19, Pallas kernels: 13.5 us -> 13.1 us  [run(): pl.pallas_call(body, out_shape=[jax.ShapeDtypeStruct(s, d) for s, d in ou...]
  transfers between devices with their start and end apart: 14 -> 13, of which waited for: 4 -> 3; matrix products, arithmetic and copies ran while one was open for 0% -> 0% of each run, Pallas kernels for 7% -> 7%
where the time goes in v10:
time: 85.6 us; the launch traced here: 85.2 us
  blocking collectives  50.4 us (59%)
  Pallas kernels  13.1 us (15%)
  starting transfers between devices  11.8 us (14%)
  waiting for transfers between devices  9.01 us (11%)
  between operations  0.93 us (1%)
    all_to_all x1, blocking collectives, local(): lax.all_to_all(answer, everyone, split_axis=0, concat_axis=0, tiled=True)  29.1 us
    all_to_all x1, blocking collectives, local(): lax.all_to_all(sent, ('y', 'obs'), split_axis=0, concat_axis=0, tiled=True)  21.4 us
    pallas_call x19, Pallas kernels, run(): pl.pallas_call(body, out_shape=[jax.ShapeDtypeStruct(s, d) for s, d in ou...  13.1 us
    ppermute x3, waiting for transfers between devices, plane_sum(): lax.ppermute(pay, everyone, [((owner_plane(p) + s) % planes * spans + pla...  6.39 us
    ppermute x3, starting transfers between devices, plane_sum(): lax.ppermute(pay, everyone, [((owner_plane(p) + s) % planes * spans + pla...  5.35 us
    ppermute x7, starting transfers between devices, local(): received = lax.ppermute(y, everyone, [(owner(k), owner(k + 1))])  5.04 us
    ppermute x2, waiting for transfers between devices, swap(): return lax.ppermute(x, 'obs', [(i, i ^ bit) for i in range(peers)])  2.59 us
  transfers between devices with their start and end apart: 13, of which 3 were waited for; matrix products, arithmetic and copies ran while one was open for 0% of the time, Pallas kernels for 7%

profile of v10, /device:TPU:0, one launch (start us, length us, event | category | flops | bytes accessed | tf_op | source)
XLA Modules:
  0.0 85.2 jit_solution(8530354432050491376)
XLA Ops:
  0.6 2.2 %shard_map.104 = bf16[8,136,512]{2,1,0:T(8,128)(2,1)} custom-call(s32[8]{0:T(128)} %day.1, s32[8]{0:T(128)} %count.1, bf16[1024,512]{1,0:T(8,128)(2,1)} %rows.1, bf16[8,128]{1,0:T(8,128)(2,1)} %bitcast.2, f32[1,128]{1,0:T(1,128)} %bitcast.3, f32[2,512]{1,0:T(2,128)} %damping.1), custom_call_target="tpu_custom_call" | custom-call | bytes 1055296 | tf_op jit(solution)/shard_map/pallas_call | solution.py:22
  2.9 21.4 %all_to_all.10.got = bf16[8,136,512]{2,1,0:T(8,128)(2,1)S(1)} all-to-all(bf16[8,136,512]{2,1,0:T(8,128)(2,1)} %shard_map.104), channel_id=1, replica_groups=mesh['z'=4,'y'=2,'obs'=4] {'y','obs'}, dimensions={0} | all-to-all | bytes 2228224 | tf_op jit(solution)/shard_map/all_to_all | solution.py:560
  24.2 1.2 %shard_map.105 = (f32[20,128,128]{2,1,0:T(8,128)S(1)}, f32[128,128]{1,0:T(8,128)S(1)}, bf16[17,128,128]{2,1,0:T(8,128)(2,1)S(1)}, f32[1,512]{1,0:T(1,128)S(1)}, f32[128,512]{1,0:T(8,128)S(1)}) custom-call(bf16[8,136,512]{2,1,0:T(8,128)(2,1)S(1)} %all_to_all.10.got, f32[128,512]{1,0:T(8,128)S(1)} %copy-done.2), custom_call_target="tpu_custom_call" | custom-call | flops 1073741824 | bytes 1376256 | tf_op jit(solution)/shard_map/pallas_call | solution.py:22
  25.4 0.6 collective-permute-start.4
  26.1 0.7 collective-permute-start.3
  26.8 0.7 collective-permute-start.2
  27.5 4.0 %collective-permute-start.1 = (bf16[17,128,128]{2,1,0:T(8,128)(2,1)S(1)}, bf16[17,128,128]{2,1,0:T(8,128)(2,1)S(1)}, u32[]{:S(2)}, u32[]{:S(2)}) collective-permute-start(bf16[17,128,128]{2,1,0:T(8,128)(2,1)S(1)} %get-tuple-element.54), channel_id=1, source_target_pairs={{0,9},{9,17},{11,19},{2,11},{6,15},{15,23},{13,21},{4,13}} | collective-permute-start | bytes 1671176 | tf_op jit(solution)/shard_map/ppermute | solution.py:579
  31.4 0.7 collective-permute-start
  32.1 1.3 %collective-permute-done.4.two = f32[128,512]{1,0:T(8,128)S(1)} collective-permute-done((f32[128,512]{1,0:T(8,128)S(1)}, f32[128,512]{1,0:T(8,128)S(1)}, u32[]{:S(2)}, u32[]{:S(2)}) %collective-permute-start.4) | collective-permute-done | bytes 262176 | tf_op jit(solution)/shard_map/ppermute | solution.py:576
  33.6 0.6 shard_map.106
  34.2 1.3 %collective-permute-done.5.got = f32[2,128,512]{2,1,0:T(8,128)S(1)} collective-permute-done((f32[2,128,512]{2,1,0:T(8,128)S(1)}, f32[2,128,512]{2,1,0:T(8,128)S(1)}, u32[]{:S(2)}, u32[]{:S(2)}) %collective-permute-start.5) | collective-permute-done | bytes 524320 | tf_op jit(solution)/shard_map/ppermute | solution.py:576
  35.9 6.4 %collective-permute-done.1.g3 = bf16[17,128,128]{2,1,0:T(8,128)(2,1)S(1)} collective-permute-done((bf16[17,128,128]{2,1,0:T(8,128)(2,1)S(1)}, bf16[17,128,128]{2,1,0:T(8,128)(2,1)S(1)}, u32[]{:S(2)}, u32[]{:S(2)}) %collective-permute-start.1) | collective-permute-done | bytes 557088 | tf_op jit(solution)/shard_map/ppermute | solution.py:579
  42.2 0.9 %shard_map.109 = (bf16[2,512,512]{2,1,0:T(8,128)(2,1)S(1)}, bf16[2,512,512]{2,1,0:T(8,128)(2,1)S(1)}, f32[2,1,512]{2,1,0:T(1,128)S(1)}, f32[2,512]{1,0:T(2,128)S...) custom-call(f32[20,128,128]{2,1,0:T(8,128)S(1)} %get-tuple-element.52.own, f32[128,128]{1,0:T(8,128)S(1)} %get-tuple-element.53.extra, ...), custom_call_target="tpu_custom_call" | custom-call | bytes 6227968 | tf_op jit(solution)/shard_map/pallas_call | solution.py:22
  43.1 0.7 collective-permute-start.6
  43.8 3.8 %shard_map.111 = (bf16[512,512]{1,0:T(8,128)(2,1)S(1)}, bf16[512,512]{1,0:T(8,128)(2,1)S(1)}, bf16[512,512]{1,0:T(8,128)(2,1)S(1)}, bf16[512,512]{1,0:T(8,128)(2,1)S(1)}, f32[8,512]{1,0:T(8,128)S(1)}) custom-call(f32[1,512]{1,0:T(1,128)S(1)} %get-tuple-element.63.after, bf16[2,512,512]{2,1,0:T(8,128)(2,1)S(1)} %get-tuple-element.65.omhi, ...), custom_call_target="tpu_custom_call" | custom-call | flops 3221225472 | bytes 4204544 | tf_op jit(solution)/shard_map/pallas_call | solution.py:22
  47.6 0.7 collective-permute-start.7
  48.3 1.1 %shard_map.113 = (bf16[512,512]{1,0:T(8,128)(2,1)S(1)}, bf16[512,512]{1,0:T(8,128)(2,1)S(1)}, f32[1,512]{1,0:T(1,128)S(1)}) custom-call(f32[1,512]{1,0:T(1,128)S(1)} %get-tuple-element.68.after, bf16[512,512]{1,0:T(8,128)(2,1)S(1)} %get-tuple-element.75.b1hi, bf16[512,512]{1,0:T(8,128)(2,1)S(1)} %get-tuple-element.76.b1lo, ...), custom_call_target="tpu_custom_call" | custom-call | bytes 2115584 | tf_op jit(solution)/shard_map/pallas_call | solution.py:22
  49.7 0.9 %collective-permute-start.8 = (f32[1,512]{1,0:T(1,128)S(1)}, f32[1,512]{1,0:T(1,128)S(1)}, u32[]{:S(2)}, u32[]{:S(2)}) collective-permute-start(f32[1,512]{1,0:T(1,128)S(1)} %get-tuple-element.85), channel_id=1, source_target_pairs={{19,11}} | collective-permute-start | bytes 6152 | tf_op jit(solution)/shard_map/ppermute | solution.py:602
  50.8 0.7 collective-permute-start.9
  51.8 0.7 collective-permute-start.10
  52.7 0.7 collective-permute-start.11
  53.7 0.7 collective-permute-start.12
  54.4 1.2 %shard_map.121 = f32[32,8,128]{2,1,0:T(8,128)S(1)} custom-call(f32[1,512]{1,0:T(1,128)S(1)} %get-tuple-element.94.acc, f32[1,512]{1,0:T(1,128)S(1)} %collective-permute-done.12.got, bf16[512,512]{1,0:T(8,128)(2,1)S(1)} %get-tuple-element.75.b1hi, bf16[512,512]{1,0:T(8,128)(2,1)S(1)} %get-tuple-element.76.b1lo, bf16[512,512]{1,0:T(8,128)(2,1)S(1)} %get-tuple-element.77.b2hi, ...), custom_call_target="tpu_custom_call" | custom-call | bytes 14751744 | tf_op jit(solution)/shard_map/pallas_call | solution.py:22
  55.6 29.1 %all_to_all.11.parts = f32[32,8,128]{2,1,0:T(8,128)S(1)} all-to-all(f32[32,8,128]{2,1,0:T(8,128)S(1)} %shard_map.121), channel_id=1, replica_groups=mesh['z'=4,'y'=2,'obs'=4] {'z','y','obs'}, dimensions={0} | all-to-all | bytes 262144 | tf_op jit(solution)/shard_map/all_to_all | solution.py:650
  (29 shorter events, 2.2 us)
Async XLA Ops:
  2.8 21.4 %copy-start.2 = (f32[128,512]{1,0:T(8,128)S(1)}, f32[128,512]{1,0:T(8,128)}, u32[]{:S(2)}) copy-start(f32[128,512]{1,0:T(8,128)} %gain.1) | copy-start | bytes 786436
  24.2 9.4 %copy-start.1 = (f32[512,512]{1,0:T(8,128)S(1)}, f32[512,512]{1,0:T(8,128)}, u32[]{:S(2)}) copy-start(f32[512,512]{1,0:T(8,128)} %cov.1) | copy-start | bytes 3145732
  25.4 8.2 %copy-start = (f32[512,512]{1,0:T(8,128)S(1)}, f32[512,512]{1,0:T(8,128)}, u32[]{:S(2)}) copy-start(f32[512,512]{1,0:T(8,128)} %trans.1) | copy-start | bytes 3145732
  25.4 8.0 %collective-permute-start.4 = (f32[128,512]{1,0:T(8,128)S(1)}, f32[128,512]{1,0:T(8,128)S(1)}, u32[]{:S(2)}, u32[]{:S(2)}) collective-permute-start(f32[128,512]{1,0:T(8,128)S(1)} %get-tuple-element.60.one), channel_id=1, source_target_pairs={{0,2},{1,3},{2,0},{3,1},{4,6},{5,7},{6,4},{7,5},{8,10},{9,11},{10,... | collective-permute-start | bytes 786440 | tf_op jit(solution)/shard_map/ppermute | solution.py:576
  26.1 9.8 %collective-permute-start.3 = (bf16[17,128,128]{2,1,0:T(8,128)(2,1)S(1)}, bf16[17,128,128]{2,1,0:T(8,128)(2,1)S(1)}, u32[]{:S(2)}, u32[]{:S(2)}) collective-permute-start(bf16[17,128,128]{2,1,0:T(8,128)(2,1)S(1)} %get-tuple-element.54), channel_id=1, source_target_pairs={{24,9},{1,17},{3,19},{26,11},{30,15},{7,23},{5,21},{28,13}} | collective-permute-start | bytes 1671176 | tf_op jit(solution)/shard_map/ppermute | solution.py:579
  26.8 9.1 %collective-permute-start.2 = (bf16[17,128,128]{2,1,0:T(8,128)(2,1)S(1)}, bf16[17,128,128]{2,1,0:T(8,128)(2,1)S(1)}, u32[]{:S(2)}, u32[]{:S(2)}) collective-permute-start(bf16[17,128,128]{2,1,0:T(8,128)(2,1)S(1)} %get-tuple-element.54), channel_id=1, source_target_pairs={{16,9},{25,17},{27,19},{18,11},{22,15},{31,23},{29,21},{20,13}} | collective-permute-start | bytes 1671176 | tf_op jit(solution)/shard_map/ppermute | solution.py:579
  27.5 14.8 %collective-permute-start.1 = (bf16[17,128,128]{2,1,0:T(8,128)(2,1)S(1)}, bf16[17,128,128]{2,1,0:T(8,128)(2,1)S(1)}, u32[]{:S(2)}, u32[]{:S(2)}) collective-permute-start(bf16[17,128,128]{2,1,0:T(8,128)(2,1)S(1)} %get-tuple-element.54), channel_id=1, source_target_pairs={{0,9},{9,17},{11,19},{2,11},{6,15},{15,23},{13,21},{4,13}} | collective-permute-start | bytes 1671176 | tf_op jit(solution)/shard_map/ppermute | solution.py:579
  31.4 10.8 %collective-permute-start = (bf16[17,128,128]{2,1,0:T(8,128)(2,1)S(1)}, bf16[17,128,128]{2,1,0:T(8,128)(2,1)S(1)}, u32[]{:S(2)}, u32[]{:S(2)}) collective-permute-start(bf16[17,128,128]{2,1,0:T(8,128)(2,1)S(1)} %get-tuple-element.54), channel_id=1, source_target_pairs={{8,9},{10,11},{14,15},{12,13}} | collective-permute-start | bytes 1671176 | tf_op jit(solution)/shard_map/ppermute | solution.py:583
  33.5 2.0 %collective-permute-start.5 = (f32[2,128,512]{2,1,0:T(8,128)S(1)}, f32[2,128,512]{2,1,0:T(8,128)S(1)}, u32[]{:S(2)}, u32[]{:S(2)}) collective-permute-start(f32[2,128,512]{2,1,0:T(8,128)S(1)} %shard_map.107.held), channel_id=1, source_target_pairs={{0,1},{1,0},{2,3},{3,2},{4,5},{5,4},{6,7},{7,6},{8,9},{9,8},{10,11... | collective-permute-start | bytes 1572872 | tf_op jit(solution)/shard_map/ppermute | solution.py:576
  43.1 4.5 %collective-permute-start.6 = (f32[1,512]{1,0:T(1,128)S(1)}, f32[1,512]{1,0:T(1,128)S(1)}, u32[]{:S(2)}, u32[]{:S(2)}) collective-permute-start(f32[1,512]{1,0:T(1,128)S(1)} %get-tuple-element.63.after), channel_id=1, source_target_pairs={{9,17}} | collective-permute-start | bytes 6152 | tf_op jit(solution)/shard_map/ppermute | solution.py:602
  47.6 1.9 %collective-permute-start.7 = (f32[1,512]{1,0:T(1,128)S(1)}, f32[1,512]{1,0:T(1,128)S(1)}, u32[]{:S(2)}, u32[]{:S(2)}) collective-permute-start(f32[1,512]{1,0:T(1,128)S(1)} %get-tuple-element.68.after), channel_id=1, source_target_pairs={{17,19}} | collective-permute-start | bytes 6152 | tf_op jit(solution)/shard_map/ppermute | solution.py:602
  49.7 0.9 %collective-permute-start.8 = (f32[1,512]{1,0:T(1,128)S(1)}, f32[1,512]{1,0:T(1,128)S(1)}, u32[]{:S(2)}, u32[]{:S(2)}) collective-permute-start(f32[1,512]{1,0:T(1,128)S(1)} %get-tuple-element.85), channel_id=1, source_target_pairs={{19,11}} | collective-permute-start | bytes 6152 | tf_op jit(solution)/shard_map/ppermute | solution.py:602
  50.8 0.8 collective-permute-start.9
  51.8 0.7 collective-permute-start.10
  52.7 0.7 collective-permute-start.11
  53.7 0.7 collective-permute-start.12

commit v11 on v10

--- a/solution.py
+++ b/solution.py
@@ -414,7 +414,7 @@
 
     @pl.when(span >= spans - 2)
     def _():
-        @pl.loop(0, khi.shape[0])
+        @pl.loop(spans - 1 - span, khi.shape[0])
         def _(k):
             scaled = whole_of(mthi, mtlo) * table[pl.ds(2 * (spans - 2 - k) + 1, 1), :]
             khi[k], klo[k] = split(mm(scaled, mthi[...], mtlo[...]))
@@ -624,20 +624,15 @@
                 [(offset, ANY), extra, first, second, third],
                 [smalls],
             )
-            side = table
+            ahead = run(
+                pairs_kernel,
+                [((min(spans - 1, 7),) + full, BF16)] * 2 + [(full, BF16)] * 4 + [((8, width), F32)],
+                [(y, ANY), b1hi, b1lo, bchi, bclo, off, offset, table, pthi, ptlo, mthi, mtlo],
+                [pltpu.VMEM(full, F32)],
+            )
+            side = ahead[0]
         elif k < spans - 2:
             acc, y = run(hop_kernel, [row, row], [(side, ANY), acc, received, bchi, bclo, offset])
-            if k == 2:
-                ahead = run(
-                    pairs_kernel,
-                    [((min(spans - 1, 7),) + full, BF16)] * 2 + [(full, BF16)] * 4 + [((8, width), F32)],
-                    [
-                        (y, ANY), b1hi, b1lo, bchi, bclo, off, offset, table, pthi, ptlo, mthi, mtlo
-                    ],
-                    [pltpu.VMEM(full, F32)],
-                )
-                side = ahead[0]
-
     (answer,) = run(
         last_kernel,
         [((spans * peers, 8, LANES), F32)],

time: 85.6 us -> 84.8 us (level)
  no operation moved by 1% of the time
where the time goes in v11:
time: 84.8 us; the launch traced here: 84.5 us
  blocking collectives  49.7 us (59%)
  Pallas kernels  13.2 us (16%)
  starting transfers between devices  11.6 us (14%)
  waiting for transfers between devices  9.01 us (11%)
  between operations  0.93 us (1%)
    all_to_all x1, blocking collectives, local(): lax.all_to_all(answer, everyone, split_axis=0, concat_axis=0, tiled=True)  28.3 us
    all_to_all x1, blocking collectives, local(): lax.all_to_all(sent, ('y', 'obs'), split_axis=0, concat_axis=0, tiled=True)  21.4 us
    pallas_call x19, Pallas kernels, run(): pl.pallas_call(body, out_shape=[jax.ShapeDtypeStruct(s, d) for s, d in ou...  13.2 us
    ppermute x3, waiting for transfers between devices, plane_sum(): lax.ppermute(pay, everyone, [((owner_plane(p) + s) % planes * spans + pla...  6.39 us
    ppermute x3, starting transfers between devices, plane_sum(): lax.ppermute(pay, everyone, [((owner_plane(p) + s) % planes * spans + pla...  5.35 us
    ppermute x7, starting transfers between devices, local(): received = lax.ppermute(y, everyone, [(owner(k), owner(k + 1))])  4.86 us
    ppermute x2, waiting for transfers between devices, swap(): return lax.ppermute(x, 'obs', [(i, i ^ bit) for i in range(peers)])  2.59 us
  transfers between devices with their start and end apart: 13, of which 3 were waited for; matrix products, arithmetic and copies ran while one was open for 0% of the time, Pallas kernels for 7%

profile of v11, /device:TPU:0, one launch (start us, length us, event | category | flops | bytes accessed | tf_op | source)
XLA Modules:
  0.0 84.5 jit_solution(13066906705572350826)
XLA Ops:
  0.6 2.2 %shard_map.104 = bf16[8,136,512]{2,1,0:T(8,128)(2,1)} custom-call(s32[8]{0:T(128)} %day.1, s32[8]{0:T(128)} %count.1, bf16[1024,512]{1,0:T(8,128)(2,1)} %rows.1, bf16[8,128]{1,0:T(8,128)(2,1)} %bitcast.2, f32[1,128]{1,0:T(1,128)} %bitcast.3, f32[2,512]{1,0:T(2,128)} %damping.1), custom_call_target="tpu_custom_call" | custom-call | bytes 1055296 | tf_op jit(solution)/shard_map/pallas_call | solution.py:22
  2.9 21.4 %all_to_all.10.got = bf16[8,136,512]{2,1,0:T(8,128)(2,1)S(1)} all-to-all(bf16[8,136,512]{2,1,0:T(8,128)(2,1)} %shard_map.104), channel_id=1, replica_groups=mesh['z'=4,'y'=2,'obs'=4] {'y','obs'}, dimensions={0} | all-to-all | bytes 2228224 | tf_op jit(solution)/shard_map/all_to_all | solution.py:560
  24.2 1.2 %shard_map.105 = (f32[20,128,128]{2,1,0:T(8,128)S(1)}, f32[128,128]{1,0:T(8,128)S(1)}, bf16[17,128,128]{2,1,0:T(8,128)(2,1)S(1)}, f32[1,512]{1,0:T(1,128)S(1)}, f32[128,512]{1,0:T(8,128)S(1)}) custom-call(bf16[8,136,512]{2,1,0:T(8,128)(2,1)S(1)} %all_to_all.10.got, f32[128,512]{1,0:T(8,128)S(1)} %copy-done.2), custom_call_target="tpu_custom_call" | custom-call | flops 1073741824 | bytes 1376256 | tf_op jit(solution)/shard_map/pallas_call | solution.py:22
  25.4 0.6 collective-permute-start.4
  26.1 0.7 collective-permute-start.3
  26.8 0.7 collective-permute-start.2
  27.5 4.0 %collective-permute-start.1 = (bf16[17,128,128]{2,1,0:T(8,128)(2,1)S(1)}, bf16[17,128,128]{2,1,0:T(8,128)(2,1)S(1)}, u32[]{:S(2)}, u32[]{:S(2)}) collective-permute-start(bf16[17,128,128]{2,1,0:T(8,128)(2,1)S(1)} %get-tuple-element.54), channel_id=1, source_target_pairs={{0,9},{9,17},{11,19},{2,11},{6,15},{15,23},{13,21},{4,13}} | collective-permute-start | bytes 1671176 | tf_op jit(solution)/shard_map/ppermute | solution.py:579
  31.4 0.7 collective-permute-start
  32.1 1.3 %collective-permute-done.4.two = f32[128,512]{1,0:T(8,128)S(1)} collective-permute-done((f32[128,512]{1,0:T(8,128)S(1)}, f32[128,512]{1,0:T(8,128)S(1)}, u32[]{:S(2)}, u32[]{:S(2)}) %collective-permute-start.4) | collective-permute-done | bytes 262176 | tf_op jit(solution)/shard_map/ppermute | solution.py:576
  33.6 0.6 shard_map.106
  34.2 1.3 %collective-permute-done.5.got = f32[2,128,512]{2,1,0:T(8,128)S(1)} collective-permute-done((f32[2,128,512]{2,1,0:T(8,128)S(1)}, f32[2,128,512]{2,1,0:T(8,128)S(1)}, u32[]{:S(2)}, u32[]{:S(2)}) %collective-permute-start.5) | collective-permute-done | bytes 524320 | tf_op jit(solution)/shard_map/ppermute | solution.py:576
  35.9 6.4 %collective-permute-done.1.g3 = bf16[17,128,128]{2,1,0:T(8,128)(2,1)S(1)} collective-permute-done((bf16[17,128,128]{2,1,0:T(8,128)(2,1)S(1)}, bf16[17,128,128]{2,1,0:T(8,128)(2,1)S(1)}, u32[]{:S(2)}, u32[]{:S(2)}) %collective-permute-start.1) | collective-permute-done | bytes 557088 | tf_op jit(solution)/shard_map/ppermute | solution.py:579
  42.2 0.9 %shard_map.109 = (bf16[2,512,512]{2,1,0:T(8,128)(2,1)S(1)}, bf16[2,512,512]{2,1,0:T(8,128)(2,1)S(1)}, f32[2,1,512]{2,1,0:T(1,128)S(1)}, f32[2,512]{1,0:T(2,128)S...) custom-call(f32[20,128,128]{2,1,0:T(8,128)S(1)} %get-tuple-element.52.own, f32[128,128]{1,0:T(8,128)S(1)} %get-tuple-element.53.extra, ...), custom_call_target="tpu_custom_call" | custom-call | bytes 6227968 | tf_op jit(solution)/shard_map/pallas_call | solution.py:22
  43.1 0.7 collective-permute-start.6
  43.8 3.7 %shard_map.111 = (bf16[512,512]{1,0:T(8,128)(2,1)S(1)}, bf16[512,512]{1,0:T(8,128)(2,1)S(1)}, bf16[512,512]{1,0:T(8,128)(2,1)S(1)}, bf16[512,512]{1,0:T(8,128)(2,1)S(1)}, f32[8,512]{1,0:T(8,128)S(1)}) custom-call(f32[1,512]{1,0:T(1,128)S(1)} %get-tuple-element.63.after, bf16[2,512,512]{2,1,0:T(8,128)(2,1)S(1)} %get-tuple-element.65.omhi, ...), custom_call_target="tpu_custom_call" | custom-call | flops 3221225472 | bytes 4204544 | tf_op jit(solution)/shard_map/pallas_call | solution.py:22
  47.6 0.7 collective-permute-start.7
  48.3 1.1 %shard_map.113 = (bf16[512,512]{1,0:T(8,128)(2,1)S(1)}, bf16[512,512]{1,0:T(8,128)(2,1)S(1)}, f32[1,512]{1,0:T(1,128)S(1)}) custom-call(f32[1,512]{1,0:T(1,128)S(1)} %get-tuple-element.68.after, bf16[512,512]{1,0:T(8,128)(2,1)S(1)} %get-tuple-element.75.b1hi, bf16[512,512]{1,0:T(8,128)(2,1)S(1)} %get-tuple-element.76.b1lo, ...), custom_call_target="tpu_custom_call" | custom-call | bytes 2115584 | tf_op jit(solution)/shard_map/pallas_call | solution.py:22
  49.9 0.7 collective-permute-start.8
  50.9 0.7 collective-permute-start.9
  51.8 0.7 collective-permute-start.10
  52.7 0.7 collective-permute-start.11
  53.6 0.7 collective-permute-start.12
  54.4 1.2 %shard_map.121 = f32[32,8,128]{2,1,0:T(8,128)S(1)} custom-call(f32[1,512]{1,0:T(1,128)S(1)} %get-tuple-element.94.acc, f32[1,512]{1,0:T(1,128)S(1)} %collective-permute-done.12.got, bf16[512,512]{1,0:T(8,128)(2,1)S(1)} %get-tuple-element.75.b1hi, bf16[512,512]{1,0:T(8,128)(2,1)S(1)} %get-tuple-element.76.b1lo, bf16[512,512]{1,0:T(8,128)(2,1)S(1)} %get-tuple-element.77.b2hi, ...), custom_call_target="tpu_custom_call" | custom-call | bytes 14751744 | tf_op jit(solution)/shard_map/pallas_call | solution.py:22
  55.6 28.3 %all_to_all.11.parts = f32[32,8,128]{2,1,0:T(8,128)S(1)} all-to-all(f32[32,8,128]{2,1,0:T(8,128)S(1)} %shard_map.121), channel_id=1, replica_groups=mesh['z'=4,'y'=2,'obs'=4] {'z','y','obs'}, dimensions={0} | all-to-all | bytes 262144 | tf_op jit(solution)/shard_map/all_to_all | solution.py:645
  (29 shorter events, 2.5 us)
Async XLA Ops:
  2.8 21.4 %copy-start.2 = (f32[128,512]{1,0:T(8,128)S(1)}, f32[128,512]{1,0:T(8,128)}, u32[]{:S(2)}) copy-start(f32[128,512]{1,0:T(8,128)} %gain.1) | copy-start | bytes 786436
  24.2 9.4 %copy-start.1 = (f32[512,512]{1,0:T(8,128)S(1)}, f32[512,512]{1,0:T(8,128)}, u32[]{:S(2)}) copy-start(f32[512,512]{1,0:T(8,128)} %cov.1) | copy-start | bytes 3145732
  25.4 8.2 %copy-start = (f32[512,512]{1,0:T(8,128)S(1)}, f32[512,512]{1,0:T(8,128)}, u32[]{:S(2)}) copy-start(f32[512,512]{1,0:T(8,128)} %trans.1) | copy-start | bytes 3145732
  25.4 8.0 %collective-permute-start.4 = (f32[128,512]{1,0:T(8,128)S(1)}, f32[128,512]{1,0:T(8,128)S(1)}, u32[]{:S(2)}, u32[]{:S(2)}) collective-permute-start(f32[128,512]{1,0:T(8,128)S(1)} %get-tuple-element.60.one), channel_id=1, source_target_pairs={{0,2},{1,3},{2,0},{3,1},{4,6},{5,7},{6,4},{7,5},{8,10},{9,11},{10,... | collective-permute-start | bytes 786440 | tf_op jit(solution)/shard_map/ppermute | solution.py:576
  26.1 9.8 %collective-permute-start.3 = (bf16[17,128,128]{2,1,0:T(8,128)(2,1)S(1)}, bf16[17,128,128]{2,1,0:T(8,128)(2,1)S(1)}, u32[]{:S(2)}, u32[]{:S(2)}) collective-permute-start(bf16[17,128,128]{2,1,0:T(8,128)(2,1)S(1)} %get-tuple-element.54), channel_id=1, source_target_pairs={{24,9},{1,17},{3,19},{26,11},{30,15},{7,23},{5,21},{28,13}} | collective-permute-start | bytes 1671176 | tf_op jit(solution)/shard_map/ppermute | solution.py:579
  26.8 9.1 %collective-permute-start.2 = (bf16[17,128,128]{2,1,0:T(8,128)(2,1)S(1)}, bf16[17,128,128]{2,1,0:T(8,128)(2,1)S(1)}, u32[]{:S(2)}, u32[]{:S(2)}) collective-permute-start(bf16[17,128,128]{2,1,0:T(8,128)(2,1)S(1)} %get-tuple-element.54), channel_id=1, source_target_pairs={{16,9},{25,17},{27,19},{18,11},{22,15},{31,23},{29,21},{20,13}} | collective-permute-start | bytes 1671176 | tf_op jit(solution)/shard_map/ppermute | solution.py:579
  27.5 14.8 %collective-permute-start.1 = (bf16[17,128,128]{2,1,0:T(8,128)(2,1)S(1)}, bf16[17,128,128]{2,1,0:T(8,128)(2,1)S(1)}, u32[]{:S(2)}, u32[]{:S(2)}) collective-permute-start(bf16[17,128,128]{2,1,0:T(8,128)(2,1)S(1)} %get-tuple-element.54), channel_id=1, source_target_pairs={{0,9},{9,17},{11,19},{2,11},{6,15},{15,23},{13,21},{4,13}} | collective-permute-start | bytes 1671176 | tf_op jit(solution)/shard_map/ppermute | solution.py:579
  31.4 10.8 %collective-permute-start = (bf16[17,128,128]{2,1,0:T(8,128)(2,1)S(1)}, bf16[17,128,128]{2,1,0:T(8,128)(2,1)S(1)}, u32[]{:S(2)}, u32[]{:S(2)}) collective-permute-start(bf16[17,128,128]{2,1,0:T(8,128)(2,1)S(1)} %get-tuple-element.54), channel_id=1, source_target_pairs={{8,9},{10,11},{14,15},{12,13}} | collective-permute-start | bytes 1671176 | tf_op jit(solution)/shard_map/ppermute | solution.py:583
  33.5 2.0 %collective-permute-start.5 = (f32[2,128,512]{2,1,0:T(8,128)S(1)}, f32[2,128,512]{2,1,0:T(8,128)S(1)}, u32[]{:S(2)}, u32[]{:S(2)}) collective-permute-start(f32[2,128,512]{2,1,0:T(8,128)S(1)} %shard_map.107.held), channel_id=1, source_target_pairs={{0,1},{1,0},{2,3},{3,2},{4,5},{5,4},{6,7},{7,6},{8,9},{9,8},{10,11... | collective-permute-start | bytes 1572872 | tf_op jit(solution)/shard_map/ppermute | solution.py:576
  43.1 4.4 %collective-permute-start.6 = (f32[1,512]{1,0:T(1,128)S(1)}, f32[1,512]{1,0:T(1,128)S(1)}, u32[]{:S(2)}, u32[]{:S(2)}) collective-permute-start(f32[1,512]{1,0:T(1,128)S(1)} %get-tuple-element.63.after), channel_id=1, source_target_pairs={{9,17}} | collective-permute-start | bytes 6152 | tf_op jit(solution)/shard_map/ppermute | solution.py:602
  47.6 2.1 %collective-permute-start.7 = (f32[1,512]{1,0:T(1,128)S(1)}, f32[1,512]{1,0:T(1,128)S(1)}, u32[]{:S(2)}, u32[]{:S(2)}) collective-permute-start(f32[1,512]{1,0:T(1,128)S(1)} %get-tuple-element.68.after), channel_id=1, source_target_pairs={{17,19}} | collective-permute-start | bytes 6152 | tf_op jit(solution)/shard_map/ppermute | solution.py:602
  49.9 0.7 collective-permute-start.8
  50.9 0.7 collective-permute-start.9
  51.8 0.7 collective-permute-start.10
  52.7 0.7 collective-permute-start.11
  53.6 0.7 collective-permute-start.12

commit v12 on v11

--- a/solution.py
+++ b/solution.py
@@ -405,40 +405,31 @@
 
 
 def pairs_kernel(
-    after, b1hi, b1lo, bchi, bclo, off, offset, table, pthi, ptlo, mthi, mtlo,
-    khi, klo, ohi, olo, ehi, elo, shift, held,
+    after, b1hi, b1lo, bchi, bclo, off, offset, table, pthi, ptlo, mthi, mtlo, khi, klo, ehi, elo, shift
 ):
-    span = here()[1]
     total = table.shape[0]
     spans = total // 2
 
-    @pl.when(span >= spans - 2)
+    @pl.when(here()[1] == spans - 1)
     def _():
-        @pl.loop(spans - 1 - span, khi.shape[0])
+        @pl.loop(0, khi.shape[0])
         def _(k):
             scaled = whole_of(mthi, mtlo) * table[pl.ds(2 * (spans - 2 - k) + 1, 1), :]
             khi[k], klo[k] = split(mm(scaled, mthi[...], mtlo[...]))
 
-        within = table[pl.ds(2 * span + 1, 1), :]
-        after_d = table[pl.ds(jnp.minimum(2 * span + 2, total - 1), 1), :] * jnp.where(span == spans - 1, 0.0, 1.0)
-        one, two = off[0:1, :], offset[...]
-        odd = two - mv(mv(two, pthi[...], ptlo[...]) * (after_d * after_d), mthi[...], mtlo[...])
-        even = one + mv(
-            odd * within - mv(one, pthi[...], ptlo[...]) * (within * within), mthi[...], mtlo[...]
-        )
-        shift[0:1, :] = odd
-        shift[1:2, :] = even
-        moved = mm(whole_of(bchi, bclo), pthi[...], ptlo[...]) * (after_d * after_d)
-        held[...] = whole_of(bchi, bclo) - mm(moved, mthi[...], mtlo[...])
-        ohi[...], olo[...] = split(held[...])
-        moved = mm(whole_of(b1hi, b1lo), pthi[...], ptlo[...]) * (within * within)
-        moved = held[...] * within - moved
-        ehi[...], elo[...] = split(whole_of(b1hi, b1lo) + mm(moved, mthi[...], mtlo[...]))
+        within = table[total - 1 : total, :]
+        one = off[0:1, :]
+        ahead = mv(one, pthi[...], ptlo[...]) * (within * within)
+        shift[0:1, :] = one + mv(offset[...] * within - ahead, mthi[...], mtlo[...])
+        whole = whole_of(b1hi, b1lo)
+        ahead = mm(whole, pthi[...], ptlo[...]) * (within * within)
+        moved = whole_of(bchi, bclo) * within - ahead
+        ehi[...], elo[...] = split(whole + mm(moved, mthi[...], mtlo[...]))
 
 
 def last_kernel(
     acc, got, b1hi, b1lo, b2hi, b2lo, bchi, bclo, off, offset, table, pthi, ptlo, mthi, mtlo,
-    khi, klo, ohi, olo, ehi, elo, shift, out, shares, means,
+    khi, klo, ehi, elo, shift, out, shares, means,
 ):
     span = here()[1]
     total, width = shares.shape
@@ -452,7 +443,7 @@
         shares[pl.ds(t, 1), :] = v
         return v
 
-    @pl.when(span < spans - 2)
+    @pl.when(span < spans - 1)
     def _():
         state = acc[...] + got[...]
         one = mv(state, b1hi[...], b1lo[...]) + off[0:1, :]
@@ -467,29 +458,26 @@
         means[0:2, :] = both
         lax.fori_loop(0, 2 * span, step, even)
 
-    @pl.when(span >= spans - 2)
+    @pl.when(span == spans - 1)
     def _():
         state = acc[...] + got[...]
-        even = mv(state, ehi[...], elo[...]) + shift[1:2, :]
-        v, damped_rows = even, []
+        v, damped_rows = mv(state, ehi[...], elo[...]) + shift[0:1, :], []
+        shares[total - 2 : total - 1, :] = v
         for k in range(khi.shape[0]):
             t = 2 * (spans - 1 - k)
-            damped = v * table[t : t + 1, :]
-            damped_rows.append(damped)
-            reached = mv(damped, khi[k], klo[k])
-            v = reached if k else jnp.where(span == spans - 1, reached, v)
+            damped_rows.append(v * table[t : t + 1, :])
+            v = mv(damped_rows[-1], khi[k], klo[k])
             shares[t - 2 : t - 1, :] = v
-        odd = mv(state, ohi[...], olo[...]) + shift[0:1, :]
+        two = mv(state, bchi[...], bclo[...]) + offset[...]
         means[0:1, :] = mv(state, b1hi[...], b1lo[...]) + off[0:1, :]
-        means[1:2, :] = mv(state, bchi[...], bclo[...]) + offset[...]
+        means[1:2, :] = two
+        shares[total - 1 : total, :] = two
         batch = jnp.concatenate(damped_rows + [jnp.zeros((1, width), F32)] * (-len(damped_rows) % 8), 0)
         batch = mm(batch, mthi[...], mtlo[...])
         for k in range(khi.shape[0]):
             t = 2 * (spans - 1 - k)
             shares[t - 1 : t, :] = batch[k : k + 1]
-        shares[pl.ds(2 * span + 1, 1), :] = odd
-        shares[pl.ds(2 * span, 1), :] = even
-        lax.fori_loop(2 * khi.shape[0] - 2 * (spans - 1 - span), 2 * span, step, v)
+        lax.fori_loop(2 * khi.shape[0], 2 * span, step, v)
 
     for c in range(spans):
         for q in range(chunks):
@@ -626,9 +614,8 @@
             )
             ahead = run(
                 pairs_kernel,
-                [((min(spans - 1, 7),) + full, BF16)] * 2 + [(full, BF16)] * 4 + [((8, width), F32)],
+                [((min(spans - 1, 7),) + full, BF16)] * 2 + [(full, BF16)] * 2 + [((8, width), F32)],
                 [(y, ANY), b1hi, b1lo, bchi, bclo, off, offset, table, pthi, ptlo, mthi, mtlo],
-                [pltpu.VMEM(full, F32)],
             )
             side = ahead[0]
         elif k < spans - 2:

time: 84.8 us -> 84.3 us (level)
  no operation moved by 1% of the time
where the time goes in v12:
time: 84.3 us; the launch traced here: 83.9 us
  blocking collectives  49.2 us (58%)
  Pallas kernels  13.2 us (16%)
  starting transfers between devices  11.6 us (14%)
  waiting for transfers between devices  9.01 us (11%)
  between operations  0.93 us (1%)
    all_to_all x1, blocking collectives, local(): lax.all_to_all(answer, everyone, split_axis=0, concat_axis=0, tiled=True)  27.8 us
    all_to_all x1, blocking collectives, local(): lax.all_to_all(sent, ('y', 'obs'), split_axis=0, concat_axis=0, tiled=True)  21.4 us
    pallas_call x19, Pallas kernels, run(): pl.pallas_call(body, out_shape=[jax.ShapeDtypeStruct(s, d) for s, d in ou...  13.2 us
    ppermute x3, waiting for transfers between devices, plane_sum(): lax.ppermute(pay, everyone, [((owner_plane(p) + s) % planes * spans + pla...  6.39 us
    ppermute x3, starting transfers between devices, plane_sum(): lax.ppermute(pay, everyone, [((owner_plane(p) + s) % planes * spans + pla...  5.35 us
    ppermute x7, starting transfers between devices, local(): received = lax.ppermute(y, everyone, [(owner(k), owner(k + 1))])  4.86 us
    ppermute x2, waiting for transfers between devices, swap(): return lax.ppermute(x, 'obs', [(i, i ^ bit) for i in range(peers)])  2.59 us
  transfers between devices with their start and end apart: 13, of which 3 were waited for; matrix products, arithmetic and copies ran while one was open for 0% of the time, Pallas kernels for 7%

profile of v12, /device:TPU:0, one launch (start us, length us, event | category | flops | bytes accessed | tf_op | source)
XLA Modules:
  0.0 83.9 jit_solution(4025890001913181510)
XLA Ops:
  0.6 2.2 %shard_map.104 = bf16[8,136,512]{2,1,0:T(8,128)(2,1)} custom-call(s32[8]{0:T(128)} %day.1, s32[8]{0:T(128)} %count.1, bf16[1024,512]{1,0:T(8,128)(2,1)} %rows.1, bf16[8,128]{1,0:T(8,128)(2,1)} %bitcast.2, f32[1,128]{1,0:T(1,128)} %bitcast.3, f32[2,512]{1,0:T(2,128)} %damping.1), custom_call_target="tpu_custom_call" | custom-call | bytes 1055296 | tf_op jit(solution)/shard_map/pallas_call | solution.py:22
  2.9 21.4 %all_to_all.10.got = bf16[8,136,512]{2,1,0:T(8,128)(2,1)S(1)} all-to-all(bf16[8,136,512]{2,1,0:T(8,128)(2,1)} %shard_map.104), channel_id=1, replica_groups=mesh['z'=4,'y'=2,'obs'=4] {'y','obs'}, dimensions={0} | all-to-all | bytes 2228224 | tf_op jit(solution)/shard_map/all_to_all | solution.py:548
  24.2 1.2 %shard_map.105 = (f32[20,128,128]{2,1,0:T(8,128)S(1)}, f32[128,128]{1,0:T(8,128)S(1)}, bf16[17,128,128]{2,1,0:T(8,128)(2,1)S(1)}, f32[1,512]{1,0:T(1,128)S(1)}, f32[128,512]{1,0:T(8,128)S(1)}) custom-call(bf16[8,136,512]{2,1,0:T(8,128)(2,1)S(1)} %all_to_all.10.got, f32[128,512]{1,0:T(8,128)S(1)} %copy-done.2), custom_call_target="tpu_custom_call" | custom-call | flops 1073741824 | bytes 1376256 | tf_op jit(solution)/shard_map/pallas_call | solution.py:22
  25.4 0.6 collective-permute-start.4
  26.1 0.7 collective-permute-start.3
  26.8 0.7 collective-permute-start.2
  27.5 4.0 %collective-permute-start.1 = (bf16[17,128,128]{2,1,0:T(8,128)(2,1)S(1)}, bf16[17,128,128]{2,1,0:T(8,128)(2,1)S(1)}, u32[]{:S(2)}, u32[]{:S(2)}) collective-permute-start(bf16[17,128,128]{2,1,0:T(8,128)(2,1)S(1)} %get-tuple-element.52), channel_id=1, source_target_pairs={{0,9},{9,17},{11,19},{2,11},{6,15},{15,23},{13,21},{4,13}} | collective-permute-start | bytes 1671176 | tf_op jit(solution)/shard_map/ppermute | solution.py:567
  31.4 0.7 collective-permute-start
  32.1 1.3 %collective-permute-done.4.two = f32[128,512]{1,0:T(8,128)S(1)} collective-permute-done((f32[128,512]{1,0:T(8,128)S(1)}, f32[128,512]{1,0:T(8,128)S(1)}, u32[]{:S(2)}, u32[]{:S(2)}) %collective-permute-start.4) | collective-permute-done | bytes 262176 | tf_op jit(solution)/shard_map/ppermute | solution.py:564
  33.6 0.6 shard_map.106
  34.2 1.3 %collective-permute-done.5.got = f32[2,128,512]{2,1,0:T(8,128)S(1)} collective-permute-done((f32[2,128,512]{2,1,0:T(8,128)S(1)}, f32[2,128,512]{2,1,0:T(8,128)S(1)}, u32[]{:S(2)}, u32[]{:S(2)}) %collective-permute-start.5) | collective-permute-done | bytes 524320 | tf_op jit(solution)/shard_map/ppermute | solution.py:564
  35.9 6.4 %collective-permute-done.1.g3 = bf16[17,128,128]{2,1,0:T(8,128)(2,1)S(1)} collective-permute-done((bf16[17,128,128]{2,1,0:T(8,128)(2,1)S(1)}, bf16[17,128,128]{2,1,0:T(8,128)(2,1)S(1)}, u32[]{:S(2)}, u32[]{:S(2)}) %collective-permute-start.1) | collective-permute-done | bytes 557088 | tf_op jit(solution)/shard_map/ppermute | solution.py:567
  42.2 0.9 %shard_map.109 = (bf16[2,512,512]{2,1,0:T(8,128)(2,1)S(1)}, bf16[2,512,512]{2,1,0:T(8,128)(2,1)S(1)}, f32[2,1,512]{2,1,0:T(1,128)S(1)}, f32[2,512]{1,0:T(2,128)S...) custom-call(f32[20,128,128]{2,1,0:T(8,128)S(1)} %get-tuple-element.50.own, f32[128,128]{1,0:T(8,128)S(1)} %get-tuple-element.51.extra, ...), custom_call_target="tpu_custom_call" | custom-call | bytes 6227968 | tf_op jit(solution)/shard_map/pallas_call | solution.py:22
  43.1 0.7 collective-permute-start.6
  43.8 3.7 %shard_map.111 = (bf16[512,512]{1,0:T(8,128)(2,1)S(1)}, bf16[512,512]{1,0:T(8,128)(2,1)S(1)}, bf16[512,512]{1,0:T(8,128)(2,1)S(1)}, bf16[512,512]{1,0:T(8,128)(2,1)S(1)}, f32[8,512]{1,0:T(8,128)S(1)}) custom-call(f32[1,512]{1,0:T(1,128)S(1)} %get-tuple-element.61.after, bf16[2,512,512]{2,1,0:T(8,128)(2,1)S(1)} %get-tuple-element.63.omhi, ...), custom_call_target="tpu_custom_call" | custom-call | flops 3221225472 | bytes 4204544 | tf_op jit(solution)/shard_map/pallas_call | solution.py:22
  47.6 0.7 collective-permute-start.7
  48.3 1.1 %shard_map.113 = (bf16[512,512]{1,0:T(8,128)(2,1)S(1)}, bf16[512,512]{1,0:T(8,128)(2,1)S(1)}, f32[1,512]{1,0:T(1,128)S(1)}) custom-call(f32[1,512]{1,0:T(1,128)S(1)} %get-tuple-element.66.after, bf16[512,512]{1,0:T(8,128)(2,1)S(1)} %get-tuple-element.73.b1hi, bf16[512,512]{1,0:T(8,128)(2,1)S(1)} %get-tuple-element.74.b1lo, ...), custom_call_target="tpu_custom_call" | custom-call | bytes 2115584 | tf_op jit(solution)/shard_map/pallas_call | solution.py:22
  49.9 0.7 collective-permute-start.8
  50.8 0.7 collective-permute-start.9
  51.7 0.7 collective-permute-start.10
  52.7 0.7 collective-permute-start.11
  53.6 0.7 collective-permute-start.12
  54.3 1.2 %shard_map.121 = f32[32,8,128]{2,1,0:T(8,128)S(1)} custom-call(f32[1,512]{1,0:T(1,128)S(1)} %get-tuple-element.92.acc, f32[1,512]{1,0:T(1,128)S(1)} %collective-permute-done.12.got, bf16[512,512]{1,0:T(8,128)(2,1)S(1)} %get-tuple-element.73.b1hi, bf16[512,512]{1,0:T(8,128)(2,1)S(1)} %get-tuple-element.74.b1lo, bf16[512,512]{1,0:T(8,128)(2,1)S(1)} %get-tuple-element.75.b2hi, ...), custom_call_target="tpu_custom_call" | custom-call | bytes 13703168 | tf_op jit(solution)/shard_map/pallas_call | solution.py:22
  55.6 27.8 %all_to_all.11.parts = f32[32,8,128]{2,1,0:T(8,128)S(1)} all-to-all(f32[32,8,128]{2,1,0:T(8,128)S(1)} %shard_map.121), channel_id=1, replica_groups=mesh['z'=4,'y'=2,'obs'=4] {'z','y','obs'}, dimensions={0} | all-to-all | bytes 262144 | tf_op jit(solution)/shard_map/all_to_all | solution.py:632
  (29 shorter events, 2.4 us)
Async XLA Ops:
  2.8 21.4 %copy-start.2 = (f32[128,512]{1,0:T(8,128)S(1)}, f32[128,512]{1,0:T(8,128)}, u32[]{:S(2)}) copy-start(f32[128,512]{1,0:T(8,128)} %gain.1) | copy-start | bytes 786436
  24.2 9.4 %copy-start.1 = (f32[512,512]{1,0:T(8,128)S(1)}, f32[512,512]{1,0:T(8,128)}, u32[]{:S(2)}) copy-start(f32[512,512]{1,0:T(8,128)} %cov.1) | copy-start | bytes 3145732
  25.4 8.2 %copy-start = (f32[512,512]{1,0:T(8,128)S(1)}, f32[512,512]{1,0:T(8,128)}, u32[]{:S(2)}) copy-start(f32[512,512]{1,0:T(8,128)} %trans.1) | copy-start | bytes 3145732
  25.4 8.0 %collective-permute-start.4 = (f32[128,512]{1,0:T(8,128)S(1)}, f32[128,512]{1,0:T(8,128)S(1)}, u32[]{:S(2)}, u32[]{:S(2)}) collective-permute-start(f32[128,512]{1,0:T(8,128)S(1)} %get-tuple-element.58.one), channel_id=1, source_target_pairs={{0,2},{1,3},{2,0},{3,1},{4,6},{5,7},{6,4},{7,5},{8,10},{9,11},{10,... | collective-permute-start | bytes 786440 | tf_op jit(solution)/shard_map/ppermute | solution.py:564
  26.1 9.8 %collective-permute-start.3 = (bf16[17,128,128]{2,1,0:T(8,128)(2,1)S(1)}, bf16[17,128,128]{2,1,0:T(8,128)(2,1)S(1)}, u32[]{:S(2)}, u32[]{:S(2)}) collective-permute-start(bf16[17,128,128]{2,1,0:T(8,128)(2,1)S(1)} %get-tuple-element.52), channel_id=1, source_target_pairs={{24,9},{1,17},{3,19},{26,11},{30,15},{7,23},{5,21},{28,13}} | collective-permute-start | bytes 1671176 | tf_op jit(solution)/shard_map/ppermute | solution.py:567
  26.8 9.1 %collective-permute-start.2 = (bf16[17,128,128]{2,1,0:T(8,128)(2,1)S(1)}, bf16[17,128,128]{2,1,0:T(8,128)(2,1)S(1)}, u32[]{:S(2)}, u32[]{:S(2)}) collective-permute-start(bf16[17,128,128]{2,1,0:T(8,128)(2,1)S(1)} %get-tuple-element.52), channel_id=1, source_target_pairs={{16,9},{25,17},{27,19},{18,11},{22,15},{31,23},{29,21},{20,13}} | collective-permute-start | bytes 1671176 | tf_op jit(solution)/shard_map/ppermute | solution.py:567
  27.5 14.8 %collective-permute-start.1 = (bf16[17,128,128]{2,1,0:T(8,128)(2,1)S(1)}, bf16[17,128,128]{2,1,0:T(8,128)(2,1)S(1)}, u32[]{:S(2)}, u32[]{:S(2)}) collective-permute-start(bf16[17,128,128]{2,1,0:T(8,128)(2,1)S(1)} %get-tuple-element.52), channel_id=1, source_target_pairs={{0,9},{9,17},{11,19},{2,11},{6,15},{15,23},{13,21},{4,13}} | collective-permute-start | bytes 1671176 | tf_op jit(solution)/shard_map/ppermute | solution.py:567
  31.4 10.8 %collective-permute-start = (bf16[17,128,128]{2,1,0:T(8,128)(2,1)S(1)}, bf16[17,128,128]{2,1,0:T(8,128)(2,1)S(1)}, u32[]{:S(2)}, u32[]{:S(2)}) collective-permute-start(bf16[17,128,128]{2,1,0:T(8,128)(2,1)S(1)} %get-tuple-element.52), channel_id=1, source_target_pairs={{8,9},{10,11},{14,15},{12,13}} | collective-permute-start | bytes 1671176 | tf_op jit(solution)/shard_map/ppermute | solution.py:571
  33.5 2.0 %collective-permute-start.5 = (f32[2,128,512]{2,1,0:T(8,128)S(1)}, f32[2,128,512]{2,1,0:T(8,128)S(1)}, u32[]{:S(2)}, u32[]{:S(2)}) collective-permute-start(f32[2,128,512]{2,1,0:T(8,128)S(1)} %shard_map.107.held), channel_id=1, source_target_pairs={{0,1},{1,0},{2,3},{3,2},{4,5},{5,4},{6,7},{7,6},{8,9},{9,8},{10,11... | collective-permute-start | bytes 1572872 | tf_op jit(solution)/shard_map/ppermute | solution.py:564
  43.1 4.4 %collective-permute-start.6 = (f32[1,512]{1,0:T(1,128)S(1)}, f32[1,512]{1,0:T(1,128)S(1)}, u32[]{:S(2)}, u32[]{:S(2)}) collective-permute-start(f32[1,512]{1,0:T(1,128)S(1)} %get-tuple-element.61.after), channel_id=1, source_target_pairs={{9,17}} | collective-permute-start | bytes 6152 | tf_op jit(solution)/shard_map/ppermute | solution.py:590
  47.6 2.1 %collective-permute-start.7 = (f32[1,512]{1,0:T(1,128)S(1)}, f32[1,512]{1,0:T(1,128)S(1)}, u32[]{:S(2)}, u32[]{:S(2)}) collective-permute-start(f32[1,512]{1,0:T(1,128)S(1)} %get-tuple-element.66.after), channel_id=1, source_target_pairs={{17,19}} | collective-permute-start | bytes 6152 | tf_op jit(solution)/shard_map/ppermute | solution.py:590
  49.9 0.7 collective-permute-start.8
  50.8 0.7 collective-permute-start.9
  51.7 0.7 collective-permute-start.10
  52.7 0.7 collective-permute-start.11
  53.6 0.7 collective-permute-start.12

commit v13 on v12

--- a/solution.py
+++ b/solution.py
@@ -358,31 +358,44 @@
         y[...] = jnp.zeros(y.shape, F32)
 
 
-def second_kernel(acc, got, mine, pthi, ptlo, omhi, omlo, info, chi, clo, total, y):
+def maps_kernel(after, omhi, omlo, info, chi, clo, pt, damping, b1hi, b1lo, b2hi, b2lo, off, zhi, zlo):
+    for day in range(2):
+        off[day : day + 1, :] = mv(info[day], chi[...], clo[...])
+
+    def seen(day):
+        return mm(omhi[day].astype(F32) + omlo[day].astype(F32), chi[...], clo[...])
+
+    def step(day):
+        moved = pt[...] * damping[day : day + 1, :]
+        return moved - mm(moved, *split(seen(day)))
+
+    b1hi[...], b1lo[...] = split(step(0))
+
+    @pl.when(here()[1] != 1)
+    def _():
+        b2hi[...], b2lo[...] = split(step(1))
+
+    @pl.when(here()[1] == 1)
+    def _():
+        zhi[...], zlo[...] = split(seen(1))
+
+
+def second_kernel(acc, got, mine, b1hi, b1lo, off, zhi, zlo, pthi, ptlo, total, y):
     total[...] = acc[...] + got[...]
     y[...] = jnp.zeros(y.shape, F32)
 
     @pl.when(here()[1] == 1)
     def _():
-        state = acc[...] + got[...]
-        for day in range(2):
-            state = one_day(day, state, mine, pthi, ptlo, omhi, omlo, info, chi, clo)
-        y[...] = state
-
-
-def maps_kernel(after, omhi, omlo, info, chi, clo, pt, damping, *rest):
-    late = len(rest) == 10
-    b1hi, b1lo, b2hi, b2lo, off = rest[-5:]
-    parts = ((b1hi, b1lo), (b2hi, b2lo))
-
-    @pl.when((here()[1] == 1) == late)
-    def _():
-        for day in range(2):
-            moved = pt[...] * damping[day : day + 1, :]
-            taken = mm(moved, omhi[day], omlo[day])
-            step = moved - mm(taken, chi[...], clo[...])
-            parts[day][0][...], parts[day][1][...] = split(step)
-            off[day : day + 1, :] = mv(info[day], chi[...], clo[...])
+        state = mv(acc[...] + got[...], b1hi[...], b1lo[...]) + off[0:1, :]
+        moved = mv(state, pthi[...], ptlo[...]) * mine[1:2, :]
+        y[...] = moved - mv(moved, zhi[...], zlo[...]) + off[1:2, :]
+
+
+def rest_kernel(after, pt, damping, zhi, zlo, old_hi, old_lo, b2hi, b2lo):
+    @pl.when(here()[1] == 1)
+    def _():
+        moved = pt[...] * damping[1:2, :]
+        b2hi[...], b2lo[...] = split(moved - mm(moved, zhi[...], zlo[...]))
 
 
 def both_kernel(after, b1hi, b1lo, b2hi, b2lo, off, bchi, bclo, offset):
@@ -410,13 +423,17 @@
     total = table.shape[0]
     spans = total // 2
 
-    @pl.when(here()[1] == spans - 1)
-    def _():
-        @pl.loop(0, khi.shape[0])
+    span = here()[1]
+
+    @pl.when(span >= spans - 2)
+    def _():
+        @pl.loop(spans - 1 - span, khi.shape[0])
         def _(k):
             scaled = whole_of(mthi, mtlo) * table[pl.ds(2 * (spans - 2 - k) + 1, 1), :]
             khi[k], klo[k] = split(mm(scaled, mthi[...], mtlo[...]))
 
+    @pl.when(span == spans - 1)
+    def _():
         within = table[total - 1 : total, :]
         one = off[0:1, :]
         ahead = mv(one, pthi[...], ptlo[...]) * (within * within)
@@ -456,28 +473,40 @@
         shares[pl.ds(2 * span + 1, 1), :] = const[1:2]
         shares[pl.ds(2 * span, 1), :] = even
         means[0:2, :] = both
-        lax.fori_loop(0, 2 * span, step, even)
-
-    @pl.when(span == spans - 1)
-    def _():
-        state = acc[...] + got[...]
-        v, damped_rows = mv(state, ehi[...], elo[...]) + shift[0:1, :], []
-        shares[total - 2 : total - 1, :] = v
-        for k in range(khi.shape[0]):
+        means[2:3, :] = even
+
+    def descend(v, start):
+        damped_rows, days = [], range(start, khi.shape[0])
+        for k in days:
             t = 2 * (spans - 1 - k)
             damped_rows.append(v * table[t : t + 1, :])
             v = mv(damped_rows[-1], khi[k], klo[k])
             shares[t - 2 : t - 1, :] = v
+        batch = jnp.concatenate(damped_rows + [jnp.zeros((1, width), F32)] * (-len(damped_rows) % 8), 0)
+        batch = mm(batch, mthi[...], mtlo[...])
+        for n, k in enumerate(days):
+            t = 2 * (spans - 1 - k)
+            shares[t - 1 : t, :] = batch[n : n + 1]
+        lax.fori_loop(2 * len(days), 2 * span, step, v)
+
+    @pl.when(span < spans - 2)
+    def _():
+        lax.fori_loop(0, 2 * span, step, means[2:3, :])
+
+    @pl.when(span == spans - 2)
+    def _():
+        descend(means[2:3, :], 1)
+
+    @pl.when(span == spans - 1)
+    def _():
+        state = acc[...] + got[...]
+        v = mv(state, ehi[...], elo[...]) + shift[0:1, :]
+        shares[total - 2 : total - 1, :] = v
+        descend(v, 0)
         two = mv(state, bchi[...], bclo[...]) + offset[...]
         means[0:1, :] = mv(state, b1hi[...], b1lo[...]) + off[0:1, :]
         means[1:2, :] = two
         shares[total - 1 : total, :] = two
-        batch = jnp.concatenate(damped_rows + [jnp.zeros((1, width), F32)] * (-len(damped_rows) % 8), 0)
-        batch = mm(batch, mthi[...], mtlo[...])
-        for k in range(khi.shape[0]):
-            t = 2 * (spans - 1 - k)
-            shares[t - 1 : t, :] = batch[k : k + 1]
-        lax.fori_loop(2 * khi.shape[0], 2 * span, step, v)
 
     for c in range(spans):
         for q in range(chunks):
@@ -589,19 +618,21 @@
     for k in range(spans - 1):
         received = lax.ppermute(y, everyone, [(owner(k), owner(k + 1))])
         if k == 0:
-            maps = [(full, BF16)] * 4 + [((8, width), F32)]
-            given = [omhi, omlo, info, chi, clo, pt, mine]
-            flops = 24 * width**3
-            days_maps = run(maps_kernel, maps, [(y, ANY), *given], flops=flops)
+            b1hi, b1lo, b2hi, b2lo, off, zhi, zlo = run(
+                maps_kernel,
+                [(full, BF16)] * 4 + [((8, width), F32)] + [(full, BF16)] * 2,
+                [(y, ANY), omhi, omlo, info, chi, clo, pt, mine],
+                flops=24 * width**3,
+            )
             acc, y = run(
-                second_kernel, [row, row], [acc, received, mine, pthi, ptlo, omhi, omlo, info, chi, clo]
-            )
-            b1hi, b1lo, b2hi, b2lo, off = run(
-                maps_kernel,
-                maps,
-                [(y, ANY), *given, *days_maps],
-                flops=flops,
-                same={8 + n: n for n in range(5)},
+                second_kernel, [row, row], [acc, received, mine, b1hi, b1lo, off, zhi, zlo, pthi, ptlo]
+            )
+            b2hi, b2lo = run(
+                rest_kernel,
+                [(full, BF16)] * 2,
+                [(y, ANY), pt, mine, zhi, zlo, b2hi, b2lo],
+                flops=6 * width**3,
+                same={5: 0, 6: 1},
             )
             bchi, bclo, offset = run(
                 both_kernel, [(full, BF16)] * 2 + [row], [(y, ANY), b1hi, b1lo, b2hi, b2lo, off]

time: 84.3 us -> 83.3 us (0.988)
  blocking collectives: 49.2 us -> 47.8 us
    all_to_all x1, blocking collectives: 27.8 us -> 26.5 us  [local(): lax.all_to_all(answer, everyone, split_axis=0, concat_axis=0, tiled=True)]
  transfers between devices with their start and end apart: 13 -> 13, of which waited for: 3 -> 3; matrix products, arithmetic and copies ran while one was open for 0% -> 0% of each run, Pallas kernels for 7% -> 8%
where the time goes in v13:
time: 83.3 us; the launch traced here: 83 us
  blocking collectives  47.8 us (57%)
  Pallas kernels  13.6 us (16%)
  starting transfers between devices  11.6 us (14%)
  waiting for transfers between devices  9 us (11%)
  between operations  0.94 us (1%)
    all_to_all x1, blocking collectives, local(): lax.all_to_all(answer, everyone, split_axis=0, concat_axis=0, tiled=True)  26.5 us
    all_to_all x1, blocking collectives, local(): lax.all_to_all(sent, ('y', 'obs'), split_axis=0, concat_axis=0, tiled=True)  21.4 us
    pallas_call x19, Pallas kernels, run(): pl.pallas_call(body, out_shape=[jax.ShapeDtypeStruct(s, d) for s, d in ou...  13.6 us
    ppermute x3, waiting for transfers between devices, plane_sum(): lax.ppermute(pay, everyone, [((owner_plane(p) + s) % planes * spans + pla...  6.39 us
    ppermute x3, starting transfers between devices, plane_sum(): lax.ppermute(pay, everyone, [((owner_plane(p) + s) % planes * spans + pla...  5.35 us
    ppermute x7, starting transfers between devices, local(): received = lax.ppermute(y, everyone, [(owner(k), owner(k + 1))])  4.86 us
    ppermute x2, waiting for transfers between devices, swap(): return lax.ppermute(x, 'obs', [(i, i ^ bit) for i in range(peers)])  2.59 us
  transfers between devices with their start and end apart: 13, of which 3 were waited for; matrix products, arithmetic and copies ran while one was open for 0% of the time, Pallas kernels for 8%

profile of v13, /device:TPU:0, one launch (start us, length us, event | category | flops | bytes accessed | tf_op | source)
XLA Modules:
  0.0 83.0 jit_solution(9658275824584041546)
XLA Ops:
  0.6 2.2 %shard_map.104 = bf16[8,136,512]{2,1,0:T(8,128)(2,1)} custom-call(s32[8]{0:T(128)} %day.1, s32[8]{0:T(128)} %count.1, bf16[1024,512]{1,0:T(8,128)(2,1)} %rows.1, bf16[8,128]{1,0:T(8,128)(2,1)} %bitcast.2, f32[1,128]{1,0:T(1,128)} %bitcast.3, f32[2,512]{1,0:T(2,128)} %damping.1), custom_call_target="tpu_custom_call" | custom-call | bytes 1055296 | tf_op jit(solution)/shard_map/pallas_call | solution.py:22
  2.9 21.4 %all_to_all.10.got = bf16[8,136,512]{2,1,0:T(8,128)(2,1)S(1)} all-to-all(bf16[8,136,512]{2,1,0:T(8,128)(2,1)} %shard_map.104), channel_id=1, replica_groups=mesh['z'=4,'y'=2,'obs'=4] {'y','obs'}, dimensions={0} | all-to-all | bytes 2228224 | tf_op jit(solution)/shard_map/all_to_all | solution.py:577
  24.2 1.2 %shard_map.105 = (f32[20,128,128]{2,1,0:T(8,128)S(1)}, f32[128,128]{1,0:T(8,128)S(1)}, bf16[17,128,128]{2,1,0:T(8,128)(2,1)S(1)}, f32[1,512]{1,0:T(1,128)S(1)}, f32[128,512]{1,0:T(8,128)S(1)}) custom-call(bf16[8,136,512]{2,1,0:T(8,128)(2,1)S(1)} %all_to_all.10.got, f32[128,512]{1,0:T(8,128)S(1)} %copy-done.2), custom_call_target="tpu_custom_call" | custom-call | flops 1073741824 | bytes 1376256 | tf_op jit(solution)/shard_map/pallas_call | solution.py:22
  25.4 0.6 collective-permute-start.4
  26.1 0.7 collective-permute-start.3
  26.8 0.7 collective-permute-start.2
  27.5 4.0 %collective-permute-start.1 = (bf16[17,128,128]{2,1,0:T(8,128)(2,1)S(1)}, bf16[17,128,128]{2,1,0:T(8,128)(2,1)S(1)}, u32[]{:S(2)}, u32[]{:S(2)}) collective-permute-start(bf16[17,128,128]{2,1,0:T(8,128)(2,1)S(1)} %get-tuple-element.51), channel_id=1, source_target_pairs={{0,9},{9,17},{11,19},{2,11},{6,15},{15,23},{13,21},{4,13}} | collective-permute-start | bytes 1671176 | tf_op jit(solution)/shard_map/ppermute | solution.py:596
  31.4 0.7 collective-permute-start
  32.1 1.3 %collective-permute-done.4.two = f32[128,512]{1,0:T(8,128)S(1)} collective-permute-done((f32[128,512]{1,0:T(8,128)S(1)}, f32[128,512]{1,0:T(8,128)S(1)}, u32[]{:S(2)}, u32[]{:S(2)}) %collective-permute-start.4) | collective-permute-done | bytes 262176 | tf_op jit(solution)/shard_map/ppermute | solution.py:593
  33.6 0.6 shard_map.106
  34.2 1.3 %collective-permute-done.5.got = f32[2,128,512]{2,1,0:T(8,128)S(1)} collective-permute-done((f32[2,128,512]{2,1,0:T(8,128)S(1)}, f32[2,128,512]{2,1,0:T(8,128)S(1)}, u32[]{:S(2)}, u32[]{:S(2)}) %collective-permute-start.5) | collective-permute-done | bytes 524320 | tf_op jit(solution)/shard_map/ppermute | solution.py:593
  35.9 6.4 %collective-permute-done.1.g3 = bf16[17,128,128]{2,1,0:T(8,128)(2,1)S(1)} collective-permute-done((bf16[17,128,128]{2,1,0:T(8,128)(2,1)S(1)}, bf16[17,128,128]{2,1,0:T(8,128)(2,1)S(1)}, u32[]{:S(2)}, u32[]{:S(2)}) %collective-permute-start.1) | collective-permute-done | bytes 557088 | tf_op jit(solution)/shard_map/ppermute | solution.py:596
  42.2 0.9 %shard_map.109 = (bf16[2,512,512]{2,1,0:T(8,128)(2,1)S(1)}, bf16[2,512,512]{2,1,0:T(8,128)(2,1)S(1)}, f32[2,1,512]{2,1,0:T(1,128)S(1)}, f32[2,512]{1,0:T(2,128)S...) custom-call(f32[20,128,128]{2,1,0:T(8,128)S(1)} %get-tuple-element.49.own, f32[128,128]{1,0:T(8,128)S(1)} %get-tuple-element.50.extra, ...), custom_call_target="tpu_custom_call" | custom-call | bytes 6227968 | tf_op jit(solution)/shard_map/pallas_call | solution.py:22
  43.1 0.7 collective-permute-start.6
  43.8 4.1 %shard_map.110 = (bf16[512,512]{1,0:T(8,128)(2,1)S(1)}, bf16[512,512]{1,0:T(8,128)(2,1)S(1)}, bf16[512,512]{1,0:T(8,128)(2,1)S(1)}, bf16[512,512]{1,0:T(8,128)(2...) custom-call(f32[1,512]{1,0:T(1,128)S(1)} %get-tuple-element.60.after, ...), custom_call_target="tpu_custom_call" | custom-call | flops 3221225472 | bytes 4204544 | tf_op jit(solution)/shard_map/pallas_call | solution.py:22
  48.0 0.7 collective-permute-start.7
  48.7 1.1 %shard_map.113 = (bf16[512,512]{1,0:T(8,128)(2,1)S(1)}, bf16[512,512]{1,0:T(8,128)(2,1)S(1)}, f32[1,512]{1,0:T(1,128)S(1)}) custom-call(f32[1,512]{1,0:T(1,128)S(1)} %get-tuple-element.71.after, bf16[512,512]{1,0:T(8,128)(2,1)S(1)} %get-tuple-element.66.b1hi, bf16[512,512]{1,0:T(8,128)(2,1)S(1)} %get-tuple-element.67.b1lo, ...), custom_call_target="tpu_custom_call" | custom-call | bytes 2115584 | tf_op jit(solution)/shard_map/pallas_call | solution.py:22
  50.3 0.7 collective-permute-start.8
  51.2 0.7 collective-permute-start.9
  52.1 0.7 collective-permute-start.10
  53.1 0.7 collective-permute-start.11
  54.0 0.7 collective-permute-start.12
  54.7 1.2 %shard_map.121 = f32[32,8,128]{2,1,0:T(8,128)S(1)} custom-call(f32[1,512]{1,0:T(1,128)S(1)} %get-tuple-element.90.acc, f32[1,512]{1,0:T(1,128)S(1)} %collective-permute-done.12.got, bf16[512,512]{1,0:T(8,128)(2,1)S(1)} %get-tuple-element.66.b1hi, bf16[512,512]{1,0:T(8,128)(2,1)S(1)} %get-tuple-element.67.b1lo, bf16[512,512]{1,0:T(8,128)(2,1)S(1)} %get-tuple-element.74.b2hi, ...), custom_call_target="tpu_custom_call" | custom-call | bytes 13703168 | tf_op jit(solution)/shard_map/pallas_call | solution.py:22
  55.9 26.5 %all_to_all.11.parts = f32[32,8,128]{2,1,0:T(8,128)S(1)} all-to-all(f32[32,8,128]{2,1,0:T(8,128)S(1)} %shard_map.121), channel_id=1, replica_groups=mesh['z'=4,'y'=2,'obs'=4] {'z','y','obs'}, dimensions={0} | all-to-all | bytes 262144 | tf_op jit(solution)/shard_map/all_to_all | solution.py:663
  (29 shorter events, 2.4 us)
Async XLA Ops:
  2.8 21.4 %copy-start.2 = (f32[128,512]{1,0:T(8,128)S(1)}, f32[128,512]{1,0:T(8,128)}, u32[]{:S(2)}) copy-start(f32[128,512]{1,0:T(8,128)} %gain.1) | copy-start | bytes 786436
  24.2 9.4 %copy-start.1 = (f32[512,512]{1,0:T(8,128)S(1)}, f32[512,512]{1,0:T(8,128)}, u32[]{:S(2)}) copy-start(f32[512,512]{1,0:T(8,128)} %cov.1) | copy-start | bytes 3145732
  25.4 8.2 %copy-start = (f32[512,512]{1,0:T(8,128)S(1)}, f32[512,512]{1,0:T(8,128)}, u32[]{:S(2)}) copy-start(f32[512,512]{1,0:T(8,128)} %trans.1) | copy-start | bytes 3145732
  25.4 8.0 %collective-permute-start.4 = (f32[128,512]{1,0:T(8,128)S(1)}, f32[128,512]{1,0:T(8,128)S(1)}, u32[]{:S(2)}, u32[]{:S(2)}) collective-permute-start(f32[128,512]{1,0:T(8,128)S(1)} %get-tuple-element.57.one), channel_id=1, source_target_pairs={{0,2},{1,3},{2,0},{3,1},{4,6},{5,7},{6,4},{7,5},{8,10},{9,11},{10,... | collective-permute-start | bytes 786440 | tf_op jit(solution)/shard_map/ppermute | solution.py:593
  26.1 9.8 %collective-permute-start.3 = (bf16[17,128,128]{2,1,0:T(8,128)(2,1)S(1)}, bf16[17,128,128]{2,1,0:T(8,128)(2,1)S(1)}, u32[]{:S(2)}, u32[]{:S(2)}) collective-permute-start(bf16[17,128,128]{2,1,0:T(8,128)(2,1)S(1)} %get-tuple-element.51), channel_id=1, source_target_pairs={{24,9},{1,17},{3,19},{26,11},{30,15},{7,23},{5,21},{28,13}} | collective-permute-start | bytes 1671176 | tf_op jit(solution)/shard_map/ppermute | solution.py:596
  26.8 9.1 %collective-permute-start.2 = (bf16[17,128,128]{2,1,0:T(8,128)(2,1)S(1)}, bf16[17,128,128]{2,1,0:T(8,128)(2,1)S(1)}, u32[]{:S(2)}, u32[]{:S(2)}) collective-permute-start(bf16[17,128,128]{2,1,0:T(8,128)(2,1)S(1)} %get-tuple-element.51), channel_id=1, source_target_pairs={{16,9},{25,17},{27,19},{18,11},{22,15},{31,23},{29,21},{20,13}} | collective-permute-start | bytes 1671176 | tf_op jit(solution)/shard_map/ppermute | solution.py:596
  27.5 14.8 %collective-permute-start.1 = (bf16[17,128,128]{2,1,0:T(8,128)(2,1)S(1)}, bf16[17,128,128]{2,1,0:T(8,128)(2,1)S(1)}, u32[]{:S(2)}, u32[]{:S(2)}) collective-permute-start(bf16[17,128,128]{2,1,0:T(8,128)(2,1)S(1)} %get-tuple-element.51), channel_id=1, source_target_pairs={{0,9},{9,17},{11,19},{2,11},{6,15},{15,23},{13,21},{4,13}} | collective-permute-start | bytes 1671176 | tf_op jit(solution)/shard_map/ppermute | solution.py:596
  31.4 10.8 %collective-permute-start = (bf16[17,128,128]{2,1,0:T(8,128)(2,1)S(1)}, bf16[17,128,128]{2,1,0:T(8,128)(2,1)S(1)}, u32[]{:S(2)}, u32[]{:S(2)}) collective-permute-start(bf16[17,128,128]{2,1,0:T(8,128)(2,1)S(1)} %get-tuple-element.51), channel_id=1, source_target_pairs={{8,9},{10,11},{14,15},{12,13}} | collective-permute-start | bytes 1671176 | tf_op jit(solution)/shard_map/ppermute | solution.py:600
  33.5 2.0 %collective-permute-start.5 = (f32[2,128,512]{2,1,0:T(8,128)S(1)}, f32[2,128,512]{2,1,0:T(8,128)S(1)}, u32[]{:S(2)}, u32[]{:S(2)}) collective-permute-start(f32[2,128,512]{2,1,0:T(8,128)S(1)} %shard_map.107.held), channel_id=1, source_target_pairs={{0,1},{1,0},{2,3},{3,2},{4,5},{5,4},{6,7},{7,6},{8,9},{9,8},{10,11... | collective-permute-start | bytes 1572872 | tf_op jit(solution)/shard_map/ppermute | solution.py:593
  43.1 4.8 %collective-permute-start.6 = (f32[1,512]{1,0:T(1,128)S(1)}, f32[1,512]{1,0:T(1,128)S(1)}, u32[]{:S(2)}, u32[]{:S(2)}) collective-permute-start(f32[1,512]{1,0:T(1,128)S(1)} %get-tuple-element.60.after), channel_id=1, source_target_pairs={{9,17}} | collective-permute-start | bytes 6152 | tf_op jit(solution)/shard_map/ppermute | solution.py:619
  48.0 2.1 %collective-permute-start.7 = (f32[1,512]{1,0:T(1,128)S(1)}, f32[1,512]{1,0:T(1,128)S(1)}, u32[]{:S(2)}, u32[]{:S(2)}) collective-permute-start(f32[1,512]{1,0:T(1,128)S(1)} %get-tuple-element.71.after), channel_id=1, source_target_pairs={{17,19}} | collective-permute-start | bytes 6152 | tf_op jit(solution)/shard_map/ppermute | solution.py:619
  50.3 0.7 collective-permute-start.8
  51.2 0.7 collective-permute-start.9
  52.1 0.7 collective-permute-start.10
  53.1 0.7 collective-permute-start.11
  54.0 0.7 collective-permute-start.12

commit v14 on v13

--- a/solution.py
+++ b/solution.py
@@ -219,11 +219,12 @@
         pay[small_at + n] = extra[n * LANES : (n + 1) * LANES, :].astype(BF16)
 
 
-def prep_kernel(trans, cov, pt, pthi, ptlo, chi, clo):
+def prep_kernel(trans, cov, prior, pt, pthi, ptlo, chi, clo, ahead):
     whole = trans[...].T
     pt[...] = whole
     pthi[...], ptlo[...] = split(whole)
     chi[...], clo[...] = split(cov[...])
+    ahead[...] = mv(prior[...], pthi[...], ptlo[...])
 
 
 def stack_kernel(one, two, out):
@@ -250,8 +251,8 @@
     return first[0:2] + (first[2:4] + second[0:2])
 
 
-def one_day(day, state, damping, pthi, ptlo, omhi, omlo, info, chi, clo):
-    moved = mv(state, pthi[...], ptlo[...]) * damping[day : day + 1, :]
+def one_day(day, ahead, damping, omhi, omlo, info, chi, clo):
+    moved = ahead * damping[day : day + 1, :]
     gap = mv(moved, omhi[day], omlo[day]) - info[day]
     return moved - mv(gap, chi[...], clo[...])
 
@@ -286,7 +287,7 @@
 
 
 def owner_kernel(
-    own, extra, g4, g3, g1, g2, prior, pthi, ptlo, chi, clo, after, omhi, omlo, info, mine, start, y, small
+    own, extra, g4, g3, g1, g2, prior, ahead, pthi, ptlo, chi, clo, after, omhi, omlo, info, mine, start, y, small
 ):
     ids = here()
     planes = 4
@@ -345,11 +346,10 @@
 
     @pl.when(first)
     def _():
-        state = prior[...]
-        for day in range(2):
-            unpack(day)
-            state = one_day(day, state, mine, pthi, ptlo, omhi, omlo, info, chi, clo)
-        y[...] = state
+        unpack(0)
+        state = one_day(0, ahead[...], mine, omhi, omlo, info, chi, clo)
+        unpack(1)
+        y[...] = one_day(1, mv(state, pthi[...], ptlo[...]), mine, omhi, omlo, info, chi, clo)
 
     @pl.when(jnp.logical_not(first))
     def _():
@@ -358,26 +358,39 @@
         y[...] = jnp.zeros(y.shape, F32)
 
 
-def maps_kernel(after, omhi, omlo, info, chi, clo, pt, damping, b1hi, b1lo, b2hi, b2lo, off, zhi, zlo):
-    for day in range(2):
-        off[day : day + 1, :] = mv(info[day], chi[...], clo[...])
-
-    def seen(day):
-        return mm(omhi[day].astype(F32) + omlo[day].astype(F32), chi[...], clo[...])
-
-    def step(day):
-        moved = pt[...] * damping[day : day + 1, :]
-        return moved - mm(moved, *split(seen(day)))
-
-    b1hi[...], b1lo[...] = split(step(0))
-
-    @pl.when(here()[1] != 1)
-    def _():
-        b2hi[...], b2lo[...] = split(step(1))
-
+def seen(day, omhi, omlo, chi, clo):
+    return mm(omhi[day].astype(F32) + omlo[day].astype(F32), chi[...], clo[...])
+
+
+def early_kernel(after, omhi, omlo, info, chi, clo, pt, damping, b1hi, b1lo, off, zhi, zlo):
     @pl.when(here()[1] == 1)
     def _():
-        zhi[...], zlo[...] = split(seen(1))
+        for day in range(2):
+            off[day : day + 1, :] = mv(info[day], chi[...], clo[...])
+        moved = pt[...] * damping[0:1, :]
+        b1hi[...], b1lo[...] = split(moved - mm(moved, *split(seen(0, omhi, omlo, chi, clo))))
+        zhi[...], zlo[...] = split(seen(1, omhi, omlo, chi, clo))
+
+
+def maps_kernel(
+    after, omhi, omlo, info, chi, clo, pt, damping, zhi, zlo, old1, old2, old3, b1hi, b1lo, off, b2hi, b2lo
+):
+    second = here()[1] == 1
+
+    @pl.when(jnp.logical_not(second))
+    def _():
+        parts = ((b1hi, b1lo), (b2hi, b2lo))
+        for day in range(2):
+            moved = pt[...] * damping[day : day + 1, :]
+            parts[day][0][...], parts[day][1][...] = split(
+                moved - mm(moved, *split(seen(day, omhi, omlo, chi, clo)))
+            )
+            off[day : day + 1, :] = mv(info[day], chi[...], clo[...])
+
+    @pl.when(second)
+    def _():
+        moved = pt[...] * damping[1:2, :]
+        b2hi[...], b2lo[...] = split(moved - mm(moved, zhi[...], zlo[...]))
 
 
 def second_kernel(acc, got, mine, b1hi, b1lo, off, zhi, zlo, pthi, ptlo, total, y):
@@ -389,13 +402,6 @@
         state = mv(acc[...] + got[...], b1hi[...], b1lo[...]) + off[0:1, :]
         moved = mv(state, pthi[...], ptlo[...]) * mine[1:2, :]
         y[...] = moved - mv(moved, zhi[...], zlo[...]) + off[1:2, :]
-
-
-def rest_kernel(after, pt, damping, zhi, zlo, old_hi, old_lo, b2hi, b2lo):
-    @pl.when(here()[1] == 1)
-    def _():
-        moved = pt[...] * damping[1:2, :]
-        b2hi[...], b2lo[...] = split(moved - mm(moved, zhi[...], zlo[...]))
 
 
 def both_kernel(after, b1hi, b1lo, b2hi, b2lo, off, bchi, bclo, offset):
@@ -603,36 +609,35 @@
     third, first, second = plane_sum(3), plane_sum(1), plane_sum(2)
     (gains,) = run(stack_kernel, [((2,) + gain.shape, F32)], [gain, swap(gain, 2)])
     mthi, mtlo = run(gain_kernel, [(full, BF16)] * 2, [gains, swap(gains, 1)])
-    pt, pthi, ptlo, chi, clo = run(
-        prep_kernel, [(full, F32)] + [(full, BF16)] * 4, [propagator_matrix, analysis_cov]
+    pt, pthi, ptlo, chi, clo, ahead = run(
+        prep_kernel, [(full, F32)] + [(full, BF16)] * 4 + [row], [propagator_matrix, analysis_cov, prior]
     )
     smalls = pltpu.VMEM((planes + 1, extra_tiles * LANES, LANES), F32)
     omhi, omlo, info, mine, acc, y = run(
         owner_kernel,
         [((days,) + full, BF16)] * 2 + [((days, 1, width), F32), ((days, width), F32), row, row],
         [
-            own, extra, fourth, third, first, second, prior, pthi, ptlo, chi, clo, (mthi, ANY)
+            own, extra, fourth, third, first, second, prior, ahead, pthi, ptlo, chi, clo, (mthi, ANY)
         ],
         [smalls],
     )
     for k in range(spans - 1):
         received = lax.ppermute(y, everyone, [(owner(k), owner(k + 1))])
         if k == 0:
-            b1hi, b1lo, b2hi, b2lo, off, zhi, zlo = run(
-                maps_kernel,
-                [(full, BF16)] * 4 + [((8, width), F32)] + [(full, BF16)] * 2,
-                [(y, ANY), omhi, omlo, info, chi, clo, pt, mine],
-                flops=24 * width**3,
+            given = [omhi, omlo, info, chi, clo, pt, mine]
+            half = [(full, BF16)] * 2
+            b1hi, b1lo, off, zhi, zlo = run(
+                early_kernel, half + [((8, width), F32)] + half, [(y, ANY), *given], flops=18 * width**3
             )
             acc, y = run(
                 second_kernel, [row, row], [acc, received, mine, b1hi, b1lo, off, zhi, zlo, pthi, ptlo]
             )
-            b2hi, b2lo = run(
-                rest_kernel,
-                [(full, BF16)] * 2,
-                [(y, ANY), pt, mine, zhi, zlo, b2hi, b2lo],
-                flops=6 * width**3,
-                same={5: 0, 6: 1},
+            b1hi, b1lo, off, b2hi, b2lo = run(
+                maps_kernel,
+                half + [((8, width), F32)] + half,
+                [(y, ANY), *given, zhi, zlo, b1hi, b1lo, off],
+                flops=24 * width**3,
+                same={10: 0, 11: 1, 12: 2},
             )
             bchi, bclo, offset = run(
                 both_kernel, [(full, BF16)] * 2 + [row], [(y, ANY), b1hi, b1lo, b2hi, b2lo, off]

time: 83.3 us -> 82.2 us (0.987)
    all_to_all x1, blocking collectives: 26.5 us -> 25.6 us  [local(): lax.all_to_all(answer, everyone, split_axis=0, concat_axis=0, tiled=True)]
where the time goes in v14:
time: 82.2 us; the launch traced here: 81.8 us
  blocking collectives  47 us (57%)
  Pallas kernels  13.4 us (16%)
  starting transfers between devices  11.6 us (14%)
  waiting for transfers between devices  8.93 us (11%)
  between operations  0.94 us (1%)
    all_to_all x1, blocking collectives, local(): lax.all_to_all(answer, everyone, split_axis=0, concat_axis=0, tiled=True)  25.6 us
    all_to_all x1, blocking collectives, local(): lax.all_to_all(sent, ('y', 'obs'), split_axis=0, concat_axis=0, tiled=True)  21.4 us
    pallas_call x19, Pallas kernels, run(): pl.pallas_call(body, out_shape=[jax.ShapeDtypeStruct(s, d) for s, d in ou...  13.4 us
    ppermute x3, waiting for transfers between devices, plane_sum(): lax.ppermute(pay, everyone, [((owner_plane(p) + s) % planes * spans + pla...  6.39 us
    ppermute x3, starting transfers between devices, plane_sum(): lax.ppermute(pay, everyone, [((owner_plane(p) + s) % planes * spans + pla...  5.35 us
    ppermute x7, starting transfers between devices, local(): received = lax.ppermute(y, everyone, [(owner(k), owner(k + 1))])  4.86 us
    ppermute x2, waiting for transfers between devices, swap(): return lax.ppermute(x, 'obs', [(i, i ^ bit) for i in range(peers)])  2.52 us
  transfers between devices with their start and end apart: 13, of which 3 were waited for; matrix products, arithmetic and copies ran while one was open for 0% of the time, Pallas kernels for 8%

profile of v14, /device:TPU:0, one launch (start us, length us, event | category | flops | bytes accessed | tf_op | source)
XLA Modules:
  0.0 81.8 jit_solution(17295701891690446313)
XLA Ops:
  0.6 2.2 %shard_map.104 = bf16[8,136,512]{2,1,0:T(8,128)(2,1)} custom-call(s32[8]{0:T(128)} %day.1, s32[8]{0:T(128)} %count.1, bf16[1024,512]{1,0:T(8,128)(2,1)} %rows.1, bf16[8,128]{1,0:T(8,128)(2,1)} %bitcast.2, f32[1,128]{1,0:T(1,128)} %bitcast.3, f32[2,512]{1,0:T(2,128)} %damping.1), custom_call_target="tpu_custom_call" | custom-call | bytes 1055296 | tf_op jit(solution)/shard_map/pallas_call | solution.py:22
  2.9 21.4 %all_to_all.10.got = bf16[8,136,512]{2,1,0:T(8,128)(2,1)S(1)} all-to-all(bf16[8,136,512]{2,1,0:T(8,128)(2,1)} %shard_map.104), channel_id=1, replica_groups=mesh['z'=4,'y'=2,'obs'=4] {'y','obs'}, dimensions={0} | all-to-all | bytes 2228224 | tf_op jit(solution)/shard_map/all_to_all | solution.py:583
  24.2 1.2 %shard_map.105 = (f32[20,128,128]{2,1,0:T(8,128)S(1)}, f32[128,128]{1,0:T(8,128)S(1)}, bf16[17,128,128]{2,1,0:T(8,128)(2,1)S(1)}, f32[1,512]{1,0:T(1,128)S(1)}, f32[128,512]{1,0:T(8,128)S(1)}) custom-call(bf16[8,136,512]{2,1,0:T(8,128)(2,1)S(1)} %all_to_all.10.got, f32[128,512]{1,0:T(8,128)S(1)} %copy-done.2), custom_call_target="tpu_custom_call" | custom-call | flops 1073741824 | bytes 1376256 | tf_op jit(solution)/shard_map/pallas_call | solution.py:22
  25.4 0.6 collective-permute-start.4
  26.1 0.7 collective-permute-start.3
  26.8 0.7 collective-permute-start.2
  27.5 4.0 %collective-permute-start.1 = (bf16[17,128,128]{2,1,0:T(8,128)(2,1)S(1)}, bf16[17,128,128]{2,1,0:T(8,128)(2,1)S(1)}, u32[]{:S(2)}, u32[]{:S(2)}) collective-permute-start(bf16[17,128,128]{2,1,0:T(8,128)(2,1)S(1)} %get-tuple-element.53), channel_id=1, source_target_pairs={{0,9},{9,17},{11,19},{2,11},{6,15},{15,23},{13,21},{4,13}} | collective-permute-start | bytes 1671176 | tf_op jit(solution)/shard_map/ppermute | solution.py:602
  31.4 0.7 collective-permute-start
  32.1 1.3 %collective-permute-done.4.two = f32[128,512]{1,0:T(8,128)S(1)} collective-permute-done((f32[128,512]{1,0:T(8,128)S(1)}, f32[128,512]{1,0:T(8,128)S(1)}, u32[]{:S(2)}, u32[]{:S(2)}) %collective-permute-start.4) | collective-permute-done | bytes 262176 | tf_op jit(solution)/shard_map/ppermute | solution.py:599
  33.6 0.7 shard_map.106
  34.3 1.2 %collective-permute-done.5.got = f32[2,128,512]{2,1,0:T(8,128)S(1)} collective-permute-done((f32[2,128,512]{2,1,0:T(8,128)S(1)}, f32[2,128,512]{2,1,0:T(8,128)S(1)}, u32[]{:S(2)}, u32[]{:S(2)}) %collective-permute-start.5) | collective-permute-done | bytes 524320 | tf_op jit(solution)/shard_map/ppermute | solution.py:599
  35.9 6.4 %collective-permute-done.1.g3 = bf16[17,128,128]{2,1,0:T(8,128)(2,1)S(1)} collective-permute-done((bf16[17,128,128]{2,1,0:T(8,128)(2,1)S(1)}, bf16[17,128,128]{2,1,0:T(8,128)(2,1)S(1)}, u32[]{:S(2)}, u32[]{:S(2)}) %collective-permute-start.1) | collective-permute-done | bytes 557088 | tf_op jit(solution)/shard_map/ppermute | solution.py:602
  42.2 0.9 %shard_map.109 = (bf16[2,512,512]{2,1,0:T(8,128)(2,1)S(1)}, bf16[2,512,512]{2,1,0:T(8,128)(2,1)S(1)}, f32[2,1,512]{2,1,0:T(1,128)S(1)}, f32[2,512]{1,0:T(2,128)S...) custom-call(f32[20,128,128]{2,1,0:T(8,128)S(1)} %get-tuple-element.51.own, f32[128,128]{1,0:T(8,128)S(1)} %get-tuple-element.52.extra, ...), custom_call_target="tpu_custom_call" | custom-call | bytes 6230016 | tf_op jit(solution)/shard_map/pallas_call | solution.py:22
  43.1 0.7 collective-permute-start.6
  43.9 0.7 collective-permute-start.7
  44.6 4.0 %shard_map.112 = (bf16[512,512]{1,0:T(8,128)(2,1)S(1)}, bf16[512,512]{1,0:T(8,128)(2,1)S(1)}, f32[8,512]{1,0:T(8,128)S(1)}, bf16[512,512]{1,0:T(8,128)(2,1)S(1)}, bf16[512,512]{1,0:T(8,128)(2,1)S(1)}) custom-call(f32[1,512]{1,0:T(1,128)S(1)} %get-tuple-element.74.after, ...), custom_call_target="tpu_custom_call", output_to_operand_aliasing={{0}: (10, {}), {1}: (11, {}), {2}: (12, {})} | custom-call | flops 3221225472 | bytes 6318080 | tf_op jit(solution)/shard_map/pallas_call | solution.py:22
  48.6 1.1 %shard_map.113 = (bf16[512,512]{1,0:T(8,128)(2,1)S(1)}, bf16[512,512]{1,0:T(8,128)(2,1)S(1)}, f32[1,512]{1,0:T(1,128)S(1)}) custom-call(f32[1,512]{1,0:T(1,128)S(1)} %get-tuple-element.74.after, bf16[512,512]{1,0:T(8,128)(2,1)S(1)} %get-tuple-element.75.b1hi, bf16[512,512]{1,0:T(8,128)(2,1)S(1)} %get-tuple-element.76.b1lo, ...), custom_call_target="tpu_custom_call" | custom-call | bytes 2115584 | tf_op jit(solution)/shard_map/pallas_call | solution.py:22
  50.0 0.7 collective-permute-start.8
  50.9 0.7 collective-permute-start.9
  51.9 0.7 collective-permute-start.10
  52.8 0.7 collective-permute-start.11
  53.7 0.7 collective-permute-start.12
  54.4 1.2 %shard_map.121 = f32[32,8,128]{2,1,0:T(8,128)S(1)} custom-call(f32[1,512]{1,0:T(1,128)S(1)} %get-tuple-element.94.acc, f32[1,512]{1,0:T(1,128)S(1)} %collective-permute-done.12.got, bf16[512,512]{1,0:T(8,128)(2,1)S(1)} %get-tuple-element.75.b1hi, bf16[512,512]{1,0:T(8,128)(2,1)S(1)} %get-tuple-element.76.b1lo, bf16[512,512]{1,0:T(8,128)(2,1)S(1)} %get-tuple-element.77.b2hi, ...), custom_call_target="tpu_custom_call" | custom-call | bytes 13703168 | tf_op jit(solution)/shard_map/pallas_call | solution.py:22
  55.7 25.6 %all_to_all.11.parts = f32[32,8,128]{2,1,0:T(8,128)S(1)} all-to-all(f32[32,8,128]{2,1,0:T(8,128)S(1)} %shard_map.121), channel_id=1, replica_groups=mesh['z'=4,'y'=2,'obs'=4] {'z','y','obs'}, dimensions={0} | all-to-all | bytes 262144 | tf_op jit(solution)/shard_map/all_to_all | solution.py:668
  (29 shorter events, 2.2 us)
Async XLA Ops:
  2.8 21.4 %copy-start.2 = (f32[128,512]{1,0:T(8,128)S(1)}, f32[128,512]{1,0:T(8,128)}, u32[]{:S(2)}) copy-start(f32[128,512]{1,0:T(8,128)} %gain.1) | copy-start | bytes 786436
  24.2 9.4 %copy-start.1 = (f32[512,512]{1,0:T(8,128)S(1)}, f32[512,512]{1,0:T(8,128)}, u32[]{:S(2)}) copy-start(f32[512,512]{1,0:T(8,128)} %cov.1) | copy-start | bytes 3145732
  25.4 8.2 %copy-start = (f32[512,512]{1,0:T(8,128)S(1)}, f32[512,512]{1,0:T(8,128)}, u32[]{:S(2)}) copy-start(f32[512,512]{1,0:T(8,128)} %trans.1) | copy-start | bytes 3145732
  25.4 8.0 %collective-permute-start.4 = (f32[128,512]{1,0:T(8,128)S(1)}, f32[128,512]{1,0:T(8,128)S(1)}, u32[]{:S(2)}, u32[]{:S(2)}) collective-permute-start(f32[128,512]{1,0:T(8,128)S(1)} %get-tuple-element.60.one), channel_id=1, source_target_pairs={{0,2},{1,3},{2,0},{3,1},{4,6},{5,7},{6,4},{7,5},{8,10},{9,11},{10,... | collective-permute-start | bytes 786440 | tf_op jit(solution)/shard_map/ppermute | solution.py:599
  26.1 9.8 %collective-permute-start.3 = (bf16[17,128,128]{2,1,0:T(8,128)(2,1)S(1)}, bf16[17,128,128]{2,1,0:T(8,128)(2,1)S(1)}, u32[]{:S(2)}, u32[]{:S(2)}) collective-permute-start(bf16[17,128,128]{2,1,0:T(8,128)(2,1)S(1)} %get-tuple-element.53), channel_id=1, source_target_pairs={{24,9},{1,17},{3,19},{26,11},{30,15},{7,23},{5,21},{28,13}} | collective-permute-start | bytes 1671176 | tf_op jit(solution)/shard_map/ppermute | solution.py:602
  26.8 9.1 %collective-permute-start.2 = (bf16[17,128,128]{2,1,0:T(8,128)(2,1)S(1)}, bf16[17,128,128]{2,1,0:T(8,128)(2,1)S(1)}, u32[]{:S(2)}, u32[]{:S(2)}) collective-permute-start(bf16[17,128,128]{2,1,0:T(8,128)(2,1)S(1)} %get-tuple-element.53), channel_id=1, source_target_pairs={{16,9},{25,17},{27,19},{18,11},{22,15},{31,23},{29,21},{20,13}} | collective-permute-start | bytes 1671176 | tf_op jit(solution)/shard_map/ppermute | solution.py:602
  27.5 14.8 %collective-permute-start.1 = (bf16[17,128,128]{2,1,0:T(8,128)(2,1)S(1)}, bf16[17,128,128]{2,1,0:T(8,128)(2,1)S(1)}, u32[]{:S(2)}, u32[]{:S(2)}) collective-permute-start(bf16[17,128,128]{2,1,0:T(8,128)(2,1)S(1)} %get-tuple-element.53), channel_id=1, source_target_pairs={{0,9},{9,17},{11,19},{2,11},{6,15},{15,23},{13,21},{4,13}} | collective-permute-start | bytes 1671176 | tf_op jit(solution)/shard_map/ppermute | solution.py:602
  31.4 10.8 %collective-permute-start = (bf16[17,128,128]{2,1,0:T(8,128)(2,1)S(1)}, bf16[17,128,128]{2,1,0:T(8,128)(2,1)S(1)}, u32[]{:S(2)}, u32[]{:S(2)}) collective-permute-start(bf16[17,128,128]{2,1,0:T(8,128)(2,1)S(1)} %get-tuple-element.53), channel_id=1, source_target_pairs={{8,9},{10,11},{14,15},{12,13}} | collective-permute-start | bytes 1671176 | tf_op jit(solution)/shard_map/ppermute | solution.py:606
  33.5 2.0 %collective-permute-start.5 = (f32[2,128,512]{2,1,0:T(8,128)S(1)}, f32[2,128,512]{2,1,0:T(8,128)S(1)}, u32[]{:S(2)}, u32[]{:S(2)}) collective-permute-start(f32[2,128,512]{2,1,0:T(8,128)S(1)} %shard_map.107.held), channel_id=1, source_target_pairs={{0,1},{1,0},{2,3},{3,2},{4,5},{5,4},{6,7},{7,6},{8,9},{9,8},{10,11... | collective-permute-start | bytes 1572872 | tf_op jit(solution)/shard_map/ppermute | solution.py:599
  43.1 0.7 collective-permute-start.6
  43.9 5.9 %collective-permute-start.7 = (f32[1,512]{1,0:T(1,128)S(1)}, f32[1,512]{1,0:T(1,128)S(1)}, u32[]{:S(2)}, u32[]{:S(2)}) collective-permute-start(f32[1,512]{1,0:T(1,128)S(1)} %get-tuple-element.74.after), channel_id=1, source_target_pairs={{17,19}} | collective-permute-start | bytes 6152 | tf_op jit(solution)/shard_map/ppermute | solution.py:625
  50.0 0.7 collective-permute-start.8
  50.9 0.7 collective-permute-start.9
  51.9 0.7 collective-permute-start.10
  52.8 0.7 collective-permute-start.11
  53.7 0.7 collective-permute-start.12

commit v15 on v14

--- a/solution.py
+++ b/solution.py
@@ -71,13 +71,9 @@
     return first[0:1] + (first[1:2] + second[0:1])
 
 
-def parts3(x):
-    out = []
-    for _ in range(3):
-        piece = x.astype(BF16).astype(F32)
-        out.append(piece)
-        x = x - piece
-    return out
+def parts(x):
+    top = x.astype(BF16).astype(F32)
+    return [top, (x - top).astype(BF16).astype(F32)]
 
 
 def place(span):
@@ -89,49 +85,45 @@
 
 
 EXTRA = 8
-DIAG, DAMP = 24, 48
+DIAG, DAMP = 16, 32
 
 
 def pack_kernel(
-    day, count, rows, values, prior, damping, out, day_s, count_s, values_v, prior_v, damping_v, stage, sems
+    day, count, rows, values, prior, damping, out, day_s, count_s, values_v, prior_v, damping_v, rows_v, stage, sems
 ):
     blocks = out.shape[0]
-    slots = out.shape[1] - EXTRA
-    width = out.shape[2]
+    slots = rows_v.shape[1]
+    chunks = rows_v.shape[2] // LANES
     small = [(day, day_s), (count, count_s), (values, values_v), (prior, prior_v), (damping, damping_v)]
     copies = [pltpu.make_async_copy(src, dst, sems.at[n]) for n, (src, dst) in enumerate(small)]
     large = [
-        pltpu.make_async_copy(
-            rows.at[pl.ds(k * slots, slots)], stage.at[place(k), pl.ds(0, slots)], sems.at[len(small) + k]
-        )
+        pltpu.make_async_copy(rows.at[pl.ds(k * slots, slots)], rows_v.at[k], sems.at[len(small) + k])
+        for k in range(blocks)
+    ]
+    sends = [
+        pltpu.make_async_copy(stage.at[place(k)], out.at[place(k)], sems.at[len(small) + blocks + k])
         for k in range(blocks)
     ]
     for copy in copies + large:
         copy.start()
     for copy in copies:
         copy.wait()
-    first, second, third = parts3(prior_v[...])
-    below = jnp.concatenate(
-        [jnp.concatenate([second, third, jnp.zeros((1, width - 2 * LANES), F32)], 1)] + parts3(damping_v[...]), 0
-    )
+    mine = damping_v[:, 0:LANES]
+    for q in range(1, chunks):
+        mine = jnp.where(lax.axis_index("obs") == q, damping_v[:, q * LANES : (q + 1) * LANES], mine)
+    below = parts(prior_v[...]) + parts(mine)
+    below = jnp.concatenate(below, 0)
     held = values_v[...].astype(F32)
+    lane = lax.broadcasted_iota(jnp.int32, (1, LANES), 1)
     for k in range(blocks):
-        line = jnp.concatenate(
-            [
-                held[k : k + 1, :],
-                jnp.full((1, LANES), day_s[k], jnp.int32).astype(F32),
-                jnp.full((1, LANES), count_s[k], jnp.int32).astype(F32),
-                first,
-            ],
-            1,
-        )
-        stage[place(k), slots : slots + EXTRA, :] = jnp.concatenate([line, below], 0).astype(BF16)
-    sends = [
-        pltpu.make_async_copy(stage.at[place(k)], out.at[place(k)], sems.at[len(small) + blocks + k])
-        for k in range(blocks)
-    ]
+        marks = jnp.where(lane < LANES // 2, day_s[k], count_s[k]).astype(F32)
+        stage[place(k), chunks * slots : chunks * slots + EXTRA, :] = jnp.concatenate(
+            [held[k : k + 1, :], marks, below], 0
+        ).astype(BF16)
     for k in range(blocks):
         large[k].wait()
+        for j in range(chunks):
+            stage[place(k), j * slots : (j + 1) * slots, :] = rows_v[k, :, j * LANES : (j + 1) * LANES]
         sends[k].start()
     for copy in sends:
         copy.wait()
@@ -139,28 +131,38 @@
 
 def gram_kernel(got, gain, own, extra, pay, prior, gain_out, turned, marks):
     blocks = got.shape[0]
-    slots = got.shape[1] - EXTRA
-    width = got.shape[2]
-    chunks = width // LANES
+    chunks = turned.shape[0] // LANES
+    slots = (got.shape[1] - EXTRA) // chunks
+    width = chunks * LANES
     tiles = triangle(width)
     group = min(blocks, 8)
     half = 2 * LANES
     gain_out[...] = gain[...]
     extra[...] = jnp.zeros(extra.shape, F32)
 
+    def below(k):
+        return got[k, chunks * slots : chunks * slots + EXTRA, :].astype(F32)
+
     def one(first, fresh):
         for k in range(group):
             at = slice(k * slots, (k + 1) * slots)
-            line = got[first + k, slots : slots + EXTRA, :].astype(F32)
-            valid = lax.broadcasted_iota(jnp.int32, (1, slots), 1).astype(F32) < line[0:1, 2 * LANES : 3 * LANES]
-            day = line[0:1, LANES : 2 * LANES]
-            values = line[0:1, 0:LANES]
+            line = below(first + k)
+            slot = lax.broadcasted_iota(jnp.int32, (1, slots), 1).astype(F32)
+            valid = slot < jnp.broadcast_to(line[1:2, LANES - 1 : LANES], (1, slots))
+            day = jnp.broadcast_to(line[1:2, 0:1], (1, slots))
             kept = [jnp.where(valid & (day == d), 1.0, 0.0) for d in (0.0, 1.0)]
             marks[:, at] = jnp.concatenate(
-                kept + [kept[0] * values, kept[1] * values, jnp.zeros((12, slots), F32)], 0
+                kept + [kept[0] * line[0:1], kept[1] * line[0:1], jnp.zeros((12, slots), F32)], 0
             ).astype(BF16)
-            turned[:, at] = got[first + k, 0:slots, :].T
-        source = jnp.concatenate([got[first + k, 0:slots, :] for k in range(group)], 0)
+            for j in range(chunks):
+                turned[j * LANES : (j + 1) * LANES, at] = got[first + k, j * slots : (j + 1) * slots, :].T
+        source = jnp.concatenate(
+            [
+                jnp.concatenate([got[first + k, j * slots : (j + 1) * slots, :] for j in range(chunks)], 1)
+                for k in range(group)
+            ],
+            0,
+        )
         info = jnp.dot(marks[...], source, preferred_element_type=F32)
         for d in range(2):
             for top in range(0, width, half):
@@ -174,7 +176,7 @@
                         own[at] = piece if fresh else own[at] + piece
             for j in range(chunks):
                 piece = info[2 + d : 3 + d, j * LANES : (j + 1) * LANES]
-                r = 12 * d + j
+                r = 8 * d + j
                 extra[r : r + 1, :] = piece if fresh else extra[r : r + 1, :] + piece
 
     if blocks == group:
@@ -190,33 +192,34 @@
     column = lax.broadcasted_iota(jnp.int32, (LANES, LANES), 1)
     sides = [n for n, (i, j) in enumerate(tiles) if i != j]
     middles = [n for n, (i, j) in enumerate(tiles) if i == j]
+
+    def send(n, piece):
+        pay[n * LANES : (n + 1) * LANES, :] = piece.astype(BF16)
+
     for d in range(2):
-        for part, piece in enumerate(parts3(extra[12 * d : 12 * d + chunks, :])):
-            extra[12 * d + 4 * part : 12 * d + 4 * part + chunks, :] = piece
+        for part, piece in enumerate(parts(extra[8 * d : 8 * d + chunks, :])):
+            extra[8 * d + 4 * part : 8 * d + 4 * part + chunks, :] = piece
         for m, n in enumerate(sides):
-            pay[d * len(sides) + m] = own[d * len(tiles) + n].astype(BF16)
+            send(d * len(sides) + m, own[d * len(tiles) + n])
     for i, n in enumerate(middles):
         squares = [own[d * len(tiles) + n] for d in range(2)]
-        pay[2 * len(sides) + i] = jnp.where(row >= column, squares[0], squares[1]).astype(BF16)
+        send(2 * len(sides) + i, jnp.where(row >= column, squares[0], squares[1]))
         for d in range(2):
             line = jnp.sum(jnp.where(row == column, squares[d], 0.0), axis=0, keepdims=True)
-            for part, piece in enumerate(parts3(line)):
-                r = DIAG + 12 * d + 4 * part + i
+            for part, piece in enumerate(parts(line)):
+                r = DIAG + 8 * d + 4 * part + i
                 extra[r : r + 1, :] = piece
     for q in range(chunks):
-        line = got[q, slots : slots + EXTRA, :].astype(F32)
-        prior[:, q * LANES : (q + 1) * LANES] = line[0:1, 3 * LANES : 4 * LANES] + (
-            line[1:2, 0:LANES] + line[1:2, LANES : 2 * LANES]
-        )
+        line = below(q)
+        prior[:, q * LANES : (q + 1) * LANES] = line[2:3] + line[3:4]
     for y in range(blocks // 4):
-        line = got[4 * y, slots : slots + EXTRA, :].astype(F32)
-        for k in range(6):
-            for j in range(chunks):
-                r = DAMP + 24 * y + 4 * k + j
-                extra[r : r + 1, :] = line[2 + k : 3 + k, j * LANES : (j + 1) * LANES]
-    small_at = pay.shape[0] - extra.shape[0] // LANES
-    for n in range(extra.shape[0] // LANES):
-        pay[small_at + n] = extra[n * LANES : (n + 1) * LANES, :].astype(BF16)
+        for q in range(chunks):
+            line = below(4 * y + q)
+            for part in range(2):
+                for d in range(2):
+                    r = DAMP + 16 * y + 8 * d + 4 * part + q
+                    extra[r : r + 1, :] = line[4 + 2 * part + d : 5 + 2 * part + d]
+    pay[pay.shape[0] - extra.shape[0] :, :] = extra[...].astype(BF16)
 
 
 def prep_kernel(trans, cov, prior, pt, pthi, ptlo, chi, clo, ahead):
@@ -258,17 +261,13 @@
 
 
 def spread(extra, got, small):
-    small_at = got[0].shape[0] - extra.shape[0] // LANES
     small[0] = extra[...]
     for s, part in enumerate(got):
-        for n in range(extra.shape[0] // LANES):
-            small[s + 1, n * LANES : (n + 1) * LANES, :] = part[small_at + n].astype(F32)
-
-
-def line_of(small, s, first, gap):
-    return small[s, first : first + 1, :] + (
-        small[s, first + gap : first + gap + 1, :] + small[s, first + 2 * gap : first + 2 * gap + 1, :]
-    )
+        small[s + 1] = part[part.shape[0] - extra.shape[0] :, :].astype(F32)
+
+
+def line_of(small, s, first):
+    return small[s, first : first + 1, :] + small[s, first + 4 : first + 5, :]
 
 
 def table_kernel(after, extra, g1, g2, g3, table, small):
@@ -282,7 +281,7 @@
         for k in range(held):
             for day in range(2):
                 table[pl.ds(2 * (plane * held + k) + day, 1), :] = jnp.concatenate(
-                    [line_of(small, s, DAMP + 24 * k + 4 * day + j, 8) for j in range(chunks)], 1
+                    [line_of(small, s, DAMP + 16 * k + 8 * day + j) for j in range(chunks)], 1
                 )
 
 
@@ -300,14 +299,12 @@
     column = lax.broadcasted_iota(jnp.int32, (LANES, LANES), 1)
     spread(extra, got, small)
 
-    def line(s, first, gap):
-        return line_of(small, s, first, gap)
-
-    def summed(first, gap):
-        others = line(1, first, gap) + (line(2, first, gap) + (line(3, first, gap) + line(4, first, gap)))
-        return line(0, first, gap) * share + others
-
-    def added(at):
+    def summed(first):
+        others = line_of(small, 1, first) + line_of(small, 2, first) + (line_of(small, 3, first) + line_of(small, 4, first))
+        return line_of(small, 0, first) * share + others
+
+    def added(n):
+        at = slice(n * LANES, (n + 1) * LANES)
         return (g1[at].astype(F32) + g2[at].astype(F32)) + (g3[at].astype(F32) + g4[at].astype(F32))
 
     def put(day, i, j, piece):
@@ -322,7 +319,7 @@
         for i, n in enumerate(middles):
             both = added(2 * len(sides) + i)
             part = jnp.where(row < column if day else row > column, both, 0.0)
-            others = sum(line(s, DIAG + 12 * day + i, 4) for s in range(1, 5))
+            others = sum(line_of(small, s, DIAG + 8 * day + i) for s in range(1, 5))
             piece = own[day * len(tiles) + n] * share + (part + part.T)
             put(day, i, i, piece + jnp.where(row == column, others, 0.0))
         for m, n in enumerate(sides):
@@ -332,14 +329,14 @@
             put(day, j, i, piece.T)
 
     for day in range(2):
-        info[day] = jnp.concatenate([summed(12 * day + j, 4) for j in range(chunks)], 1)
+        info[day] = jnp.concatenate([summed(8 * day + j) for j in range(chunks)], 1)
     held = ids[5]
     source = lax.rem(ids[1] // held - ids[0] + planes, planes)
     for day in range(2):
         for j in range(chunks):
-            r = DAMP + 24 * lax.rem(ids[1], held) + 4 * day + j
-            mine[day : day + 1, j * LANES : (j + 1) * LANES] = small[source, pl.ds(r, 1), :] + (
-                small[source, pl.ds(r + 8, 1), :] + small[source, pl.ds(r + 16, 1), :]
+            r = DAMP + 16 * lax.rem(ids[1], held) + 8 * day + j
+            mine[day : day + 1, j * LANES : (j + 1) * LANES] = (
+                small[source, pl.ds(r, 1), :] + small[source, pl.ds(r + 4, 1), :]
             )
     first = (ids[1] == 0) & (ids[0] == owner_plane(0))
     start[...] = jnp.where(first, prior[...], 0.0)
@@ -552,11 +549,12 @@
         return owner_plane(span) * spans + (place(span) | 1)
 
     tiles = len(triangle(width))
-    extra_tiles = -(-(DAMP + 24 * held) // LANES)
+    extra_rows = DAMP + 16 * held
+    chunks = width // LANES
     full, row = (width, width), ((1, width), F32)
     sent = run(
         pack_kernel,
-        [((blocks, slots + EXTRA, width), BF16)],
+        [((blocks, chunks * slots + EXTRA, LANES), BF16)],
         [
             (x, HBM)
             for x in (
@@ -574,7 +572,8 @@
             pltpu.VMEM((blocks, slots), BF16),
             pltpu.VMEM((1, width // peers), F32),
             pltpu.VMEM((days, width), F32),
-            pltpu.VMEM((blocks, slots + EXTRA, width), BF16),
+            pltpu.VMEM((blocks, slots, width), BF16),
+            pltpu.VMEM((blocks, chunks * slots + EXTRA, LANES), BF16),
             pltpu.SemaphoreType.DMA((5 + 2 * blocks,)),
         ],
         limit=60,
@@ -586,8 +585,8 @@
         gram_kernel,
         [
             ((2 * tiles, LANES, LANES), F32),
-            ((extra_tiles * LANES, LANES), F32),
-            ((2 * tiles - width // LANES + extra_tiles, LANES, LANES), BF16),
+            ((extra_rows, LANES), F32),
+            (((2 * tiles - chunks) * LANES + extra_rows, LANES), BF16),
             row,
             (unattenuated_multiplier.shape, F32),
         ],
@@ -612,7 +611,7 @@
     pt, pthi, ptlo, chi, clo, ahead = run(
         prep_kernel, [(full, F32)] + [(full, BF16)] * 4 + [row], [propagator_matrix, analysis_cov, prior]
     )
-    smalls = pltpu.VMEM((planes + 1, extra_tiles * LANES, LANES), F32)
+    smalls = pltpu.VMEM((planes + 1, extra_rows, LANES), F32)
     omhi, omlo, info, mine, acc, y = run(
         owner_kernel,
         [((days,) + full, BF16)] * 2 + [((days, 1, width), F32), ((days, width), F32), row, row],

time: 82.2 us -> 81.6 us (level)
  no operation moved by 1% of the time
where the time goes in v15:
time: 81.6 us; the launch traced here: 81.2 us
  blocking collectives  46.5 us (57%)
  Pallas kernels  13.4 us (16%)
  starting transfers between devices  11.7 us (14%)
  waiting for transfers between devices  8.57 us (11%)
  between operations  0.94 us (1%)
    all_to_all x1, blocking collectives, local(): lax.all_to_all(answer, everyone, split_axis=0, concat_axis=0, tiled=True)  25.7 us
    all_to_all x1, blocking collectives, local(): lax.all_to_all(sent, ('y', 'obs'), split_axis=0, concat_axis=0, tiled=True)  20.8 us
    pallas_call x19, Pallas kernels, run(): pl.pallas_call(body, out_shape=[jax.ShapeDtypeStruct(s, d) for s, d in ou...  13.4 us
    ppermute x3, waiting for transfers between devices, plane_sum(): lax.ppermute(pay, everyone, [((owner_plane(p) + s) % planes * spans + pla...  5.9 us
    ppermute x3, starting transfers between devices, plane_sum(): lax.ppermute(pay, everyone, [((owner_plane(p) + s) % planes * spans + pla...  5.48 us
    ppermute x7, starting transfers between devices, local(): received = lax.ppermute(y, everyone, [(owner(k), owner(k + 1))])  4.86 us
    ppermute x2, waiting for transfers between devices, swap(): return lax.ppermute(x, 'obs', [(i, i ^ bit) for i in range(peers)])  2.66 us
  transfers between devices with their start and end apart: 13, of which 3 were waited for; matrix products, arithmetic and copies ran while one was open for 0% of the time, Pallas kernels for 8%

profile of v15, /device:TPU:0, one launch (start us, length us, event | category | flops | bytes accessed | tf_op | source)
XLA Modules:
  0.0 81.2 jit_solution(5478963870997195769)
XLA Ops:
  0.6 2.2 %shard_map.104 = bf16[8,520,128]{2,1,0:T(8,128)(2,1)} custom-call(s32[8]{0:T(128)} %day.1, s32[8]{0:T(128)} %count.1, bf16[1024,512]{1,0:T(8,128)(2,1)} %rows.1, bf16[8,128]{1,0:T(8,128)(2,1)} %bitcast.2, f32[1,128]{1,0:T(1,128)} %bitcast.3, f32[2,512]{1,0:T(2,128)} %damping.1), custom_call_target="tpu_custom_call" | custom-call | bytes 1055296 | tf_op jit(solution)/shard_map/pallas_call | solution.py:22
  2.9 20.8 %all_to_all.10.got = bf16[8,520,128]{2,1,0:T(8,128)(2,1)S(1)} all-to-all(bf16[8,520,128]{2,1,0:T(8,128)(2,1)} %shard_map.104), channel_id=1, replica_groups=mesh['z'=4,'y'=2,'obs'=4] {'y','obs'}, dimensions={0} | all-to-all | bytes 2129920 | tf_op jit(solution)/shard_map/all_to_all | solution.py:582
  23.7 1.2 %shard_map.105 = (f32[20,128,128]{2,1,0:T(8,128)S(1)}, f32[64,128]{1,0:T(8,128)S(1)}, bf16[2112,128]{1,0:T(8,128)(2,1)S(1)}, f32[1,512]{1,0:T(1,128)S(1)}, f32[128,512]{1,0:T(8,128)S(1)}) custom-call(bf16[8,520,128]{2,1,0:T(8,128)(2,1)S(1)} %all_to_all.10.got, f32[128,512]{1,0:T(8,128)S(1)} %copy-done.2), custom_call_target="tpu_custom_call" | custom-call | flops 1073741824 | bytes 1327104 | tf_op jit(solution)/shard_map/pallas_call | solution.py:22
  25.0 0.6 collective-permute-start.4
  25.6 0.7 collective-permute-start.3
  26.3 0.7 collective-permute-start.2
  27.0 4.1 %collective-permute-start.1 = (bf16[2112,128]{1,0:T(8,128)(2,1)S(1)}, bf16[2112,128]{1,0:T(8,128)(2,1)S(1)}, u32[]{:S(2)}, u32[]{:S(2)}) collective-permute-start(bf16[2112,128]{1,0:T(8,128)(2,1)S(1)} %get-tuple-element.53), channel_id=1, source_target_pairs={{0,9},{9,17},{11,19},{2,11},{6,15},{15,23},{13,21},{4,13}} | collective-permute-start | bytes 1622024 | tf_op jit(solution)/shard_map/ppermute | solution.py:601
  31.1 0.7 collective-permute-start
  31.8 1.5 %collective-permute-done.4.two = f32[128,512]{1,0:T(8,128)S(1)} collective-permute-done((f32[128,512]{1,0:T(8,128)S(1)}, f32[128,512]{1,0:T(8,128)S(1)}, u32[]{:S(2)}, u32[]{:S(2)}) %collective-permute-start.4) | collective-permute-done | bytes 262176 | tf_op jit(solution)/shard_map/ppermute | solution.py:598
  33.4 0.7 shard_map.106
  34.1 1.2 %collective-permute-done.5.got = f32[2,128,512]{2,1,0:T(8,128)S(1)} collective-permute-done((f32[2,128,512]{2,1,0:T(8,128)S(1)}, f32[2,128,512]{2,1,0:T(8,128)S(1)}, u32[]{:S(2)}, u32[]{:S(2)}) %collective-permute-start.5) | collective-permute-done | bytes 524320 | tf_op jit(solution)/shard_map/ppermute | solution.py:598
  35.6 5.9 %collective-permute-done.1.g3 = bf16[2112,128]{1,0:T(8,128)(2,1)S(1)} collective-permute-done((bf16[2112,128]{1,0:T(8,128)(2,1)S(1)}, bf16[2112,128]{1,0:T(8,128)(2,1)S(1)}, u32[]{:S(2)}, u32[]{:S(2)}) %collective-permute-start.1) | collective-permute-done | bytes 540704 | tf_op jit(solution)/shard_map/ppermute | solution.py:601
  41.5 0.9 %shard_map.109 = (bf16[2,512,512]{2,1,0:T(8,128)(2,1)S(1)}, bf16[2,512,512]{2,1,0:T(8,128)(2,1)S(1)}, f32[2,1,512]{2,1,0:T(1,128)S(1)}, f32[2,512]{1,0:T(2,128)S...) custom-call(f32[20,128,128]{2,1,0:T(8,128)S(1)} %get-tuple-element.51.own, f32[64,128]{1,0:T(8,128)S(1)} %get-tuple-element.52.extra, ...), custom_call_target="tpu_custom_call" | custom-call | bytes 6131712 | tf_op jit(solution)/shard_map/pallas_call | solution.py:22
  42.4 0.7 collective-permute-start.6
  43.2 0.7 collective-permute-start.7
  43.8 4.0 %shard_map.112 = (bf16[512,512]{1,0:T(8,128)(2,1)S(1)}, bf16[512,512]{1,0:T(8,128)(2,1)S(1)}, f32[8,512]{1,0:T(8,128)S(1)}, bf16[512,512]{1,0:T(8,128)(2,1)S(1)}, bf16[512,512]{1,0:T(8,128)(2,1)S(1)}) custom-call(f32[1,512]{1,0:T(1,128)S(1)} %get-tuple-element.74.after, ...), custom_call_target="tpu_custom_call", output_to_operand_aliasing={{0}: (10, {}), {1}: (11, {}), {2}: (12, {})} | custom-call | flops 3221225472 | bytes 6318080 | tf_op jit(solution)/shard_map/pallas_call | solution.py:22
  47.9 1.1 %shard_map.113 = (bf16[512,512]{1,0:T(8,128)(2,1)S(1)}, bf16[512,512]{1,0:T(8,128)(2,1)S(1)}, f32[1,512]{1,0:T(1,128)S(1)}) custom-call(f32[1,512]{1,0:T(1,128)S(1)} %get-tuple-element.74.after, bf16[512,512]{1,0:T(8,128)(2,1)S(1)} %get-tuple-element.75.b1hi, bf16[512,512]{1,0:T(8,128)(2,1)S(1)} %get-tuple-element.76.b1lo, ...), custom_call_target="tpu_custom_call" | custom-call | bytes 2115584 | tf_op jit(solution)/shard_map/pallas_call | solution.py:22
  49.3 0.7 collective-permute-start.8
  50.2 0.7 collective-permute-start.9
  51.1 0.7 collective-permute-start.10
  52.1 0.7 collective-permute-start.11
  53.0 0.7 collective-permute-start.12
  53.7 1.2 %shard_map.121 = f32[32,8,128]{2,1,0:T(8,128)S(1)} custom-call(f32[1,512]{1,0:T(1,128)S(1)} %get-tuple-element.94.acc, f32[1,512]{1,0:T(1,128)S(1)} %collective-permute-done.12.got, bf16[512,512]{1,0:T(8,128)(2,1)S(1)} %get-tuple-element.75.b1hi, bf16[512,512]{1,0:T(8,128)(2,1)S(1)} %get-tuple-element.76.b1lo, bf16[512,512]{1,0:T(8,128)(2,1)S(1)} %get-tuple-element.77.b2hi, ...), custom_call_target="tpu_custom_call" | custom-call | bytes 13703168 | tf_op jit(solution)/shard_map/pallas_call | solution.py:22
  54.9 25.7 %all_to_all.11.parts = f32[32,8,128]{2,1,0:T(8,128)S(1)} all-to-all(f32[32,8,128]{2,1,0:T(8,128)S(1)} %shard_map.121), channel_id=1, replica_groups=mesh['z'=4,'y'=2,'obs'=4] {'z','y','obs'}, dimensions={0} | all-to-all | bytes 262144 | tf_op jit(solution)/shard_map/all_to_all | solution.py:667
  (29 shorter events, 2.2 us)
Async XLA Ops:
  2.9 20.9 %copy-start.2 = (f32[128,512]{1,0:T(8,128)S(1)}, f32[128,512]{1,0:T(8,128)}, u32[]{:S(2)}) copy-start(f32[128,512]{1,0:T(8,128)} %gain.1) | copy-start | bytes 786436
  23.7 9.7 %copy-start.1 = (f32[512,512]{1,0:T(8,128)S(1)}, f32[512,512]{1,0:T(8,128)}, u32[]{:S(2)}) copy-start(f32[512,512]{1,0:T(8,128)} %cov.1) | copy-start | bytes 3145732
  24.9 8.4 %copy-start = (f32[512,512]{1,0:T(8,128)S(1)}, f32[512,512]{1,0:T(8,128)}, u32[]{:S(2)}) copy-start(f32[512,512]{1,0:T(8,128)} %trans.1) | copy-start | bytes 3145732
  25.0 8.3 %collective-permute-start.4 = (f32[128,512]{1,0:T(8,128)S(1)}, f32[128,512]{1,0:T(8,128)S(1)}, u32[]{:S(2)}, u32[]{:S(2)}) collective-permute-start(f32[128,512]{1,0:T(8,128)S(1)} %get-tuple-element.60.one), channel_id=1, source_target_pairs={{0,2},{1,3},{2,0},{3,1},{4,6},{5,7},{6,4},{7,5},{8,10},{9,11},{10,... | collective-permute-start | bytes 786440 | tf_op jit(solution)/shard_map/ppermute | solution.py:598
  25.6 10.0 %collective-permute-start.3 = (bf16[2112,128]{1,0:T(8,128)(2,1)S(1)}, bf16[2112,128]{1,0:T(8,128)(2,1)S(1)}, u32[]{:S(2)}, u32[]{:S(2)}) collective-permute-start(bf16[2112,128]{1,0:T(8,128)(2,1)S(1)} %get-tuple-element.53), channel_id=1, source_target_pairs={{24,9},{1,17},{3,19},{26,11},{30,15},{7,23},{5,21},{28,13}} | collective-permute-start | bytes 1622024 | tf_op jit(solution)/shard_map/ppermute | solution.py:601
  26.3 9.4 %collective-permute-start.2 = (bf16[2112,128]{1,0:T(8,128)(2,1)S(1)}, bf16[2112,128]{1,0:T(8,128)(2,1)S(1)}, u32[]{:S(2)}, u32[]{:S(2)}) collective-permute-start(bf16[2112,128]{1,0:T(8,128)(2,1)S(1)} %get-tuple-element.53), channel_id=1, source_target_pairs={{16,9},{25,17},{27,19},{18,11},{22,15},{31,23},{29,21},{20,13}} | collective-permute-start | bytes 1622024 | tf_op jit(solution)/shard_map/ppermute | solution.py:601
  27.0 14.6 %collective-permute-start.1 = (bf16[2112,128]{1,0:T(8,128)(2,1)S(1)}, bf16[2112,128]{1,0:T(8,128)(2,1)S(1)}, u32[]{:S(2)}, u32[]{:S(2)}) collective-permute-start(bf16[2112,128]{1,0:T(8,128)(2,1)S(1)} %get-tuple-element.53), channel_id=1, source_target_pairs={{0,9},{9,17},{11,19},{2,11},{6,15},{15,23},{13,21},{4,13}} | collective-permute-start | bytes 1622024 | tf_op jit(solution)/shard_map/ppermute | solution.py:601
  31.1 10.5 %collective-permute-start = (bf16[2112,128]{1,0:T(8,128)(2,1)S(1)}, bf16[2112,128]{1,0:T(8,128)(2,1)S(1)}, u32[]{:S(2)}, u32[]{:S(2)}) collective-permute-start(bf16[2112,128]{1,0:T(8,128)(2,1)S(1)} %get-tuple-element.53), channel_id=1, source_target_pairs={{8,9},{10,11},{14,15},{12,13}} | collective-permute-start | bytes 1622024 | tf_op jit(solution)/shard_map/ppermute | solution.py:605
  33.3 2.0 %collective-permute-start.5 = (f32[2,128,512]{2,1,0:T(8,128)S(1)}, f32[2,128,512]{2,1,0:T(8,128)S(1)}, u32[]{:S(2)}, u32[]{:S(2)}) collective-permute-start(f32[2,128,512]{2,1,0:T(8,128)S(1)} %shard_map.107.held), channel_id=1, source_target_pairs={{0,1},{1,0},{2,3},{3,2},{4,5},{5,4},{6,7},{7,6},{8,9},{9,8},{10,11... | collective-permute-start | bytes 1572872 | tf_op jit(solution)/shard_map/ppermute | solution.py:598
  42.4 0.7 collective-permute-start.6
  43.2 5.9 %collective-permute-start.7 = (f32[1,512]{1,0:T(1,128)S(1)}, f32[1,512]{1,0:T(1,128)S(1)}, u32[]{:S(2)}, u32[]{:S(2)}) collective-permute-start(f32[1,512]{1,0:T(1,128)S(1)} %get-tuple-element.74.after), channel_id=1, source_target_pairs={{17,19}} | collective-permute-start | bytes 6152 | tf_op jit(solution)/shard_map/ppermute | solution.py:624
  49.3 0.7 collective-permute-start.8
  50.2 0.7 collective-permute-start.9
  51.1 0.7 collective-permute-start.10
  52.1 0.7 collective-permute-start.11
  53.0 0.7 collective-permute-start.12

commit v16 on v15

--- a/solution.py
+++ b/solution.py
@@ -41,8 +41,13 @@
     for bit in range(1, spans.bit_length()):
         span = span ^ (seat >> bit)
     c = z * held + y
-    seat = c ^ (c >> 1)
+    kept = jnp.where((c == spans - 3) | (c == spans - 1), c - 1, c)
+    seat = kept ^ (kept >> 1)
     return z, span, o, c, (1 + (seat & 1)) * spans + (seat | 1), held
+
+
+def doubled(span, spans):
+    return (span == spans - 4) | (span == spans - 2)
 
 
 def triangle(width):
@@ -247,11 +252,13 @@
 
 
 def few(x, hi, lo):
+    n = x.shape[0]
     top = x.astype(BF16).astype(F32)
-    both = jnp.concatenate([top, x - top, jnp.zeros((4, x.shape[1]), F32)], 0).astype(BF16)
+    blank = [jnp.zeros((8 - 2 * n, x.shape[1]), F32)] if n < 4 else []
+    both = jnp.concatenate([top, x - top] + blank, 0).astype(BF16)
     first = jnp.dot(both, hi, preferred_element_type=F32)
     second = jnp.dot(both, lo, preferred_element_type=F32)
-    return first[0:2] + (first[2:4] + second[0:2])
+    return first[0:n] + (first[n : 2 * n] + second[0:n])
 
 
 def one_day(day, ahead, damping, omhi, omlo, info, chi, clo):
@@ -285,6 +292,94 @@
                 )
 
 
+def sums(extra, got, small):
+    share = jnp.where(here()[0] == 2, 1.0, 0.0)
+    spread(extra, got, small)
+
+    def summed(first):
+        others = line_of(small, 1, first) + line_of(small, 2, first) + (line_of(small, 3, first) + line_of(small, 4, first))
+        return line_of(small, 0, first) * share + others
+
+    def added(n):
+        at = slice(n * LANES, (n + 1) * LANES)
+        one, two, three, four = (part[at].astype(F32) for part in got)
+        return (one + two) + (three + four)
+
+    return share, summed, added
+
+
+def relay_kernel(after, own, extra, g4, g3, g1, g2, out, small, rows):
+    span = here()[1]
+    spans = lax.axis_size("z") * lax.axis_size("y")
+    chunks = 4
+    tiles = triangle(chunks * LANES)
+    row = lax.broadcasted_iota(jnp.int32, (LANES, LANES), 0)
+    column = lax.broadcasted_iota(jnp.int32, (LANES, LANES), 1)
+    sides = [n for n, (i, j) in enumerate(tiles) if i != j]
+    middles = [n for n, (i, j) in enumerate(tiles) if i == j]
+
+    @pl.when((span == spans - 3) | (span == spans - 1))
+    def _():
+        share, summed, added = sums(extra, (g1, g2, g3, g4), small)
+
+        def send(n, piece):
+            out[n * LANES : (n + 1) * LANES, :] = (piece * share + added(n)).astype(BF16)
+
+        for d in range(2):
+            for m, n in enumerate(sides):
+                send(d * len(sides) + m, own[d * len(tiles) + n])
+        for i, n in enumerate(middles):
+            send(2 * len(sides) + i, jnp.where(row >= column, own[n], own[len(tiles) + n]))
+        rows[...] = jnp.zeros(rows.shape, F32)
+        for first in (0, 8, DIAG, DIAG + 8):
+            for j in range(chunks):
+                for part, piece in enumerate(parts(summed(first + j))):
+                    r = first + 4 * part + j
+                    rows[r : r + 1, :] = piece
+        out[out.shape[0] - rows.shape[0] :, :] = rows[...].astype(BF16)
+
+
+def next_kernel(after, relay, chi, clo, zhi, zlo, off, whole, rows):
+    spans = lax.axis_size("z") * lax.axis_size("y")
+    width = whole.shape[0]
+    chunks = width // LANES
+    tiles = triangle(width)
+    row = lax.broadcasted_iota(jnp.int32, (LANES, LANES), 0)
+    column = lax.broadcasted_iota(jnp.int32, (LANES, LANES), 1)
+    sides = [(i, j) for i, j in tiles if i != j]
+
+    @pl.when(doubled(here()[1], spans))
+    def _():
+        rows[...] = relay[relay.shape[0] - rows.shape[0] :, :].astype(F32)
+
+        def line(r):
+            return rows[r : r + 1, :] + rows[r + 4 : r + 5, :]
+
+        def tile(n):
+            return relay[n * LANES : (n + 1) * LANES, :].astype(F32)
+
+        def put(i, j, piece):
+            whole[i * LANES : (i + 1) * LANES, j * LANES : (j + 1) * LANES] = piece
+
+        for day in range(2):
+            for i in range(chunks):
+                both = tile(2 * len(sides) + i)
+                part = jnp.where(row < column if day else row > column, both, 0.0)
+                put(i, i, part + part.T + jnp.where(row == column, line(DIAG + 8 * day + i), 0.0))
+            for m, (i, j) in enumerate(sides):
+                piece = tile(day * len(sides) + m)
+                put(i, j, piece)
+                put(j, i, piece.T)
+            zhi[day], zlo[day] = split(mm(whole[...], chi[...], clo[...]))
+            info = jnp.concatenate([line(8 * day + j) for j in range(chunks)], 1)
+            off[day : day + 1, :] = mv(info, chi[...], clo[...])
+
+
+def next_day(day, state, damping, pthi, ptlo, zhi, zlo, off):
+    moved = mv(state, pthi[...], ptlo[...]) * damping
+    return moved - mv(moved, zhi[day], zlo[day]) + off[day : day + 1, :]
+
+
 def owner_kernel(
     own, extra, g4, g3, g1, g2, prior, ahead, pthi, ptlo, chi, clo, after, omhi, omlo, info, mine, start, y, small
 ):
@@ -294,18 +389,9 @@
     chunks = width // LANES
     tiles = triangle(width)
     got = (g1, g2, g3, g4)
-    share = jnp.where(ids[0] == 2, 1.0, 0.0)
     row = lax.broadcasted_iota(jnp.int32, (LANES, LANES), 0)
     column = lax.broadcasted_iota(jnp.int32, (LANES, LANES), 1)
-    spread(extra, got, small)
-
-    def summed(first):
-        others = line_of(small, 1, first) + line_of(small, 2, first) + (line_of(small, 3, first) + line_of(small, 4, first))
-        return line_of(small, 0, first) * share + others
-
-    def added(n):
-        at = slice(n * LANES, (n + 1) * LANES)
-        return (g1[at].astype(F32) + g2[at].astype(F32)) + (g3[at].astype(F32) + g4[at].astype(F32))
+    share, summed, added = sums(extra, got, small)
 
     def put(day, i, j, piece):
         hi, lo = split(piece)
@@ -372,9 +458,11 @@
 def maps_kernel(
     after, omhi, omlo, info, chi, clo, pt, damping, zhi, zlo, old1, old2, old3, b1hi, b1lo, off, b2hi, b2lo
 ):
-    second = here()[1] == 1
-
-    @pl.when(jnp.logical_not(second))
+    span = here()[1]
+    spans = lax.axis_size("z") * lax.axis_size("y")
+    second = span == 1
+
+    @pl.when(jnp.logical_not(second | (span == spans - 3) | (span == spans - 1)))
     def _():
         parts = ((b1hi, b1lo), (b2hi, b2lo))
         for day in range(2):
@@ -416,45 +504,51 @@
     y[...] = mv(state, bchi[...], bclo[...]) + offset[...]
 
 
+def days_kernel(acc, got, b1hi, b1lo, b2hi, b2lo, off, total, y):
+    state = acc[...] + got[...]
+    total[...] = state
+    state = mv(state, b1hi[...], b1lo[...]) + off[0:1, :]
+    y[...] = mv(state, b2hi[...], b2lo[...]) + off[1:2, :]
+
+
+def double_kernel(after, acc, got, bchi, bclo, offset, table, pthi, ptlo, zhi, zlo, off, total, y):
+    spans = table.shape[0] // 2
+    total[...] = acc[...] + got[...]
+    y[...] = jnp.zeros(y.shape, F32)
+
+    @pl.when(here()[1] == spans - 4)
+    def _():
+        state = mv(acc[...] + got[...], bchi[...], bclo[...]) + offset[...]
+        for day in range(2):
+            r = 2 * (spans - 3) + day
+            state = next_day(day, state, table[r : r + 1, :], pthi, ptlo, zhi, zlo, off)
+        y[...] = state
+
+
 def whole_of(hi, lo):
     return hi[...].astype(F32) + lo[...].astype(F32)
 
 
-def pairs_kernel(
-    after, b1hi, b1lo, bchi, bclo, off, offset, table, pthi, ptlo, mthi, mtlo, khi, klo, ehi, elo, shift
-):
-    total = table.shape[0]
-    spans = total // 2
-
-    span = here()[1]
-
-    @pl.when(span >= spans - 2)
-    def _():
-        @pl.loop(spans - 1 - span, khi.shape[0])
+def pairs_kernel(after, table, mthi, mtlo, khi, klo):
+    spans = table.shape[0] // 2
+
+    @pl.when(here()[1] == spans - 2)
+    def _():
+        @pl.loop(0, khi.shape[0])
         def _(k):
-            scaled = whole_of(mthi, mtlo) * table[pl.ds(2 * (spans - 2 - k) + 1, 1), :]
+            scaled = whole_of(mthi, mtlo) * table[pl.ds(2 * (spans - 3 - k) + 1, 1), :]
             khi[k], klo[k] = split(mm(scaled, mthi[...], mtlo[...]))
-
-    @pl.when(span == spans - 1)
-    def _():
-        within = table[total - 1 : total, :]
-        one = off[0:1, :]
-        ahead = mv(one, pthi[...], ptlo[...]) * (within * within)
-        shift[0:1, :] = one + mv(offset[...] * within - ahead, mthi[...], mtlo[...])
-        whole = whole_of(b1hi, b1lo)
-        ahead = mm(whole, pthi[...], ptlo[...]) * (within * within)
-        moved = whole_of(bchi, bclo) * within - ahead
-        ehi[...], elo[...] = split(whole + mm(moved, mthi[...], mtlo[...]))
 
 
 def last_kernel(
     acc, got, b1hi, b1lo, b2hi, b2lo, bchi, bclo, off, offset, table, pthi, ptlo, mthi, mtlo,
-    khi, klo, ehi, elo, shift, out, shares, means,
+    zhi, zlo, next_off, khi, klo, out, shares, means,
 ):
     span = here()[1]
     total, width = shares.shape
     spans = total // 2
     chunks = width // LANES
+    twice = doubled(span, spans)
     shares[...] = jnp.zeros(shares.shape, F32)
 
     def step(k, v):
@@ -463,53 +557,59 @@
         shares[pl.ds(t, 1), :] = v
         return v
 
-    @pl.when(span < spans - 1)
+    def own_days(rows, damped):
+        both = jnp.concatenate(rows, 0)
+        ahead = jnp.concatenate(damped, 0)
+        const = both - few(few(both, pthi[...], ptlo[...]) * ahead * ahead, mthi[...], mtlo[...])
+        n = len(rows)
+        means[0:n, :] = both
+        v = const[n - 1 : n]
+        shares[pl.ds(2 * span + n - 1, 1), :] = v
+        for i in range(n - 2, -1, -1):
+            v = const[i : i + 1] + mv(v * damped[i], mthi[...], mtlo[...])
+            shares[pl.ds(2 * span + i, 1), :] = v
+        means[4:5, :] = v
+
+    @pl.when(span < spans - 4)
     def _():
         state = acc[...] + got[...]
         one = mv(state, b1hi[...], b1lo[...]) + off[0:1, :]
         two = mv(one, b2hi[...], b2lo[...]) + off[1:2, :]
-        both = jnp.concatenate([one, two], 0)
-        within = table[pl.ds(2 * span + 1, 1), :]
-        damped = jnp.concatenate([within, table[pl.ds(2 * span + 2, 1), :]], 0)
-        const = both - few(few(both, pthi[...], ptlo[...]) * damped * damped, mthi[...], mtlo[...])
-        even = const[0:1] + mv(const[1:2] * within, mthi[...], mtlo[...])
-        shares[pl.ds(2 * span + 1, 1), :] = const[1:2]
-        shares[pl.ds(2 * span, 1), :] = even
-        means[0:2, :] = both
-        means[2:3, :] = even
-
-    def descend(v, start):
-        damped_rows, days = [], range(start, khi.shape[0])
-        for k in days:
-            t = 2 * (spans - 1 - k)
+        own_days([one, two], [table[pl.ds(2 * span + 1 + i, 1), :] for i in range(2)])
+
+    @pl.when(twice)
+    def _():
+        state = acc[...] + got[...]
+        rows = [
+            mv(state, b1hi[...], b1lo[...]) + off[0:1, :],
+            mv(state, bchi[...], bclo[...]) + offset[...],
+        ]
+        for day in range(2):
+            damping = table[pl.ds(2 * span + 2 + day, 1), :]
+            rows.append(next_day(day, rows[-1], damping, pthi, ptlo, zhi, zlo, next_off))
+        damped = [table[pl.ds(2 * span + 1 + i, 1), :] for i in range(3)]
+        beyond = table[pl.ds(jnp.minimum(2 * span + 4, total - 1), 1), :]
+        damped.append(beyond * jnp.where(span == spans - 2, 0.0, 1.0))
+        own_days(rows, damped)
+
+    @pl.when(span < spans - 2)
+    def _():
+        lax.fori_loop(0, jnp.where((span < spans - 4) | twice, 2 * span, 0), step, means[4:5, :])
+
+    @pl.when(span == spans - 2)
+    def _():
+        v, damped_rows = means[4:5, :], []
+        for k in range(khi.shape[0]):
+            t = 2 * (spans - 2 - k)
             damped_rows.append(v * table[t : t + 1, :])
             v = mv(damped_rows[-1], khi[k], klo[k])
             shares[t - 2 : t - 1, :] = v
         batch = jnp.concatenate(damped_rows + [jnp.zeros((1, width), F32)] * (-len(damped_rows) % 8), 0)
         batch = mm(batch, mthi[...], mtlo[...])
-        for n, k in enumerate(days):
-            t = 2 * (spans - 1 - k)
-            shares[t - 1 : t, :] = batch[n : n + 1]
-        lax.fori_loop(2 * len(days), 2 * span, step, v)
-
-    @pl.when(span < spans - 2)
-    def _():
-        lax.fori_loop(0, 2 * span, step, means[2:3, :])
-
-    @pl.when(span == spans - 2)
-    def _():
-        descend(means[2:3, :], 1)
-
-    @pl.when(span == spans - 1)
-    def _():
-        state = acc[...] + got[...]
-        v = mv(state, ehi[...], elo[...]) + shift[0:1, :]
-        shares[total - 2 : total - 1, :] = v
-        descend(v, 0)
-        two = mv(state, bchi[...], bclo[...]) + offset[...]
-        means[0:1, :] = mv(state, b1hi[...], b1lo[...]) + off[0:1, :]
-        means[1:2, :] = two
-        shares[total - 1 : total, :] = two
+        for k in range(khi.shape[0]):
+            t = 2 * (spans - 2 - k)
+            shares[t - 1 : t, :] = batch[k : k + 1]
+        lax.fori_loop(2 * khi.shape[0], 2 * span, step, v)
 
     for c in range(spans):
         for q in range(chunks):
@@ -517,12 +617,17 @@
     for q in range(chunks):
         out[span * chunks + q, 2:4, :] = means[0:2, q * LANES : (q + 1) * LANES]
 
+    @pl.when(twice)
+    def _():
+        for q in range(chunks):
+            out[(span + 1) * chunks + q, 2:4, :] = means[2:4, q * LANES : (q + 1) * LANES]
+
 
 def add_kernel(parts, filt, smooth):
-    ids = here()
     spans = parts.shape[0] // 4
-    filt[...] = parts[ids[4], 2:4, :]
-    smooth[...] = sum(parts[owner_plane(c) * spans + (place(c) | 1), 0:2, :] for c in range(spans))
+    owners = [*range(spans - 4), spans - 4, spans - 2]
+    filt[...] = parts[here()[4], 2:4, :]
+    smooth[...] = sum(parts[owner_plane(c) * spans + (place(c) | 1), 0:2, :] for c in owners)
 
 
 def local(
@@ -620,11 +725,21 @@
         ],
         [smalls],
     )
-    for k in range(spans - 1):
-        received = lax.ppermute(y, everyone, [(owner(k), owner(k + 1))])
+    (packed,) = run(
+        relay_kernel,
+        [(pay.shape, BF16)],
+        [(y, ANY), own, extra, fourth, third, first, second],
+        [smalls, pltpu.VMEM((extra_rows, LANES), F32)],
+    )
+    relay = lax.ppermute(
+        packed, everyone, [(owner(p + 1), owner(p)) for p in (spans - 4, spans - 2)]
+    )
+    chain = [*range(spans - 3), spans - 2]
+    half = [(full, BF16)] * 2
+    for k, (source, target) in enumerate(zip(chain, chain[1:])):
+        received = lax.ppermute(y, everyone, [(owner(source), owner(target))])
         if k == 0:
             given = [omhi, omlo, info, chi, clo, pt, mine]
-            half = [(full, BF16)] * 2
             b1hi, b1lo, off, zhi, zlo = run(
                 early_kernel, half + [((8, width), F32)] + half, [(y, ANY), *given], flops=18 * width**3
             )
@@ -638,8 +753,10 @@
                 flops=24 * width**3,
                 same={10: 0, 11: 1, 12: 2},
             )
+        elif k == 1:
+            acc, y = run(days_kernel, [row, row], [acc, received, b1hi, b1lo, b2hi, b2lo, off])
             bchi, bclo, offset = run(
-                both_kernel, [(full, BF16)] * 2 + [row], [(y, ANY), b1hi, b1lo, b2hi, b2lo, off]
+                both_kernel, half + [row], [(y, ANY), b1hi, b1lo, b2hi, b2lo, off]
             )
             (table,) = run(
                 table_kernel,
@@ -647,20 +764,31 @@
                 [(offset, ANY), extra, first, second, third],
                 [smalls],
             )
-            ahead = run(
-                pairs_kernel,
-                [((min(spans - 1, 7),) + full, BF16)] * 2 + [(full, BF16)] * 2 + [((8, width), F32)],
-                [(y, ANY), b1hi, b1lo, bchi, bclo, off, offset, table, pthi, ptlo, mthi, mtlo],
-            )
-            side = ahead[0]
-        elif k < spans - 2:
-            acc, y = run(hop_kernel, [row, row], [(side, ANY), acc, received, bchi, bclo, offset])
+            khi, klo = run(
+                pairs_kernel, [((min(spans - 2, 5),) + full, BF16)] * 2, [(y, ANY), table, mthi, mtlo]
+            )
+            nexthi, nextlo, next_off = run(
+                next_kernel,
+                [((days,) + full, BF16)] * 2 + [((8, width), F32)],
+                [(khi, ANY), relay, chi, clo],
+                [pltpu.VMEM(full, F32), pltpu.VMEM((extra_rows, LANES), F32)],
+            )
+        elif target == spans - 4:
+            acc, y = run(
+                double_kernel,
+                [row, row],
+                [
+                    (nexthi, ANY), acc, received, bchi, bclo, offset, table, pthi, ptlo, nexthi, nextlo, next_off
+                ],
+            )
+        elif target != spans - 2:
+            acc, y = run(hop_kernel, [row, row], [(nexthi, ANY), acc, received, bchi, bclo, offset])
     (answer,) = run(
         last_kernel,
         [((spans * peers, 8, LANES), F32)],
         [
             acc, received, b1hi, b1lo, b2hi, b2lo, bchi, bclo, off, offset, table, pthi, ptlo, mthi, mtlo,
-            *ahead,
+            nexthi, nextlo, next_off, khi, klo,
         ],
         [pltpu.VMEM((spans * days, width), F32), pltpu.VMEM((8, width), F32)],
     )

time: 81.6 us -> 81.5 us (level)
  blocking collectives: 46.5 us -> 47.5 us
    all_to_all x1, blocking collectives: 25.7 us -> 26.6 us  [local(): lax.all_to_all(answer, everyone, split_axis=0, concat_axis=0, tiled=True)]
    ppermute x7 -> x6, starting transfers between devices: 4.86 us -> 4.05 us  [the longest x5 3.35 us: local(): received = lax.ppermute(y, everyone, [(owner(source), owner(target))])]
  transfers between devices with their start and end apart: 13 -> 12, of which waited for: 3 -> 3; matrix products, arithmetic and copies ran while one was open for 0% -> 0% of each run, Pallas kernels for 8% -> 8%
where the time goes in v16:
time: 81.5 us; the launch traced here: 81.2 us
  blocking collectives  47.5 us (58%)
  Pallas kernels  13.3 us (16%)
  starting transfers between devices  10.9 us (13%)
  waiting for transfers between devices  8.57 us (11%)
  between operations  0.95 us (1%)
    all_to_all x1, blocking collectives, local(): lax.all_to_all(answer, everyone, split_axis=0, concat_axis=0, tiled=True)  26.6 us
    all_to_all x1, blocking collectives, local(): lax.all_to_all(sent, ('y', 'obs'), split_axis=0, concat_axis=0, tiled=True)  20.8 us
    pallas_call x19, Pallas kernels, run(): pl.pallas_call(body, out_shape=[jax.ShapeDtypeStruct(s, d) for s, d in ou...  13.3 us
    ppermute x3, waiting for transfers between devices, plane_sum(): lax.ppermute(pay, everyone, [((owner_plane(p) + s) % planes * spans + pla...  5.91 us
    ppermute x3, starting transfers between devices, plane_sum(): lax.ppermute(pay, everyone, [((owner_plane(p) + s) % planes * spans + pla...  5.48 us
    ppermute x5, starting transfers between devices, local(): received = lax.ppermute(y, everyone, [(owner(source), owner(target))])  3.35 us
    ppermute x2, waiting for transfers between devices, swap(): return lax.ppermute(x, 'obs', [(i, i ^ bit) for i in range(peers)])  2.65 us
  transfers between devices with their start and end apart: 12, of which 3 were waited for; matrix products, arithmetic and copies ran while one was open for 0% of the time, Pallas kernels for 8%

profile of v16, /device:TPU:0, one launch (start us, length us, event | category | flops | bytes accessed | tf_op | source)
XLA Modules:
  0.0 81.2 jit_solution(16689749415469709773)
XLA Ops:
  0.6 2.2 %shard_map.104 = bf16[8,520,128]{2,1,0:T(8,128)(2,1)} custom-call(s32[8]{0:T(128)} %day.1, s32[8]{0:T(128)} %count.1, bf16[1024,512]{1,0:T(8,128)(2,1)} %rows.1, bf16[8,128]{1,0:T(8,128)(2,1)} %bitcast.2, f32[1,128]{1,0:T(1,128)} %bitcast.3, f32[2,512]{1,0:T(2,128)} %damping.1), custom_call_target="tpu_custom_call" | custom-call | bytes 1055296 | tf_op jit(solution)/shard_map/pallas_call | solution.py:22
  2.9 20.8 %all_to_all.10.got = bf16[8,520,128]{2,1,0:T(8,128)(2,1)S(1)} all-to-all(bf16[8,520,128]{2,1,0:T(8,128)(2,1)} %shard_map.104), channel_id=1, replica_groups=mesh['z'=4,'y'=2,'obs'=4] {'y','obs'}, dimensions={0} | all-to-all | bytes 2129920 | tf_op jit(solution)/shard_map/all_to_all | solution.py:687
  23.7 1.2 %shard_map.105 = (f32[20,128,128]{2,1,0:T(8,128)S(1)}, f32[64,128]{1,0:T(8,128)S(1)}, bf16[2112,128]{1,0:T(8,128)(2,1)S(1)}, f32[1,512]{1,0:T(1,128)S(1)}, f32[128,512]{1,0:T(8,128)S(1)}) custom-call(bf16[8,520,128]{2,1,0:T(8,128)(2,1)S(1)} %all_to_all.10.got, f32[128,512]{1,0:T(8,128)S(1)} %copy-done.2), custom_call_target="tpu_custom_call" | custom-call | flops 1073741824 | bytes 1327104 | tf_op jit(solution)/shard_map/pallas_call | solution.py:22
  25.0 0.6 collective-permute-start.4
  25.6 0.7 collective-permute-start.3
  26.3 0.7 collective-permute-start.2
  27.0 4.1 %collective-permute-start.1 = (bf16[2112,128]{1,0:T(8,128)(2,1)S(1)}, bf16[2112,128]{1,0:T(8,128)(2,1)S(1)}, u32[]{:S(2)}, u32[]{:S(2)}) collective-permute-start(bf16[2112,128]{1,0:T(8,128)(2,1)S(1)} %get-tuple-element.49), channel_id=1, source_target_pairs={{0,9},{9,17},{11,19},{2,11},{6,15},{15,23},{13,21},{4,13}} | collective-permute-start | bytes 1622024 | tf_op jit(solution)/shard_map/ppermute | solution.py:706
  31.1 0.7 collective-permute-start
  31.8 1.5 %collective-permute-done.4.two = f32[128,512]{1,0:T(8,128)S(1)} collective-permute-done((f32[128,512]{1,0:T(8,128)S(1)}, f32[128,512]{1,0:T(8,128)S(1)}, u32[]{:S(2)}, u32[]{:S(2)}) %collective-permute-start.4) | collective-permute-done | bytes 262176 | tf_op jit(solution)/shard_map/ppermute | solution.py:703
  33.4 0.7 shard_map.106
  34.1 1.2 %collective-permute-done.5.got = f32[2,128,512]{2,1,0:T(8,128)S(1)} collective-permute-done((f32[2,128,512]{2,1,0:T(8,128)S(1)}, f32[2,128,512]{2,1,0:T(8,128)S(1)}, u32[]{:S(2)}, u32[]{:S(2)}) %collective-permute-start.5) | collective-permute-done | bytes 524320 | tf_op jit(solution)/shard_map/ppermute | solution.py:703
  35.6 5.9 %collective-permute-done.1.g3 = bf16[2112,128]{1,0:T(8,128)(2,1)S(1)} collective-permute-done((bf16[2112,128]{1,0:T(8,128)(2,1)S(1)}, bf16[2112,128]{1,0:T(8,128)(2,1)S(1)}, u32[]{:S(2)}, u32[]{:S(2)}) %collective-permute-start.1) | collective-permute-done | bytes 540704 | tf_op jit(solution)/shard_map/ppermute | solution.py:706
  41.6 0.9 %shard_map.109 = (bf16[2,512,512]{2,1,0:T(8,128)(2,1)S(1)}, bf16[2,512,512]{2,1,0:T(8,128)(2,1)S(1)}, f32[2,1,512]{2,1,0:T(1,128)S(1)}, f32[2,512]{1,0:T(2,128)S...) custom-call(f32[20,128,128]{2,1,0:T(8,128)S(1)} %get-tuple-element.47.own, f32[64,128]{1,0:T(8,128)S(1)} %get-tuple-element.48.extra, ...), custom_call_target="tpu_custom_call" | custom-call | bytes 6131712 | tf_op jit(solution)/shard_map/pallas_call | solution.py:22
  42.5 0.7 collective-permute-start.8
  43.2 0.7 collective-permute-start.6
  43.9 0.7 collective-permute-start.7
  44.6 4.1 %shard_map.112 = (bf16[512,512]{1,0:T(8,128)(2,1)S(1)}, bf16[512,512]{1,0:T(8,128)(2,1)S(1)}, f32[8,512]{1,0:T(8,128)S(1)}, bf16[512,512]{1,0:T(8,128)(2,1)S(1)}, bf16[512,512]{1,0:T(8,128)(2,1)S(1)}) custom-call(f32[1,512]{1,0:T(1,128)S(1)} %get-tuple-element.71.after, ...), custom_call_target="tpu_custom_call", output_to_operand_aliasing={{0}: (10, {}), {1}: (11, {}), {2}: (12, {})} | custom-call | flops 3221225472 | bytes 6318080 | tf_op jit(solution)/shard_map/pallas_call | solution.py:22
  49.2 0.7 collective-permute-start.9
  49.9 1.1 %shard_map.114 = (bf16[512,512]{1,0:T(8,128)(2,1)S(1)}, bf16[512,512]{1,0:T(8,128)(2,1)S(1)}, f32[1,512]{1,0:T(1,128)S(1)}) custom-call(f32[1,512]{1,0:T(1,128)S(1)} %get-tuple-element.77.after, bf16[512,512]{1,0:T(8,128)(2,1)S(1)} %get-tuple-element.72.b1hi, bf16[512,512]{1,0:T(8,128)(2,1)S(1)} %get-tuple-element.73.b1lo, ...), custom_call_target="tpu_custom_call" | custom-call | bytes 2115584 | tf_op jit(solution)/shard_map/pallas_call | solution.py:22
  51.3 0.7 collective-permute-start.10
  52.1 0.7 collective-permute-start.11
  52.8 1.2 %shard_map.121 = f32[32,8,128]{2,1,0:T(8,128)S(1)} custom-call(f32[1,512]{1,0:T(1,128)S(1)} %get-tuple-element.89.acc, f32[1,512]{1,0:T(1,128)S(1)} %collective-permute-done.11.got, bf16[512,512]{1,0:T(8,128)(2,1)S(1)} %get-tuple-element.72.b1hi, bf16[512,512]{1,0:T(8,128)(2,1)S(1)} %get-tuple-element.73.b1lo, bf16[512,512]{1,0:T(8,128)(2,1)S(1)} %get-tuple-element.74.b2hi, ...), custom_call_target="tpu_custom_call" | custom-call | bytes 12654592 | tf_op jit(solution)/shard_map/pallas_call | solution.py:22
  54.0 26.6 %all_to_all.11.parts = f32[32,8,128]{2,1,0:T(8,128)S(1)} all-to-all(f32[32,8,128]{2,1,0:T(8,128)S(1)} %shard_map.121), channel_id=1, replica_groups=mesh['z'=4,'y'=2,'obs'=4] {'z','y','obs'}, dimensions={0} | all-to-all | bytes 262144 | tf_op jit(solution)/shard_map/all_to_all | solution.py:795
  80.6 0.6 shard_map.122
  (27 shorter events, 1.4 us)
Async XLA Ops:
  2.9 20.9 %copy-start.2 = (f32[128,512]{1,0:T(8,128)S(1)}, f32[128,512]{1,0:T(8,128)}, u32[]{:S(2)}) copy-start(f32[128,512]{1,0:T(8,128)} %gain.1) | copy-start | bytes 786436
  23.7 9.7 %copy-start.1 = (f32[512,512]{1,0:T(8,128)S(1)}, f32[512,512]{1,0:T(8,128)}, u32[]{:S(2)}) copy-start(f32[512,512]{1,0:T(8,128)} %cov.1) | copy-start | bytes 3145732
  25.0 8.4 %copy-start = (f32[512,512]{1,0:T(8,128)S(1)}, f32[512,512]{1,0:T(8,128)}, u32[]{:S(2)}) copy-start(f32[512,512]{1,0:T(8,128)} %trans.1) | copy-start | bytes 3145732
  25.0 8.3 %collective-permute-start.4 = (f32[128,512]{1,0:T(8,128)S(1)}, f32[128,512]{1,0:T(8,128)S(1)}, u32[]{:S(2)}, u32[]{:S(2)}) collective-permute-start(f32[128,512]{1,0:T(8,128)S(1)} %get-tuple-element.56.one), channel_id=1, source_target_pairs={{0,2},{1,3},{2,0},{3,1},{4,6},{5,7},{6,4},{7,5},{8,10},{9,11},{10,... | collective-permute-start | bytes 786440 | tf_op jit(solution)/shard_map/ppermute | solution.py:703
  25.6 10.0 %collective-permute-start.3 = (bf16[2112,128]{1,0:T(8,128)(2,1)S(1)}, bf16[2112,128]{1,0:T(8,128)(2,1)S(1)}, u32[]{:S(2)}, u32[]{:S(2)}) collective-permute-start(bf16[2112,128]{1,0:T(8,128)(2,1)S(1)} %get-tuple-element.49), channel_id=1, source_target_pairs={{24,9},{1,17},{3,19},{26,11},{30,15},{7,23},{5,21},{28,13}} | collective-permute-start | bytes 1622024 | tf_op jit(solution)/shard_map/ppermute | solution.py:706
  26.3 9.4 %collective-permute-start.2 = (bf16[2112,128]{1,0:T(8,128)(2,1)S(1)}, bf16[2112,128]{1,0:T(8,128)(2,1)S(1)}, u32[]{:S(2)}, u32[]{:S(2)}) collective-permute-start(bf16[2112,128]{1,0:T(8,128)(2,1)S(1)} %get-tuple-element.49), channel_id=1, source_target_pairs={{16,9},{25,17},{27,19},{18,11},{22,15},{31,23},{29,21},{20,13}} | collective-permute-start | bytes 1622024 | tf_op jit(solution)/shard_map/ppermute | solution.py:706
  27.0 14.6 %collective-permute-start.1 = (bf16[2112,128]{1,0:T(8,128)(2,1)S(1)}, bf16[2112,128]{1,0:T(8,128)(2,1)S(1)}, u32[]{:S(2)}, u32[]{:S(2)}) collective-permute-start(bf16[2112,128]{1,0:T(8,128)(2,1)S(1)} %get-tuple-element.49), channel_id=1, source_target_pairs={{0,9},{9,17},{11,19},{2,11},{6,15},{15,23},{13,21},{4,13}} | collective-permute-start | bytes 1622024 | tf_op jit(solution)/shard_map/ppermute | solution.py:706
  31.1 10.5 %collective-permute-start = (bf16[2112,128]{1,0:T(8,128)(2,1)S(1)}, bf16[2112,128]{1,0:T(8,128)(2,1)S(1)}, u32[]{:S(2)}, u32[]{:S(2)}) collective-permute-start(bf16[2112,128]{1,0:T(8,128)(2,1)S(1)} %get-tuple-element.49), channel_id=1, source_target_pairs={{8,9},{10,11},{14,15},{12,13}} | collective-permute-start | bytes 1622024 | tf_op jit(solution)/shard_map/ppermute | solution.py:710
  33.3 2.0 %collective-permute-start.5 = (f32[2,128,512]{2,1,0:T(8,128)S(1)}, f32[2,128,512]{2,1,0:T(8,128)S(1)}, u32[]{:S(2)}, u32[]{:S(2)}) collective-permute-start(f32[2,128,512]{2,1,0:T(8,128)S(1)} %shard_map.107.held), channel_id=1, source_target_pairs={{0,1},{1,0},{2,3},{3,2},{4,5},{5,4},{6,7},{7,6},{8,9},{9,8},{10,11... | collective-permute-start | bytes 1572872 | tf_op jit(solution)/shard_map/ppermute | solution.py:703
  42.5 8.6 %collective-permute-start.8 = (bf16[2112,128]{1,0:T(8,128)(2,1)S(1)}, bf16[2112,128]{1,0:T(8,128)(2,1)S(1)}, u32[]{:S(2)}, u32[]{:S(2)}) collective-permute-start(bf16[2112,128]{1,0:T(8,128)(2,1)S(1)} %shard_map.117), channel_id=1, source_target_pairs={{23,15},{13,21}} | collective-permute-start | bytes 1622024 | tf_op jit(solution)/shard_map/ppermute | solution.py:734
  43.2 0.7 collective-permute-start.6
  43.9 4.8 %collective-permute-start.7 = (f32[1,512]{1,0:T(1,128)S(1)}, f32[1,512]{1,0:T(1,128)S(1)}, u32[]{:S(2)}, u32[]{:S(2)}) collective-permute-start(f32[1,512]{1,0:T(1,128)S(1)} %get-tuple-element.71.after), channel_id=1, source_target_pairs={{17,19}} | collective-permute-start | bytes 6152 | tf_op jit(solution)/shard_map/ppermute | solution.py:740
  49.2 1.9 %collective-permute-start.9 = (f32[1,512]{1,0:T(1,128)S(1)}, f32[1,512]{1,0:T(1,128)S(1)}, u32[]{:S(2)}, u32[]{:S(2)}) collective-permute-start(f32[1,512]{1,0:T(1,128)S(1)} %get-tuple-element.77.after), channel_id=1, source_target_pairs={{19,11}} | collective-permute-start | bytes 6152 | tf_op jit(solution)/shard_map/ppermute | solution.py:740
  51.3 0.7 collective-permute-start.10
  52.1 0.7 collective-permute-start.11

commit v17 on v16

--- a/solution.py
+++ b/solution.py
@@ -765,15 +765,15 @@
                 [smalls],
             )
             khi, klo = run(
-                pairs_kernel, [((min(spans - 2, 5),) + full, BF16)] * 2, [(y, ANY), table, mthi, mtlo]
-            )
+                pairs_kernel, [((min(spans - 2, 4),) + full, BF16)] * 2, [(y, ANY), table, mthi, mtlo]
+            )
+        elif target == spans - 4:
             nexthi, nextlo, next_off = run(
                 next_kernel,
                 [((days,) + full, BF16)] * 2 + [((8, width), F32)],
-                [(khi, ANY), relay, chi, clo],
+                [(y, ANY), relay, chi, clo],
                 [pltpu.VMEM(full, F32), pltpu.VMEM((extra_rows, LANES), F32)],
             )
-        elif target == spans - 4:
             acc, y = run(
                 double_kernel,
                 [row, row],
@@ -782,7 +782,7 @@
                 ],
             )
         elif target != spans - 2:
-            acc, y = run(hop_kernel, [row, row], [(nexthi, ANY), acc, received, bchi, bclo, offset])
+            acc, y = run(hop_kernel, [row, row], [(khi, ANY), acc, received, bchi, bclo, offset])
     (answer,) = run(
         last_kernel,
         [((spans * peers, 8, LANES), F32)],

time: 81.5 us -> 81.6 us (level)
  blocking collectives: 47.5 us -> 51.1 us
  waiting for transfers between devices: 8.57 us -> 6.2 us
  starting transfers between devices: 10.9 us -> 9.73 us
    all_to_all x1, blocking collectives: 26.6 us -> 30.2 us  [local(): lax.all_to_all(answer, everyone, split_axis=0, concat_axis=0, tiled=True)]
    ppermute x3, waiting for transfers between devices: 5.91 us -> 2.38 us  [plane_sum(): lax.ppermute(pay, everyone, [((owner_plane(p) + s) % planes * spans + pla...]
    ppermute x3, starting transfers between devices: 5.48 us -> 4.28 us  [plane_sum(): lax.ppermute(pay, everyone, [((owner_plane(p) + s) % planes * spans + pla...]
    ppermute x2, waiting for transfers between devices: 2.65 us -> 3.81 us  [swap(): return lax.ppermute(x, 'obs', [(i, i ^ bit) for i in range(peers)])]
  transfers between devices with their start and end apart: 12 -> 12, of which waited for: 3 -> 3; matrix products, arithmetic and copies ran while one was open for 0% -> 0% of each run, Pallas kernels for 8% -> 9%
where the time goes in v17:
time: 81.6 us; the launch traced here: 81.3 us
  blocking collectives  51.1 us (63%)
  Pallas kernels  13.4 us (16%)
  starting transfers between devices  9.73 us (12%)
  waiting for transfers between devices  6.2 us (8%)
  between operations  0.94 us (1%)
    all_to_all x1, blocking collectives, local(): lax.all_to_all(answer, everyone, split_axis=0, concat_axis=0, tiled=True)  30.2 us
    all_to_all x1, blocking collectives, local(): lax.all_to_all(sent, ('y', 'obs'), split_axis=0, concat_axis=0, tiled=True)  20.8 us
    pallas_call x19, Pallas kernels, run(): pl.pallas_call(body, out_shape=[jax.ShapeDtypeStruct(s, d) for s, d in ou...  13.4 us
    ppermute x3, starting transfers between devices, plane_sum(): lax.ppermute(pay, everyone, [((owner_plane(p) + s) % planes * spans + pla...  4.28 us
    ppermute x2, waiting for transfers between devices, swap(): return lax.ppermute(x, 'obs', [(i, i ^ bit) for i in range(peers)])  3.81 us
    ppermute x5, starting transfers between devices, local(): received = lax.ppermute(y, everyone, [(owner(source), owner(target))])  3.35 us
    ppermute x3, waiting for transfers between devices, plane_sum(): lax.ppermute(pay, everyone, [((owner_plane(p) + s) % planes * spans + pla...  2.38 us
  transfers between devices with their start and end apart: 12, of which 3 were waited for; matrix products, arithmetic and copies ran while one was open for 0% of the time, Pallas kernels for 9%

profile of v17, /device:TPU:0, one launch (start us, length us, event | category | flops | bytes accessed | tf_op | source)
XLA Modules:
  0.0 81.3 jit_solution(892570114948561372)
XLA Ops:
  0.6 2.2 %shard_map.104 = bf16[8,520,128]{2,1,0:T(8,128)(2,1)} custom-call(s32[8]{0:T(128)} %day.1, s32[8]{0:T(128)} %count.1, bf16[1024,512]{1,0:T(8,128)(2,1)} %rows.1, bf16[8,128]{1,0:T(8,128)(2,1)} %bitcast.2, f32[1,128]{1,0:T(1,128)} %bitcast.3, f32[2,512]{1,0:T(2,128)} %damping.1), custom_call_target="tpu_custom_call" | custom-call | bytes 1055296 | tf_op jit(solution)/shard_map/pallas_call | solution.py:22
  2.9 20.8 %all_to_all.10.got = bf16[8,520,128]{2,1,0:T(8,128)(2,1)S(1)} all-to-all(bf16[8,520,128]{2,1,0:T(8,128)(2,1)} %shard_map.104), channel_id=1, replica_groups=mesh['z'=4,'y'=2,'obs'=4] {'y','obs'}, dimensions={0} | all-to-all | bytes 2129920 | tf_op jit(solution)/shard_map/all_to_all | solution.py:687
  23.7 1.2 %shard_map.105 = (f32[20,128,128]{2,1,0:T(8,128)S(1)}, f32[64,128]{1,0:T(8,128)S(1)}, bf16[2112,128]{1,0:T(8,128)(2,1)S(1)}, f32[1,512]{1,0:T(1,128)S(1)}, f32[128,512]{1,0:T(8,128)S(1)}) custom-call(bf16[8,520,128]{2,1,0:T(8,128)(2,1)S(1)} %all_to_all.10.got, f32[128,512]{1,0:T(8,128)S(1)} %copy-done.2), custom_call_target="tpu_custom_call" | custom-call | flops 1073741824 | bytes 1327104 | tf_op jit(solution)/shard_map/pallas_call | solution.py:22
  25.0 0.6 collective-permute-start.4
  25.6 2.9 %collective-permute-start.1 = (bf16[2112,128]{1,0:T(8,128)(2,1)S(1)}, bf16[2112,128]{1,0:T(8,128)(2,1)S(1)}, u32[]{:S(2)}, u32[]{:S(2)}) collective-permute-start(bf16[2112,128]{1,0:T(8,128)(2,1)S(1)} %get-tuple-element.49), channel_id=1, source_target_pairs={{0,9},{9,17},{11,19},{2,11},{6,15},{15,23},{13,21},{4,13}} | collective-permute-start | bytes 1622024 | tf_op jit(solution)/shard_map/ppermute | solution.py:706
  28.5 0.7 collective-permute-start.2
  29.2 0.7 collective-permute-start.3
  29.9 0.7 collective-permute-start
  30.6 2.7 %collective-permute-done.4.two = f32[128,512]{1,0:T(8,128)S(1)} collective-permute-done((f32[128,512]{1,0:T(8,128)S(1)}, f32[128,512]{1,0:T(8,128)S(1)}, u32[]{:S(2)}, u32[]{:S(2)}) %collective-permute-start.4) | collective-permute-done | bytes 262176 | tf_op jit(solution)/shard_map/ppermute | solution.py:703
  33.4 0.7 shard_map.106
  34.1 1.1 %collective-permute-done.5.got = f32[2,128,512]{2,1,0:T(8,128)S(1)} collective-permute-done((f32[2,128,512]{2,1,0:T(8,128)S(1)}, f32[2,128,512]{2,1,0:T(8,128)S(1)}, u32[]{:S(2)}, u32[]{:S(2)}) %collective-permute-start.5) | collective-permute-done | bytes 524320 | tf_op jit(solution)/shard_map/ppermute | solution.py:703
  35.6 2.4 %collective-permute-done.1.g3 = bf16[2112,128]{1,0:T(8,128)(2,1)S(1)} collective-permute-done((bf16[2112,128]{1,0:T(8,128)(2,1)S(1)}, bf16[2112,128]{1,0:T(8,128)(2,1)S(1)}, u32[]{:S(2)}, u32[]{:S(2)}) %collective-permute-start.1) | collective-permute-done | bytes 540704 | tf_op jit(solution)/shard_map/ppermute | solution.py:706
  38.0 0.9 %shard_map.109 = (bf16[2,512,512]{2,1,0:T(8,128)(2,1)S(1)}, bf16[2,512,512]{2,1,0:T(8,128)(2,1)S(1)}, f32[2,1,512]{2,1,0:T(1,128)S(1)}, f32[2,512]{1,0:T(2,128)S...) custom-call(f32[20,128,128]{2,1,0:T(8,128)S(1)} %get-tuple-element.47.own, f32[64,128]{1,0:T(8,128)S(1)} %get-tuple-element.48.extra, ...), custom_call_target="tpu_custom_call" | custom-call | bytes 6131712 | tf_op jit(solution)/shard_map/pallas_call | solution.py:22
  38.9 0.7 collective-permute-start.9
  39.6 0.7 collective-permute-start.6
  40.4 0.7 collective-permute-start.7
  41.1 4.2 %shard_map.112 = (bf16[512,512]{1,0:T(8,128)(2,1)S(1)}, bf16[512,512]{1,0:T(8,128)(2,1)S(1)}, f32[8,512]{1,0:T(8,128)S(1)}, bf16[512,512]{1,0:T(8,128)(2,1)S(1)}, bf16[512,512]{1,0:T(8,128)(2,1)S(1)}) custom-call(f32[1,512]{1,0:T(1,128)S(1)} %get-tuple-element.71.after, ...), custom_call_target="tpu_custom_call", output_to_operand_aliasing={{0}: (10, {}), {1}: (11, {}), {2}: (12, {})} | custom-call | flops 3221225472 | bytes 6318080 | tf_op jit(solution)/shard_map/pallas_call | solution.py:22
  45.7 0.7 collective-permute-start.8
  46.4 1.1 %shard_map.114 = (bf16[512,512]{1,0:T(8,128)(2,1)S(1)}, bf16[512,512]{1,0:T(8,128)(2,1)S(1)}, f32[1,512]{1,0:T(1,128)S(1)}) custom-call(f32[1,512]{1,0:T(1,128)S(1)} %get-tuple-element.77.after, bf16[512,512]{1,0:T(8,128)(2,1)S(1)} %get-tuple-element.72.b1hi, bf16[512,512]{1,0:T(8,128)(2,1)S(1)} %get-tuple-element.73.b1lo, ...), custom_call_target="tpu_custom_call" | custom-call | bytes 2115584 | tf_op jit(solution)/shard_map/pallas_call | solution.py:22
  47.8 0.7 collective-permute-start.10
  48.6 0.7 collective-permute-start.11
  49.3 1.2 %shard_map.121 = f32[32,8,128]{2,1,0:T(8,128)S(1)} custom-call(f32[1,512]{1,0:T(1,128)S(1)} %get-tuple-element.89.acc, f32[1,512]{1,0:T(1,128)S(1)} %collective-permute-done.11.got, bf16[512,512]{1,0:T(8,128)(2,1)S(1)} %get-tuple-element.72.b1hi, bf16[512,512]{1,0:T(8,128)(2,1)S(1)} %get-tuple-element.73.b1lo, bf16[512,512]{1,0:T(8,128)(2,1)S(1)} %get-tuple-element.74.b2hi, ...), custom_call_target="tpu_custom_call" | custom-call | bytes 11606016 | tf_op jit(solution)/shard_map/pallas_call | solution.py:22
  50.5 30.2 %all_to_all.11.parts = f32[32,8,128]{2,1,0:T(8,128)S(1)} all-to-all(f32[32,8,128]{2,1,0:T(8,128)S(1)} %shard_map.121), channel_id=1, replica_groups=mesh['z'=4,'y'=2,'obs'=4] {'z','y','obs'}, dimensions={0} | all-to-all | bytes 262144 | tf_op jit(solution)/shard_map/all_to_all | solution.py:795
  80.7 0.6 shard_map.122
  (27 shorter events, 1.4 us)
Async XLA Ops:
  2.9 20.9 %copy-start.2 = (f32[128,512]{1,0:T(8,128)S(1)}, f32[128,512]{1,0:T(8,128)}, u32[]{:S(2)}) copy-start(f32[128,512]{1,0:T(8,128)} %gain.1) | copy-start | bytes 786436
  23.7 9.7 %copy-start.1 = (f32[512,512]{1,0:T(8,128)S(1)}, f32[512,512]{1,0:T(8,128)}, u32[]{:S(2)}) copy-start(f32[512,512]{1,0:T(8,128)} %cov.1) | copy-start | bytes 3145732
  25.0 8.4 %copy-start = (f32[512,512]{1,0:T(8,128)S(1)}, f32[512,512]{1,0:T(8,128)}, u32[]{:S(2)}) copy-start(f32[512,512]{1,0:T(8,128)} %trans.1) | copy-start | bytes 3145732
  25.0 8.3 %collective-permute-start.4 = (f32[128,512]{1,0:T(8,128)S(1)}, f32[128,512]{1,0:T(8,128)S(1)}, u32[]{:S(2)}, u32[]{:S(2)}) collective-permute-start(f32[128,512]{1,0:T(8,128)S(1)} %get-tuple-element.56.one), channel_id=1, source_target_pairs={{0,2},{1,3},{2,0},{3,1},{4,6},{5,7},{6,4},{7,5},{8,10},{9,11},{10,... | collective-permute-start | bytes 786440 | tf_op jit(solution)/shard_map/ppermute | solution.py:703
  25.6 12.4 %collective-permute-start.1 = (bf16[2112,128]{1,0:T(8,128)(2,1)S(1)}, bf16[2112,128]{1,0:T(8,128)(2,1)S(1)}, u32[]{:S(2)}, u32[]{:S(2)}) collective-permute-start(bf16[2112,128]{1,0:T(8,128)(2,1)S(1)} %get-tuple-element.49), channel_id=1, source_target_pairs={{0,9},{9,17},{11,19},{2,11},{6,15},{15,23},{13,21},{4,13}} | collective-permute-start | bytes 1622024 | tf_op jit(solution)/shard_map/ppermute | solution.py:706
  28.5 9.5 %collective-permute-start.2 = (bf16[2112,128]{1,0:T(8,128)(2,1)S(1)}, bf16[2112,128]{1,0:T(8,128)(2,1)S(1)}, u32[]{:S(2)}, u32[]{:S(2)}) collective-permute-start(bf16[2112,128]{1,0:T(8,128)(2,1)S(1)} %get-tuple-element.49), channel_id=1, source_target_pairs={{16,9},{25,17},{27,19},{18,11},{22,15},{31,23},{29,21},{20,13}} | collective-permute-start | bytes 1622024 | tf_op jit(solution)/shard_map/ppermute | solution.py:706
  29.2 8.8 %collective-permute-start.3 = (bf16[2112,128]{1,0:T(8,128)(2,1)S(1)}, bf16[2112,128]{1,0:T(8,128)(2,1)S(1)}, u32[]{:S(2)}, u32[]{:S(2)}) collective-permute-start(bf16[2112,128]{1,0:T(8,128)(2,1)S(1)} %get-tuple-element.49), channel_id=1, source_target_pairs={{24,9},{1,17},{3,19},{26,11},{30,15},{7,23},{5,21},{28,13}} | collective-permute-start | bytes 1622024 | tf_op jit(solution)/shard_map/ppermute | solution.py:706
  29.9 8.1 %collective-permute-start = (bf16[2112,128]{1,0:T(8,128)(2,1)S(1)}, bf16[2112,128]{1,0:T(8,128)(2,1)S(1)}, u32[]{:S(2)}, u32[]{:S(2)}) collective-permute-start(bf16[2112,128]{1,0:T(8,128)(2,1)S(1)} %get-tuple-element.49), channel_id=1, source_target_pairs={{8,9},{10,11},{14,15},{12,13}} | collective-permute-start | bytes 1622024 | tf_op jit(solution)/shard_map/ppermute | solution.py:710
  33.3 2.0 %collective-permute-start.5 = (f32[2,128,512]{2,1,0:T(8,128)S(1)}, f32[2,128,512]{2,1,0:T(8,128)S(1)}, u32[]{:S(2)}, u32[]{:S(2)}) collective-permute-start(f32[2,128,512]{2,1,0:T(8,128)S(1)} %shard_map.107.held), channel_id=1, source_target_pairs={{0,1},{1,0},{2,3},{3,2},{4,5},{5,4},{6,7},{7,6},{8,9},{9,8},{10,11... | collective-permute-start | bytes 1572872 | tf_op jit(solution)/shard_map/ppermute | solution.py:703
  38.9 9.6 %collective-permute-start.9 = (bf16[2112,128]{1,0:T(8,128)(2,1)S(1)}, bf16[2112,128]{1,0:T(8,128)(2,1)S(1)}, u32[]{:S(2)}, u32[]{:S(2)}) collective-permute-start(bf16[2112,128]{1,0:T(8,128)(2,1)S(1)} %shard_map.118), channel_id=1, source_target_pairs={{23,15},{13,21}} | collective-permute-start | bytes 1622024 | tf_op jit(solution)/shard_map/ppermute | solution.py:734
  39.6 0.7 collective-permute-start.6
  40.4 4.8 %collective-permute-start.7 = (f32[1,512]{1,0:T(1,128)S(1)}, f32[1,512]{1,0:T(1,128)S(1)}, u32[]{:S(2)}, u32[]{:S(2)}) collective-permute-start(f32[1,512]{1,0:T(1,128)S(1)} %get-tuple-element.71.after), channel_id=1, source_target_pairs={{17,19}} | collective-permute-start | bytes 6152 | tf_op jit(solution)/shard_map/ppermute | solution.py:740
  45.7 1.9 %collective-permute-start.8 = (f32[1,512]{1,0:T(1,128)S(1)}, f32[1,512]{1,0:T(1,128)S(1)}, u32[]{:S(2)}, u32[]{:S(2)}) collective-permute-start(f32[1,512]{1,0:T(1,128)S(1)} %get-tuple-element.77.after), channel_id=1, source_target_pairs={{19,11}} | collective-permute-start | bytes 6152 | tf_op jit(solution)/shard_map/ppermute | solution.py:740
  47.8 0.8 collective-permute-start.10
  48.6 0.7 collective-permute-start.11

commit v18 on v17

--- a/solution.py
+++ b/solution.py
@@ -381,7 +381,7 @@
 
 
 def owner_kernel(
-    own, extra, g4, g3, g1, g2, prior, ahead, pthi, ptlo, chi, clo, after, omhi, omlo, info, mine, start, y, small
+    own, extra, g4, g2, g1, g3, prior, ahead, pthi, ptlo, chi, clo, after, omhi, omlo, info, mine, start, y, small
 ):
     ids = here()
     planes = 4
@@ -710,7 +710,7 @@
     fourth = lax.ppermute(
         pay, everyone, [(spans + place(p), owner(p)) for p in range(spans) if place(p) % 2 == 0]
     )
-    third, first, second = plane_sum(3), plane_sum(1), plane_sum(2)
+    second, first, third = plane_sum(2), plane_sum(1), plane_sum(3)
     (gains,) = run(stack_kernel, [((2,) + gain.shape, F32)], [gain, swap(gain, 2)])
     mthi, mtlo = run(gain_kernel, [(full, BF16)] * 2, [gains, swap(gains, 1)])
     pt, pthi, ptlo, chi, clo, ahead = run(
@@ -721,7 +721,7 @@
         owner_kernel,
         [((days,) + full, BF16)] * 2 + [((days, 1, width), F32), ((days, width), F32), row, row],
         [
-            own, extra, fourth, third, first, second, prior, ahead, pthi, ptlo, chi, clo, (mthi, ANY)
+            own, extra, fourth, second, first, third, prior, ahead, pthi, ptlo, chi, clo, (mthi, ANY)
         ],
         [smalls],
     )

time: 81.6 us -> 80.9 us (level)
  blocking collectives: 51.1 us -> 46.7 us
  waiting for transfers between devices: 6.2 us -> 8.54 us
  starting transfers between devices: 9.73 us -> 10.9 us
    all_to_all x1, blocking collectives: 30.2 us -> 25.9 us  [local(): lax.all_to_all(answer, everyone, split_axis=0, concat_axis=0, tiled=True)]
    ppermute x3, waiting for transfers between devices: 2.38 us -> 5.91 us  [plane_sum(): lax.ppermute(pay, everyone, [((owner_plane(p) + s) % planes * spans + pla...]
    ppermute x2, waiting for transfers between devices: 3.81 us -> 2.62 us  [swap(): return lax.ppermute(x, 'obs', [(i, i ^ bit) for i in range(peers)])]
    ppermute x3, starting transfers between devices: 4.28 us -> 5.48 us  [plane_sum(): lax.ppermute(pay, everyone, [((owner_plane(p) + s) % planes * spans + pla...]
where the time goes in v18:
time: 80.9 us; the launch traced here: 80.5 us
  blocking collectives  46.7 us (58%)
  Pallas kernels  13.3 us (16%)
  starting transfers between devices  10.9 us (13%)
  waiting for transfers between devices  8.54 us (11%)
  between operations  0.95 us (1%)
    all_to_all x1, blocking collectives, local(): lax.all_to_all(answer, everyone, split_axis=0, concat_axis=0, tiled=True)  25.9 us
    all_to_all x1, blocking collectives, local(): lax.all_to_all(sent, ('y', 'obs'), split_axis=0, concat_axis=0, tiled=True)  20.8 us
    pallas_call x19, Pallas kernels, run(): pl.pallas_call(body, out_shape=[jax.ShapeDtypeStruct(s, d) for s, d in ou...  13.3 us
    ppermute x3, waiting for transfers between devices, plane_sum(): lax.ppermute(pay, everyone, [((owner_plane(p) + s) % planes * spans + pla...  5.91 us
    ppermute x3, starting transfers between devices, plane_sum(): lax.ppermute(pay, everyone, [((owner_plane(p) + s) % planes * spans + pla...  5.48 us
    ppermute x5, starting transfers between devices, local(): received = lax.ppermute(y, everyone, [(owner(source), owner(target))])  3.35 us
    ppermute x2, waiting for transfers between devices, swap(): return lax.ppermute(x, 'obs', [(i, i ^ bit) for i in range(peers)])  2.62 us
  transfers between devices with their start and end apart: 12, of which 3 were waited for; matrix products, arithmetic and copies ran while one was open for 0% of the time, Pallas kernels for 9%

profile of v18, /device:TPU:0, one launch (start us, length us, event | category | flops | bytes accessed | tf_op | source)
XLA Modules:
  0.0 80.5 jit_solution(5290445648390031550)
XLA Ops:
  0.6 2.2 %shard_map.104 = bf16[8,520,128]{2,1,0:T(8,128)(2,1)} custom-call(s32[8]{0:T(128)} %day.1, s32[8]{0:T(128)} %count.1, bf16[1024,512]{1,0:T(8,128)(2,1)} %rows.1, bf16[8,128]{1,0:T(8,128)(2,1)} %bitcast.2, f32[1,128]{1,0:T(1,128)} %bitcast.3, f32[2,512]{1,0:T(2,128)} %damping.1), custom_call_target="tpu_custom_call" | custom-call | bytes 1055296 | tf_op jit(solution)/shard_map/pallas_call | solution.py:22
  2.9 20.8 %all_to_all.10.got = bf16[8,520,128]{2,1,0:T(8,128)(2,1)S(1)} all-to-all(bf16[8,520,128]{2,1,0:T(8,128)(2,1)} %shard_map.104), channel_id=1, replica_groups=mesh['z'=4,'y'=2,'obs'=4] {'y','obs'}, dimensions={0} | all-to-all | bytes 2129920 | tf_op jit(solution)/shard_map/all_to_all | solution.py:687
  23.7 1.2 %shard_map.105 = (f32[20,128,128]{2,1,0:T(8,128)S(1)}, f32[64,128]{1,0:T(8,128)S(1)}, bf16[2112,128]{1,0:T(8,128)(2,1)S(1)}, f32[1,512]{1,0:T(1,128)S(1)}, f32[128,512]{1,0:T(8,128)S(1)}) custom-call(bf16[8,520,128]{2,1,0:T(8,128)(2,1)S(1)} %all_to_all.10.got, f32[128,512]{1,0:T(8,128)S(1)} %copy-done.2), custom_call_target="tpu_custom_call" | custom-call | flops 1073741824 | bytes 1327104 | tf_op jit(solution)/shard_map/pallas_call | solution.py:22
  25.0 0.6 collective-permute-start.4
  25.6 0.7 collective-permute-start.1
  26.3 0.7 collective-permute-start.2
  27.0 4.1 %collective-permute-start.3 = (bf16[2112,128]{1,0:T(8,128)(2,1)S(1)}, bf16[2112,128]{1,0:T(8,128)(2,1)S(1)}, u32[]{:S(2)}, u32[]{:S(2)}) collective-permute-start(bf16[2112,128]{1,0:T(8,128)(2,1)S(1)} %get-tuple-element.49), channel_id=1, source_target_pairs={{0,9},{9,17},{11,19},{2,11},{6,15},{15,23},{13,21},{4,13}} | collective-permute-start | bytes 1622024 | tf_op jit(solution)/shard_map/ppermute | solution.py:706
  31.1 0.7 collective-permute-start
  31.8 1.5 %collective-permute-done.4.two = f32[128,512]{1,0:T(8,128)S(1)} collective-permute-done((f32[128,512]{1,0:T(8,128)S(1)}, f32[128,512]{1,0:T(8,128)S(1)}, u32[]{:S(2)}, u32[]{:S(2)}) %collective-permute-start.4) | collective-permute-done | bytes 262176 | tf_op jit(solution)/shard_map/ppermute | solution.py:703
  33.4 0.7 shard_map.106
  34.1 1.1 %collective-permute-done.5.got = f32[2,128,512]{2,1,0:T(8,128)S(1)} collective-permute-done((f32[2,128,512]{2,1,0:T(8,128)S(1)}, f32[2,128,512]{2,1,0:T(8,128)S(1)}, u32[]{:S(2)}, u32[]{:S(2)}) %collective-permute-start.5) | collective-permute-done | bytes 524320 | tf_op jit(solution)/shard_map/ppermute | solution.py:703
  35.6 5.9 %collective-permute-done.3.g3 = bf16[2112,128]{1,0:T(8,128)(2,1)S(1)} collective-permute-done((bf16[2112,128]{1,0:T(8,128)(2,1)S(1)}, bf16[2112,128]{1,0:T(8,128)(2,1)S(1)}, u32[]{:S(2)}, u32[]{:S(2)}) %collective-permute-start.3) | collective-permute-done | bytes 540704 | tf_op jit(solution)/shard_map/ppermute | solution.py:706
  41.6 0.9 %shard_map.109 = (bf16[2,512,512]{2,1,0:T(8,128)(2,1)S(1)}, bf16[2,512,512]{2,1,0:T(8,128)(2,1)S(1)}, f32[2,1,512]{2,1,0:T(1,128)S(1)}, f32[2,512]{1,0:T(2,128)S...) custom-call(f32[20,128,128]{2,1,0:T(8,128)S(1)} %get-tuple-element.47.own, f32[64,128]{1,0:T(8,128)S(1)} %get-tuple-element.48.extra, ...), custom_call_target="tpu_custom_call" | custom-call | bytes 6131712 | tf_op jit(solution)/shard_map/pallas_call | solution.py:22
  42.5 0.7 collective-permute-start.9
  43.2 0.7 collective-permute-start.6
  43.9 0.7 collective-permute-start.7
  44.6 4.2 %shard_map.112 = (bf16[512,512]{1,0:T(8,128)(2,1)S(1)}, bf16[512,512]{1,0:T(8,128)(2,1)S(1)}, f32[8,512]{1,0:T(8,128)S(1)}, bf16[512,512]{1,0:T(8,128)(2,1)S(1)}, bf16[512,512]{1,0:T(8,128)(2,1)S(1)}) custom-call(f32[1,512]{1,0:T(1,128)S(1)} %get-tuple-element.71.after, ...), custom_call_target="tpu_custom_call", output_to_operand_aliasing={{0}: (10, {}), {1}: (11, {}), {2}: (12, {})} | custom-call | flops 3221225472 | bytes 6318080 | tf_op jit(solution)/shard_map/pallas_call | solution.py:22
  49.3 0.7 collective-permute-start.8
  49.9 1.1 %shard_map.114 = (bf16[512,512]{1,0:T(8,128)(2,1)S(1)}, bf16[512,512]{1,0:T(8,128)(2,1)S(1)}, f32[1,512]{1,0:T(1,128)S(1)}) custom-call(f32[1,512]{1,0:T(1,128)S(1)} %get-tuple-element.77.after, bf16[512,512]{1,0:T(8,128)(2,1)S(1)} %get-tuple-element.72.b1hi, bf16[512,512]{1,0:T(8,128)(2,1)S(1)} %get-tuple-element.73.b1lo, ...), custom_call_target="tpu_custom_call" | custom-call | bytes 2115584 | tf_op jit(solution)/shard_map/pallas_call | solution.py:22
  51.3 0.7 collective-permute-start.10
  52.1 0.7 collective-permute-start.11
  52.8 1.2 %shard_map.121 = f32[32,8,128]{2,1,0:T(8,128)S(1)} custom-call(f32[1,512]{1,0:T(1,128)S(1)} %get-tuple-element.89.acc, f32[1,512]{1,0:T(1,128)S(1)} %collective-permute-done.11.got, bf16[512,512]{1,0:T(8,128)(2,1)S(1)} %get-tuple-element.72.b1hi, bf16[512,512]{1,0:T(8,128)(2,1)S(1)} %get-tuple-element.73.b1lo, bf16[512,512]{1,0:T(8,128)(2,1)S(1)} %get-tuple-element.74.b2hi, ...), custom_call_target="tpu_custom_call" | custom-call | bytes 11606016 | tf_op jit(solution)/shard_map/pallas_call | solution.py:22
  54.0 25.9 %all_to_all.11.parts = f32[32,8,128]{2,1,0:T(8,128)S(1)} all-to-all(f32[32,8,128]{2,1,0:T(8,128)S(1)} %shard_map.121), channel_id=1, replica_groups=mesh['z'=4,'y'=2,'obs'=4] {'z','y','obs'}, dimensions={0} | all-to-all | bytes 262144 | tf_op jit(solution)/shard_map/all_to_all | solution.py:795
  79.9 0.6 shard_map.122
  (27 shorter events, 1.4 us)
Async XLA Ops:
  2.9 20.9 %copy-start.2 = (f32[128,512]{1,0:T(8,128)S(1)}, f32[128,512]{1,0:T(8,128)}, u32[]{:S(2)}) copy-start(f32[128,512]{1,0:T(8,128)} %gain.1) | copy-start | bytes 786436
  23.7 9.7 %copy-start.1 = (f32[512,512]{1,0:T(8,128)S(1)}, f32[512,512]{1,0:T(8,128)}, u32[]{:S(2)}) copy-start(f32[512,512]{1,0:T(8,128)} %cov.1) | copy-start | bytes 3145732
  25.0 8.4 %copy-start = (f32[512,512]{1,0:T(8,128)S(1)}, f32[512,512]{1,0:T(8,128)}, u32[]{:S(2)}) copy-start(f32[512,512]{1,0:T(8,128)} %trans.1) | copy-start | bytes 3145732
  25.0 8.3 %collective-permute-start.4 = (f32[128,512]{1,0:T(8,128)S(1)}, f32[128,512]{1,0:T(8,128)S(1)}, u32[]{:S(2)}, u32[]{:S(2)}) collective-permute-start(f32[128,512]{1,0:T(8,128)S(1)} %get-tuple-element.56.one), channel_id=1, source_target_pairs={{0,2},{1,3},{2,0},{3,1},{4,6},{5,7},{6,4},{7,5},{8,10},{9,11},{10,... | collective-permute-start | bytes 786440 | tf_op jit(solution)/shard_map/ppermute | solution.py:703
  25.6 10.0 %collective-permute-start.1 = (bf16[2112,128]{1,0:T(8,128)(2,1)S(1)}, bf16[2112,128]{1,0:T(8,128)(2,1)S(1)}, u32[]{:S(2)}, u32[]{:S(2)}) collective-permute-start(bf16[2112,128]{1,0:T(8,128)(2,1)S(1)} %get-tuple-element.49), channel_id=1, source_target_pairs={{24,9},{1,17},{3,19},{26,11},{30,15},{7,23},{5,21},{28,13}} | collective-permute-start | bytes 1622024 | tf_op jit(solution)/shard_map/ppermute | solution.py:706
  26.3 9.4 %collective-permute-start.2 = (bf16[2112,128]{1,0:T(8,128)(2,1)S(1)}, bf16[2112,128]{1,0:T(8,128)(2,1)S(1)}, u32[]{:S(2)}, u32[]{:S(2)}) collective-permute-start(bf16[2112,128]{1,0:T(8,128)(2,1)S(1)} %get-tuple-element.49), channel_id=1, source_target_pairs={{16,9},{25,17},{27,19},{18,11},{22,15},{31,23},{29,21},{20,13}} | collective-permute-start | bytes 1622024 | tf_op jit(solution)/shard_map/ppermute | solution.py:706
  27.0 14.6 %collective-permute-start.3 = (bf16[2112,128]{1,0:T(8,128)(2,1)S(1)}, bf16[2112,128]{1,0:T(8,128)(2,1)S(1)}, u32[]{:S(2)}, u32[]{:S(2)}) collective-permute-start(bf16[2112,128]{1,0:T(8,128)(2,1)S(1)} %get-tuple-element.49), channel_id=1, source_target_pairs={{0,9},{9,17},{11,19},{2,11},{6,15},{15,23},{13,21},{4,13}} | collective-permute-start | bytes 1622024 | tf_op jit(solution)/shard_map/ppermute | solution.py:706
  31.1 10.5 %collective-permute-start = (bf16[2112,128]{1,0:T(8,128)(2,1)S(1)}, bf16[2112,128]{1,0:T(8,128)(2,1)S(1)}, u32[]{:S(2)}, u32[]{:S(2)}) collective-permute-start(bf16[2112,128]{1,0:T(8,128)(2,1)S(1)} %get-tuple-element.49), channel_id=1, source_target_pairs={{8,9},{10,11},{14,15},{12,13}} | collective-permute-start | bytes 1622024 | tf_op jit(solution)/shard_map/ppermute | solution.py:710
  33.3 2.0 %collective-permute-start.5 = (f32[2,128,512]{2,1,0:T(8,128)S(1)}, f32[2,128,512]{2,1,0:T(8,128)S(1)}, u32[]{:S(2)}, u32[]{:S(2)}) collective-permute-start(f32[2,128,512]{2,1,0:T(8,128)S(1)} %shard_map.107.held), channel_id=1, source_target_pairs={{0,1},{1,0},{2,3},{3,2},{4,5},{5,4},{6,7},{7,6},{8,9},{9,8},{10,11... | collective-permute-start | bytes 1572872 | tf_op jit(solution)/shard_map/ppermute | solution.py:703
  42.5 9.6 %collective-permute-start.9 = (bf16[2112,128]{1,0:T(8,128)(2,1)S(1)}, bf16[2112,128]{1,0:T(8,128)(2,1)S(1)}, u32[]{:S(2)}, u32[]{:S(2)}) collective-permute-start(bf16[2112,128]{1,0:T(8,128)(2,1)S(1)} %shard_map.118), channel_id=1, source_target_pairs={{23,15},{13,21}} | collective-permute-start | bytes 1622024 | tf_op jit(solution)/shard_map/ppermute | solution.py:734
  43.2 0.7 collective-permute-start.6
  43.9 4.8 %collective-permute-start.7 = (f32[1,512]{1,0:T(1,128)S(1)}, f32[1,512]{1,0:T(1,128)S(1)}, u32[]{:S(2)}, u32[]{:S(2)}) collective-permute-start(f32[1,512]{1,0:T(1,128)S(1)} %get-tuple-element.71.after), channel_id=1, source_target_pairs={{17,19}} | collective-permute-start | bytes 6152 | tf_op jit(solution)/shard_map/ppermute | solution.py:740
  49.3 1.9 %collective-permute-start.8 = (f32[1,512]{1,0:T(1,128)S(1)}, f32[1,512]{1,0:T(1,128)S(1)}, u32[]{:S(2)}, u32[]{:S(2)}) collective-permute-start(f32[1,512]{1,0:T(1,128)S(1)} %get-tuple-element.77.after), channel_id=1, source_target_pairs={{19,11}} | collective-permute-start | bytes 6152 | tf_op jit(solution)/shard_map/ppermute | solution.py:740
  51.3 0.8 collective-permute-start.10
  52.1 0.7 collective-permute-start.11

commit v19 on v17

--- a/solution.py
+++ b/solution.py
@@ -529,20 +529,20 @@
     return hi[...].astype(F32) + lo[...].astype(F32)
 
 
-def pairs_kernel(after, table, mthi, mtlo, khi, klo):
+def pairs_kernel(skip, after, table, mthi, mtlo, khi, klo):
     spans = table.shape[0] // 2
 
     @pl.when(here()[1] == spans - 2)
     def _():
         @pl.loop(0, khi.shape[0])
         def _(k):
-            scaled = whole_of(mthi, mtlo) * table[pl.ds(2 * (spans - 3 - k) + 1, 1), :]
+            scaled = whole_of(mthi, mtlo) * table[pl.ds(2 * (spans - 3 - skip - k) + 1, 1), :]
             khi[k], klo[k] = split(mm(scaled, mthi[...], mtlo[...]))
 
 
 def last_kernel(
     acc, got, b1hi, b1lo, b2hi, b2lo, bchi, bclo, off, offset, table, pthi, ptlo, mthi, mtlo,
-    zhi, zlo, next_off, khi, klo, out, shares, means,
+    zhi, zlo, next_off, khi, klo, more_khi, more_klo, out, shares, means,
 ):
     span = here()[1]
     total, width = shares.shape
@@ -599,17 +599,18 @@
     @pl.when(span == spans - 2)
     def _():
         v, damped_rows = means[4:5, :], []
-        for k in range(khi.shape[0]):
-            t = 2 * (spans - 2 - k)
+        pairs = [(a, b, k) for a, b in ((khi, klo), (more_khi, more_klo)) for k in range(a.shape[0])]
+        for n, (a, b, k) in enumerate(pairs):
+            t = 2 * (spans - 2 - n)
             damped_rows.append(v * table[t : t + 1, :])
-            v = mv(damped_rows[-1], khi[k], klo[k])
+            v = mv(damped_rows[-1], a[k], b[k])
             shares[t - 2 : t - 1, :] = v
         batch = jnp.concatenate(damped_rows + [jnp.zeros((1, width), F32)] * (-len(damped_rows) % 8), 0)
         batch = mm(batch, mthi[...], mtlo[...])
-        for k in range(khi.shape[0]):
-            t = 2 * (spans - 2 - k)
-            shares[t - 1 : t, :] = batch[k : k + 1]
-        lax.fori_loop(2 * khi.shape[0], 2 * span, step, v)
+        for n in range(len(pairs)):
+            t = 2 * (spans - 2 - n)
+            shares[t - 1 : t, :] = batch[n : n + 1]
+        lax.fori_loop(2 * len(pairs), 2 * span, step, v)
 
     for c in range(spans):
         for q in range(chunks):
@@ -710,7 +711,7 @@
     fourth = lax.ppermute(
         pay, everyone, [(spans + place(p), owner(p)) for p in range(spans) if place(p) % 2 == 0]
     )
-    third, first, second = plane_sum(3), plane_sum(1), plane_sum(2)
+    second, first, third = plane_sum(2), plane_sum(1), plane_sum(3)
     (gains,) = run(stack_kernel, [((2,) + gain.shape, F32)], [gain, swap(gain, 2)])
     mthi, mtlo = run(gain_kernel, [(full, BF16)] * 2, [gains, swap(gains, 1)])
     pt, pthi, ptlo, chi, clo, ahead = run(
@@ -765,7 +766,7 @@
                 [smalls],
             )
             khi, klo = run(
-                pairs_kernel, [((min(spans - 2, 4),) + full, BF16)] * 2, [(y, ANY), table, mthi, mtlo]
+                functools.partial(pairs_kernel, 0), [((2,) + full, BF16)] * 2, [(y, ANY), table, mthi, mtlo]
             )
         elif target == spans - 4:
             nexthi, nextlo, next_off = run(
@@ -783,12 +784,16 @@
             )
         elif target != spans - 2:
             acc, y = run(hop_kernel, [row, row], [(khi, ANY), acc, received, bchi, bclo, offset])
+        if target == spans - 4:
+            more_khi, more_klo = run(
+                functools.partial(pairs_kernel, 2), [((4,) + full, BF16)] * 2, [(y, ANY), table, mthi, mtlo]
+            )
     (answer,) = run(
         last_kernel,
         [((spans * peers, 8, LANES), F32)],
         [
             acc, received, b1hi, b1lo, b2hi, b2lo, bchi, bclo, off, offset, table, pthi, ptlo, mthi, mtlo,
-            nexthi, nextlo, next_off, khi, klo,
+            nexthi, nextlo, next_off, khi, klo, more_khi, more_klo,
         ],
         [pltpu.VMEM((spans * days, width), F32), pltpu.VMEM((8, width), F32)],
     )

time: 81.6 us -> 79.2 us (0.971)
  blocking collectives: 51.1 us -> 45.2 us
  waiting for transfers between devices: 6.2 us -> 8.58 us
  starting transfers between devices: 9.73 us -> 10.9 us
    all_to_all x1, blocking collectives: 30.2 us -> 24.4 us  [local(): lax.all_to_all(answer, everyone, split_axis=0, concat_axis=0, tiled=True)]
    ppermute x3, waiting for transfers between devices: 2.38 us -> 5.91 us  [plane_sum(): lax.ppermute(pay, everyone, [((owner_plane(p) + s) % planes * spans + pla...]
    ppermute x3, starting transfers between devices: 4.28 us -> 5.48 us  [plane_sum(): lax.ppermute(pay, everyone, [((owner_plane(p) + s) % planes * spans + pla...]
    ppermute x2, waiting for transfers between devices: 3.81 us -> 2.65 us  [swap(): return lax.ppermute(x, 'obs', [(i, i ^ bit) for i in range(peers)])]
    pallas_call x19 -> x20, Pallas kernels: 13.4 us -> 13.2 us  [run(): pl.pallas_call(body, out_shape=[jax.ShapeDtypeStruct(s, d) for s, d in ou...]
where the time goes in v19:
time: 79.2 us; the launch traced here: 78.9 us
  blocking collectives  45.2 us (57%)
  Pallas kernels  13.2 us (17%)
  starting transfers between devices  10.9 us (14%)
  waiting for transfers between devices  8.58 us (11%)
  between operations  0.96 us (1%)
    all_to_all x1, blocking collectives, local(): lax.all_to_all(answer, everyone, split_axis=0, concat_axis=0, tiled=True)  24.4 us
    all_to_all x1, blocking collectives, local(): lax.all_to_all(sent, ('y', 'obs'), split_axis=0, concat_axis=0, tiled=True)  20.8 us
    pallas_call x20, Pallas kernels, run(): pl.pallas_call(body, out_shape=[jax.ShapeDtypeStruct(s, d) for s, d in ou...  13.2 us
    ppermute x3, waiting for transfers between devices, plane_sum(): lax.ppermute(pay, everyone, [((owner_plane(p) + s) % planes * spans + pla...  5.91 us
    ppermute x3, starting transfers between devices, plane_sum(): lax.ppermute(pay, everyone, [((owner_plane(p) + s) % planes * spans + pla...  5.48 us
    ppermute x5, starting transfers between devices, local(): received = lax.ppermute(y, everyone, [(owner(source), owner(target))])  3.35 us
    ppermute x2, waiting for transfers between devices, swap(): return lax.ppermute(x, 'obs', [(i, i ^ bit) for i in range(peers)])  2.65 us
  transfers between devices with their start and end apart: 12, of which 3 were waited for; matrix products, arithmetic and copies ran while one was open for 0% of the time, Pallas kernels for 9%

profile of v19, /device:TPU:0, one launch (start us, length us, event | category | flops | bytes accessed | tf_op | source)
XLA Modules:
  0.0 78.9 jit_solution(12553555245725855461)
XLA Ops:
  0.6 2.2 %shard_map.104 = bf16[8,520,128]{2,1,0:T(8,128)(2,1)} custom-call(s32[8]{0:T(128)} %day.1, s32[8]{0:T(128)} %count.1, bf16[1024,512]{1,0:T(8,128)(2,1)} %rows.1, bf16[8,128]{1,0:T(8,128)(2,1)} %bitcast.2, f32[1,128]{1,0:T(1,128)} %bitcast.3, f32[2,512]{1,0:T(2,128)} %damping.1), custom_call_target="tpu_custom_call" | custom-call | bytes 1055296 | tf_op jit(solution)/shard_map/pallas_call | solution.py:22
  2.9 20.8 %all_to_all.10.got = bf16[8,520,128]{2,1,0:T(8,128)(2,1)S(1)} all-to-all(bf16[8,520,128]{2,1,0:T(8,128)(2,1)} %shard_map.104), channel_id=1, replica_groups=mesh['z'=4,'y'=2,'obs'=4] {'y','obs'}, dimensions={0} | all-to-all | bytes 2129920 | tf_op jit(solution)/shard_map/all_to_all | solution.py:688
  23.7 1.2 %shard_map.105 = (f32[20,128,128]{2,1,0:T(8,128)S(1)}, f32[64,128]{1,0:T(8,128)S(1)}, bf16[2112,128]{1,0:T(8,128)(2,1)S(1)}, f32[1,512]{1,0:T(1,128)S(1)}, f32[128,512]{1,0:T(8,128)S(1)}) custom-call(bf16[8,520,128]{2,1,0:T(8,128)(2,1)S(1)} %all_to_all.10.got, f32[128,512]{1,0:T(8,128)S(1)} %copy-done.2), custom_call_target="tpu_custom_call" | custom-call | flops 1073741824 | bytes 1327104 | tf_op jit(solution)/shard_map/pallas_call | solution.py:22
  25.0 0.6 collective-permute-start.4
  25.6 0.7 collective-permute-start.3
  26.3 0.7 collective-permute-start.2
  27.0 4.1 %collective-permute-start.1 = (bf16[2112,128]{1,0:T(8,128)(2,1)S(1)}, bf16[2112,128]{1,0:T(8,128)(2,1)S(1)}, u32[]{:S(2)}, u32[]{:S(2)}) collective-permute-start(bf16[2112,128]{1,0:T(8,128)(2,1)S(1)} %get-tuple-element.51), channel_id=1, source_target_pairs={{0,9},{9,17},{11,19},{2,11},{6,15},{15,23},{13,21},{4,13}} | collective-permute-start | bytes 1622024 | tf_op jit(solution)/shard_map/ppermute | solution.py:707
  31.1 0.7 collective-permute-start
  31.8 1.5 %collective-permute-done.4.two = f32[128,512]{1,0:T(8,128)S(1)} collective-permute-done((f32[128,512]{1,0:T(8,128)S(1)}, f32[128,512]{1,0:T(8,128)S(1)}, u32[]{:S(2)}, u32[]{:S(2)}) %collective-permute-start.4) | collective-permute-done | bytes 262176 | tf_op jit(solution)/shard_map/ppermute | solution.py:704
  33.4 0.7 shard_map.106
  34.1 1.2 %collective-permute-done.5.got = f32[2,128,512]{2,1,0:T(8,128)S(1)} collective-permute-done((f32[2,128,512]{2,1,0:T(8,128)S(1)}, f32[2,128,512]{2,1,0:T(8,128)S(1)}, u32[]{:S(2)}, u32[]{:S(2)}) %collective-permute-start.5) | collective-permute-done | bytes 524320 | tf_op jit(solution)/shard_map/ppermute | solution.py:704
  35.6 5.9 %collective-permute-done.1.g3 = bf16[2112,128]{1,0:T(8,128)(2,1)S(1)} collective-permute-done((bf16[2112,128]{1,0:T(8,128)(2,1)S(1)}, bf16[2112,128]{1,0:T(8,128)(2,1)S(1)}, u32[]{:S(2)}, u32[]{:S(2)}) %collective-permute-start.1) | collective-permute-done | bytes 540704 | tf_op jit(solution)/shard_map/ppermute | solution.py:707
  41.6 0.9 %shard_map.109 = (bf16[2,512,512]{2,1,0:T(8,128)(2,1)S(1)}, bf16[2,512,512]{2,1,0:T(8,128)(2,1)S(1)}, f32[2,1,512]{2,1,0:T(1,128)S(1)}, f32[2,512]{1,0:T(2,128)S...) custom-call(f32[20,128,128]{2,1,0:T(8,128)S(1)} %get-tuple-element.49.own, f32[64,128]{1,0:T(8,128)S(1)} %get-tuple-element.50.extra, ...), custom_call_target="tpu_custom_call" | custom-call | bytes 6131712 | tf_op jit(solution)/shard_map/pallas_call | solution.py:22
  42.4 0.7 collective-permute-start.9
  43.2 0.7 collective-permute-start.6
  43.9 0.7 collective-permute-start.7
  44.6 4.0 %shard_map.112 = (bf16[512,512]{1,0:T(8,128)(2,1)S(1)}, bf16[512,512]{1,0:T(8,128)(2,1)S(1)}, f32[8,512]{1,0:T(8,128)S(1)}, bf16[512,512]{1,0:T(8,128)(2,1)S(1)}, bf16[512,512]{1,0:T(8,128)(2,1)S(1)}) custom-call(f32[1,512]{1,0:T(1,128)S(1)} %get-tuple-element.73.after, ...), custom_call_target="tpu_custom_call", output_to_operand_aliasing={{0}: (10, {}), {1}: (11, {}), {2}: (12, {})} | custom-call | flops 3221225472 | bytes 6318080 | tf_op jit(solution)/shard_map/pallas_call | solution.py:22
  49.1 0.7 collective-permute-start.8
  49.8 1.1 %shard_map.114 = (bf16[512,512]{1,0:T(8,128)(2,1)S(1)}, bf16[512,512]{1,0:T(8,128)(2,1)S(1)}, f32[1,512]{1,0:T(1,128)S(1)}) custom-call(f32[1,512]{1,0:T(1,128)S(1)} %get-tuple-element.79.after, bf16[512,512]{1,0:T(8,128)(2,1)S(1)} %get-tuple-element.74.b1hi, bf16[512,512]{1,0:T(8,128)(2,1)S(1)} %get-tuple-element.75.b1lo, ...), custom_call_target="tpu_custom_call" | custom-call | bytes 2115584 | tf_op jit(solution)/shard_map/pallas_call | solution.py:22
  51.2 0.7 collective-permute-start.10
  52.0 0.7 collective-permute-start.11
  52.7 1.2 %shard_map.122 = f32[32,8,128]{2,1,0:T(8,128)S(1)} custom-call(f32[1,512]{1,0:T(1,128)S(1)} %get-tuple-element.91.acc, f32[1,512]{1,0:T(1,128)S(1)} %collective-permute-done.11.got, bf16[512,512]{1,0:T(8,128)(2,1)S(1)} %get-tuple-element.74.b1hi, bf16[512,512]{1,0:T(8,128)(2,1)S(1)} %get-tuple-element.75.b1lo, bf16[512,512]{1,0:T(8,128)(2,1)S(1)} %get-tuple-element.76.b2hi, ...), custom_call_target="tpu_custom_call" | custom-call | bytes 13703168 | tf_op jit(solution)/shard_map/pallas_call | solution.py:22
  53.9 24.4 %all_to_all.11.parts = f32[32,8,128]{2,1,0:T(8,128)S(1)} all-to-all(f32[32,8,128]{2,1,0:T(8,128)S(1)} %shard_map.122), channel_id=1, replica_groups=mesh['z'=4,'y'=2,'obs'=4] {'z','y','obs'}, dimensions={0} | all-to-all | bytes 262144 | tf_op jit(solution)/shard_map/all_to_all | solution.py:800
  78.3 0.6 shard_map.123
  (28 shorter events, 1.4 us)
Async XLA Ops:
  2.9 20.9 %copy-start.2 = (f32[128,512]{1,0:T(8,128)S(1)}, f32[128,512]{1,0:T(8,128)}, u32[]{:S(2)}) copy-start(f32[128,512]{1,0:T(8,128)} %gain.1) | copy-start | bytes 786436
  23.7 9.7 %copy-start.1 = (f32[512,512]{1,0:T(8,128)S(1)}, f32[512,512]{1,0:T(8,128)}, u32[]{:S(2)}) copy-start(f32[512,512]{1,0:T(8,128)} %cov.1) | copy-start | bytes 3145732
  24.9 8.4 %copy-start = (f32[512,512]{1,0:T(8,128)S(1)}, f32[512,512]{1,0:T(8,128)}, u32[]{:S(2)}) copy-start(f32[512,512]{1,0:T(8,128)} %trans.1) | copy-start | bytes 3145732
  25.0 8.3 %collective-permute-start.4 = (f32[128,512]{1,0:T(8,128)S(1)}, f32[128,512]{1,0:T(8,128)S(1)}, u32[]{:S(2)}, u32[]{:S(2)}) collective-permute-start(f32[128,512]{1,0:T(8,128)S(1)} %get-tuple-element.58.one), channel_id=1, source_target_pairs={{0,2},{1,3},{2,0},{3,1},{4,6},{5,7},{6,4},{7,5},{8,10},{9,11},{10,... | collective-permute-start | bytes 786440 | tf_op jit(solution)/shard_map/ppermute | solution.py:704
  25.6 10.0 %collective-permute-start.3 = (bf16[2112,128]{1,0:T(8,128)(2,1)S(1)}, bf16[2112,128]{1,0:T(8,128)(2,1)S(1)}, u32[]{:S(2)}, u32[]{:S(2)}) collective-permute-start(bf16[2112,128]{1,0:T(8,128)(2,1)S(1)} %get-tuple-element.51), channel_id=1, source_target_pairs={{24,9},{1,17},{3,19},{26,11},{30,15},{7,23},{5,21},{28,13}} | collective-permute-start | bytes 1622024 | tf_op jit(solution)/shard_map/ppermute | solution.py:707
  26.3 9.4 %collective-permute-start.2 = (bf16[2112,128]{1,0:T(8,128)(2,1)S(1)}, bf16[2112,128]{1,0:T(8,128)(2,1)S(1)}, u32[]{:S(2)}, u32[]{:S(2)}) collective-permute-start(bf16[2112,128]{1,0:T(8,128)(2,1)S(1)} %get-tuple-element.51), channel_id=1, source_target_pairs={{16,9},{25,17},{27,19},{18,11},{22,15},{31,23},{29,21},{20,13}} | collective-permute-start | bytes 1622024 | tf_op jit(solution)/shard_map/ppermute | solution.py:707
  27.0 14.6 %collective-permute-start.1 = (bf16[2112,128]{1,0:T(8,128)(2,1)S(1)}, bf16[2112,128]{1,0:T(8,128)(2,1)S(1)}, u32[]{:S(2)}, u32[]{:S(2)}) collective-permute-start(bf16[2112,128]{1,0:T(8,128)(2,1)S(1)} %get-tuple-element.51), channel_id=1, source_target_pairs={{0,9},{9,17},{11,19},{2,11},{6,15},{15,23},{13,21},{4,13}} | collective-permute-start | bytes 1622024 | tf_op jit(solution)/shard_map/ppermute | solution.py:707
  31.1 10.5 %collective-permute-start = (bf16[2112,128]{1,0:T(8,128)(2,1)S(1)}, bf16[2112,128]{1,0:T(8,128)(2,1)S(1)}, u32[]{:S(2)}, u32[]{:S(2)}) collective-permute-start(bf16[2112,128]{1,0:T(8,128)(2,1)S(1)} %get-tuple-element.51), channel_id=1, source_target_pairs={{8,9},{10,11},{14,15},{12,13}} | collective-permute-start | bytes 1622024 | tf_op jit(solution)/shard_map/ppermute | solution.py:711
  33.3 2.0 %collective-permute-start.5 = (f32[2,128,512]{2,1,0:T(8,128)S(1)}, f32[2,128,512]{2,1,0:T(8,128)S(1)}, u32[]{:S(2)}, u32[]{:S(2)}) collective-permute-start(f32[2,128,512]{2,1,0:T(8,128)S(1)} %shard_map.107.held), channel_id=1, source_target_pairs={{0,1},{1,0},{2,3},{3,2},{4,5},{5,4},{6,7},{7,6},{8,9},{9,8},{10,11... | collective-permute-start | bytes 1572872 | tf_op jit(solution)/shard_map/ppermute | solution.py:704
  42.4 9.4 %collective-permute-start.9 = (bf16[2112,128]{1,0:T(8,128)(2,1)S(1)}, bf16[2112,128]{1,0:T(8,128)(2,1)S(1)}, u32[]{:S(2)}, u32[]{:S(2)}) collective-permute-start(bf16[2112,128]{1,0:T(8,128)(2,1)S(1)} %shard_map.118), channel_id=1, source_target_pairs={{23,15},{13,21}} | collective-permute-start | bytes 1622024 | tf_op jit(solution)/shard_map/ppermute | solution.py:735
  43.2 0.7 collective-permute-start.6
  43.9 4.7 %collective-permute-start.7 = (f32[1,512]{1,0:T(1,128)S(1)}, f32[1,512]{1,0:T(1,128)S(1)}, u32[]{:S(2)}, u32[]{:S(2)}) collective-permute-start(f32[1,512]{1,0:T(1,128)S(1)} %get-tuple-element.73.after), channel_id=1, source_target_pairs={{17,19}} | collective-permute-start | bytes 6152 | tf_op jit(solution)/shard_map/ppermute | solution.py:741
  49.1 1.9 %collective-permute-start.8 = (f32[1,512]{1,0:T(1,128)S(1)}, f32[1,512]{1,0:T(1,128)S(1)}, u32[]{:S(2)}, u32[]{:S(2)}) collective-permute-start(f32[1,512]{1,0:T(1,128)S(1)} %get-tuple-element.79.after), channel_id=1, source_target_pairs={{19,11}} | collective-permute-start | bytes 6152 | tf_op jit(solution)/shard_map/ppermute | solution.py:741
  51.2 0.8 collective-permute-start.10
  52.0 0.7 collective-permute-start.11

commit v20 on v19

--- a/solution.py
+++ b/solution.py
@@ -377,7 +377,7 @@
 
 def next_day(day, state, damping, pthi, ptlo, zhi, zlo, off):
     moved = mv(state, pthi[...], ptlo[...]) * damping
-    return moved - mv(moved, zhi[day], zlo[day]) + off[day : day + 1, :]
+    return moved, moved - mv(moved, zhi[day], zlo[day]) + off[day : day + 1, :]
 
 
 def owner_kernel(
@@ -445,48 +445,47 @@
     return mm(omhi[day].astype(F32) + omlo[day].astype(F32), chi[...], clo[...])
 
 
-def early_kernel(after, omhi, omlo, info, chi, clo, pt, damping, b1hi, b1lo, off, zhi, zlo):
+def early_kernel(after, omhi, omlo, info, chi, clo, pt, damping, b1hi, b1lo, off):
     @pl.when(here()[1] == 1)
     def _():
-        for day in range(2):
-            off[day : day + 1, :] = mv(info[day], chi[...], clo[...])
+        off[0:1, :] = mv(info[0], chi[...], clo[...])
         moved = pt[...] * damping[0:1, :]
         b1hi[...], b1lo[...] = split(moved - mm(moved, *split(seen(0, omhi, omlo, chi, clo))))
-        zhi[...], zlo[...] = split(seen(1, omhi, omlo, chi, clo))
 
 
 def maps_kernel(
-    after, omhi, omlo, info, chi, clo, pt, damping, zhi, zlo, old1, old2, old3, b1hi, b1lo, off, b2hi, b2lo
+    after, omhi, omlo, info, chi, clo, pt, damping, old1, old2, old3, b1hi, b1lo, off, b2hi, b2lo
 ):
     span = here()[1]
     spans = lax.axis_size("z") * lax.axis_size("y")
-    second = span == 1
-
-    @pl.when(jnp.logical_not(second | (span == spans - 3) | (span == spans - 1)))
-    def _():
-        parts = ((b1hi, b1lo), (b2hi, b2lo))
-        for day in range(2):
-            moved = pt[...] * damping[day : day + 1, :]
-            parts[day][0][...], parts[day][1][...] = split(
-                moved - mm(moved, *split(seen(day, omhi, omlo, chi, clo)))
-            )
-            off[day : day + 1, :] = mv(info[day], chi[...], clo[...])
-
-    @pl.when(second)
-    def _():
-        moved = pt[...] * damping[1:2, :]
-        b2hi[...], b2lo[...] = split(moved - mm(moved, zhi[...], zlo[...]))
-
-
-def second_kernel(acc, got, mine, b1hi, b1lo, off, zhi, zlo, pthi, ptlo, total, y):
+    relays = (span == spans - 3) | (span == spans - 1)
+    parts = ((b1hi, b1lo), (b2hi, b2lo))
+
+    def make(day):
+        moved = pt[...] * damping[day : day + 1, :]
+        parts[day][0][...], parts[day][1][...] = split(
+            moved - mm(moved, *split(seen(day, omhi, omlo, chi, clo)))
+        )
+        off[day : day + 1, :] = mv(info[day], chi[...], clo[...])
+
+    @pl.when(jnp.logical_not(relays | (span == 1)))
+    def _():
+        make(0)
+
+    @pl.when(jnp.logical_not(relays))
+    def _():
+        make(1)
+
+
+def second_kernel(acc, got, mine, b1hi, b1lo, off, omhi, omlo, info, chi, clo, pthi, ptlo, total, y):
     total[...] = acc[...] + got[...]
     y[...] = jnp.zeros(y.shape, F32)
 
     @pl.when(here()[1] == 1)
     def _():
         state = mv(acc[...] + got[...], b1hi[...], b1lo[...]) + off[0:1, :]
-        moved = mv(state, pthi[...], ptlo[...]) * mine[1:2, :]
-        y[...] = moved - mv(moved, zhi[...], zlo[...]) + off[1:2, :]
+        ahead = mv(state, pthi[...], ptlo[...])
+        y[...] = one_day(1, ahead, mine, omhi, omlo, info, chi, clo)
 
 
 def both_kernel(after, b1hi, b1lo, b2hi, b2lo, off, bchi, bclo, offset):
@@ -521,7 +520,7 @@
         state = mv(acc[...] + got[...], bchi[...], bclo[...]) + offset[...]
         for day in range(2):
             r = 2 * (spans - 3) + day
-            state = next_day(day, state, table[r : r + 1, :], pthi, ptlo, zhi, zlo, off)
+            _, state = next_day(day, state, table[r : r + 1, :], pthi, ptlo, zhi, zlo, off)
         y[...] = state
 
 
@@ -557,16 +556,12 @@
         shares[pl.ds(t, 1), :] = v
         return v
 
-    def own_days(rows, damped):
-        both = jnp.concatenate(rows, 0)
-        ahead = jnp.concatenate(damped, 0)
-        const = both - few(few(both, pthi[...], ptlo[...]) * ahead * ahead, mthi[...], mtlo[...])
-        n = len(rows)
-        means[0:n, :] = both
-        v = const[n - 1 : n]
+    def own_days(const, damped):
+        n = len(const)
+        v = const[-1]
         shares[pl.ds(2 * span + n - 1, 1), :] = v
         for i in range(n - 2, -1, -1):
-            v = const[i : i + 1] + mv(v * damped[i], mthi[...], mtlo[...])
+            v = const[i] + mv(v * damped[i], mthi[...], mtlo[...])
             shares[pl.ds(2 * span + i, 1), :] = v
         means[4:5, :] = v
 
@@ -575,7 +570,12 @@
         state = acc[...] + got[...]
         one = mv(state, b1hi[...], b1lo[...]) + off[0:1, :]
         two = mv(one, b2hi[...], b2lo[...]) + off[1:2, :]
-        own_days([one, two], [table[pl.ds(2 * span + 1 + i, 1), :] for i in range(2)])
+        both = jnp.concatenate([one, two], 0)
+        damped = [table[pl.ds(2 * span + 1 + i, 1), :] for i in range(2)]
+        ahead = jnp.concatenate(damped, 0)
+        const = both - few(few(both, pthi[...], ptlo[...]) * ahead * ahead, mthi[...], mtlo[...])
+        means[0:2, :] = both
+        own_days([const[0:1], const[1:2]], damped)
 
     @pl.when(twice)
     def _():
@@ -584,13 +584,29 @@
             mv(state, b1hi[...], b1lo[...]) + off[0:1, :],
             mv(state, bchi[...], bclo[...]) + offset[...],
         ]
+        damped = [table[pl.ds(2 * span + 1 + i, 1), :] for i in range(3)]
+        ahead = [mv(rows[0], pthi[...], ptlo[...]) * damped[0]]
         for day in range(2):
-            damping = table[pl.ds(2 * span + 2 + day, 1), :]
-            rows.append(next_day(day, rows[-1], damping, pthi, ptlo, zhi, zlo, next_off))
-        damped = [table[pl.ds(2 * span + 1 + i, 1), :] for i in range(3)]
-        beyond = table[pl.ds(jnp.minimum(2 * span + 4, total - 1), 1), :]
-        damped.append(beyond * jnp.where(span == spans - 2, 0.0, 1.0))
-        own_days(rows, damped)
+            moved, after = next_day(day, rows[-1], damped[1 + day], pthi, ptlo, zhi, zlo, next_off)
+            ahead.append(moved)
+            rows.append(after)
+        taken = [a * d for a, d in zip(ahead, damped)]
+        taken = few(jnp.concatenate(taken + [jnp.zeros((1, width), F32)], 0), mthi[...], mtlo[...])
+        means[0:4, :] = jnp.concatenate(rows, 0)
+        means[5:8, :] = jnp.concatenate(rows[:3], 0) - taken[0:3]
+        means[4:5, :] = rows[3]
+
+    @pl.when(span == spans - 4)
+    def _():
+        beyond = table[pl.ds(2 * span + 4, 1), :]
+        four = means[3:4, :]
+        ahead = mv(four, pthi[...], ptlo[...]) * beyond * beyond
+        means[4:5, :] = four - mv(ahead, mthi[...], mtlo[...])
+
+    @pl.when(twice)
+    def _():
+        const = [means[5:6, :], means[6:7, :], means[7:8, :], means[4:5, :]]
+        own_days(const, [table[pl.ds(2 * span + 1 + i, 1), :] for i in range(3)])
 
     @pl.when(span < spans - 2)
     def _():
@@ -741,18 +757,20 @@
         received = lax.ppermute(y, everyone, [(owner(source), owner(target))])
         if k == 0:
             given = [omhi, omlo, info, chi, clo, pt, mine]
-            b1hi, b1lo, off, zhi, zlo = run(
-                early_kernel, half + [((8, width), F32)] + half, [(y, ANY), *given], flops=18 * width**3
+            b1hi, b1lo, off = run(
+                early_kernel, half + [((8, width), F32)], [(y, ANY), *given], flops=12 * width**3
             )
             acc, y = run(
-                second_kernel, [row, row], [acc, received, mine, b1hi, b1lo, off, zhi, zlo, pthi, ptlo]
+                second_kernel,
+                [row, row],
+                [acc, received, mine, b1hi, b1lo, off, omhi, omlo, info, chi, clo, pthi, ptlo],
             )
             b1hi, b1lo, off, b2hi, b2lo = run(
                 maps_kernel,
                 half + [((8, width), F32)] + half,
-                [(y, ANY), *given, zhi, zlo, b1hi, b1lo, off],
+                [(y, ANY), *given, b1hi, b1lo, off],
                 flops=24 * width**3,
-                same={10: 0, 11: 1, 12: 2},
+                same={8: 0, 9: 1, 10: 2},
             )
         elif k == 1:
             acc, y = run(days_kernel, [row, row], [acc, received, b1hi, b1lo, b2hi, b2lo, off])

time: 79.2 us -> 79.1 us (level)
  no operation moved by 1% of the time
where the time goes in v20:
time: 79.1 us; the launch traced here: 78.8 us
  blocking collectives  45 us (57%)
  Pallas kernels  13.4 us (17%)
  starting transfers between devices  10.9 us (14%)
  waiting for transfers between devices  8.57 us (11%)
  between operations  0.95 us (1%)
    all_to_all x1, blocking collectives, local(): lax.all_to_all(answer, everyone, split_axis=0, concat_axis=0, tiled=True)  24.1 us
    all_to_all x1, blocking collectives, local(): lax.all_to_all(sent, ('y', 'obs'), split_axis=0, concat_axis=0, tiled=True)  20.8 us
    pallas_call x20, Pallas kernels, run(): pl.pallas_call(body, out_shape=[jax.ShapeDtypeStruct(s, d) for s, d in ou...  13.4 us
    ppermute x3, waiting for transfers between devices, plane_sum(): lax.ppermute(pay, everyone, [((owner_plane(p) + s) % planes * spans + pla...  5.91 us
    ppermute x3, starting transfers between devices, plane_sum(): lax.ppermute(pay, everyone, [((owner_plane(p) + s) % planes * spans + pla...  5.48 us
    ppermute x5, starting transfers between devices, local(): received = lax.ppermute(y, everyone, [(owner(source), owner(target))])  3.35 us
    ppermute x2, waiting for transfers between devices, swap(): return lax.ppermute(x, 'obs', [(i, i ^ bit) for i in range(peers)])  2.64 us
  transfers between devices with their start and end apart: 12, of which 3 were waited for; matrix products, arithmetic and copies ran while one was open for 0% of the time, Pallas kernels for 9%

profile of v20, /device:TPU:0, one launch (start us, length us, event | category | flops | bytes accessed | tf_op | source)
XLA Modules:
  0.0 78.8 jit_solution(11774708891353935015)
XLA Ops:
  0.6 2.2 %shard_map.104 = bf16[8,520,128]{2,1,0:T(8,128)(2,1)} custom-call(s32[8]{0:T(128)} %day.1, s32[8]{0:T(128)} %count.1, bf16[1024,512]{1,0:T(8,128)(2,1)} %rows.1, bf16[8,128]{1,0:T(8,128)(2,1)} %bitcast.2, f32[1,128]{1,0:T(1,128)} %bitcast.3, f32[2,512]{1,0:T(2,128)} %damping.1), custom_call_target="tpu_custom_call" | custom-call | bytes 1055296 | tf_op jit(solution)/shard_map/pallas_call | solution.py:22
  2.9 20.8 %all_to_all.10.got = bf16[8,520,128]{2,1,0:T(8,128)(2,1)S(1)} all-to-all(bf16[8,520,128]{2,1,0:T(8,128)(2,1)} %shard_map.104), channel_id=1, replica_groups=mesh['z'=4,'y'=2,'obs'=4] {'y','obs'}, dimensions={0} | all-to-all | bytes 2129920 | tf_op jit(solution)/shard_map/all_to_all | solution.py:704
  23.7 1.2 %shard_map.105 = (f32[20,128,128]{2,1,0:T(8,128)S(1)}, f32[64,128]{1,0:T(8,128)S(1)}, bf16[2112,128]{1,0:T(8,128)(2,1)S(1)}, f32[1,512]{1,0:T(1,128)S(1)}, f32[128,512]{1,0:T(8,128)S(1)}) custom-call(bf16[8,520,128]{2,1,0:T(8,128)(2,1)S(1)} %all_to_all.10.got, f32[128,512]{1,0:T(8,128)S(1)} %copy-done.2), custom_call_target="tpu_custom_call" | custom-call | flops 1073741824 | bytes 1327104 | tf_op jit(solution)/shard_map/pallas_call | solution.py:22
  25.0 0.6 collective-permute-start.4
  25.6 0.7 collective-permute-start.3
  26.3 0.7 collective-permute-start.2
  27.0 4.1 %collective-permute-start.1 = (bf16[2112,128]{1,0:T(8,128)(2,1)S(1)}, bf16[2112,128]{1,0:T(8,128)(2,1)S(1)}, u32[]{:S(2)}, u32[]{:S(2)}) collective-permute-start(bf16[2112,128]{1,0:T(8,128)(2,1)S(1)} %get-tuple-element.49), channel_id=1, source_target_pairs={{0,9},{9,17},{11,19},{2,11},{6,15},{15,23},{13,21},{4,13}} | collective-permute-start | bytes 1622024 | tf_op jit(solution)/shard_map/ppermute | solution.py:723
  31.1 0.7 collective-permute-start
  31.8 1.5 %collective-permute-done.4.two = f32[128,512]{1,0:T(8,128)S(1)} collective-permute-done((f32[128,512]{1,0:T(8,128)S(1)}, f32[128,512]{1,0:T(8,128)S(1)}, u32[]{:S(2)}, u32[]{:S(2)}) %collective-permute-start.4) | collective-permute-done | bytes 262176 | tf_op jit(solution)/shard_map/ppermute | solution.py:720
  33.4 0.7 shard_map.106
  34.1 1.2 %collective-permute-done.5.got = f32[2,128,512]{2,1,0:T(8,128)S(1)} collective-permute-done((f32[2,128,512]{2,1,0:T(8,128)S(1)}, f32[2,128,512]{2,1,0:T(8,128)S(1)}, u32[]{:S(2)}, u32[]{:S(2)}) %collective-permute-start.5) | collective-permute-done | bytes 524320 | tf_op jit(solution)/shard_map/ppermute | solution.py:720
  35.6 5.9 %collective-permute-done.1.g3 = bf16[2112,128]{1,0:T(8,128)(2,1)S(1)} collective-permute-done((bf16[2112,128]{1,0:T(8,128)(2,1)S(1)}, bf16[2112,128]{1,0:T(8,128)(2,1)S(1)}, u32[]{:S(2)}, u32[]{:S(2)}) %collective-permute-start.1) | collective-permute-done | bytes 540704 | tf_op jit(solution)/shard_map/ppermute | solution.py:723
  41.6 0.9 %shard_map.109 = (bf16[2,512,512]{2,1,0:T(8,128)(2,1)S(1)}, bf16[2,512,512]{2,1,0:T(8,128)(2,1)S(1)}, f32[2,1,512]{2,1,0:T(1,128)S(1)}, f32[2,512]{1,0:T(2,128)S...) custom-call(f32[20,128,128]{2,1,0:T(8,128)S(1)} %get-tuple-element.47.own, f32[64,128]{1,0:T(8,128)S(1)} %get-tuple-element.48.extra, ...), custom_call_target="tpu_custom_call" | custom-call | bytes 6131712 | tf_op jit(solution)/shard_map/pallas_call | solution.py:22
  42.5 0.7 collective-permute-start.9
  43.2 0.7 collective-permute-start.6
  43.9 0.7 collective-permute-start.7
  44.6 4.0 %shard_map.112 = (bf16[512,512]{1,0:T(8,128)(2,1)S(1)}, bf16[512,512]{1,0:T(8,128)(2,1)S(1)}, f32[8,512]{1,0:T(8,128)S(1)}, bf16[512,512]{1,0:T(8,128)(2,1)S(1)}, bf16[512,512]{1,0:T(8,128)(2,1)S(1)}) custom-call(f32[1,512]{1,0:T(1,128)S(1)} %get-tuple-element.69.after, ...), custom_call_target="tpu_custom_call", output_to_operand_aliasing={{0}: (8, {}), {1}: (9, {}), {2}: (10, {})} | custom-call | flops 3221225472 | bytes 5269504 | tf_op jit(solution)/shard_map/pallas_call | solution.py:22
  49.1 0.7 collective-permute-start.8
  49.8 1.1 %shard_map.114 = (bf16[512,512]{1,0:T(8,128)(2,1)S(1)}, bf16[512,512]{1,0:T(8,128)(2,1)S(1)}, f32[1,512]{1,0:T(1,128)S(1)}) custom-call(f32[1,512]{1,0:T(1,128)S(1)} %get-tuple-element.75.after, bf16[512,512]{1,0:T(8,128)(2,1)S(1)} %get-tuple-element.70.b1hi, bf16[512,512]{1,0:T(8,128)(2,1)S(1)} %get-tuple-element.71.b1lo, ...), custom_call_target="tpu_custom_call" | custom-call | bytes 2115584 | tf_op jit(solution)/shard_map/pallas_call | solution.py:22
  51.4 0.7 collective-permute-start.10
  52.2 0.7 collective-permute-start.11
  52.9 1.2 %shard_map.122 = f32[32,8,128]{2,1,0:T(8,128)S(1)} custom-call(f32[1,512]{1,0:T(1,128)S(1)} %get-tuple-element.87.acc, f32[1,512]{1,0:T(1,128)S(1)} %collective-permute-done.11.got, bf16[512,512]{1,0:T(8,128)(2,1)S(1)} %get-tuple-element.70.b1hi, bf16[512,512]{1,0:T(8,128)(2,1)S(1)} %get-tuple-element.71.b1lo, bf16[512,512]{1,0:T(8,128)(2,1)S(1)} %get-tuple-element.72.b2hi, ...), custom_call_target="tpu_custom_call" | custom-call | bytes 13703168 | tf_op jit(solution)/shard_map/pallas_call | solution.py:22
  54.1 24.1 %all_to_all.11.parts = f32[32,8,128]{2,1,0:T(8,128)S(1)} all-to-all(f32[32,8,128]{2,1,0:T(8,128)S(1)} %shard_map.122), channel_id=1, replica_groups=mesh['z'=4,'y'=2,'obs'=4] {'z','y','obs'}, dimensions={0} | all-to-all | bytes 262144 | tf_op jit(solution)/shard_map/all_to_all | solution.py:818
  78.2 0.6 shard_map.123
  (28 shorter events, 1.6 us)
Async XLA Ops:
  2.9 20.9 %copy-start.2 = (f32[128,512]{1,0:T(8,128)S(1)}, f32[128,512]{1,0:T(8,128)}, u32[]{:S(2)}) copy-start(f32[128,512]{1,0:T(8,128)} %gain.1) | copy-start | bytes 786436
  23.7 9.7 %copy-start.1 = (f32[512,512]{1,0:T(8,128)S(1)}, f32[512,512]{1,0:T(8,128)}, u32[]{:S(2)}) copy-start(f32[512,512]{1,0:T(8,128)} %cov.1) | copy-start | bytes 3145732
  24.9 8.4 %copy-start = (f32[512,512]{1,0:T(8,128)S(1)}, f32[512,512]{1,0:T(8,128)}, u32[]{:S(2)}) copy-start(f32[512,512]{1,0:T(8,128)} %trans.1) | copy-start | bytes 3145732
  25.0 8.3 %collective-permute-start.4 = (f32[128,512]{1,0:T(8,128)S(1)}, f32[128,512]{1,0:T(8,128)S(1)}, u32[]{:S(2)}, u32[]{:S(2)}) collective-permute-start(f32[128,512]{1,0:T(8,128)S(1)} %get-tuple-element.56.one), channel_id=1, source_target_pairs={{0,2},{1,3},{2,0},{3,1},{4,6},{5,7},{6,4},{7,5},{8,10},{9,11},{10,... | collective-permute-start | bytes 786440 | tf_op jit(solution)/shard_map/ppermute | solution.py:720
  25.6 10.0 %collective-permute-start.3 = (bf16[2112,128]{1,0:T(8,128)(2,1)S(1)}, bf16[2112,128]{1,0:T(8,128)(2,1)S(1)}, u32[]{:S(2)}, u32[]{:S(2)}) collective-permute-start(bf16[2112,128]{1,0:T(8,128)(2,1)S(1)} %get-tuple-element.49), channel_id=1, source_target_pairs={{24,9},{1,17},{3,19},{26,11},{30,15},{7,23},{5,21},{28,13}} | collective-permute-start | bytes 1622024 | tf_op jit(solution)/shard_map/ppermute | solution.py:723
  26.3 9.4 %collective-permute-start.2 = (bf16[2112,128]{1,0:T(8,128)(2,1)S(1)}, bf16[2112,128]{1,0:T(8,128)(2,1)S(1)}, u32[]{:S(2)}, u32[]{:S(2)}) collective-permute-start(bf16[2112,128]{1,0:T(8,128)(2,1)S(1)} %get-tuple-element.49), channel_id=1, source_target_pairs={{16,9},{25,17},{27,19},{18,11},{22,15},{31,23},{29,21},{20,13}} | collective-permute-start | bytes 1622024 | tf_op jit(solution)/shard_map/ppermute | solution.py:723
  27.0 14.6 %collective-permute-start.1 = (bf16[2112,128]{1,0:T(8,128)(2,1)S(1)}, bf16[2112,128]{1,0:T(8,128)(2,1)S(1)}, u32[]{:S(2)}, u32[]{:S(2)}) collective-permute-start(bf16[2112,128]{1,0:T(8,128)(2,1)S(1)} %get-tuple-element.49), channel_id=1, source_target_pairs={{0,9},{9,17},{11,19},{2,11},{6,15},{15,23},{13,21},{4,13}} | collective-permute-start | bytes 1622024 | tf_op jit(solution)/shard_map/ppermute | solution.py:723
  31.1 10.5 %collective-permute-start = (bf16[2112,128]{1,0:T(8,128)(2,1)S(1)}, bf16[2112,128]{1,0:T(8,128)(2,1)S(1)}, u32[]{:S(2)}, u32[]{:S(2)}) collective-permute-start(bf16[2112,128]{1,0:T(8,128)(2,1)S(1)} %get-tuple-element.49), channel_id=1, source_target_pairs={{8,9},{10,11},{14,15},{12,13}} | collective-permute-start | bytes 1622024 | tf_op jit(solution)/shard_map/ppermute | solution.py:727
  33.3 2.0 %collective-permute-start.5 = (f32[2,128,512]{2,1,0:T(8,128)S(1)}, f32[2,128,512]{2,1,0:T(8,128)S(1)}, u32[]{:S(2)}, u32[]{:S(2)}) collective-permute-start(f32[2,128,512]{2,1,0:T(8,128)S(1)} %shard_map.107.held), channel_id=1, source_target_pairs={{0,1},{1,0},{2,3},{3,2},{4,5},{5,4},{6,7},{7,6},{8,9},{9,8},{10,11... | collective-permute-start | bytes 1572872 | tf_op jit(solution)/shard_map/ppermute | solution.py:720
  42.5 9.6 %collective-permute-start.9 = (bf16[2112,128]{1,0:T(8,128)(2,1)S(1)}, bf16[2112,128]{1,0:T(8,128)(2,1)S(1)}, u32[]{:S(2)}, u32[]{:S(2)}) collective-permute-start(bf16[2112,128]{1,0:T(8,128)(2,1)S(1)} %shard_map.118), channel_id=1, source_target_pairs={{23,15},{13,21}} | collective-permute-start | bytes 1622024 | tf_op jit(solution)/shard_map/ppermute | solution.py:751
  43.2 0.7 collective-permute-start.6
  43.9 4.7 %collective-permute-start.7 = (f32[1,512]{1,0:T(1,128)S(1)}, f32[1,512]{1,0:T(1,128)S(1)}, u32[]{:S(2)}, u32[]{:S(2)}) collective-permute-start(f32[1,512]{1,0:T(1,128)S(1)} %get-tuple-element.69.after), channel_id=1, source_target_pairs={{17,19}} | collective-permute-start | bytes 6152 | tf_op jit(solution)/shard_map/ppermute | solution.py:757
  49.1 2.0 %collective-permute-start.8 = (f32[1,512]{1,0:T(1,128)S(1)}, f32[1,512]{1,0:T(1,128)S(1)}, u32[]{:S(2)}, u32[]{:S(2)}) collective-permute-start(f32[1,512]{1,0:T(1,128)S(1)} %get-tuple-element.75.after), channel_id=1, source_target_pairs={{19,11}} | collective-permute-start | bytes 6152 | tf_op jit(solution)/shard_map/ppermute | solution.py:757
  51.4 0.8 collective-permute-start.10
  52.2 0.7 collective-permute-start.11

commit v21 on v20

--- a/solution.py
+++ b/solution.py
@@ -36,14 +36,14 @@
     held, peers = lax.axis_size("y"), lax.axis_size("obs")
     spans = held * peers
     at = y * peers + o
-    seat = jnp.where(z == 1, at - lax.rem(at, 2), at)
+    seat = jnp.where(z == 2, at - lax.rem(at, 2), at) ^ (spans // 2)
     span = seat
     for bit in range(1, spans.bit_length()):
         span = span ^ (seat >> bit)
     c = z * held + y
     kept = jnp.where((c == spans - 3) | (c == spans - 1), c - 1, c)
-    seat = kept ^ (kept >> 1)
-    return z, span, o, c, (1 + (seat & 1)) * spans + (seat | 1), held
+    seat = place(kept)
+    return z, span, o, c, (2 - (seat & 1)) * spans + (seat | 1), held
 
 
 def doubled(span, spans):
@@ -82,11 +82,11 @@
 
 
 def place(span):
-    return span ^ (span >> 1)
+    return span ^ (span >> 1) ^ (lax.axis_size("z") * lax.axis_size("y") // 2)
 
 
 def owner_plane(span):
-    return 1 + place(span) % 2
+    return 2 - place(span) % 2
 
 
 EXTRA = 8
@@ -293,7 +293,7 @@
 
 
 def sums(extra, got, small):
-    share = jnp.where(here()[0] == 2, 1.0, 0.0)
+    share = jnp.where(here()[0] == 1, 1.0, 0.0)
     spread(extra, got, small)
 
     def summed(first):
@@ -725,7 +725,7 @@
         )
 
     fourth = lax.ppermute(
-        pay, everyone, [(spans + place(p), owner(p)) for p in range(spans) if place(p) % 2 == 0]
+        pay, everyone, [(2 * spans + place(p), owner(p)) for p in range(spans) if place(p) % 2 == 0]
     )
     second, first, third = plane_sum(2), plane_sum(1), plane_sum(3)
     (gains,) = run(stack_kernel, [((2,) + gain.shape, F32)], [gain, swap(gain, 2)])

time: 79.1 us -> 79.1 us (level)
  blocking collectives: 45 us -> 50 us
  Pallas kernels: 13.4 us -> 8.69 us
    all_to_all x1, blocking collectives: 24.1 us -> 29.2 us  [local(): lax.all_to_all(answer, everyone, split_axis=0, concat_axis=0, tiled=True)]
    pallas_call x20, Pallas kernels: 13.4 us -> 8.69 us  [run(): pl.pallas_call(body, out_shape=[jax.ShapeDtypeStruct(s, d) for s, d in ou...]
  transfers between devices with their start and end apart: 12 -> 12, of which waited for: 3 -> 3; matrix products, arithmetic and copies ran while one was open for 0% -> 0% of each run, Pallas kernels for 9% -> 4%
where the time goes in v21:
time: 79.1 us; the launch traced here: 78.7 us
  blocking collectives  50 us (63%)
  starting transfers between devices  10.7 us (14%)
  Pallas kernels  8.69 us (11%)
  waiting for transfers between devices  8.32 us (11%)
  between operations  0.94 us (1%)
    all_to_all x1, blocking collectives, local(): lax.all_to_all(answer, everyone, split_axis=0, concat_axis=0, tiled=True)  29.2 us
    all_to_all x1, blocking collectives, local(): lax.all_to_all(sent, ('y', 'obs'), split_axis=0, concat_axis=0, tiled=True)  20.8 us
    pallas_call x20, Pallas kernels, run(): pl.pallas_call(body, out_shape=[jax.ShapeDtypeStruct(s, d) for s, d in ou...  8.69 us
    ppermute x3, waiting for transfers between devices, plane_sum(): lax.ppermute(pay, everyone, [((owner_plane(p) + s) % planes * spans + pla...  5.5 us
    ppermute x3, starting transfers between devices, plane_sum(): lax.ppermute(pay, everyone, [((owner_plane(p) + s) % planes * spans + pla...  5.31 us
    ppermute x5, starting transfers between devices, local(): received = lax.ppermute(y, everyone, [(owner(source), owner(target))])  3.35 us
    ppermute x2, waiting for transfers between devices, swap(): return lax.ppermute(x, 'obs', [(i, i ^ bit) for i in range(peers)])  2.81 us
  transfers between devices with their start and end apart: 12, of which 3 were waited for; matrix products, arithmetic and copies ran while one was open for 0% of the time, Pallas kernels for 4%

profile of v21, /device:TPU:0, one launch (start us, length us, event | category | flops | bytes accessed | tf_op | source)
XLA Modules:
  0.0 78.7 jit_solution(1466828496791174058)
XLA Ops:
  0.6 2.2 %shard_map.104 = bf16[8,520,128]{2,1,0:T(8,128)(2,1)} custom-call(s32[8]{0:T(128)} %day.1, s32[8]{0:T(128)} %count.1, bf16[1024,512]{1,0:T(8,128)(2,1)} %rows.1, bf16[8,128]{1,0:T(8,128)(2,1)} %bitcast.2, f32[1,128]{1,0:T(1,128)} %bitcast.3, f32[2,512]{1,0:T(2,128)} %damping.1), custom_call_target="tpu_custom_call" | custom-call | bytes 1055296 | tf_op jit(solution)/shard_map/pallas_call | solution.py:22
  2.9 20.8 %all_to_all.10.got = bf16[8,520,128]{2,1,0:T(8,128)(2,1)S(1)} all-to-all(bf16[8,520,128]{2,1,0:T(8,128)(2,1)} %shard_map.104), channel_id=1, replica_groups=mesh['z'=4,'y'=2,'obs'=4] {'y','obs'}, dimensions={0} | all-to-all | bytes 2129920 | tf_op jit(solution)/shard_map/all_to_all | solution.py:704
  23.7 1.2 %shard_map.105 = (f32[20,128,128]{2,1,0:T(8,128)S(1)}, f32[64,128]{1,0:T(8,128)S(1)}, bf16[2112,128]{1,0:T(8,128)(2,1)S(1)}, f32[1,512]{1,0:T(1,128)S(1)}, f32[128,512]{1,0:T(8,128)S(1)}) custom-call(bf16[8,520,128]{2,1,0:T(8,128)(2,1)S(1)} %all_to_all.10.got, f32[128,512]{1,0:T(8,128)S(1)} %copy-done.2), custom_call_target="tpu_custom_call" | custom-call | flops 1073741824 | bytes 1327104 | tf_op jit(solution)/shard_map/pallas_call | solution.py:22
  25.0 0.6 collective-permute-start.4
  25.6 3.9 %collective-permute-start.3 = (bf16[2112,128]{1,0:T(8,128)(2,1)S(1)}, bf16[2112,128]{1,0:T(8,128)(2,1)S(1)}, u32[]{:S(2)}, u32[]{:S(2)}) collective-permute-start(bf16[2112,128]{1,0:T(8,128)(2,1)S(1)} %get-tuple-element.49), channel_id=1, source_target_pairs={{4,21},{29,13},{31,15},{6,23},{2,19},{27,11},{25,9},{0,17}} | collective-permute-start | bytes 1622024 | tf_op jit(solution)/shard_map/ppermute | solution.py:723
  29.5 0.7 collective-permute-start.2
  30.2 0.7 collective-permute-start.1
  30.9 0.7 collective-permute-start
  31.6 1.6 %collective-permute-done.4.two = f32[128,512]{1,0:T(8,128)S(1)} collective-permute-done((f32[128,512]{1,0:T(8,128)S(1)}, f32[128,512]{1,0:T(8,128)S(1)}, u32[]{:S(2)}, u32[]{:S(2)}) %collective-permute-start.4) | collective-permute-done | bytes 262176 | tf_op jit(solution)/shard_map/ppermute | solution.py:720
  33.4 0.7 shard_map.106
  34.1 1.2 %collective-permute-done.5.got = f32[2,128,512]{2,1,0:T(8,128)S(1)} collective-permute-done((f32[2,128,512]{2,1,0:T(8,128)S(1)}, f32[2,128,512]{2,1,0:T(8,128)S(1)}, u32[]{:S(2)}, u32[]{:S(2)}) %collective-permute-start.5) | collective-permute-done | bytes 524320 | tf_op jit(solution)/shard_map/ppermute | solution.py:720
  35.6 5.5 %collective-permute-done.3.g2 = bf16[2112,128]{1,0:T(8,128)(2,1)S(1)} collective-permute-done((bf16[2112,128]{1,0:T(8,128)(2,1)S(1)}, bf16[2112,128]{1,0:T(8,128)(2,1)S(1)}, u32[]{:S(2)}, u32[]{:S(2)}) %collective-permute-start.3) | collective-permute-done | bytes 540704 | tf_op jit(solution)/shard_map/ppermute | solution.py:723
  41.1 0.9 %shard_map.109 = (bf16[2,512,512]{2,1,0:T(8,128)(2,1)S(1)}, bf16[2,512,512]{2,1,0:T(8,128)(2,1)S(1)}, f32[2,1,512]{2,1,0:T(1,128)S(1)}, f32[2,512]{1,0:T(2,128)S...) custom-call(f32[20,128,128]{2,1,0:T(8,128)S(1)} %get-tuple-element.47.own, f32[64,128]{1,0:T(8,128)S(1)} %get-tuple-element.48.extra, ...), custom_call_target="tpu_custom_call" | custom-call | bytes 6131712 | tf_op jit(solution)/shard_map/pallas_call | solution.py:22
  42.0 0.5 shard_map.118
  42.5 0.7 collective-permute-start.9
  43.2 0.7 collective-permute-start.6
  43.9 0.7 collective-permute-start.7
  44.6 0.5 shard_map.113
  45.1 0.7 collective-permute-start.8
  45.8 1.1 %shard_map.114 = (bf16[512,512]{1,0:T(8,128)(2,1)S(1)}, bf16[512,512]{1,0:T(8,128)(2,1)S(1)}, f32[1,512]{1,0:T(1,128)S(1)}) custom-call(f32[1,512]{1,0:T(1,128)S(1)} %get-tuple-element.75.after, bf16[512,512]{1,0:T(8,128)(2,1)S(1)} %get-tuple-element.70.b1hi, bf16[512,512]{1,0:T(8,128)(2,1)S(1)} %get-tuple-element.71.b1lo, ...), custom_call_target="tpu_custom_call" | custom-call | bytes 2115584 | tf_op jit(solution)/shard_map/pallas_call | solution.py:22
  47.4 0.7 collective-permute-start.10
  48.2 0.7 collective-permute-start.11
  49.0 29.2 %all_to_all.11.parts = f32[32,8,128]{2,1,0:T(8,128)S(1)} all-to-all(f32[32,8,128]{2,1,0:T(8,128)S(1)} %shard_map.122), channel_id=1, replica_groups=mesh['z'=4,'y'=2,'obs'=4] {'z','y','obs'}, dimensions={0} | all-to-all | bytes 262144 | tf_op jit(solution)/shard_map/all_to_all | solution.py:818
  78.2 0.6 shard_map.123
  (28 shorter events, 1.2 us)
Async XLA Ops:
  2.9 20.9 %copy-start.2 = (f32[128,512]{1,0:T(8,128)S(1)}, f32[128,512]{1,0:T(8,128)}, u32[]{:S(2)}) copy-start(f32[128,512]{1,0:T(8,128)} %gain.1) | copy-start | bytes 786436
  23.7 9.7 %copy-start.1 = (f32[512,512]{1,0:T(8,128)S(1)}, f32[512,512]{1,0:T(8,128)}, u32[]{:S(2)}) copy-start(f32[512,512]{1,0:T(8,128)} %cov.1) | copy-start | bytes 3145732
  25.0 8.4 %copy-start = (f32[512,512]{1,0:T(8,128)S(1)}, f32[512,512]{1,0:T(8,128)}, u32[]{:S(2)}) copy-start(f32[512,512]{1,0:T(8,128)} %trans.1) | copy-start | bytes 3145732
  25.0 8.3 %collective-permute-start.4 = (f32[128,512]{1,0:T(8,128)S(1)}, f32[128,512]{1,0:T(8,128)S(1)}, u32[]{:S(2)}, u32[]{:S(2)}) collective-permute-start(f32[128,512]{1,0:T(8,128)S(1)} %get-tuple-element.56.one), channel_id=1, source_target_pairs={{0,2},{1,3},{2,0},{3,1},{4,6},{5,7},{6,4},{7,5},{8,10},{9,11},{10,... | collective-permute-start | bytes 786440 | tf_op jit(solution)/shard_map/ppermute | solution.py:720
  25.6 15.5 %collective-permute-start.3 = (bf16[2112,128]{1,0:T(8,128)(2,1)S(1)}, bf16[2112,128]{1,0:T(8,128)(2,1)S(1)}, u32[]{:S(2)}, u32[]{:S(2)}) collective-permute-start(bf16[2112,128]{1,0:T(8,128)(2,1)S(1)} %get-tuple-element.49), channel_id=1, source_target_pairs={{4,21},{29,13},{31,15},{6,23},{2,19},{27,11},{25,9},{0,17}} | collective-permute-start | bytes 1622024 | tf_op jit(solution)/shard_map/ppermute | solution.py:723
  29.5 11.6 %collective-permute-start.2 = (bf16[2112,128]{1,0:T(8,128)(2,1)S(1)}, bf16[2112,128]{1,0:T(8,128)(2,1)S(1)}, u32[]{:S(2)}, u32[]{:S(2)}) collective-permute-start(bf16[2112,128]{1,0:T(8,128)(2,1)S(1)} %get-tuple-element.49), channel_id=1, source_target_pairs={{28,21},{21,13},{23,15},{30,23},{26,19},{19,11},{17,9},{24,17}} | collective-permute-start | bytes 1622024 | tf_op jit(solution)/shard_map/ppermute | solution.py:723
  30.2 10.9 %collective-permute-start.1 = (bf16[2112,128]{1,0:T(8,128)(2,1)S(1)}, bf16[2112,128]{1,0:T(8,128)(2,1)S(1)}, u32[]{:S(2)}, u32[]{:S(2)}) collective-permute-start(bf16[2112,128]{1,0:T(8,128)(2,1)S(1)} %get-tuple-element.49), channel_id=1, source_target_pairs={{12,21},{5,13},{7,15},{14,23},{10,19},{3,11},{1,9},{8,17}} | collective-permute-start | bytes 1622024 | tf_op jit(solution)/shard_map/ppermute | solution.py:723
  30.9 10.2 %collective-permute-start = (bf16[2112,128]{1,0:T(8,128)(2,1)S(1)}, bf16[2112,128]{1,0:T(8,128)(2,1)S(1)}, u32[]{:S(2)}, u32[]{:S(2)}) collective-permute-start(bf16[2112,128]{1,0:T(8,128)(2,1)S(1)} %get-tuple-element.49), channel_id=1, source_target_pairs={{20,21},{22,23},{18,19},{16,17}} | collective-permute-start | bytes 1622024 | tf_op jit(solution)/shard_map/ppermute | solution.py:727
  33.3 2.0 %collective-permute-start.5 = (f32[2,128,512]{2,1,0:T(8,128)S(1)}, f32[2,128,512]{2,1,0:T(8,128)S(1)}, u32[]{:S(2)}, u32[]{:S(2)}) collective-permute-start(f32[2,128,512]{2,1,0:T(8,128)S(1)} %shard_map.107.held), channel_id=1, source_target_pairs={{0,1},{1,0},{2,3},{3,2},{4,5},{5,4},{6,7},{7,6},{8,9},{9,8},{10,11... | collective-permute-start | bytes 1572872 | tf_op jit(solution)/shard_map/ppermute | solution.py:720
  42.5 5.6 %collective-permute-start.9 = (bf16[2112,128]{1,0:T(8,128)(2,1)S(1)}, bf16[2112,128]{1,0:T(8,128)(2,1)S(1)}, u32[]{:S(2)}, u32[]{:S(2)}) collective-permute-start(bf16[2112,128]{1,0:T(8,128)(2,1)S(1)} %shard_map.118), channel_id=1, source_target_pairs={{11,19},{17,9}} | collective-permute-start | bytes 1622024 | tf_op jit(solution)/shard_map/ppermute | solution.py:751
  43.2 0.7 collective-permute-start.6
  43.9 0.7 collective-permute-start.7
  45.1 2.0 %collective-permute-start.8 = (f32[1,512]{1,0:T(1,128)S(1)}, f32[1,512]{1,0:T(1,128)S(1)}, u32[]{:S(2)}, u32[]{:S(2)}) collective-permute-start(f32[1,512]{1,0:T(1,128)S(1)} %get-tuple-element.75.after), channel_id=1, source_target_pairs={{15,23}} | collective-permute-start | bytes 6152 | tf_op jit(solution)/shard_map/ppermute | solution.py:757
  47.4 0.8 collective-permute-start.10
  48.2 0.7 collective-permute-start.11

commit v22 on v20

--- a/solution.py
+++ b/solution.py
@@ -36,13 +36,13 @@
     held, peers = lax.axis_size("y"), lax.axis_size("obs")
     spans = held * peers
     at = y * peers + o
-    seat = jnp.where(z == 1, at - lax.rem(at, 2), at)
+    seat = jnp.where(z == 1, at - lax.rem(at, 2), at) ^ (spans // 2 + 1)
     span = seat
     for bit in range(1, spans.bit_length()):
         span = span ^ (seat >> bit)
     c = z * held + y
     kept = jnp.where((c == spans - 3) | (c == spans - 1), c - 1, c)
-    seat = kept ^ (kept >> 1)
+    seat = place(kept)
     return z, span, o, c, (1 + (seat & 1)) * spans + (seat | 1), held
 
 
@@ -82,7 +82,7 @@
 
 
 def place(span):
-    return span ^ (span >> 1)
+    return span ^ (span >> 1) ^ (lax.axis_size("z") * lax.axis_size("y") // 2 + 1)
 
 
 def owner_plane(span):

time: 79.1 us -> 78.2 us (0.989)
  blocking collectives: 45 us -> 33.3 us
  Pallas kernels: 13.4 us -> 24.1 us
    all_to_all x1, blocking collectives: 24.1 us -> 12.5 us  [local(): lax.all_to_all(answer, everyone, split_axis=0, concat_axis=0, tiled=True)]
    pallas_call x20, Pallas kernels: 13.4 us -> 24.1 us  [run(): pl.pallas_call(body, out_shape=[jax.ShapeDtypeStruct(s, d) for s, d in ou...]
  transfers between devices with their start and end apart: 12 -> 12, of which waited for: 3 -> 3; matrix products, arithmetic and copies ran while one was open for 0% -> 0% of each run, Pallas kernels for 9% -> 20%
where the time goes in v22:
time: 78.2 us; the launch traced here: 77.9 us
  blocking collectives  33.3 us (43%)
  Pallas kernels  24.1 us (31%)
  starting transfers between devices  10.9 us (14%)
  waiting for transfers between devices  8.59 us (11%)
  between operations  0.95 us (1%)
    pallas_call x20, Pallas kernels, run(): pl.pallas_call(body, out_shape=[jax.ShapeDtypeStruct(s, d) for s, d in ou...  24.1 us
    all_to_all x1, blocking collectives, local(): lax.all_to_all(sent, ('y', 'obs'), split_axis=0, concat_axis=0, tiled=True)  20.8 us
    all_to_all x1, blocking collectives, local(): lax.all_to_all(answer, everyone, split_axis=0, concat_axis=0, tiled=True)  12.5 us
    ppermute x3, waiting for transfers between devices, plane_sum(): lax.ppermute(pay, everyone, [((owner_plane(p) + s) % planes * spans + pla...  5.91 us
    ppermute x3, starting transfers between devices, plane_sum(): lax.ppermute(pay, everyone, [((owner_plane(p) + s) % planes * spans + pla...  5.47 us
    ppermute x5, starting transfers between devices, local(): received = lax.ppermute(y, everyone, [(owner(source), owner(target))])  3.35 us
    ppermute x2, waiting for transfers between devices, swap(): return lax.ppermute(x, 'obs', [(i, i ^ bit) for i in range(peers)])  2.63 us
  transfers between devices with their start and end apart: 12, of which 3 were waited for; matrix products, arithmetic and copies ran while one was open for 0% of the time, Pallas kernels for 20%

profile of v22, /device:TPU:0, one launch (start us, length us, event | category | flops | bytes accessed | tf_op | source)
XLA Modules:
  0.0 77.9 jit_solution(1928300324044462361)
XLA Ops:
  0.6 2.2 %shard_map.104 = bf16[8,520,128]{2,1,0:T(8,128)(2,1)} custom-call(s32[8]{0:T(128)} %day.1, s32[8]{0:T(128)} %count.1, bf16[1024,512]{1,0:T(8,128)(2,1)} %rows.1, bf16[8,128]{1,0:T(8,128)(2,1)} %bitcast.2, f32[1,128]{1,0:T(1,128)} %bitcast.3, f32[2,512]{1,0:T(2,128)} %damping.1), custom_call_target="tpu_custom_call" | custom-call | bytes 1055296 | tf_op jit(solution)/shard_map/pallas_call | solution.py:22
  2.9 20.8 %all_to_all.10.got = bf16[8,520,128]{2,1,0:T(8,128)(2,1)S(1)} all-to-all(bf16[8,520,128]{2,1,0:T(8,128)(2,1)} %shard_map.104), channel_id=1, replica_groups=mesh['z'=4,'y'=2,'obs'=4] {'y','obs'}, dimensions={0} | all-to-all | bytes 2129920 | tf_op jit(solution)/shard_map/all_to_all | solution.py:704
  23.7 1.2 %shard_map.105 = (f32[20,128,128]{2,1,0:T(8,128)S(1)}, f32[64,128]{1,0:T(8,128)S(1)}, bf16[2112,128]{1,0:T(8,128)(2,1)S(1)}, f32[1,512]{1,0:T(1,128)S(1)}, f32[128,512]{1,0:T(8,128)S(1)}) custom-call(bf16[8,520,128]{2,1,0:T(8,128)(2,1)S(1)} %all_to_all.10.got, f32[128,512]{1,0:T(8,128)S(1)} %copy-done.2), custom_call_target="tpu_custom_call" | custom-call | flops 1073741824 | bytes 1327104 | tf_op jit(solution)/shard_map/pallas_call | solution.py:22
  25.6 0.7 collective-permute-start.3
  26.3 0.7 collective-permute-start.2
  27.0 4.1 %collective-permute-start.1 = (bf16[2112,128]{1,0:T(8,128)(2,1)S(1)}, bf16[2112,128]{1,0:T(8,128)(2,1)S(1)}, u32[]{:S(2)}, u32[]{:S(2)}) collective-permute-start(bf16[2112,128]{1,0:T(8,128)(2,1)S(1)} %get-tuple-element.49), channel_id=1, source_target_pairs={{13,21},{4,13},{6,15},{15,23},{11,19},{2,11},{0,9},{9,17}} | collective-permute-start | bytes 1622024 | tf_op jit(solution)/shard_map/ppermute | solution.py:723
  31.1 0.7 collective-permute-start
  31.8 1.5 %collective-permute-done.4.two = f32[128,512]{1,0:T(8,128)S(1)} collective-permute-done((f32[128,512]{1,0:T(8,128)S(1)}, f32[128,512]{1,0:T(8,128)S(1)}, u32[]{:S(2)}, u32[]{:S(2)}) %collective-permute-start.4) | collective-permute-done | bytes 262176 | tf_op jit(solution)/shard_map/ppermute | solution.py:720
  33.4 0.7 shard_map.106
  34.1 1.2 %collective-permute-done.5.got = f32[2,128,512]{2,1,0:T(8,128)S(1)} collective-permute-done((f32[2,128,512]{2,1,0:T(8,128)S(1)}, f32[2,128,512]{2,1,0:T(8,128)S(1)}, u32[]{:S(2)}, u32[]{:S(2)}) %collective-permute-start.5) | collective-permute-done | bytes 524320 | tf_op jit(solution)/shard_map/ppermute | solution.py:720
  35.6 5.9 %collective-permute-done.1.g3 = bf16[2112,128]{1,0:T(8,128)(2,1)S(1)} collective-permute-done((bf16[2112,128]{1,0:T(8,128)(2,1)S(1)}, bf16[2112,128]{1,0:T(8,128)(2,1)S(1)}, u32[]{:S(2)}, u32[]{:S(2)}) %collective-permute-start.1) | collective-permute-done | bytes 540704 | tf_op jit(solution)/shard_map/ppermute | solution.py:723
  41.6 0.9 %shard_map.109 = (bf16[2,512,512]{2,1,0:T(8,128)(2,1)S(1)}, bf16[2,512,512]{2,1,0:T(8,128)(2,1)S(1)}, f32[2,1,512]{2,1,0:T(1,128)S(1)}, f32[2,512]{1,0:T(2,128)S...) custom-call(f32[20,128,128]{2,1,0:T(8,128)S(1)} %get-tuple-element.47.own, f32[64,128]{1,0:T(8,128)S(1)} %get-tuple-element.48.extra, ...), custom_call_target="tpu_custom_call" | custom-call | bytes 6131712 | tf_op jit(solution)/shard_map/pallas_call | solution.py:22
  42.5 0.7 collective-permute-start.9
  43.2 0.7 collective-permute-start.6
  44.6 4.0 %shard_map.112 = (bf16[512,512]{1,0:T(8,128)(2,1)S(1)}, bf16[512,512]{1,0:T(8,128)(2,1)S(1)}, f32[8,512]{1,0:T(8,128)S(1)}, bf16[512,512]{1,0:T(8,128)(2,1)S(1)}, bf16[512,512]{1,0:T(8,128)(2,1)S(1)}) custom-call(f32[1,512]{1,0:T(1,128)S(1)} %get-tuple-element.69.after, ...), custom_call_target="tpu_custom_call", output_to_operand_aliasing={{0}: (8, {}), {1}: (9, {}), {2}: (10, {})} | custom-call | flops 3221225472 | bytes 5269504 | tf_op jit(solution)/shard_map/pallas_call | solution.py:22
  49.1 0.7 collective-permute-start.8
  49.8 1.1 %shard_map.114 = (bf16[512,512]{1,0:T(8,128)(2,1)S(1)}, bf16[512,512]{1,0:T(8,128)(2,1)S(1)}, f32[1,512]{1,0:T(1,128)S(1)}) custom-call(f32[1,512]{1,0:T(1,128)S(1)} %get-tuple-element.75.after, bf16[512,512]{1,0:T(8,128)(2,1)S(1)} %get-tuple-element.70.b1hi, bf16[512,512]{1,0:T(8,128)(2,1)S(1)} %get-tuple-element.71.b1lo, ...), custom_call_target="tpu_custom_call" | custom-call | bytes 2115584 | tf_op jit(solution)/shard_map/pallas_call | solution.py:22
  50.9 2.2 %shard_map.116 = (bf16[2,512,512]{2,1,0:T(8,128)(2,1)S(1)}, bf16[2,512,512]{2,1,0:T(8,128)(2,1)S(1)}) custom-call(f32[1,512]{1,0:T(1,128)S(1)} %get-tuple-element.75.after, f32[16,512]{1,0:T(8,128)S(1)} %shard_map.115.table, bf16[512,512]{1,0:T(8,128)(2,1)S(1)} %get-tuple-element.57.after.mthi, bf16[512,512]{1,0:T(8,128)(2,1)S(1)} %get-tuple-element.77.mtlo), custom_call_target="tpu_custom_call" | custom-call | bytes 1083392 | tf_op jit(solution)/shard_map/pallas_call | solution.py:22
  53.3 0.7 collective-permute-start.10
  54.0 2.1 %shard_map.119 = (bf16[2,512,512]{2,1,0:T(8,128)(2,1)S(1)}, bf16[2,512,512]{2,1,0:T(8,128)(2,1)S(1)}, f32[8,512]{1,0:T(8,128)S(1)}) custom-call(f32[1,512]{1,0:T(1,128)S(1)} %get-tuple-element.82.after, bf16[2112,128]{1,0:T(8,128)(2,1)S(1)} %collective-permute-done.9.relay, bf16[512,512]{1,0:T(8,128)(2,1)S(1)} %get-tuple-element.54.chi, ...), custom_call_target="tpu_custom_call" | custom-call | bytes 1591296 | tf_op jit(solution)/shard_map/pallas_call | solution.py:22
  56.3 0.7 collective-permute-start.11
  56.9 4.0 %shard_map.121 = (bf16[4,512,512]{2,1,0:T(8,128)(2,1)S(1)}, bf16[4,512,512]{2,1,0:T(8,128)(2,1)S(1)}) custom-call(f32[1,512]{1,0:T(1,128)S(1)} %get-tuple-element.88.after, f32[16,512]{1,0:T(8,128)S(1)} %shard_map.115.table, bf16[512,512]{1,0:T(8,128)(2,1)S(1)} %get-tuple-element.57.after.mthi, bf16[512,512]{1,0:T(8,128)(2,1)S(1)} %get-tuple-element.77.mtlo), custom_call_target="tpu_custom_call" | custom-call | bytes 1083392 | tf_op jit(solution)/shard_map/pallas_call | solution.py:22
  60.9 3.9 %shard_map.122 = f32[32,8,128]{2,1,0:T(8,128)S(1)} custom-call(f32[1,512]{1,0:T(1,128)S(1)} %get-tuple-element.87.acc, f32[1,512]{1,0:T(1,128)S(1)} %collective-permute-done.11.got, bf16[512,512]{1,0:T(8,128)(2,1)S(1)} %get-tuple-element.70.b1hi, bf16[512,512]{1,0:T(8,128)(2,1)S(1)} %get-tuple-element.71.b1lo, bf16[512,512]{1,0:T(8,128)(2,1)S(1)} %get-tuple-element.72.b2hi, ...), custom_call_target="tpu_custom_call" | custom-call | bytes 13703168 | tf_op jit(solution)/shard_map/pallas_call | solution.py:22
  64.8 12.5 %all_to_all.11.parts = f32[32,8,128]{2,1,0:T(8,128)S(1)} all-to-all(f32[32,8,128]{2,1,0:T(8,128)S(1)} %shard_map.122), channel_id=1, replica_groups=mesh['z'=4,'y'=2,'obs'=4] {'z','y','obs'}, dimensions={0} | all-to-all | bytes 262144 | tf_op jit(solution)/shard_map/all_to_all | solution.py:818
  (28 shorter events, 3.2 us)
Async XLA Ops:
  2.9 20.9 %copy-start.2 = (f32[128,512]{1,0:T(8,128)S(1)}, f32[128,512]{1,0:T(8,128)}, u32[]{:S(2)}) copy-start(f32[128,512]{1,0:T(8,128)} %gain.1) | copy-start | bytes 786436
  23.7 9.7 %copy-start.1 = (f32[512,512]{1,0:T(8,128)S(1)}, f32[512,512]{1,0:T(8,128)}, u32[]{:S(2)}) copy-start(f32[512,512]{1,0:T(8,128)} %cov.1) | copy-start | bytes 3145732
  25.0 8.4 %copy-start = (f32[512,512]{1,0:T(8,128)S(1)}, f32[512,512]{1,0:T(8,128)}, u32[]{:S(2)}) copy-start(f32[512,512]{1,0:T(8,128)} %trans.1) | copy-start | bytes 3145732
  25.0 8.3 %collective-permute-start.4 = (f32[128,512]{1,0:T(8,128)S(1)}, f32[128,512]{1,0:T(8,128)S(1)}, u32[]{:S(2)}, u32[]{:S(2)}) collective-permute-start(f32[128,512]{1,0:T(8,128)S(1)} %get-tuple-element.56.one), channel_id=1, source_target_pairs={{0,2},{1,3},{2,0},{3,1},{4,6},{5,7},{6,4},{7,5},{8,10},{9,11},{10,... | collective-permute-start | bytes 786440 | tf_op jit(solution)/shard_map/ppermute | solution.py:720
  25.6 10.0 %collective-permute-start.3 = (bf16[2112,128]{1,0:T(8,128)(2,1)S(1)}, bf16[2112,128]{1,0:T(8,128)(2,1)S(1)}, u32[]{:S(2)}, u32[]{:S(2)}) collective-permute-start(bf16[2112,128]{1,0:T(8,128)(2,1)S(1)} %get-tuple-element.49), channel_id=1, source_target_pairs={{5,21},{28,13},{30,15},{7,23},{3,19},{26,11},{24,9},{1,17}} | collective-permute-start | bytes 1622024 | tf_op jit(solution)/shard_map/ppermute | solution.py:723
  26.3 9.3 %collective-permute-start.2 = (bf16[2112,128]{1,0:T(8,128)(2,1)S(1)}, bf16[2112,128]{1,0:T(8,128)(2,1)S(1)}, u32[]{:S(2)}, u32[]{:S(2)}) collective-permute-start(bf16[2112,128]{1,0:T(8,128)(2,1)S(1)} %get-tuple-element.49), channel_id=1, source_target_pairs={{29,21},{20,13},{22,15},{31,23},{27,19},{18,11},{16,9},{25,17}} | collective-permute-start | bytes 1622024 | tf_op jit(solution)/shard_map/ppermute | solution.py:723
  27.0 14.6 %collective-permute-start.1 = (bf16[2112,128]{1,0:T(8,128)(2,1)S(1)}, bf16[2112,128]{1,0:T(8,128)(2,1)S(1)}, u32[]{:S(2)}, u32[]{:S(2)}) collective-permute-start(bf16[2112,128]{1,0:T(8,128)(2,1)S(1)} %get-tuple-element.49), channel_id=1, source_target_pairs={{13,21},{4,13},{6,15},{15,23},{11,19},{2,11},{0,9},{9,17}} | collective-permute-start | bytes 1622024 | tf_op jit(solution)/shard_map/ppermute | solution.py:723
  31.1 10.5 %collective-permute-start = (bf16[2112,128]{1,0:T(8,128)(2,1)S(1)}, bf16[2112,128]{1,0:T(8,128)(2,1)S(1)}, u32[]{:S(2)}, u32[]{:S(2)}) collective-permute-start(bf16[2112,128]{1,0:T(8,128)(2,1)S(1)} %get-tuple-element.49), channel_id=1, source_target_pairs={{12,13},{14,15},{10,11},{8,9}} | collective-permute-start | bytes 1622024 | tf_op jit(solution)/shard_map/ppermute | solution.py:727
  33.3 2.0 %collective-permute-start.5 = (f32[2,128,512]{2,1,0:T(8,128)S(1)}, f32[2,128,512]{2,1,0:T(8,128)S(1)}, u32[]{:S(2)}, u32[]{:S(2)}) collective-permute-start(f32[2,128,512]{2,1,0:T(8,128)S(1)} %shard_map.107.held), channel_id=1, source_target_pairs={{0,1},{1,0},{2,3},{3,2},{4,5},{5,4},{6,7},{7,6},{8,9},{9,8},{10,11... | collective-permute-start | bytes 1572872 | tf_op jit(solution)/shard_map/ppermute | solution.py:720
  42.5 11.6 %collective-permute-start.9 = (bf16[2112,128]{1,0:T(8,128)(2,1)S(1)}, bf16[2112,128]{1,0:T(8,128)(2,1)S(1)}, u32[]{:S(2)}, u32[]{:S(2)}) collective-permute-start(bf16[2112,128]{1,0:T(8,128)(2,1)S(1)} %shard_map.118), channel_id=1, source_target_pairs={{11,19},{17,9}} | collective-permute-start | bytes 1622024 | tf_op jit(solution)/shard_map/ppermute | solution.py:751
  43.2 0.7 collective-permute-start.6
  43.9 4.7 %collective-permute-start.7 = (f32[1,512]{1,0:T(1,128)S(1)}, f32[1,512]{1,0:T(1,128)S(1)}, u32[]{:S(2)}, u32[]{:S(2)}) collective-permute-start(f32[1,512]{1,0:T(1,128)S(1)} %get-tuple-element.69.after), channel_id=1, source_target_pairs={{13,15}} | collective-permute-start | bytes 6152 | tf_op jit(solution)/shard_map/ppermute | solution.py:757
  49.1 4.0 %collective-permute-start.8 = (f32[1,512]{1,0:T(1,128)S(1)}, f32[1,512]{1,0:T(1,128)S(1)}, u32[]{:S(2)}, u32[]{:S(2)}) collective-permute-start(f32[1,512]{1,0:T(1,128)S(1)} %get-tuple-element.75.after), channel_id=1, source_target_pairs={{15,23}} | collective-permute-start | bytes 6152 | tf_op jit(solution)/shard_map/ppermute | solution.py:757
  53.3 2.9 %collective-permute-start.10 = (f32[1,512]{1,0:T(1,128)S(1)}, f32[1,512]{1,0:T(1,128)S(1)}, u32[]{:S(2)}, u32[]{:S(2)}) collective-permute-start(f32[1,512]{1,0:T(1,128)S(1)} %get-tuple-element.82.after), channel_id=1, source_target_pairs={{23,19}} | collective-permute-start | bytes 6152 | tf_op jit(solution)/shard_map/ppermute | solution.py:757
  56.3 4.7 %collective-permute-start.11 = (f32[1,512]{1,0:T(1,128)S(1)}, f32[1,512]{1,0:T(1,128)S(1)}, u32[]{:S(2)}, u32[]{:S(2)}) collective-permute-start(f32[1,512]{1,0:T(1,128)S(1)} %get-tuple-element.88.after), channel_id=1, source_target_pairs={{19,9}} | collective-permute-start | bytes 6152 | tf_op jit(solution)/shard_map/ppermute | solution.py:757

commit v23 on v22

--- a/solution.py
+++ b/solution.py
@@ -808,7 +808,7 @@
             )
     (answer,) = run(
         last_kernel,
-        [((spans * peers, 8, LANES), F32)],
+        [((spans * peers, 4, LANES), F32)],
         [
             acc, received, b1hi, b1lo, b2hi, b2lo, bchi, bclo, off, offset, table, pthi, ptlo, mthi, mtlo,
             nexthi, nextlo, next_off, khi, klo, more_khi, more_klo,

time: 78.2 us -> 77.4 us (0.990)
  blocking collectives: 33.3 us -> 32.5 us
    all_to_all x1, blocking collectives: 12.5 us -> 11.7 us  [local(): lax.all_to_all(answer, everyone, split_axis=0, concat_axis=0, tiled=True)]
where the time goes in v23:
time: 77.4 us; the launch traced here: 77.1 us
  blocking collectives  32.5 us (42%)
  Pallas kernels  24.1 us (31%)
  starting transfers between devices  10.9 us (14%)
  waiting for transfers between devices  8.59 us (11%)
  between operations  0.95 us (1%)
    pallas_call x20, Pallas kernels, run(): pl.pallas_call(body, out_shape=[jax.ShapeDtypeStruct(s, d) for s, d in ou...  24.1 us
    all_to_all x1, blocking collectives, local(): lax.all_to_all(sent, ('y', 'obs'), split_axis=0, concat_axis=0, tiled=True)  20.8 us
    all_to_all x1, blocking collectives, local(): lax.all_to_all(answer, everyone, split_axis=0, concat_axis=0, tiled=True)  11.7 us
    ppermute x3, waiting for transfers between devices, plane_sum(): lax.ppermute(pay, everyone, [((owner_plane(p) + s) % planes * spans + pla...  5.91 us
    ppermute x3, starting transfers between devices, plane_sum(): lax.ppermute(pay, everyone, [((owner_plane(p) + s) % planes * spans + pla...  5.47 us
    ppermute x5, starting transfers between devices, local(): received = lax.ppermute(y, everyone, [(owner(source), owner(target))])  3.35 us
    ppermute x2, waiting for transfers between devices, swap(): return lax.ppermute(x, 'obs', [(i, i ^ bit) for i in range(peers)])  2.63 us
  transfers between devices with their start and end apart: 12, of which 3 were waited for; matrix products, arithmetic and copies ran while one was open for 0% of the time, Pallas kernels for 20%

profile of v23, /device:TPU:0, one launch (start us, length us, event | category | flops | bytes accessed | tf_op | source)
XLA Modules:
  0.0 77.1 jit_solution(1299994748286791713)
XLA Ops:
  0.6 2.2 %shard_map.104 = bf16[8,520,128]{2,1,0:T(8,128)(2,1)} custom-call(s32[8]{0:T(128)} %day.1, s32[8]{0:T(128)} %count.1, bf16[1024,512]{1,0:T(8,128)(2,1)} %rows.1, bf16[8,128]{1,0:T(8,128)(2,1)} %bitcast.2, f32[1,128]{1,0:T(1,128)} %bitcast.3, f32[2,512]{1,0:T(2,128)} %damping.1), custom_call_target="tpu_custom_call" | custom-call | bytes 1055296 | tf_op jit(solution)/shard_map/pallas_call | solution.py:22
  2.9 20.8 %all_to_all.10.got = bf16[8,520,128]{2,1,0:T(8,128)(2,1)S(1)} all-to-all(bf16[8,520,128]{2,1,0:T(8,128)(2,1)} %shard_map.104), channel_id=1, replica_groups=mesh['z'=4,'y'=2,'obs'=4] {'y','obs'}, dimensions={0} | all-to-all | bytes 2129920 | tf_op jit(solution)/shard_map/all_to_all | solution.py:704
  23.7 1.2 %shard_map.105 = (f32[20,128,128]{2,1,0:T(8,128)S(1)}, f32[64,128]{1,0:T(8,128)S(1)}, bf16[2112,128]{1,0:T(8,128)(2,1)S(1)}, f32[1,512]{1,0:T(1,128)S(1)}, f32[128,512]{1,0:T(8,128)S(1)}) custom-call(bf16[8,520,128]{2,1,0:T(8,128)(2,1)S(1)} %all_to_all.10.got, f32[128,512]{1,0:T(8,128)S(1)} %copy-done.2), custom_call_target="tpu_custom_call" | custom-call | flops 1073741824 | bytes 1327104 | tf_op jit(solution)/shard_map/pallas_call | solution.py:22
  25.6 0.7 collective-permute-start.3
  26.3 0.7 collective-permute-start.2
  27.0 4.1 %collective-permute-start.1 = (bf16[2112,128]{1,0:T(8,128)(2,1)S(1)}, bf16[2112,128]{1,0:T(8,128)(2,1)S(1)}, u32[]{:S(2)}, u32[]{:S(2)}) collective-permute-start(bf16[2112,128]{1,0:T(8,128)(2,1)S(1)} %get-tuple-element.49), channel_id=1, source_target_pairs={{13,21},{4,13},{6,15},{15,23},{11,19},{2,11},{0,9},{9,17}} | collective-permute-start | bytes 1622024 | tf_op jit(solution)/shard_map/ppermute | solution.py:723
  31.1 0.7 collective-permute-start
  31.8 1.5 %collective-permute-done.4.two = f32[128,512]{1,0:T(8,128)S(1)} collective-permute-done((f32[128,512]{1,0:T(8,128)S(1)}, f32[128,512]{1,0:T(8,128)S(1)}, u32[]{:S(2)}, u32[]{:S(2)}) %collective-permute-start.4) | collective-permute-done | bytes 262176 | tf_op jit(solution)/shard_map/ppermute | solution.py:720
  33.4 0.7 shard_map.106
  34.1 1.2 %collective-permute-done.5.got = f32[2,128,512]{2,1,0:T(8,128)S(1)} collective-permute-done((f32[2,128,512]{2,1,0:T(8,128)S(1)}, f32[2,128,512]{2,1,0:T(8,128)S(1)}, u32[]{:S(2)}, u32[]{:S(2)}) %collective-permute-start.5) | collective-permute-done | bytes 524320 | tf_op jit(solution)/shard_map/ppermute | solution.py:720
  35.6 5.9 %collective-permute-done.1.g3 = bf16[2112,128]{1,0:T(8,128)(2,1)S(1)} collective-permute-done((bf16[2112,128]{1,0:T(8,128)(2,1)S(1)}, bf16[2112,128]{1,0:T(8,128)(2,1)S(1)}, u32[]{:S(2)}, u32[]{:S(2)}) %collective-permute-start.1) | collective-permute-done | bytes 540704 | tf_op jit(solution)/shard_map/ppermute | solution.py:723
  41.6 0.9 %shard_map.109 = (bf16[2,512,512]{2,1,0:T(8,128)(2,1)S(1)}, bf16[2,512,512]{2,1,0:T(8,128)(2,1)S(1)}, f32[2,1,512]{2,1,0:T(1,128)S(1)}, f32[2,512]{1,0:T(2,128)S...) custom-call(f32[20,128,128]{2,1,0:T(8,128)S(1)} %get-tuple-element.47.own, f32[64,128]{1,0:T(8,128)S(1)} %get-tuple-element.48.extra, ...), custom_call_target="tpu_custom_call" | custom-call | bytes 6131712 | tf_op jit(solution)/shard_map/pallas_call | solution.py:22
  42.5 0.7 collective-permute-start.9
  43.2 0.7 collective-permute-start.6
  44.6 4.0 %shard_map.112 = (bf16[512,512]{1,0:T(8,128)(2,1)S(1)}, bf16[512,512]{1,0:T(8,128)(2,1)S(1)}, f32[8,512]{1,0:T(8,128)S(1)}, bf16[512,512]{1,0:T(8,128)(2,1)S(1)}, bf16[512,512]{1,0:T(8,128)(2,1)S(1)}) custom-call(f32[1,512]{1,0:T(1,128)S(1)} %get-tuple-element.69.after, ...), custom_call_target="tpu_custom_call", output_to_operand_aliasing={{0}: (8, {}), {1}: (9, {}), {2}: (10, {})} | custom-call | flops 3221225472 | bytes 5269504 | tf_op jit(solution)/shard_map/pallas_call | solution.py:22
  49.1 0.7 collective-permute-start.8
  49.8 1.1 %shard_map.114 = (bf16[512,512]{1,0:T(8,128)(2,1)S(1)}, bf16[512,512]{1,0:T(8,128)(2,1)S(1)}, f32[1,512]{1,0:T(1,128)S(1)}) custom-call(f32[1,512]{1,0:T(1,128)S(1)} %get-tuple-element.75.after, bf16[512,512]{1,0:T(8,128)(2,1)S(1)} %get-tuple-element.70.b1hi, bf16[512,512]{1,0:T(8,128)(2,1)S(1)} %get-tuple-element.71.b1lo, ...), custom_call_target="tpu_custom_call" | custom-call | bytes 2115584 | tf_op jit(solution)/shard_map/pallas_call | solution.py:22
  50.9 2.2 %shard_map.116 = (bf16[2,512,512]{2,1,0:T(8,128)(2,1)S(1)}, bf16[2,512,512]{2,1,0:T(8,128)(2,1)S(1)}) custom-call(f32[1,512]{1,0:T(1,128)S(1)} %get-tuple-element.75.after, f32[16,512]{1,0:T(8,128)S(1)} %shard_map.115.table, bf16[512,512]{1,0:T(8,128)(2,1)S(1)} %get-tuple-element.57.after.mthi, bf16[512,512]{1,0:T(8,128)(2,1)S(1)} %get-tuple-element.77.mtlo), custom_call_target="tpu_custom_call" | custom-call | bytes 1083392 | tf_op jit(solution)/shard_map/pallas_call | solution.py:22
  53.3 0.7 collective-permute-start.10
  54.0 2.1 %shard_map.119 = (bf16[2,512,512]{2,1,0:T(8,128)(2,1)S(1)}, bf16[2,512,512]{2,1,0:T(8,128)(2,1)S(1)}, f32[8,512]{1,0:T(8,128)S(1)}) custom-call(f32[1,512]{1,0:T(1,128)S(1)} %get-tuple-element.82.after, bf16[2112,128]{1,0:T(8,128)(2,1)S(1)} %collective-permute-done.9.relay, bf16[512,512]{1,0:T(8,128)(2,1)S(1)} %get-tuple-element.54.chi, ...), custom_call_target="tpu_custom_call" | custom-call | bytes 1591296 | tf_op jit(solution)/shard_map/pallas_call | solution.py:22
  56.3 0.7 collective-permute-start.11
  56.9 4.0 %shard_map.121 = (bf16[4,512,512]{2,1,0:T(8,128)(2,1)S(1)}, bf16[4,512,512]{2,1,0:T(8,128)(2,1)S(1)}) custom-call(f32[1,512]{1,0:T(1,128)S(1)} %get-tuple-element.88.after, f32[16,512]{1,0:T(8,128)S(1)} %shard_map.115.table, bf16[512,512]{1,0:T(8,128)(2,1)S(1)} %get-tuple-element.57.after.mthi, bf16[512,512]{1,0:T(8,128)(2,1)S(1)} %get-tuple-element.77.mtlo), custom_call_target="tpu_custom_call" | custom-call | bytes 1083392 | tf_op jit(solution)/shard_map/pallas_call | solution.py:22
  60.9 3.9 %shard_map.122 = f32[32,4,128]{2,1,0:T(4,128)S(1)} custom-call(f32[1,512]{1,0:T(1,128)S(1)} %get-tuple-element.87.acc, f32[1,512]{1,0:T(1,128)S(1)} %collective-permute-done.11.got, bf16[512,512]{1,0:T(8,128)(2,1)S(1)} %get-tuple-element.70.b1hi, bf16[512,512]{1,0:T(8,128)(2,1)S(1)} %get-tuple-element.71.b1lo, bf16[512,512]{1,0:T(8,128)(2,1)S(1)} %get-tuple-element.72.b2hi, ...), custom_call_target="tpu_custom_call" | custom-call | bytes 13703168 | tf_op jit(solution)/shard_map/pallas_call | solution.py:22
  64.8 11.7 %all_to_all.11.parts = f32[32,4,128]{2,1,0:T(4,128)S(1)} all-to-all(f32[32,4,128]{2,1,0:T(4,128)S(1)} %shard_map.122), channel_id=1, replica_groups=mesh['z'=4,'y'=2,'obs'=4] {'z','y','obs'}, dimensions={0} | all-to-all | bytes 131072 | tf_op jit(solution)/shard_map/all_to_all | solution.py:818
  (28 shorter events, 3.2 us)
Async XLA Ops:
  2.9 20.9 %copy-start.2 = (f32[128,512]{1,0:T(8,128)S(1)}, f32[128,512]{1,0:T(8,128)}, u32[]{:S(2)}) copy-start(f32[128,512]{1,0:T(8,128)} %gain.1) | copy-start | bytes 786436
  23.7 9.7 %copy-start.1 = (f32[512,512]{1,0:T(8,128)S(1)}, f32[512,512]{1,0:T(8,128)}, u32[]{:S(2)}) copy-start(f32[512,512]{1,0:T(8,128)} %cov.1) | copy-start | bytes 3145732
  25.0 8.4 %copy-start = (f32[512,512]{1,0:T(8,128)S(1)}, f32[512,512]{1,0:T(8,128)}, u32[]{:S(2)}) copy-start(f32[512,512]{1,0:T(8,128)} %trans.1) | copy-start | bytes 3145732
  25.0 8.3 %collective-permute-start.4 = (f32[128,512]{1,0:T(8,128)S(1)}, f32[128,512]{1,0:T(8,128)S(1)}, u32[]{:S(2)}, u32[]{:S(2)}) collective-permute-start(f32[128,512]{1,0:T(8,128)S(1)} %get-tuple-element.56.one), channel_id=1, source_target_pairs={{0,2},{1,3},{2,0},{3,1},{4,6},{5,7},{6,4},{7,5},{8,10},{9,11},{10,... | collective-permute-start | bytes 786440 | tf_op jit(solution)/shard_map/ppermute | solution.py:720
  25.6 10.0 %collective-permute-start.3 = (bf16[2112,128]{1,0:T(8,128)(2,1)S(1)}, bf16[2112,128]{1,0:T(8,128)(2,1)S(1)}, u32[]{:S(2)}, u32[]{:S(2)}) collective-permute-start(bf16[2112,128]{1,0:T(8,128)(2,1)S(1)} %get-tuple-element.49), channel_id=1, source_target_pairs={{5,21},{28,13},{30,15},{7,23},{3,19},{26,11},{24,9},{1,17}} | collective-permute-start | bytes 1622024 | tf_op jit(solution)/shard_map/ppermute | solution.py:723
  26.3 9.3 %collective-permute-start.2 = (bf16[2112,128]{1,0:T(8,128)(2,1)S(1)}, bf16[2112,128]{1,0:T(8,128)(2,1)S(1)}, u32[]{:S(2)}, u32[]{:S(2)}) collective-permute-start(bf16[2112,128]{1,0:T(8,128)(2,1)S(1)} %get-tuple-element.49), channel_id=1, source_target_pairs={{29,21},{20,13},{22,15},{31,23},{27,19},{18,11},{16,9},{25,17}} | collective-permute-start | bytes 1622024 | tf_op jit(solution)/shard_map/ppermute | solution.py:723
  27.0 14.6 %collective-permute-start.1 = (bf16[2112,128]{1,0:T(8,128)(2,1)S(1)}, bf16[2112,128]{1,0:T(8,128)(2,1)S(1)}, u32[]{:S(2)}, u32[]{:S(2)}) collective-permute-start(bf16[2112,128]{1,0:T(8,128)(2,1)S(1)} %get-tuple-element.49), channel_id=1, source_target_pairs={{13,21},{4,13},{6,15},{15,23},{11,19},{2,11},{0,9},{9,17}} | collective-permute-start | bytes 1622024 | tf_op jit(solution)/shard_map/ppermute | solution.py:723
  31.1 10.5 %collective-permute-start = (bf16[2112,128]{1,0:T(8,128)(2,1)S(1)}, bf16[2112,128]{1,0:T(8,128)(2,1)S(1)}, u32[]{:S(2)}, u32[]{:S(2)}) collective-permute-start(bf16[2112,128]{1,0:T(8,128)(2,1)S(1)} %get-tuple-element.49), channel_id=1, source_target_pairs={{12,13},{14,15},{10,11},{8,9}} | collective-permute-start | bytes 1622024 | tf_op jit(solution)/shard_map/ppermute | solution.py:727
  33.3 2.0 %collective-permute-start.5 = (f32[2,128,512]{2,1,0:T(8,128)S(1)}, f32[2,128,512]{2,1,0:T(8,128)S(1)}, u32[]{:S(2)}, u32[]{:S(2)}) collective-permute-start(f32[2,128,512]{2,1,0:T(8,128)S(1)} %shard_map.107.held), channel_id=1, source_target_pairs={{0,1},{1,0},{2,3},{3,2},{4,5},{5,4},{6,7},{7,6},{8,9},{9,8},{10,11... | collective-permute-start | bytes 1572872 | tf_op jit(solution)/shard_map/ppermute | solution.py:720
  42.5 11.6 %collective-permute-start.9 = (bf16[2112,128]{1,0:T(8,128)(2,1)S(1)}, bf16[2112,128]{1,0:T(8,128)(2,1)S(1)}, u32[]{:S(2)}, u32[]{:S(2)}) collective-permute-start(bf16[2112,128]{1,0:T(8,128)(2,1)S(1)} %shard_map.118), channel_id=1, source_target_pairs={{11,19},{17,9}} | collective-permute-start | bytes 1622024 | tf_op jit(solution)/shard_map/ppermute | solution.py:751
  43.2 0.7 collective-permute-start.6
  43.9 4.7 %collective-permute-start.7 = (f32[1,512]{1,0:T(1,128)S(1)}, f32[1,512]{1,0:T(1,128)S(1)}, u32[]{:S(2)}, u32[]{:S(2)}) collective-permute-start(f32[1,512]{1,0:T(1,128)S(1)} %get-tuple-element.69.after), channel_id=1, source_target_pairs={{13,15}} | collective-permute-start | bytes 6152 | tf_op jit(solution)/shard_map/ppermute | solution.py:757
  49.1 4.0 %collective-permute-start.8 = (f32[1,512]{1,0:T(1,128)S(1)}, f32[1,512]{1,0:T(1,128)S(1)}, u32[]{:S(2)}, u32[]{:S(2)}) collective-permute-start(f32[1,512]{1,0:T(1,128)S(1)} %get-tuple-element.75.after), channel_id=1, source_target_pairs={{15,23}} | collective-permute-start | bytes 6152 | tf_op jit(solution)/shard_map/ppermute | solution.py:757
  53.3 2.9 %collective-permute-start.10 = (f32[1,512]{1,0:T(1,128)S(1)}, f32[1,512]{1,0:T(1,128)S(1)}, u32[]{:S(2)}, u32[]{:S(2)}) collective-permute-start(f32[1,512]{1,0:T(1,128)S(1)} %get-tuple-element.82.after), channel_id=1, source_target_pairs={{23,19}} | collective-permute-start | bytes 6152 | tf_op jit(solution)/shard_map/ppermute | solution.py:757
  56.3 4.7 %collective-permute-start.11 = (f32[1,512]{1,0:T(1,128)S(1)}, f32[1,512]{1,0:T(1,128)S(1)}, u32[]{:S(2)}, u32[]{:S(2)}) collective-permute-start(f32[1,512]{1,0:T(1,128)S(1)} %get-tuple-element.88.after), channel_id=1, source_target_pairs={{19,9}} | collective-permute-start | bytes 6152 | tf_op jit(solution)/shard_map/ppermute | solution.py:757

commit v24 on v23

--- a/solution.py
+++ b/solution.py
@@ -804,7 +804,7 @@
             acc, y = run(hop_kernel, [row, row], [(khi, ANY), acc, received, bchi, bclo, offset])
         if target == spans - 4:
             more_khi, more_klo = run(
-                functools.partial(pairs_kernel, 2), [((4,) + full, BF16)] * 2, [(y, ANY), table, mthi, mtlo]
+                functools.partial(pairs_kernel, 2), [((3,) + full, BF16)] * 2, [(y, ANY), table, mthi, mtlo]
             )
     (answer,) = run(
         last_kernel,

time: 77.4 us -> 77.4 us (level)
  transfers between devices with their start and end apart: 12 -> 12, of which waited for: 3 -> 3; matrix products, arithmetic and copies ran while one was open for 0% -> 0% of each run, Pallas kernels for 20% -> 19%
where the time goes in v24:
time: 77.4 us; the launch traced here: 77.1 us
  blocking collectives  33.2 us (43%)
  Pallas kernels  23.4 us (30%)
  starting transfers between devices  10.9 us (14%)
  waiting for transfers between devices  8.6 us (11%)
  between operations  0.95 us (1%)
    pallas_call x20, Pallas kernels, run(): pl.pallas_call(body, out_shape=[jax.ShapeDtypeStruct(s, d) for s, d in ou...  23.4 us
    all_to_all x1, blocking collectives, local(): lax.all_to_all(sent, ('y', 'obs'), split_axis=0, concat_axis=0, tiled=True)  20.8 us
    all_to_all x1, blocking collectives, local(): lax.all_to_all(answer, everyone, split_axis=0, concat_axis=0, tiled=True)  12.4 us
    ppermute x3, waiting for transfers between devices, plane_sum(): lax.ppermute(pay, everyone, [((owner_plane(p) + s) % planes * spans + pla...  5.91 us
    ppermute x3, starting transfers between devices, plane_sum(): lax.ppermute(pay, everyone, [((owner_plane(p) + s) % planes * spans + pla...  5.47 us
    ppermute x5, starting transfers between devices, local(): received = lax.ppermute(y, everyone, [(owner(source), owner(target))])  3.35 us
    ppermute x2, waiting for transfers between devices, swap(): return lax.ppermute(x, 'obs', [(i, i ^ bit) for i in range(peers)])  2.63 us
  transfers between devices with their start and end apart: 12, of which 3 were waited for; matrix products, arithmetic and copies ran while one was open for 0% of the time, Pallas kernels for 19%

profile of v24, /device:TPU:0, one launch (start us, length us, event | category | flops | bytes accessed | tf_op | source)
XLA Modules:
  0.0 77.1 jit_solution(9995024113592558496)
XLA Ops:
  0.6 2.2 %shard_map.104 = bf16[8,520,128]{2,1,0:T(8,128)(2,1)} custom-call(s32[8]{0:T(128)} %day.1, s32[8]{0:T(128)} %count.1, bf16[1024,512]{1,0:T(8,128)(2,1)} %rows.1, bf16[8,128]{1,0:T(8,128)(2,1)} %bitcast.2, f32[1,128]{1,0:T(1,128)} %bitcast.3, f32[2,512]{1,0:T(2,128)} %damping.1), custom_call_target="tpu_custom_call" | custom-call | bytes 1055296 | tf_op jit(solution)/shard_map/pallas_call | solution.py:22
  2.9 20.8 %all_to_all.10.got = bf16[8,520,128]{2,1,0:T(8,128)(2,1)S(1)} all-to-all(bf16[8,520,128]{2,1,0:T(8,128)(2,1)} %shard_map.104), channel_id=1, replica_groups=mesh['z'=4,'y'=2,'obs'=4] {'y','obs'}, dimensions={0} | all-to-all | bytes 2129920 | tf_op jit(solution)/shard_map/all_to_all | solution.py:704
  23.7 1.2 %shard_map.105 = (f32[20,128,128]{2,1,0:T(8,128)S(1)}, f32[64,128]{1,0:T(8,128)S(1)}, bf16[2112,128]{1,0:T(8,128)(2,1)S(1)}, f32[1,512]{1,0:T(1,128)S(1)}, f32[128,512]{1,0:T(8,128)S(1)}) custom-call(bf16[8,520,128]{2,1,0:T(8,128)(2,1)S(1)} %all_to_all.10.got, f32[128,512]{1,0:T(8,128)S(1)} %copy-done.2), custom_call_target="tpu_custom_call" | custom-call | flops 1073741824 | bytes 1327104 | tf_op jit(solution)/shard_map/pallas_call | solution.py:22
  25.6 0.7 collective-permute-start.3
  26.3 0.7 collective-permute-start.2
  27.0 4.1 %collective-permute-start.1 = (bf16[2112,128]{1,0:T(8,128)(2,1)S(1)}, bf16[2112,128]{1,0:T(8,128)(2,1)S(1)}, u32[]{:S(2)}, u32[]{:S(2)}) collective-permute-start(bf16[2112,128]{1,0:T(8,128)(2,1)S(1)} %get-tuple-element.49), channel_id=1, source_target_pairs={{13,21},{4,13},{6,15},{15,23},{11,19},{2,11},{0,9},{9,17}} | collective-permute-start | bytes 1622024 | tf_op jit(solution)/shard_map/ppermute | solution.py:723
  31.1 0.7 collective-permute-start
  31.8 1.5 %collective-permute-done.4.two = f32[128,512]{1,0:T(8,128)S(1)} collective-permute-done((f32[128,512]{1,0:T(8,128)S(1)}, f32[128,512]{1,0:T(8,128)S(1)}, u32[]{:S(2)}, u32[]{:S(2)}) %collective-permute-start.4) | collective-permute-done | bytes 262176 | tf_op jit(solution)/shard_map/ppermute | solution.py:720
  33.4 0.7 shard_map.106
  34.1 1.2 %collective-permute-done.5.got = f32[2,128,512]{2,1,0:T(8,128)S(1)} collective-permute-done((f32[2,128,512]{2,1,0:T(8,128)S(1)}, f32[2,128,512]{2,1,0:T(8,128)S(1)}, u32[]{:S(2)}, u32[]{:S(2)}) %collective-permute-start.5) | collective-permute-done | bytes 524320 | tf_op jit(solution)/shard_map/ppermute | solution.py:720
  35.6 5.9 %collective-permute-done.1.g3 = bf16[2112,128]{1,0:T(8,128)(2,1)S(1)} collective-permute-done((bf16[2112,128]{1,0:T(8,128)(2,1)S(1)}, bf16[2112,128]{1,0:T(8,128)(2,1)S(1)}, u32[]{:S(2)}, u32[]{:S(2)}) %collective-permute-start.1) | collective-permute-done | bytes 540704 | tf_op jit(solution)/shard_map/ppermute | solution.py:723
  41.6 0.9 %shard_map.109 = (bf16[2,512,512]{2,1,0:T(8,128)(2,1)S(1)}, bf16[2,512,512]{2,1,0:T(8,128)(2,1)S(1)}, f32[2,1,512]{2,1,0:T(1,128)S(1)}, f32[2,512]{1,0:T(2,128)S...) custom-call(f32[20,128,128]{2,1,0:T(8,128)S(1)} %get-tuple-element.47.own, f32[64,128]{1,0:T(8,128)S(1)} %get-tuple-element.48.extra, ...), custom_call_target="tpu_custom_call" | custom-call | bytes 6131712 | tf_op jit(solution)/shard_map/pallas_call | solution.py:22
  42.5 0.7 collective-permute-start.9
  43.9 0.7 collective-permute-start.7
  44.6 4.0 %shard_map.112 = (bf16[512,512]{1,0:T(8,128)(2,1)S(1)}, bf16[512,512]{1,0:T(8,128)(2,1)S(1)}, f32[8,512]{1,0:T(8,128)S(1)}, bf16[512,512]{1,0:T(8,128)(2,1)S(1)}, bf16[512,512]{1,0:T(8,128)(2,1)S(1)}) custom-call(f32[1,512]{1,0:T(1,128)S(1)} %get-tuple-element.69.after, ...), custom_call_target="tpu_custom_call", output_to_operand_aliasing={{0}: (8, {}), {1}: (9, {}), {2}: (10, {})} | custom-call | flops 3221225472 | bytes 5269504 | tf_op jit(solution)/shard_map/pallas_call | solution.py:22
  49.1 0.7 collective-permute-start.8
  49.8 1.1 %shard_map.114 = (bf16[512,512]{1,0:T(8,128)(2,1)S(1)}, bf16[512,512]{1,0:T(8,128)(2,1)S(1)}, f32[1,512]{1,0:T(1,128)S(1)}) custom-call(f32[1,512]{1,0:T(1,128)S(1)} %get-tuple-element.75.after, bf16[512,512]{1,0:T(8,128)(2,1)S(1)} %get-tuple-element.70.b1hi, bf16[512,512]{1,0:T(8,128)(2,1)S(1)} %get-tuple-element.71.b1lo, ...), custom_call_target="tpu_custom_call" | custom-call | bytes 2115584 | tf_op jit(solution)/shard_map/pallas_call | solution.py:22
  50.9 2.2 %shard_map.116 = (bf16[2,512,512]{2,1,0:T(8,128)(2,1)S(1)}, bf16[2,512,512]{2,1,0:T(8,128)(2,1)S(1)}) custom-call(f32[1,512]{1,0:T(1,128)S(1)} %get-tuple-element.75.after, f32[16,512]{1,0:T(8,128)S(1)} %shard_map.115.table, bf16[512,512]{1,0:T(8,128)(2,1)S(1)} %get-tuple-element.57.after.mthi, bf16[512,512]{1,0:T(8,128)(2,1)S(1)} %get-tuple-element.77.mtlo), custom_call_target="tpu_custom_call" | custom-call | bytes 1083392 | tf_op jit(solution)/shard_map/pallas_call | solution.py:22
  53.3 0.7 collective-permute-start.10
  54.1 2.1 %shard_map.119 = (bf16[2,512,512]{2,1,0:T(8,128)(2,1)S(1)}, bf16[2,512,512]{2,1,0:T(8,128)(2,1)S(1)}, f32[8,512]{1,0:T(8,128)S(1)}) custom-call(f32[1,512]{1,0:T(1,128)S(1)} %get-tuple-element.82.after, bf16[2112,128]{1,0:T(8,128)(2,1)S(1)} %collective-permute-done.9.relay, bf16[512,512]{1,0:T(8,128)(2,1)S(1)} %get-tuple-element.54.chi, ...), custom_call_target="tpu_custom_call" | custom-call | bytes 1591296 | tf_op jit(solution)/shard_map/pallas_call | solution.py:22
  56.3 0.7 collective-permute-start.11
  56.9 3.0 %shard_map.121 = (bf16[3,512,512]{2,1,0:T(8,128)(2,1)S(1)}, bf16[3,512,512]{2,1,0:T(8,128)(2,1)S(1)}) custom-call(f32[1,512]{1,0:T(1,128)S(1)} %get-tuple-element.88.after, f32[16,512]{1,0:T(8,128)S(1)} %shard_map.115.table, bf16[512,512]{1,0:T(8,128)(2,1)S(1)} %get-tuple-element.57.after.mthi, bf16[512,512]{1,0:T(8,128)(2,1)S(1)} %get-tuple-element.77.mtlo), custom_call_target="tpu_custom_call" | custom-call | bytes 1083392 | tf_op jit(solution)/shard_map/pallas_call | solution.py:22
  60.0 4.1 %shard_map.122 = f32[32,4,128]{2,1,0:T(4,128)S(1)} custom-call(f32[1,512]{1,0:T(1,128)S(1)} %get-tuple-element.87.acc, f32[1,512]{1,0:T(1,128)S(1)} %collective-permute-done.11.got, bf16[512,512]{1,0:T(8,128)(2,1)S(1)} %get-tuple-element.70.b1hi, bf16[512,512]{1,0:T(8,128)(2,1)S(1)} %get-tuple-element.71.b1lo, bf16[512,512]{1,0:T(8,128)(2,1)S(1)} %get-tuple-element.72.b2hi, ...), custom_call_target="tpu_custom_call" | custom-call | bytes 12654592 | tf_op jit(solution)/shard_map/pallas_call | solution.py:22
  64.1 12.4 %all_to_all.11.parts = f32[32,4,128]{2,1,0:T(4,128)S(1)} all-to-all(f32[32,4,128]{2,1,0:T(4,128)S(1)} %shard_map.122), channel_id=1, replica_groups=mesh['z'=4,'y'=2,'obs'=4] {'z','y','obs'}, dimensions={0} | all-to-all | bytes 131072 | tf_op jit(solution)/shard_map/all_to_all | solution.py:818
  (28 shorter events, 3.2 us)
Async XLA Ops:
  2.9 20.9 %copy-start.2 = (f32[128,512]{1,0:T(8,128)S(1)}, f32[128,512]{1,0:T(8,128)}, u32[]{:S(2)}) copy-start(f32[128,512]{1,0:T(8,128)} %gain.1) | copy-start | bytes 786436
  23.7 9.7 %copy-start.1 = (f32[512,512]{1,0:T(8,128)S(1)}, f32[512,512]{1,0:T(8,128)}, u32[]{:S(2)}) copy-start(f32[512,512]{1,0:T(8,128)} %cov.1) | copy-start | bytes 3145732
  25.0 8.4 %copy-start = (f32[512,512]{1,0:T(8,128)S(1)}, f32[512,512]{1,0:T(8,128)}, u32[]{:S(2)}) copy-start(f32[512,512]{1,0:T(8,128)} %trans.1) | copy-start | bytes 3145732
  25.0 8.3 %collective-permute-start.4 = (f32[128,512]{1,0:T(8,128)S(1)}, f32[128,512]{1,0:T(8,128)S(1)}, u32[]{:S(2)}, u32[]{:S(2)}) collective-permute-start(f32[128,512]{1,0:T(8,128)S(1)} %get-tuple-element.56.one), channel_id=1, source_target_pairs={{0,2},{1,3},{2,0},{3,1},{4,6},{5,7},{6,4},{7,5},{8,10},{9,11},{10,... | collective-permute-start | bytes 786440 | tf_op jit(solution)/shard_map/ppermute | solution.py:720
  25.6 10.0 %collective-permute-start.3 = (bf16[2112,128]{1,0:T(8,128)(2,1)S(1)}, bf16[2112,128]{1,0:T(8,128)(2,1)S(1)}, u32[]{:S(2)}, u32[]{:S(2)}) collective-permute-start(bf16[2112,128]{1,0:T(8,128)(2,1)S(1)} %get-tuple-element.49), channel_id=1, source_target_pairs={{5,21},{28,13},{30,15},{7,23},{3,19},{26,11},{24,9},{1,17}} | collective-permute-start | bytes 1622024 | tf_op jit(solution)/shard_map/ppermute | solution.py:723
  26.3 9.3 %collective-permute-start.2 = (bf16[2112,128]{1,0:T(8,128)(2,1)S(1)}, bf16[2112,128]{1,0:T(8,128)(2,1)S(1)}, u32[]{:S(2)}, u32[]{:S(2)}) collective-permute-start(bf16[2112,128]{1,0:T(8,128)(2,1)S(1)} %get-tuple-element.49), channel_id=1, source_target_pairs={{29,21},{20,13},{22,15},{31,23},{27,19},{18,11},{16,9},{25,17}} | collective-permute-start | bytes 1622024 | tf_op jit(solution)/shard_map/ppermute | solution.py:723
  27.0 14.6 %collective-permute-start.1 = (bf16[2112,128]{1,0:T(8,128)(2,1)S(1)}, bf16[2112,128]{1,0:T(8,128)(2,1)S(1)}, u32[]{:S(2)}, u32[]{:S(2)}) collective-permute-start(bf16[2112,128]{1,0:T(8,128)(2,1)S(1)} %get-tuple-element.49), channel_id=1, source_target_pairs={{13,21},{4,13},{6,15},{15,23},{11,19},{2,11},{0,9},{9,17}} | collective-permute-start | bytes 1622024 | tf_op jit(solution)/shard_map/ppermute | solution.py:723
  31.1 10.5 %collective-permute-start = (bf16[2112,128]{1,0:T(8,128)(2,1)S(1)}, bf16[2112,128]{1,0:T(8,128)(2,1)S(1)}, u32[]{:S(2)}, u32[]{:S(2)}) collective-permute-start(bf16[2112,128]{1,0:T(8,128)(2,1)S(1)} %get-tuple-element.49), channel_id=1, source_target_pairs={{12,13},{14,15},{10,11},{8,9}} | collective-permute-start | bytes 1622024 | tf_op jit(solution)/shard_map/ppermute | solution.py:727
  33.3 2.0 %collective-permute-start.5 = (f32[2,128,512]{2,1,0:T(8,128)S(1)}, f32[2,128,512]{2,1,0:T(8,128)S(1)}, u32[]{:S(2)}, u32[]{:S(2)}) collective-permute-start(f32[2,128,512]{2,1,0:T(8,128)S(1)} %shard_map.107.held), channel_id=1, source_target_pairs={{0,1},{1,0},{2,3},{3,2},{4,5},{5,4},{6,7},{7,6},{8,9},{9,8},{10,11... | collective-permute-start | bytes 1572872 | tf_op jit(solution)/shard_map/ppermute | solution.py:720
  42.5 11.6 %collective-permute-start.9 = (bf16[2112,128]{1,0:T(8,128)(2,1)S(1)}, bf16[2112,128]{1,0:T(8,128)(2,1)S(1)}, u32[]{:S(2)}, u32[]{:S(2)}) collective-permute-start(bf16[2112,128]{1,0:T(8,128)(2,1)S(1)} %shard_map.118), channel_id=1, source_target_pairs={{11,19},{17,9}} | collective-permute-start | bytes 1622024 | tf_op jit(solution)/shard_map/ppermute | solution.py:751
  43.2 0.7 collective-permute-start.6
  43.9 4.7 %collective-permute-start.7 = (f32[1,512]{1,0:T(1,128)S(1)}, f32[1,512]{1,0:T(1,128)S(1)}, u32[]{:S(2)}, u32[]{:S(2)}) collective-permute-start(f32[1,512]{1,0:T(1,128)S(1)} %get-tuple-element.69.after), channel_id=1, source_target_pairs={{13,15}} | collective-permute-start | bytes 6152 | tf_op jit(solution)/shard_map/ppermute | solution.py:757
  49.1 4.0 %collective-permute-start.8 = (f32[1,512]{1,0:T(1,128)S(1)}, f32[1,512]{1,0:T(1,128)S(1)}, u32[]{:S(2)}, u32[]{:S(2)}) collective-permute-start(f32[1,512]{1,0:T(1,128)S(1)} %get-tuple-element.75.after), channel_id=1, source_target_pairs={{15,23}} | collective-permute-start | bytes 6152 | tf_op jit(solution)/shard_map/ppermute | solution.py:757
  53.3 2.9 %collective-permute-start.10 = (f32[1,512]{1,0:T(1,128)S(1)}, f32[1,512]{1,0:T(1,128)S(1)}, u32[]{:S(2)}, u32[]{:S(2)}) collective-permute-start(f32[1,512]{1,0:T(1,128)S(1)} %get-tuple-element.82.after), channel_id=1, source_target_pairs={{23,19}} | collective-permute-start | bytes 6152 | tf_op jit(solution)/shard_map/ppermute | solution.py:757
  56.3 3.7 %collective-permute-start.11 = (f32[1,512]{1,0:T(1,128)S(1)}, f32[1,512]{1,0:T(1,128)S(1)}, u32[]{:S(2)}, u32[]{:S(2)}) collective-permute-start(f32[1,512]{1,0:T(1,128)S(1)} %get-tuple-element.88.after), channel_id=1, source_target_pairs={{19,9}} | collective-permute-start | bytes 6152 | tf_op jit(solution)/shard_map/ppermute | solution.py:757
